TPU v7x, 32 devices: a whole 2x2x4 slice. The times are simulated.
32 devices in a mesh: pipe: 2 (over x), ep: 16 (over z, y, core).
Axes of the slice: x: 2, y: 2, z: 4, core: 2. Of those that a mesh axis runs over, the one named last changes fastest.
Arguments:
- entering: bfloat16 [2, 1536, 2048], P(None, 'ep'), may hold values from -6 to 6
- rising_prev: bfloat16 [2, 1536, 2048], P('pipe', 'ep'), may hold values from -6 to 6
- falling_cot: bfloat16 [2, 1536, 2048], P('pipe', 'ep'), may hold values from -6 to 6
- falling_saved: bfloat16 [2, 1536, 2048], P('pipe', 'ep'), may hold values from -6 to 6
- targets: bfloat16 [2, 1536, 2048], P(None, 'ep'), may hold values from -6 to 6
- norm_gain: float32 [2, 2048], P('pipe'), may hold values from 0.5 to 1.5
- exit_gain: float32 [2, 2048], P('pipe'), may hold values from 0.5 to 1.5
- w_gate: bfloat16 [2, 16, 2048, 512], P('pipe', 'ep'), may hold values from -0.125 to 0.125
- w_up: bfloat16 [2, 16, 2048, 512], P('pipe', 'ep'), may hold values from -0.125 to 0.125
- w_down: bfloat16 [2, 16, 512, 2048], P('pipe', 'ep'), may hold values from -0.25 to 0.25
- route_ids: int32 [2, 2, 1536, 8], P(None, 'pipe', 'ep'), may hold values from 0 to 15, all different within a row; in each aligned block of 96 rows (0 to 95, 96 to 191, ..., all dimensions but the last counted through in order) at most 52 rows name the same one
- route_gates: float32 [2, 2, 1536, 8], P(None, 'pipe', 'ep'), may hold values from 0.02 to 0.3
- exit_list: int32 [2, 2], replicated, may hold values 0 or 1
Outputs:
- rising_next: bfloat16 [2, 1536, 2048], P('pipe', 'ep')
- falling_next: bfloat16 [2, 1536, 2048], P('pipe', 'ep')
- exit_loss: float32 [2, 2, 1536], P(None, 'pipe', 'ep')
Inputs may be any that keep to these rules, and one draw needn't show every extreme that they name: `route_ids`: in each aligned block of 96 tokens (one device's tokens of one micro-batch at one section) a row names 8 different experts and no expert is named by more than 52 rows; in some blocks an expert is named by exactly 52 rows.
All inputs are finite; a program needn't handle non-finite values.
Results may differ from a plain program's by a relative error of at most 0.0045.
Values may be sent and summed in bfloat16 or wider, within the bound.
No kernel may reach another device: no remote copies, remote signals or barrier semaphores. Data moves between devices by JAX's collectives and lax.ppermute only.
A program may use at most 128 MiB of HBM per device.

v0:
```python
import jax
import jax.numpy as jnp
from jax import lax
from jax.sharding import PartitionSpec as P

EPSILON = 1e-06


def passed_along(block, axis, distance):
    devices = range(lax.axis_size(axis))
    route = [(i - distance, i) for i in devices if i - distance in devices]
    return lax.ppermute(block, axis, route)


def normed(values, gain_row):
    return (
        values * lax.rsqrt(jnp.mean(values * values, axis=-1, keepdims=True) + EPSILON) * gain_row
    )


def norm_pullback(values, gain_row, upstream):
    _, pullback = jax.vjp(lambda argument: normed(argument, gain_row), values)
    return pullback(upstream)[0]


def local_places(choice_ids, capacity, experts):
    flat_choices = choice_ids.reshape(-1)
    onehot = (flat_choices[:, None] == jnp.arange(experts, dtype=jnp.int32)[None, :]).astype(
        jnp.int32
    )
    earlier = jnp.cumsum(onehot, axis=0) - onehot
    slot_rank = jnp.sum(earlier * onehot, axis=1)
    return (flat_choices * capacity + slot_rank).reshape(choice_ids.shape)


def fill_rows(places, slot_values, total_rows):
    feature_width = slot_values.shape[-1]
    empty = jnp.zeros((total_rows, feature_width), jnp.bfloat16)
    return empty.at[places.reshape(-1)].set(slot_values.reshape(-1, feature_width))


def expert_forward(row_block, gate_weight, up_weight, down_weight):
    gate_proj = jnp.dot(row_block, gate_weight, preferred_element_type=jnp.float32)
    second = jnp.dot(row_block, up_weight, preferred_element_type=jnp.float32)
    hidden = (jax.nn.silu(gate_proj) * second).astype(jnp.bfloat16)
    return jnp.dot(hidden, down_weight, preferred_element_type=jnp.float32).astype(jnp.bfloat16)


def expert_backward(row_block, upstream, gate_weight, up_weight, down_weight):
    gate_proj = jnp.dot(row_block, gate_weight, preferred_element_type=jnp.float32)
    second = jnp.dot(row_block, up_weight, preferred_element_type=jnp.float32)
    contract = (((1,), (1,)), ((), ()))
    hidden_grad = lax.dot_general(
        upstream, down_weight, contract, preferred_element_type=jnp.float32
    )
    sigmoid_part = jax.nn.sigmoid(gate_proj)
    activated = gate_proj * sigmoid_part
    gate_grad = (
        hidden_grad * second * sigmoid_part * (1.0 + gate_proj * (1.0 - sigmoid_part))
    ).astype(jnp.bfloat16)
    second_grad = (hidden_grad * activated).astype(jnp.bfloat16)
    returned = lax.dot_general(gate_grad, gate_weight, contract, preferred_element_type=jnp.float32)
    returned = returned + lax.dot_general(
        second_grad, up_weight, contract, preferred_element_type=jnp.float32
    )
    return returned.astype(jnp.bfloat16)


def local(
    entering,
    rising_prev,
    falling_cot,
    falling_saved,
    targets,
    norm_gain,
    exit_gain,
    w_gate,
    w_up,
    w_down,
    route_ids,
    route_gates,
    exit_list,
):
    section_index = lax.axis_index("pipe")
    sections = lax.axis_size("pipe")
    sources = lax.axis_size("ep")
    tok_rows = entering.shape[1]
    feature_width = entering.shape[2]
    top_count = route_ids.shape[3]
    capacity = min(
        tok_rows, tok_rows * top_count // sources + 1 + tok_rows * top_count // (16 * sources)
    )
    total_rows = sources * capacity
    buffer_shape = (sources, capacity, feature_width)
    moved_rise, moved_cot = passed_along((rising_prev[0], falling_cot[0]), "pipe", 1)
    at_start = section_index == 0
    rise_in = jnp.where(at_start, entering[0], moved_rise)
    cotangent = jnp.where(at_start, entering[1], moved_cot).astype(jnp.float32)
    head_rise = jnp.take(exit_list[0], section_index).astype(jnp.float32)
    head_fall = jnp.take(exit_list[1], sections - 1 - section_index).astype(jnp.float32)
    weights = (w_gate[0, 0], w_up[0, 0], w_down[0, 0])
    norm_row = norm_gain[0]
    exit_row = exit_gain[0]
    rise_wide = rise_in.astype(jnp.float32)
    rise_places = local_places(route_ids[0, 0], capacity, sources)
    rise_normal = normed(rise_wide, norm_row).astype(jnp.bfloat16)
    rise_slots = jnp.broadcast_to(rise_normal[:, None, :], (tok_rows, top_count, feature_width))
    rise_send = fill_rows(rise_places, rise_slots, total_rows).reshape(buffer_shape)
    fall_wide = falling_saved[0].astype(jnp.float32)
    fall_places = local_places(route_ids[1, 0], capacity, sources)
    fall_normal = normed(fall_wide, norm_row).astype(jnp.bfloat16)
    fall_slots = jnp.broadcast_to(fall_normal[:, None, :], (tok_rows, top_count, feature_width))
    fall_rows_send = fill_rows(fall_places, fall_slots, total_rows).reshape(buffer_shape)
    slot_cot = (route_gates[1, 0][:, :, None] * cotangent[:, None, :]).astype(jnp.bfloat16)
    fall_cot_send = fill_rows(fall_places, slot_cot, total_rows).reshape(buffer_shape)
    got_rise = lax.all_to_all(rise_send, "ep", split_axis=0, concat_axis=0, tiled=True)
    made_rise = expert_forward(got_rise.reshape(total_rows, feature_width), *weights).reshape(
        buffer_shape
    )
    back_rise = lax.all_to_all(made_rise, "ep", split_axis=0, concat_axis=0, tiled=True)
    got_rows, got_cot = (
        lax.all_to_all(fall_rows_send, "ep", split_axis=0, concat_axis=0, tiled=True),
        lax.all_to_all(fall_cot_send, "ep", split_axis=0, concat_axis=0, tiled=True),
    )
    made_fall = expert_backward(
        got_rows.reshape(total_rows, feature_width),
        got_cot.reshape(total_rows, feature_width),
        *weights
    ).reshape(buffer_shape)
    back_fall = lax.all_to_all(made_fall, "ep", split_axis=0, concat_axis=0, tiled=True)
    rise_picked = back_rise.reshape(total_rows, feature_width)[rise_places].astype(jnp.float32)
    layer_out = rise_wide + jnp.einsum("tk,tkd->td", route_gates[0, 0], rise_picked)
    rise_diff = normed(rise_wide, exit_row) - targets[0].astype(jnp.float32)
    loss_rise = head_rise * 0.5 * jnp.mean(rise_diff * rise_diff, axis=-1)
    norm_grad = jnp.sum(
        back_fall.reshape(total_rows, feature_width)[fall_places].astype(jnp.float32), axis=1
    )
    fall_diff = normed(fall_wide, exit_row) - targets[1].astype(jnp.float32)
    fall_total = cotangent + norm_pullback(fall_wide, norm_row, norm_grad)
    fall_total = fall_total + head_fall * norm_pullback(fall_wide, exit_row, fall_diff)
    loss_fall = head_fall * 0.5 * jnp.mean(fall_diff * fall_diff, axis=-1)
    exit_loss = jnp.stack([loss_rise, loss_fall])[:, None, :]
    return (layer_out.astype(jnp.bfloat16)[None], fall_total.astype(jnp.bfloat16)[None], exit_loss)


def solution(mesh):
    placed = (
        P(None, "ep", None),
        P("pipe", "ep", None),
        P("pipe", "ep", None),
        P("pipe", "ep", None),
        P(None, "ep", None),
        P("pipe", None),
        P("pipe", None),
        P("pipe", "ep", None, None),
        P("pipe", "ep", None, None),
        P("pipe", "ep", None, None),
        P(None, "pipe", "ep", None),
        P(None, "pipe", "ep", None),
        P(),
    )
    return jax.shard_map(
        local,
        mesh=mesh,
        in_specs=placed,
        out_specs=(P("pipe", "ep", None), P("pipe", "ep", None), P(None, "pipe", "ep")),
        check_vma=False,
    )
```

profile of v0, /device:TPU:15, one launch (start us, length us, event | category | flops | bytes accessed | tf_op | source)
XLA Modules:
  0.0 563.7 jit_solution(10145245691748782124)
XLA Ops:
  0.6 0.9 fusion.76
  1.5 0.1 copy.26
  1.6 0.1 eq.66
  1.8 1.7 reduce-window.16
  3.5 0.3 slice_reduce_fusion
  3.8 0.1 mul.293
  3.9 1.2 fusion.54
  5.1 0.1 fusion.64
  5.2 1.2 fusion.42
  6.4 9.0 %scatter_custom_fusion.2 = bf16[832,2048]{1,0:T(8,128)(2,1)} fusion(s32[768]{0:T(1024)S(1)} %fusion.71, bf16[]{:T(256)} %constant.57.clone.1, bf16[96,2048]{1,0:T(8,128)(2,1)S(1)} %fusion.42), kind=kCustom, calls=%fused_computation.11 | custom fusion | bytes 3801090 | tf_op jit(solution)/shard_map/scatter | solution.py:39
  15.3 4.6 reshape.304
  19.9 6.7 %all-to-all-start.3 = ((bf16[16,52,2048]{2,1,0:T(8,128)(2,1)}), bf16[16,52,2048]{2,1,0:T(8,128)(2,1)}, u32[]{:S(2)}, u32[]{:S(2)}) async-start(bf16[16,52,2048]{2,1,0:T(8,128)(2,1)} %reshape.304), calls=%async_computation.3 | async-start | bytes 7340032 | tf_op jit(solution)/shard_map/all_to_all | solution.py:122
  26.6 1.3 collective-permute-start.1
  27.9 0.1 copy.21
  28.0 0.1 mul.295
  28.1 10.8 %collective-permute-done.1 = bf16[96,2048]{1,0:T(8,128)(2,1)S(1)} collective-permute-done((bf16[96,2048]{1,0:T(8,128)(2,1)S(1)}, bf16[96,2048]{1,0:T(8,128)(2,1)S(1)}, u32[]{:S(2)}, u32[]{:S(2)}) %collective-permute-start.1) | collective-permute-done | bytes 393248 | tf_op jit(solution)/shard_map/ppermute | solution.py:12
  38.9 1.1 fusion.60
  40.0 12.8 %scatter_custom_fusion.1 = bf16[832,2048]{1,0:T(8,128)(2,1)} fusion(s32[768]{0:T(1024)S(1)} %fusion.71, f32[96,2048]{1,0:T(8,128)S(1)} %fusion.60, f32[768]{0:T(1024)S(1)} %mul.295, bf16[]{:T(256)} %constant.57.clone.1), kind=kCustom, calls=%fused_computation.10 | custom fusion | flops 3145728 | bytes 4198402 | tf_op jit(solution)/shard_map/scatter | solution.py:39
  52.8 4.6 reshape.301
  57.3 50.5 %all-to-all-done.3 = bf16[16,52,2048]{2,1,0:T(8,128)(2,1)} async-done(((bf16[16,52,2048]{2,1,0:T(8,128)(2,1)}), bf16[16,52,2048]{2,1,0:T(8,128)(2,1)}, u32[]{:S(2)}, u32[]{:S(2)}) %all-to-all-start.3) | async-done | bytes 3407904 | tf_op jit(solution)/shard_map/all_to_all | solution.py:122
  107.8 4.9 all-to-all-start.2
  112.7 4.6 reshape.305
  117.3 5.8 %fusion.21 = f32[832,512]{1,0:T(8,128)} fusion(bf16[832,2048]{1,0:T(8,128)(2,1)} %reshape.305, bf16[1,1,2048,512]{3,2,1,0:T(8,128)(2,1)} %param.20), kind=kOutput, calls=%fused_computation.29 | convolution fusion | flops 1744830464 | bytes 7208960 | tf_op jit(solution)/shard_map/dot_general | solution.py:50
  123.1 70.9 %all-to-all-done.2 = bf16[16,52,2048]{2,1,0:T(8,128)(2,1)} async-done(((bf16[16,52,2048]{2,1,0:T(8,128)(2,1)}), bf16[16,52,2048]{2,1,0:T(8,128)(2,1)}, u32[]{:S(2)}, u32[]{:S(2)}) %all-to-all-start.2) | async-done | bytes 3407904 | tf_op jit(solution)/shard_map/all_to_all | solution.py:123
  194.0 4.6 reshape.302
  198.5 5.8 %fusion.11 = f32[832,512]{1,0:T(8,128)} fusion(bf16[832,2048]{1,0:T(8,128)(2,1)} %reshape.302, bf16[1,1,512,2048]{3,2,1,0:T(8,128)(2,1)} %param.22), kind=kOutput, calls=%fused_computation.19 | convolution fusion | flops 1744830464 | bytes 7208960 | tf_op jit(solution)/shard_map/dot_general | solution.py:53
  204.4 10.5 %fusion.19 = f32[832,2048]{1,0:T(8,128)} fusion(bf16[1,1,2048,512]{3,2,1,0:T(8,128)(2,1)} %param.20, f32[832,512]{1,0:T(8,128)} %fusion.21, f32[832,512]{1,0:T(8,128)} %fusion.11, bf16[832,2048]{1,0:T(8,128)(2,1)} %reshape.305, bf16[1,1,2048,512]{3,2,1,0:T(8,128)(2,1)S(1)} %copy-done), kind=kOutput, calls=%fused_computation.27 | convolution fusion | flops 3493920768 | bytes 17825792 | tf_op jit(solution)/shard_map/dot_general | solution.py:62
  214.9 7.7 %add_convert_fusion = bf16[832,2048]{1,0:T(8,128)(2,1)} fusion(f32[832,2048]{1,0:T(8,128)} %fusion.19, bf16[1,1,2048,512]{3,2,1,0:T(8,128)(2,1)S(1)} %copy-done, f32[832,512]{1,0:T(8,128)} %fusion.11, f32[832,512]{1,0:T(8,128)} %fusion.21), kind=kOutput, calls=%fused_computation.5 | convolution fusion | flops 1750794240 | bytes 15728640 | tf_op jit(solution)/shard_map/dot_general | solution.py:63
  222.6 4.6 reshape.306
  227.1 4.9 all-to-all-start.4
  232.0 1.5 collective-permute-start
  233.6 0.1 copy.25
  233.7 0.1 eq.58
  233.8 1.7 reduce-window.14
  235.6 0.2 slice_reduce_fusion.1
  235.8 0.1 eq.54
  235.9 0.1 reshape.385
  236.0 0.1 mul.281
  236.1 0.1 fusion.67
  236.3 8.3 %collective-permute-done = bf16[96,2048]{1,0:T(8,128)(2,1)} collective-permute-done((bf16[96,2048]{1,0:T(8,128)(2,1)}, bf16[96,2048]{1,0:T(8,128)(2,1)}, u32[]{:S(2)}, u32[]{:S(2)}) %collective-permute-start) | collective-permute-done | bytes 393248 | tf_op jit(solution)/shard_map/ppermute | solution.py:12
  244.6 2.1 fusion.48
  246.7 66.6 %all-to-all-done.4 = bf16[16,52,2048]{2,1,0:T(8,128)(2,1)} async-done(((bf16[16,52,2048]{2,1,0:T(8,128)(2,1)}), bf16[16,52,2048]{2,1,0:T(8,128)(2,1)}, u32[]{:S(2)}, u32[]{:S(2)}) %all-to-all-start.4) | async-done | bytes 3407904 | tf_op jit(solution)/shard_map/all_to_all | solution.py:130
  313.3 4.6 reshape.307
  317.8 9.5 %gather_fusion.1 = bf16[768,2048]{1,0:T(8,128)(2,1)} fusion(bf16[832,2048]{1,0:T(8,128)(2,1)} %reshape.307, s32[1024]{0:T(1024)S(1)} %pad_clamp_fusion), kind=kCustom, calls=%fused_computation.1 | custom fusion | bytes 6294528 | tf_op jit(solution)/shard_map/gather | solution.py:136
  327.4 4.2 convert_reduce_fusion
  331.5 0.9 copy-done.1
  332.4 1.6 multiply_reduce_fusion
  334.0 9.4 %scatter_custom_fusion = bf16[832,2048]{1,0:T(8,128)(2,1)} fusion(s32[768]{0:T(1024)S(1)} %fusion.70, bf16[]{:T(256)} %constant.57.clone.1, bf16[96,2048]{1,0:T(8,128)(2,1)} %get-tuple-element.39), kind=kCustom, calls=%fused_computation.15 | custom fusion | bytes 3801090 | tf_op jit(solution)/shard_map/scatter | solution.py:39
  343.4 4.6 reshape.296
  348.0 86.3 %all_to_all.25 = bf16[16,52,2048]{2,1,0:T(8,128)(2,1)} all-to-all(bf16[16,52,2048]{2,1,0:T(8,128)(2,1)} %reshape.296), channel_id=1, replica_groups=mesh['pipe'=2,'ep'=16] {'ep'}, dimensions={0} | all-to-all | bytes 6815744 | tf_op jit(solution)/shard_map/all_to_all | solution.py:116
  434.3 4.6 reshape.297
  438.8 5.8 %fusion.23 = f32[832,512]{1,0:T(8,128)} fusion(bf16[832,2048]{1,0:T(8,128)(2,1)} %reshape.297, bf16[1,1,2048,512]{3,2,1,0:T(8,128)(2,1)} %param.20), kind=kOutput, calls=%fused_computation.31 | convolution fusion | flops 1744830464 | bytes 7208960 | tf_op jit(solution)/shard_map/dot_general | solution.py:43
  444.6 8.8 %convolution_convert_fusion = bf16[832,2048]{1,0:T(8,128)(2,1)} fusion(bf16[1,1,512,2048]{3,2,1,0:T(8,128)(2,1)} %param.22, f32[832,512]{1,0:T(8,128)} %fusion.23, bf16[832,2048]{1,0:T(8,128)(2,1)} %reshape.297, bf16[1,1,2048,512]{3,2,1,0:T(8,128)(2,1)S(1)} %copy-done), kind=kOutput, calls=%fused_computation.9 | convolution fusion | flops 3493920768 | bytes 12713984 | tf_op jit(solution)/shard_map/dot_general | solution.py:46
  453.4 4.6 reshape.298
  457.9 5.3 all-to-all-start.1
  463.4 0.6 constant_dynamic-slice_fusion.1
  464.6 0.6 constant_dynamic-slice_fusion
  466.0 0.1 copy.23
  466.1 0.6 pad_maximum_fusion
  466.7 77.8 %all-to-all-done.1 = bf16[16,52,2048]{2,1,0:T(8,128)(2,1)} async-done(((bf16[16,52,2048]{2,1,0:T(8,128)(2,1)}), bf16[16,52,2048]{2,1,0:T(8,128)(2,1)}, u32[]{:S(2)}, u32[]{:S(2)}) %all-to-all-start.1) | async-done | bytes 3407904 | tf_op jit(solution)/shard_map/all_to_all | solution.py:120
  544.5 4.6 reshape.299
  549.1 9.5 %gather_fusion = bf16[768,2048]{1,0:T(8,128)(2,1)} fusion(bf16[832,2048]{1,0:T(8,128)(2,1)} %reshape.299, s32[1024]{0:T(1024)S(1)} %pad_clamp_fusion.1), kind=kCustom, calls=%fused_computation | custom fusion | bytes 6294528 | tf_op jit(solution)/shard_map/gather | solution.py:131
  558.6 3.0 fusion.5
  561.6 1.7 fusion.59
  (50 shorter events, 0.6 us)
Async XLA Ops:
  0.6 203.8 %copy-start = (bf16[1,1,2048,512]{3,2,1,0:T(8,128)(2,1)S(1)}, bf16[1,1,2048,512]{3,2,1,0:T(8,128)(2,1)}, u32[]{:S(2)}) copy-start(bf16[1,1,2048,512]{3,2,1,0:T(8,128)(2,1)} %param.21) | copy-start | bytes 6291460
  19.9 6.7 %copy-start.12 = (bf16[1,96,2048]{2,1,0:T(8,128)(2,1)S(1)}, bf16[1,96,2048]{2,1,0:T(8,128)(2,1)}, u32[]{:S(2)}) copy-start(bf16[1,96,2048]{2,1,0:T(8,128)(2,1)} %param.15) | copy-start | bytes 1179652
  19.9 8.0 %slice-start = ((f32[2,1,96,8]{2,3,1,0:T(8,128)}), f32[1,1,96,8]{2,3,1,0:T(8,128)S(1)}, s32[]{:S(2)}) async-start(f32[2,1,96,8]{2,3,1,0:T(8,128)} %param.24), calls=%async_computation.5 | async-start | bytes 8192 | tf_op jit(solution)/shard_map/slice | solution.py:114
  19.9 87.9 %all-to-all-start.3 = ((bf16[16,52,2048]{2,1,0:T(8,128)(2,1)}), bf16[16,52,2048]{2,1,0:T(8,128)(2,1)}, u32[]{:S(2)}, u32[]{:S(2)}) async-start(bf16[16,52,2048]{2,1,0:T(8,128)(2,1)} %reshape.304), calls=%async_computation.3 | async-start | bytes 7340032 | tf_op jit(solution)/shard_map/all_to_all | solution.py:122
  26.6 12.3 %collective-permute-start.1 = (bf16[96,2048]{1,0:T(8,128)(2,1)S(1)}, bf16[96,2048]{1,0:T(8,128)(2,1)S(1)}, u32[]{:S(2)}, u32[]{:S(2)}) collective-permute-start(bf16[96,2048]{1,0:T(8,128)(2,1)S(1)} %bitcast.180), channel_id=1, source_target_pairs={{0,16},{1,17},{2,18},{3,19},{4,20},{5,21},{6,22},{7,23},{8,24},{9,... | collective-permute-start | bytes 1179656 | tf_op jit(solution)/shard_map/ppermute | solution.py:12
  107.8 86.1 %all-to-all-start.2 = ((bf16[16,52,2048]{2,1,0:T(8,128)(2,1)}), bf16[16,52,2048]{2,1,0:T(8,128)(2,1)}, u32[]{:S(2)}, u32[]{:S(2)}) async-start(bf16[16,52,2048]{2,1,0:T(8,128)(2,1)} %reshape.301), calls=%async_computation.2 | async-start | bytes 7340032 | tf_op jit(solution)/shard_map/all_to_all | solution.py:123
  227.1 86.1 %all-to-all-start.4 = ((bf16[16,52,2048]{2,1,0:T(8,128)(2,1)}), bf16[16,52,2048]{2,1,0:T(8,128)(2,1)}, u32[]{:S(2)}, u32[]{:S(2)}) async-start(bf16[16,52,2048]{2,1,0:T(8,128)(2,1)} %reshape.306), calls=%async_computation.4 | async-start | bytes 7340032 | tf_op jit(solution)/shard_map/all_to_all | solution.py:130
  232.0 12.5 %collective-permute-start = (bf16[96,2048]{1,0:T(8,128)(2,1)}, bf16[96,2048]{1,0:T(8,128)(2,1)}, u32[]{:S(2)}, u32[]{:S(2)}) collective-permute-start(bf16[96,2048]{1,0:T(8,128)(2,1)} %bitcast.1), channel_id=1, source_target_pairs={{0,16},{1,17},{2,18},{3,19},{4,20},{5,21},{6,22},{7,23},{8,24},{9,... | collective-permute-start | bytes 1179656 | tf_op jit(solution)/shard_map/ppermute | solution.py:12
  327.4 5.1 copy-start.3
  327.4 5.1 copy-start.4
  327.4 5.1 copy-start.6
  327.4 5.1 copy-start.8
  327.4 5.1 copy-start.9
  331.5 0.9 copy-start.1
  457.9 5.4 copy-start.11
  457.9 8.1 %copy-start.10 = (f32[2,1,96,8]{2,3,1,0:T(8,128)S(1)}, f32[2,1,96,8]{2,3,1,0:T(8,128)}, u32[]{:S(2)}) copy-start(f32[2,1,96,8]{2,3,1,0:T(8,128)} %param.24) | copy-start | bytes 18436
  457.9 86.6 %all-to-all-start.1 = ((bf16[16,52,2048]{2,1,0:T(8,128)(2,1)}), bf16[16,52,2048]{2,1,0:T(8,128)(2,1)}, u32[]{:S(2)}, u32[]{:S(2)}) async-start(bf16[16,52,2048]{2,1,0:T(8,128)(2,1)} %reshape.298), calls=%async_computation.1 | async-start | bytes 7340032 | tf_op jit(solution)/shard_map/all_to_all | solution.py:120
  558.6 3.0 copy-start.2
  558.6 3.0 copy-start.5
  558.6 3.0 copy-start.7
where the time goes:
time: 574 us; the launch traced here: 564 us
  waiting for transfers between devices  285 us (50%)
  local copies, waits for them, and re-layouts  87.8 us (15%)
  blocking collectives  86.3 us (15%)
  matrix products  47.3 us (8%)
  other arithmetic  30.1 us (5%)
  starting transfers between devices  24.6 us (4%)
    all_to_all x1, blocking collectives, local(): lax.all_to_all(rise_send, 'ep', split_axis=0, concat_axis=0, tiled=True)  86.3 us
    all_to_all x1, waiting for transfers between devices, local(): lax.all_to_all(made_rise, 'ep', split_axis=0, concat_axis=0, tiled=True)  77.8 us
    all_to_all x1, waiting for transfers between devices, local(): lax.all_to_all(fall_cot_send, 'ep', split_axis=0, concat_axis=0, tiled=True)  70.9 us
    all_to_all x1, waiting for transfers between devices, local(): lax.all_to_all(made_fall, 'ep', split_axis=0, concat_axis=0, tiled=True)  66.6 us
    all_to_all x1, waiting for transfers between devices, local(): lax.all_to_all(fall_rows_send, 'ep', split_axis=0, concat_axis=0, tiled=T...  50.5 us
    ppermute x2, waiting for transfers between devices, passed_along(): return lax.ppermute(block, axis, route)  19.2 us
    scatter x2, local copies, waits for them, and re-layouts, fill_rows(): empty.at[places.reshape(-1)].set(slot_values.reshape(-1, feature_width))  18.3 us
    scatter x1, other arithmetic, fill_rows(): empty.at[places.reshape(-1)].set(slot_values.reshape(-1, feature_width))  12.8 us
  transfers between devices with their start and end apart: 6, of which 6 were waited for; matrix products, arithmetic and copies ran while one was open for 6% of the time, Pallas kernels for 0%

commit v1 on v0

v1 whole, which is shorter than its diff:
```python
import jax
import jax.numpy as jnp
from jax import lax
from jax.sharding import PartitionSpec as P

EPSILON = 1e-06


def passed_along(block, axis, distance):
    devices = range(lax.axis_size(axis))
    route = [(i - distance, i) for i in devices if i - distance in devices]
    return lax.ppermute(block, axis, route)


def normed(values, gain_row):
    return (
        values * lax.rsqrt(jnp.mean(values * values, axis=-1, keepdims=True) + EPSILON) * gain_row
    )


def norm_pullback(values, gain_row, upstream):
    _, pullback = jax.vjp(lambda argument: normed(argument, gain_row), values)
    return pullback(upstream)[0]


def dense_gates(choice_ids, gates, experts):
    onehot = choice_ids[:, :, None] == jnp.arange(experts, dtype=jnp.int32)[None, None, :]
    return jnp.sum(jnp.where(onehot, gates[:, :, None], 0.0), axis=1)


def in_parts(row_fn, *arrays, limit=768):
    rows = arrays[0].shape[0]
    if rows <= limit:
        return row_fn(*arrays)
    shaped = [array.reshape((rows // limit, limit) + array.shape[1:]) for array in arrays]
    out = lax.map(lambda packed: row_fn(*packed), shaped)
    return out.reshape((rows,) + out.shape[2:])


def expert_forward(rows, gate_weight, up_weight, down_weight):
    gate_proj = jnp.dot(rows, gate_weight, preferred_element_type=jnp.float32)
    second = jnp.dot(rows, up_weight, preferred_element_type=jnp.float32)
    hidden = (jax.nn.silu(gate_proj) * second).astype(jnp.bfloat16)
    return jnp.dot(hidden, down_weight, preferred_element_type=jnp.float32)


def expert_backward(rows, upstream, gate_weight, up_weight, down_weight):
    gate_proj = jnp.dot(rows, gate_weight, preferred_element_type=jnp.float32)
    second = jnp.dot(rows, up_weight, preferred_element_type=jnp.float32)
    contract = (((1,), (1,)), ((), ()))
    hidden_grad = lax.dot_general(
        upstream, down_weight, contract, preferred_element_type=jnp.float32
    )
    sigmoid_part = jax.nn.sigmoid(gate_proj)
    activated = gate_proj * sigmoid_part
    gate_grad = (
        hidden_grad * second * sigmoid_part * (1.0 + gate_proj * (1.0 - sigmoid_part))
    ).astype(jnp.bfloat16)
    second_grad = (hidden_grad * activated).astype(jnp.bfloat16)
    returned = lax.dot_general(gate_grad, gate_weight, contract, preferred_element_type=jnp.float32)
    return returned + lax.dot_general(
        second_grad, up_weight, contract, preferred_element_type=jnp.float32
    )


def local(
    entering,
    rising_prev,
    falling_cot,
    falling_saved,
    targets,
    norm_gain,
    exit_gain,
    w_gate,
    w_up,
    w_down,
    route_ids,
    route_gates,
    exit_list,
):
    section_index = lax.axis_index("pipe")
    sections = lax.axis_size("pipe")
    sources = lax.axis_size("ep")
    here = lax.axis_index("ep")
    core = here % 2
    groups = [list(range(start, sources, 2)) for start in range(2)]
    norm_row = norm_gain[0]
    exit_row = exit_gain[0]

    def gathered(block):
        return lax.all_gather(block, "ep", axis_index_groups=groups, tiled=True)

    def scattered(block):
        return lax.psum_scatter(
            block, "ep", scatter_dimension=0, axis_index_groups=groups, tiled=True
        )

    own = (w_gate[0, 0], w_up[0, 0], w_down[0, 0])
    swap = [(i, i ^ 1) for i in range(sources)]
    other = lax.ppermute(own, "ep", swap)

    fall_wide = falling_saved[0].astype(jnp.float32)
    fall_normal = normed(fall_wide, norm_row).astype(jnp.bfloat16)
    all_fall = gathered(fall_normal)

    gate_table = jnp.stack(
        [dense_gates(route_ids[m, 0], route_gates[m, 0], sources) for m in range(2)], axis=1
    )
    all_gates = gathered(gate_table)
    gates_own = lax.dynamic_index_in_dim(all_gates, here, 2, keepdims=True)
    gates_other = lax.dynamic_index_in_dim(all_gates, here + 1 - 2 * core, 2, keepdims=True)

    moved_cot, moved_rise = passed_along((falling_cot[0], rising_prev[0]), "pipe", 1)
    at_start = section_index == 0
    cot_in = jnp.where(at_start, entering[1], moved_cot)
    all_cot = gathered(cot_in)
    rise_in = jnp.where(at_start, entering[0], moved_rise)
    rise_wide = rise_in.astype(jnp.float32)
    rise_normal = normed(rise_wide, norm_row).astype(jnp.bfloat16)
    cotangent = cot_in.astype(jnp.float32)
    head_rise = jnp.take(exit_list[0], section_index).astype(jnp.float32)
    head_fall = jnp.take(exit_list[1], sections - 1 - section_index).astype(jnp.float32)

    def pair_backward(rows, upstream, gates_first, gates_second):
        made = 0.0
        for weights, gates in ((own, gates_first), (other, gates_second)):
            slot_cot = (gates[:, 1] * upstream.astype(jnp.float32)).astype(jnp.bfloat16)
            made = made + expert_backward(rows, slot_cot, *weights)
        return made.astype(jnp.bfloat16)

    def pair_forward(rows, gates_first, gates_second):
        made = 0.0
        for weights, gates in ((own, gates_first), (other, gates_second)):
            made = made + gates[:, 0] * expert_forward(rows, *weights)
        return made.astype(jnp.bfloat16)

    made_fall = in_parts(pair_backward, all_fall, all_cot, gates_own, gates_other)
    norm_grad = scattered(made_fall).astype(jnp.float32)
    if sources > 16:
        rise_normal, norm_grad = lax.optimization_barrier((rise_normal, norm_grad))
    all_rise = gathered(rise_normal)
    made_rise = in_parts(pair_forward, all_rise, gates_own, gates_other)
    layer_out = rise_wide + scattered(made_rise).astype(jnp.float32)

    rise_diff = normed(rise_wide, exit_row) - targets[0].astype(jnp.float32)
    loss_rise = head_rise * 0.5 * jnp.mean(rise_diff * rise_diff, axis=-1)
    fall_diff = normed(fall_wide, exit_row) - targets[1].astype(jnp.float32)
    fall_total = cotangent + norm_pullback(fall_wide, norm_row, norm_grad)
    fall_total = fall_total + head_fall * norm_pullback(fall_wide, exit_row, fall_diff)
    loss_fall = head_fall * 0.5 * jnp.mean(fall_diff * fall_diff, axis=-1)
    exit_loss = jnp.stack([loss_rise, loss_fall])[:, None, :]
    return (layer_out.astype(jnp.bfloat16)[None], fall_total.astype(jnp.bfloat16)[None], exit_loss)


def solution(mesh):
    placed = (
        P(None, "ep", None),
        P("pipe", "ep", None),
        P("pipe", "ep", None),
        P("pipe", "ep", None),
        P(None, "ep", None),
        P("pipe", None),
        P("pipe", None),
        P("pipe", "ep", None, None),
        P("pipe", "ep", None, None),
        P("pipe", "ep", None, None),
        P(None, "pipe", "ep", None),
        P(None, "pipe", "ep", None),
        P(),
    )
    return jax.shard_map(
        local,
        mesh=mesh,
        in_specs=placed,
        out_specs=(P("pipe", "ep", None), P("pipe", "ep", None), P(None, "pipe", "ep")),
        check_vma=False,
    )
```

time: 574 us -> 436 us (0.76)
  the two profiles are of different devices: /device:TPU:15 before, /device:TPU:0 now
where the time goes in v1:
time: 436 us
  waiting for transfers between devices  266 us (61%)
  matrix products  83.3 us (19%)
  blocking collectives  34.4 us (8%)
  local copies, waits for them, and re-layouts  15.5 us (4%)
  between operations  15.4 us (4%)
  other arithmetic  11.6 us (3%)
  starting transfers between devices  9.31 us (2%)
    reduce_scatter x2, waiting for transfers between devices, scattered(): lax.psum_scatter(block, 'ep', scatter_dimension=0, axis_index_groups=grou...  129 us
    all_gather x3, waiting for transfers between devices, gathered(): return lax.all_gather(block, 'ep', axis_index_groups=groups, tiled=True)  121 us
    all_gather x1, blocking collectives, gathered(): return lax.all_gather(block, 'ep', axis_index_groups=groups, tiled=True)  34.4 us
    dot_general x2, matrix products, expert_backward(): lax.dot_general(gate_grad, gate_weight, contract, preferred_element_type=...  24.4 us
    dot_general x2, matrix products, expert_forward(): return jnp.dot(hidden, down_weight, preferred_element_type=jnp.float32)  20 us
    ppermute x2, waiting for transfers between devices, passed_along(): return lax.ppermute(block, axis, route)  15.9 us
    slice x1, local copies, waits for them, and re-layouts, pair_backward(): slot_cot = (gates[:, 1] * upstream.astype(jnp.float32)).astype(jnp.bfloat16)  12.6 us
    dot_general x2, matrix products, expert_backward(): lax.dot_general(second_grad, up_weight, contract, preferred_element_type=...  12.1 us
  transfers between devices with their start and end apart: 10, of which 7 were waited for; matrix products, arithmetic and copies ran while one was open for 12% of the time, Pallas kernels for 0%

profile of v1, /device:TPU:0, one launch (start us, length us, event | category | flops | bytes accessed | tf_op | source)
XLA Modules:
  0.0 435.9 jit_solution(2450773634719803950)
XLA Ops:
  7.2 0.0 copy-start.7
  7.2 0.0 copy-start.8
  7.2 0.0 all-gather.8.cloned.1.call-start
  7.2 1.2 fusion.28
  8.4 1.9 fusion.14
  10.3 0.0 all-gather.8.cloned.1.call-update
  10.4 0.0 all-gather.6.cloned.1.call-start
  10.4 4.9 %collective-permute-start.4 = (bf16[96,2048]{1,0:T(8,128)(2,1)}, bf16[96,2048]{1,0:T(8,128)(2,1)S(1)}, u32[]{:S(2)}, u32[]{:S(2)}) collective-permute-start(bf16[96,2048]{1,0:T(8,128)(2,1)} %bitcast.101), channel_id=1, source_target_pairs={{0,16},{1,17},{2,18},{3,19},{4,20},{5,21},{6,22},{7,23},{8,24},{9,... | collective-permute-start | bytes 1179656 | tf_op jit(solution)/shard_map/ppermute | solution.py:12
  15.3 8.6 %collective-permute-done.4 = bf16[96,2048]{1,0:T(8,128)(2,1)S(1)} collective-permute-done((bf16[96,2048]{1,0:T(8,128)(2,1)}, bf16[96,2048]{1,0:T(8,128)(2,1)S(1)}, u32[]{:S(2)}, u32[]{:S(2)}) %collective-permute-start.4) | collective-permute-done | bytes 393248 | tf_op jit(solution)/shard_map/ppermute | solution.py:12
  23.9 1.8 bitcast_select_fusion
  25.7 0.0 all-gather.6.cloned.1.call-update
  25.8 0.0 reduce-scatter.5.cloned.1.call-start
  25.8 0.1 collective-permute-start.1
  25.9 0.5 collective-permute-start.3
  26.4 0.1 collective-permute-start.2
  26.5 0.0 copy-done.8
  26.5 0.1 copy.37
  26.6 34.4 %all_gather.12 = f32[768,2,16]{2,1,0:T(2,128)S(1)} all-gather(f32[96,2,16]{2,1,0:T(2,128)S(1)} %copy.37), channel_id=1, replica_groups={{0,2,4,6,8,10,12,14},{1,3,5,7,9,11,13,15},{16,18,20,22,24,26,28,30},{17..., dimensions={0}, use_global_device_ids=true | all-gather | bytes 110592 | tf_op jit(solution)/shard_map/all_gather | solution.py:91
  61.1 12.6 %dynamic-slice_reduce_fusion.1 = (f32[768]{0:T(1024)S(1)}, f32[768]{0:T(1024)S(1)}, f32[768]{0:T(1024)S(1)}, f32[768]{0:T(1024)S(1)}) fusion(f32[768,2,16]{2,1,0:T(2,128)S(1)} %all_gather.12, s32[]{:T(128)S(6)} %add.119, s32[]{:T(128)S(6)} %select_n.51, s32[]{:T(128)S(6)} %select_n.53), kind=kLoop, calls=%fused_computation.61 | loop fusion | bytes 24588 | tf_op jit(solution)/shard_map/slice | solution.py:127
  73.6 7.1 %all-gather.8.cloned.1.call-done = bf16[768,2048]{1,0:T(8,128)(2,1)} async-done(((bf16[96,2048]{1,0:T(8,128)(2,1)}), bf16[768,2048]{1,0:T(8,128)(2,1)}) %all-gather.8.cloned.1.call-update) | async-done | bytes 3145744 | tf_op jit(solution)/shard_map/all_gather | solution.py:91
  80.8 5.7 %fusion.47 = f32[768,512]{1,0:T(8,128)} fusion(bf16[768,2048]{1,0:T(8,128)(2,1)} %all-gather.8.cloned.1.call-done, bf16[1,1,2048,512]{3,2,1,0:T(8,128)(2,1)} %param.20), kind=kOutput, calls=%fused_computation.93 | convolution fusion | flops 1610612736 | bytes 6815744 | tf_op jit(solution)/shard_map/dot_general | solution.py:48
  86.5 0.0 collective-permute-done.1
  86.5 3.6 fusion.61
  90.0 54.3 %all-gather.6.cloned.1.call-done = bf16[768,2048]{1,0:T(8,128)(2,1)} async-done(((bf16[96,2048]{1,0:T(8,128)(2,1)}), bf16[768,2048]{1,0:T(8,128)(2,1)}) %all-gather.6.cloned.1.call-update) | async-done | bytes 3145744 | tf_op jit(solution)/shard_map/all_gather | solution.py:91
  144.4 4.5 %fusion.4 = f32[768,512]{1,0:T(8,128)S(1)} fusion(bf16[768,2048]{1,0:T(8,128)(2,1)} %all-gather.6.cloned.1.call-done, f32[768]{0:T(1024)S(1)} %get-tuple-element.43, bf16[1,1,512,2048]{3,2,1,0:T(8,128)(2,1)} %param.22), kind=kOutput, calls=%fused_computation.7 | convolution fusion | flops 1615331328 | bytes 6818816 | tf_op jit(solution)/shard_map/dot_general | solution.py:51
  148.9 0.0 collective-permute-done.3
  148.9 0.0 copy-done.11
  148.9 0.0 copy-start.14
  149.0 4.1 fusion.2
  153.0 0.0 copy-done.15
  153.0 0.0 copy-done.14
  153.1 6.1 %fusion.26 = f32[768,2048]{1,0:T(8,128)} fusion(f32[768,512]{1,0:T(8,128)S(1)} %fusion.4, f32[768,512]{1,0:T(8,128)S(1)} %copy-done.14, bf16[1,1,2048,512]{3,2,1,0:T(8,128)(2,1)} %param.21), kind=kOutput, calls=%fused_computation.47 | convolution fusion | flops 1612972032 | bytes 11534336 | tf_op jit(solution)/shard_map/dot_general | solution.py:61
  159.2 10.4 %fusion.12 = f32[768,2048]{1,0:T(8,128)} fusion(f32[768,512]{1,0:T(8,128)} %fusion.47, f32[768,512]{1,0:T(8,128)} %copy-done.15, bf16[768,2048]{1,0:T(8,128)(2,1)} %all-gather.8.cloned.1.call-done, bf16[1,1,2048,512]{3,2,1,0:T(8,128)(2,1)} %param.21, bf16[1,1,2048,512]{3,2,1,0:T(8,128)(2,1)} %param.20), kind=kOutput, calls=%fused_computation.33 | convolution fusion | flops 3225157632 | bytes 16777216 | tf_op jit(solution)/shard_map/dot_general | solution.py:60
  169.6 0.0 collective-permute-done.2
  169.6 6.0 %fusion.27 = f32[768,2048]{1,0:T(8,128)} fusion(bf16[2048,512]{1,0:T(8,128)(2,1)} %collective-permute-done.2, f32[768,512]{1,0:T(8,128)S(1)} %fusion.2, f32[768,512]{1,0:T(8,128)S(1)} %fusion.61), kind=kOutput, calls=%fused_computation.48 | convolution fusion | flops 1612972032 | bytes 11534336 | tf_op jit(solution)/shard_map/dot_general | solution.py:61
  175.6 13.9 %add_convert_fusion = bf16[768,2048]{1,0:T(8,128)(2,1)} fusion(f32[768,2048]{1,0:T(8,128)} %fusion.27, f32[768,2048]{1,0:T(8,128)} %fusion.12, f32[768,2048]{1,0:T(8,128)} %fusion.26, bf16[2048,512]{1,0:T(8,128)(2,1)} %collective-permute-done.1, f32[768,512]{1,0:T(8,128)S(1)} %fusion.61, f32[768,512]{1,0:T(8,128)S(1)} %fusion.2, ...), kind=kOutput, calls=%fused_computation.4 | convolution fusion | flops 3231449088 | bytes 32505856 | tf_op jit(solution)/shard_map/dot_general | solution.py:60
  189.6 0.0 copy-start.2
  189.6 0.0 copy-start.5
  189.6 0.0 copy-start.6
  189.6 0.0 reduce-scatter.5.cloned.1.call-update
  189.6 0.0 all-gather.4.cloned.1.call-start
  189.7 0.9 copy-done.13
  190.5 3.6 collective-permute-start
  194.1 7.3 %collective-permute-done = bf16[96,2048]{1,0:T(8,128)(2,1)S(1)} collective-permute-done((bf16[96,2048]{1,0:T(8,128)(2,1)S(1)}, bf16[96,2048]{1,0:T(8,128)(2,1)S(1)}, u32[]{:S(2)}, u32[]{:S(2)}) %collective-permute-start) | collective-permute-done | bytes 393248 | tf_op jit(solution)/shard_map/ppermute | solution.py:12
  201.4 0.2 fusion.20
  201.7 61.1 %reduce-scatter.5.cloned.1.call-done = bf16[96,2048]{1,0:T(8,128)(2,1)} async-done(((bf16[768,2048]{1,0:T(8,128)(2,1)}), bf16[96,2048]{1,0:T(8,128)(2,1)}) %reduce-scatter.5.cloned.1.call-update) | async-done | bytes 393232 | tf_op jit(solution)/shard_map/reduce_scatter | solution.py:94
  262.8 0.0 copy-done.2
  262.8 2.6 multiply_reduce_fusion
  265.4 0.0 all-gather.4.cloned.1.call-update
  265.4 0.0 reduce-scatter.3.cloned.1.call-start
  265.4 59.8 %all-gather.4.cloned.1.call-done = bf16[768,2048]{1,0:T(8,128)(2,1)} async-done(((bf16[96,2048]{1,0:T(8,128)(2,1)}), bf16[768,2048]{1,0:T(8,128)(2,1)}) %all-gather.4.cloned.1.call-update) | async-done | bytes 3145744 | tf_op jit(solution)/shard_map/all_gather | solution.py:91
  325.2 5.6 %fusion.49 = f32[768,512]{1,0:T(8,128)} fusion(bf16[768,2048]{1,0:T(8,128)(2,1)} %all-gather.4.cloned.1.call-done, bf16[1,1,2048,512]{3,2,1,0:T(8,128)(2,1)} %param.20), kind=kOutput, calls=%fused_computation.95 | convolution fusion | flops 1610612736 | bytes 6815744 | tf_op jit(solution)/shard_map/dot_general | solution.py:41
  330.8 3.4 fusion.60
  334.2 9.8 %fusion.13 = f32[768,2048]{1,0:T(8,128)} fusion(f32[768,512]{1,0:T(8,128)} %fusion.49, bf16[768,2048]{1,0:T(8,128)(2,1)} %all-gather.4.cloned.1.call-done, bf16[1,1,512,2048]{3,2,1,0:T(8,128)(2,1)} %param.22, bf16[1,1,2048,512]{3,2,1,0:T(8,128)(2,1)} %param.21), kind=kOutput, calls=%fused_computation.34 | convolution fusion | flops 3223584768 | bytes 15204352 | tf_op jit(solution)/shard_map/dot_general | solution.py:44
  344.0 10.2 %add_convert_fusion.1 = bf16[768,2048]{1,0:T(8,128)(2,1)} fusion(f32[768,2048]{1,0:T(8,128)} %fusion.13, bf16[512,2048]{1,0:T(8,128)(2,1)} %collective-permute-done.3, f32[768]{0:T(1024)S(1)} %get-tuple-element.44, f32[768]{0:T(1024)S(1)} %get-tuple-element.45, f32[768,512]{1,0:T(8,128)S(1)} %fusion.60, bf16[768,2048]{1,0:T(8,128)(2,1)} %all-gather.4.cloned.1.call-done, ...), kind=kOutput, calls=%fused_computation.5 | convolution fusion | flops 3229876224 | bytes 18356224 | tf_op jit(solution)/shard_map/dot_general | solution.py:44
  354.2 0.0 reduce-scatter.3.cloned.1.call-update
  354.2 0.6 copy-done.9
  354.9 0.6 constant_dynamic-slice_fusion.1
  356.1 0.7 constant_dynamic-slice_fusion
  357.5 0.6 pad_maximum_fusion.1
  358.1 0.0 copy-done.3
  358.1 1.4 fusion.37
  359.4 68.0 %reduce-scatter.3.cloned.1.call-done = bf16[96,2048]{1,0:T(8,128)(2,1)} async-done(((bf16[768,2048]{1,0:T(8,128)(2,1)}), bf16[96,2048]{1,0:T(8,128)(2,1)}) %reduce-scatter.3.cloned.1.call-update) | async-done | bytes 393232 | tf_op jit(solution)/shard_map/reduce_scatter | solution.py:94
  427.5 1.9 fusion.36
  (29 shorter events, 0.1 us)
Async XLA Ops:
  7.2 19.3 %copy-start.7 = (s32[2,1,96,8]{2,3,1,0:T(8,128)S(1)}, s32[2,1,96,8]{2,3,1,0:T(8,128)}, u32[]{:S(2)}) copy-start(s32[2,1,96,8]{2,3,1,0:T(8,128)} %param.23) | copy-start | bytes 18436
  7.2 19.3 %copy-start.8 = (f32[2,1,96,8]{2,3,1,0:T(8,128)S(1)}, f32[2,1,96,8]{2,3,1,0:T(8,128)}, u32[]{:S(2)}) copy-start(f32[2,1,96,8]{2,3,1,0:T(8,128)} %param.24) | copy-start | bytes 18436
  7.2 73.6 %all-gather.8.cloned.1.call-start = ((), (), s32[]{:S(2)}) async-start(), calls=%async_computation.5 | async-start | bytes 3538944 | tf_op jit(solution)/shard_map/all_gather | solution.py:91
  10.4 134.0 %all-gather.6.cloned.1.call-start = ((), (), s32[]{:S(2)}) async-start(), calls=%async_computation.4 | async-start | bytes 3538944 | tf_op jit(solution)/shard_map/all_gather | solution.py:91
  10.4 13.5 %collective-permute-start.4 = (bf16[96,2048]{1,0:T(8,128)(2,1)}, bf16[96,2048]{1,0:T(8,128)(2,1)S(1)}, u32[]{:S(2)}, u32[]{:S(2)}) collective-permute-start(bf16[96,2048]{1,0:T(8,128)(2,1)} %bitcast.101), channel_id=1, source_target_pairs={{0,16},{1,17},{2,18},{3,19},{4,20},{5,21},{6,22},{7,23},{8,24},{9,... | collective-permute-start | bytes 1179656 | tf_op jit(solution)/shard_map/ppermute | solution.py:12
  25.8 237.0 %reduce-scatter.5.cloned.1.call-start = ((), (), s32[]{:S(2)}) async-start(), calls=%async_computation.6 | async-start | bytes 3538944 | tf_op jit(solution)/shard_map/reduce_scatter | solution.py:94
  25.8 60.7 %collective-permute-start.1 = (bf16[2048,512]{1,0:T(8,128)(2,1)}, bf16[2048,512]{1,0:T(8,128)(2,1)}, u32[]{:S(2)}, u32[]{:S(2)}) collective-permute-start(bf16[2048,512]{1,0:T(8,128)(2,1)} %bitcast.9), channel_id=1, source_target_pairs={{0,1},{1,0},{2,3},{3,2},{4,5},{5,4},{6,7},{7,6},{8,9},{9,8},{10,11... | collective-permute-start | bytes 6291464 | tf_op jit(solution)/shard_map/ppermute | solution.py:100
  25.9 123.0 %collective-permute-start.3 = (bf16[512,2048]{1,0:T(8,128)(2,1)}, bf16[512,2048]{1,0:T(8,128)(2,1)}, u32[]{:S(2)}, u32[]{:S(2)}) collective-permute-start(bf16[512,2048]{1,0:T(8,128)(2,1)} %bitcast.11), channel_id=1, source_target_pairs={{0,1},{1,0},{2,3},{3,2},{4,5},{5,4},{6,7},{7,6},{8,9},{9,8},{10,11... | collective-permute-start | bytes 6291464 | tf_op jit(solution)/shard_map/ppermute | solution.py:100
  26.4 143.2 %collective-permute-start.2 = (bf16[2048,512]{1,0:T(8,128)(2,1)}, bf16[2048,512]{1,0:T(8,128)(2,1)}, u32[]{:S(2)}, u32[]{:S(2)}) collective-permute-start(bf16[2048,512]{1,0:T(8,128)(2,1)} %bitcast.10), channel_id=1, source_target_pairs={{0,1},{1,0},{2,3},{3,2},{4,5},{5,4},{6,7},{7,6},{8,9},{9,8},{10,11... | collective-permute-start | bytes 6291464 | tf_op jit(solution)/shard_map/ppermute | solution.py:100
  80.8 5.7 %copy-start.10 = (bf16[768,2048]{1,0:T(8,128)(2,1)S(1)}, bf16[768,2048]{1,0:T(8,128)(2,1)}, u32[]{:S(2)}) copy-start(bf16[768,2048]{1,0:T(8,128)(2,1)} %all-gather.8.cloned.1.call-done) | copy-start | bytes 9437188
  144.4 4.5 %copy-start.11 = (bf16[768,2048]{1,0:T(8,128)(2,1)S(1)}, bf16[768,2048]{1,0:T(8,128)(2,1)}, u32[]{:S(2)}) copy-start(bf16[768,2048]{1,0:T(8,128)(2,1)} %all-gather.6.cloned.1.call-done) | copy-start | bytes 9437188
  148.9 4.1 copy-start.15
  148.9 4.1 copy-start.14
  189.6 1.0 copy-start.13
  189.6 11.9 %copy-start.4 = (bf16[2,96,2048]{2,1,0:T(8,128)(2,1)S(1)}, bf16[2,96,2048]{2,1,0:T(8,128)(2,1)}, u32[]{:S(2)}) copy-start(bf16[2,96,2048]{2,1,0:T(8,128)(2,1)} %param.13) | copy-start | bytes 2359300
  189.6 73.2 %copy-start = (bf16[1,96,2048]{2,1,0:T(8,128)(2,1)S(1)}, bf16[1,96,2048]{2,1,0:T(8,128)(2,1)}, u32[]{:S(2)}) copy-start(bf16[1,96,2048]{2,1,0:T(8,128)(2,1)} %param.16) | copy-start | bytes 1179652
  189.6 73.2 %copy-start.2 = (bf16[2,96,2048]{2,1,0:T(8,128)(2,1)S(1)}, bf16[2,96,2048]{2,1,0:T(8,128)(2,1)}, u32[]{:S(2)}) copy-start(bf16[2,96,2048]{2,1,0:T(8,128)(2,1)} %param.17) | copy-start | bytes 2359300
  189.6 73.2 %copy-start.5 = (f32[1,2048]{1,0:T(1,128)S(1)}, f32[1,2048]{1,0:T(1,128)}, u32[]{:S(2)}) copy-start(f32[1,2048]{1,0:T(1,128)} %param.18) | copy-start | bytes 24580
  189.6 73.2 %copy-start.6 = (f32[1,2048]{1,0:T(1,128)S(1)}, f32[1,2048]{1,0:T(1,128)}, u32[]{:S(2)}) copy-start(f32[1,2048]{1,0:T(1,128)} %param.19) | copy-start | bytes 24580
  189.6 135.6 %all-gather.4.cloned.1.call-start = ((), (), s32[]{:S(2)}) async-start(), calls=%async_computation.2 | async-start | bytes 3538944 | tf_op jit(solution)/shard_map/all_gather | solution.py:91
  190.5 10.9 %collective-permute-start = (bf16[96,2048]{1,0:T(8,128)(2,1)S(1)}, bf16[96,2048]{1,0:T(8,128)(2,1)S(1)}, u32[]{:S(2)}, u32[]{:S(2)}) collective-permute-start(bf16[96,2048]{1,0:T(8,128)(2,1)S(1)} %bitcast.102), channel_id=1, source_target_pairs={{0,16},{1,17},{2,18},{3,19},{4,20},{5,21},{6,22},{7,23},{8,24},{9,... | collective-permute-start | bytes 1179656 | tf_op jit(solution)/shard_map/ppermute | solution.py:12
  265.4 162.1 %reduce-scatter.3.cloned.1.call-start = ((), (), s32[]{:S(2)}) async-start(), calls=%async_computation.3 | async-start | bytes 3538944 | tf_op jit(solution)/shard_map/reduce_scatter | solution.py:94
  325.2 5.6 %copy-start.12 = (bf16[768,2048]{1,0:T(8,128)(2,1)S(1)}, bf16[768,2048]{1,0:T(8,128)(2,1)}, u32[]{:S(2)}) copy-start(bf16[768,2048]{1,0:T(8,128)(2,1)} %all-gather.4.cloned.1.call-done) | copy-start | bytes 9437188
  354.2 0.7 copy-start.9
  354.2 3.9 copy-start.1
  354.2 3.9 copy-start.3
Sparse Core Ops, SparseCore 0:
  10.8 69.9 all-gather.7
  83.5 60.8 all-gather.5
  189.7 72.9 reduce-scatter.4
  265.5 59.6 all-gather.3
  354.3 73.1 reduce-scatter.2

commit v2 on v1

v2 whole, which is shorter than its diff:
```python
import functools
import jax
import jax.numpy as jnp
from jax import lax
from jax.experimental import pallas as pl
from jax.experimental.pallas import tpu as pltpu
from jax.sharding import PartitionSpec as P

EPSILON = 1e-06
VMEM_LIMIT = 56 * 1024 * 1024
NT = (((1,), (1,)), ((), ()))


def passed_along(block, axis, distance):
    devices = range(lax.axis_size(axis))
    route = [(i - distance, i) for i in devices if i - distance in devices]
    return lax.ppermute(block, axis, route)


def normed(values, gain_row):
    return (
        values * lax.rsqrt(jnp.mean(values * values, axis=-1, keepdims=True) + EPSILON) * gain_row
    )


def norm_pullback(values, gain_row, upstream):
    _, pullback = jax.vjp(lambda argument: normed(argument, gain_row), values)
    return pullback(upstream)[0]


def pack_kernel(experts, rows_ref, gain_ref, ids_ref, gates_ref, out_ref):
    width = rows_ref.shape[1]
    out_ref[:, :width] = normed(rows_ref[...].astype(jnp.float32), gain_ref[...]).astype(
        jnp.bfloat16
    )
    count, extra = rows_ref.shape[0], out_ref.shape[1] - width
    lane = lax.broadcasted_iota(jnp.int32, (count, extra), 1)
    table = jnp.zeros((count, extra), jnp.float32)
    for m in range(2):
        for k in range(ids_ref.shape[2]):
            place = ids_ref[m, :, k : k + 1] + 2 * m * experts
            gate = gates_ref[m, :, k : k + 1]
            high = gate.astype(jnp.bfloat16).astype(jnp.float32)
            table = jnp.where(lane == place, high, table)
            table = jnp.where(lane == place + experts, gate - high, table)
    out_ref[:, width:] = table.astype(jnp.bfloat16)


def packed_rows(rows, gain_row, ids, gates, experts):
    count, width = rows.shape
    extra = -(-4 * experts // 128) * 128
    return pl.pallas_call(
        functools.partial(pack_kernel, experts),
        out_shape=jax.ShapeDtypeStruct((count, width + extra), jnp.bfloat16),
        compiler_params=pltpu.CompilerParams(vmem_limit_bytes=VMEM_LIMIT),
        cost_estimate=pl.CostEstimate(flops=0, bytes_accessed=count * width * 8, transcendentals=0),
    )(rows, gain_row, ids, gates)


def gate_column(table, micro, experts, expert):
    lane = lax.broadcasted_iota(jnp.int32, table.shape, 1)
    place = 2 * micro * experts + expert
    chosen = (lane == place) | (lane == place + experts)
    return jnp.sum(jnp.where(chosen, table, 0.0), axis=1, keepdims=True)


def start_all(copies):
    for copy in copies:
        copy.start()


def wait_all(copies):
    for copy in copies:
        copy.wait()


def block_copies(sources, target, sems, columns=None):
    copies, start = [], 0
    for i, source in enumerate(sources):
        count = source.shape[0]
        view = source if columns is None else source.at[:, columns]
        copies.append(
            pltpu.make_async_copy(view, target.at[pl.ds(start, count)], sems.at[i])
        )
        start += count
    return copies


def write_tiles(tile, outs, columns):
    start = 0
    for out in outs:
        count = out.shape[0]
        out[:, columns] = tile[start : start + count].astype(out.dtype)
        start += count


def forward_kernel(parts, experts, width, tile, names_ref, *refs):
    packed, rows = refs[:parts], refs[parts : 2 * parts]
    weights = refs[2 * parts : 2 * parts + 6]
    outs = refs[2 * parts + 6 : 3 * parts + 6]
    (table, held, hidden, gate_w, up_w, down_w, table_sem, row_sem, weight_sem) = refs[
        3 * parts + 6 :
    ]
    extra = table.shape[1]
    table_copies = block_copies(packed, table, table_sem, pl.ds(width, extra))
    row_copies = block_copies(rows, held, row_sem)
    weight_copies = [
        [
            pltpu.make_async_copy(weights[3 * e + i], target.at[e], weight_sem.at[3 * e + i])
            for i, target in enumerate((gate_w, up_w, down_w))
        ]
        for e in range(2)
    ]
    start_all(row_copies + table_copies)
    start_all(weight_copies[0] + weight_copies[1])
    wait_all(row_copies + table_copies)
    inner = gate_w.shape[2]
    for e in range(2):
        gate = gate_column(table[...].astype(jnp.float32), 0, experts, names_ref[e])
        wait_all(weight_copies[e][:2])

        @pl.loop(0, inner // tile)
        def _(f, e=e, gate=gate):
            columns = pl.ds(pl.multiple_of(f * tile, tile), tile)
            first = jnp.dot(held[...], gate_w[e, :, columns], preferred_element_type=jnp.float32)
            second = jnp.dot(held[...], up_w[e, :, columns], preferred_element_type=jnp.float32)
            made = gate * (jax.nn.silu(first) * second)
            places = pl.ds(pl.multiple_of(e * inner + f * tile, tile), tile)
            hidden[:, places] = made.astype(jnp.bfloat16)

    wait_all([weight_copies[0][2], weight_copies[1][2]])

    @pl.loop(0, width // tile)
    def _(n):
        columns = pl.ds(pl.multiple_of(n * tile, tile), tile)
        total = jnp.dot(
            hidden[:, :inner], down_w[0, :, columns], preferred_element_type=jnp.float32
        ) + jnp.dot(hidden[:, inner:], down_w[1, :, columns], preferred_element_type=jnp.float32)
        write_tiles(total, outs, columns)


def backward_kernel(parts, experts, width, tile, names_ref, *refs):
    packed, cots = refs[:parts], refs[parts : 2 * parts]
    weights = refs[2 * parts : 2 * parts + 6]
    outs = refs[2 * parts + 6 : 3 * parts + 6]
    (held, cot, slot, grads, gate_w, up_w, down_w, row_sem, cot_sem, weight_sem) = refs[
        3 * parts + 6 :
    ]
    row_copies = block_copies(packed, held, row_sem)
    cot_copies = block_copies(cots, cot, cot_sem)
    weight_copies = [
        [
            pltpu.make_async_copy(weights[3 * e + i], target.at[e], weight_sem.at[3 * e + i])
            for i, target in enumerate((gate_w, up_w, down_w))
        ]
        for e in range(2)
    ]
    start_all(row_copies + cot_copies)
    start_all(weight_copies[0] + weight_copies[1])
    wait_all(row_copies + cot_copies)
    inner = gate_w.shape[2]
    for e in range(2):
        table = held[:, width:].astype(jnp.float32)
        gate = gate_column(table, 1, experts, names_ref[e])
        slot[...] = (gate * cot[...].astype(jnp.float32)).astype(jnp.bfloat16)
        wait_all(weight_copies[e])

        @pl.loop(0, inner // tile)
        def _(f, e=e):
            columns = pl.ds(pl.multiple_of(f * tile, tile), tile)
            rows = held[:, :width]
            first = jnp.dot(rows, gate_w[e, :, columns], preferred_element_type=jnp.float32)
            second = jnp.dot(rows, up_w[e, :, columns], preferred_element_type=jnp.float32)
            back = lax.dot_general(
                slot[...], down_w[e, columns, :], NT, preferred_element_type=jnp.float32
            )
            sigmoid_part = jax.nn.sigmoid(first)
            gate_grad = back * second * sigmoid_part * (1.0 + first * (1.0 - sigmoid_part))
            second_grad = back * (first * sigmoid_part)
            places = pl.ds(pl.multiple_of(f * tile, tile), tile)
            grads[2 * e, :, places] = gate_grad.astype(jnp.bfloat16)
            grads[2 * e + 1, :, places] = second_grad.astype(jnp.bfloat16)

    @pl.loop(0, width // tile)
    def _(n):
        columns = pl.ds(pl.multiple_of(n * tile, tile), tile)
        total = None
        for e in range(2):
            for i, weight in enumerate((gate_w, up_w)):
                term = lax.dot_general(
                    grads[2 * e + i], weight[e, columns, :], NT, preferred_element_type=jnp.float32
                )
                total = term if total is None else total + term
        write_tiles(total, outs, columns)


def expert_call(kind, names, packed, rows, weights, experts):
    parts = len(rows)
    counts = [block.shape[0] for block in rows]
    total = sum(counts)
    width = rows[0].shape[1]
    full = packed[0].shape[1]
    inner = weights[0].shape[1]
    tile = 256
    hbm = pl.BlockSpec(memory_space=pl.ANY)
    weight_scratch = [
        pltpu.VMEM((2, width, inner), jnp.bfloat16),
        pltpu.VMEM((2, width, inner), jnp.bfloat16),
        pltpu.VMEM((2, inner, width), jnp.bfloat16),
    ]
    sems = [pltpu.SemaphoreType.DMA((parts,)), pltpu.SemaphoreType.DMA((parts,))]
    sems += [pltpu.SemaphoreType.DMA((6,))]
    if kind == "forward":
        body = forward_kernel
        scratch = [
            pltpu.VMEM((total, full - width), jnp.bfloat16),
            pltpu.VMEM((total, width), jnp.bfloat16),
            pltpu.VMEM((total, 2 * inner), jnp.bfloat16),
        ]
        products = 6
    else:
        body = backward_kernel
        scratch = [
            pltpu.VMEM((total, full), jnp.bfloat16),
            pltpu.VMEM((total, width), jnp.bfloat16),
            pltpu.VMEM((total, width), jnp.bfloat16),
            pltpu.VMEM((4, total, inner), jnp.bfloat16),
        ]
        products = 10
    out = pl.pallas_call(
        functools.partial(body, parts, experts, width, tile),
        out_shape=[jax.ShapeDtypeStruct((count, width), jnp.bfloat16) for count in counts],
        in_specs=[pl.BlockSpec(memory_space=pltpu.SMEM)] + [hbm] * (2 * parts + 6),
        scratch_shapes=scratch + weight_scratch + sems,
        compiler_params=pltpu.CompilerParams(vmem_limit_bytes=VMEM_LIMIT),
        cost_estimate=pl.CostEstimate(
            flops=2 * products * total * width * inner,
            bytes_accessed=12 * width * inner,
            transcendentals=2 * total * inner,
        ),
    )(names, *packed, *rows, *weights)
    return list(out)


class Ring:
    def __init__(self, sources):
        self.chips = sources // 2
        order = list(range(0, self.chips, 2)) + list(range(1, self.chips, 2))[::-1]
        following = {order[i]: order[(i + 1) % self.chips] for i in range(self.chips)}
        pairs = [(2 * a + core, 2 * b + core) for a, b in following.items() for core in range(2)]
        self.routes = (pairs, [(b, a) for a, b in pairs])
        self.swap = [(i, i ^ 1) for i in range(sources)]

    def pass_on(self, block, way):
        return lax.ppermute(block, "ep", self.routes[way])

    def gather(self, block):
        groups = [[block]]
        behind = ahead = block
        for _ in range(self.chips // 2 - 1):
            behind, ahead = self.pass_on(behind, 0), self.pass_on(ahead, 1)
            groups.append([behind, ahead])
        half = block.shape[0] // 2
        groups.append([self.pass_on(behind[:half], 0), self.pass_on(ahead[half:], 1)])
        return groups

    def scatter_sum(self, groups):
        half = groups[-1][0].shape[0]
        forth, back = self.pass_on(groups[-1][0], 0), self.pass_on(groups[-1][1], 1)
        for distance in range(self.chips // 2 - 1, 0, -1):
            behind, ahead = groups[distance]
            if distance == self.chips // 2 - 1:
                ahead = jnp.concatenate([added(ahead[:half], forth), ahead[half:]])
                behind = jnp.concatenate([behind[:half], added(behind[half:], back)])
            else:
                ahead, behind = added(ahead, forth), added(behind, back)
            forth, back = self.pass_on(ahead, 0), self.pass_on(behind, 1)
        return [piece.astype(jnp.float32) for piece in (groups[0][0], forth, back)]


def added(first, second):
    return (first.astype(jnp.float32) + second.astype(jnp.float32)).astype(jnp.bfloat16)


def run_groups(kind, names, packed, rows, weights, experts):
    first = expert_call(
        kind, names, packed[0] + packed[1], rows[0] + rows[1], weights, experts
    )
    made = [first[:1], first[1:]]
    for near, far in zip(packed[2:], rows[2:]):
        made.append(expert_call(kind, names, near, far, weights, experts))
    return made


def local(
    entering,
    rising_prev,
    falling_cot,
    falling_saved,
    targets,
    norm_gain,
    exit_gain,
    w_gate,
    w_up,
    w_down,
    route_ids,
    route_gates,
    exit_list,
):
    section_index = lax.axis_index("pipe")
    sections = lax.axis_size("pipe")
    sources = lax.axis_size("ep")
    here = lax.axis_index("ep")
    names = jnp.stack([here, here + 1 - 2 * (here % 2)]).astype(jnp.int32)
    norm_row = norm_gain[0]
    exit_row = exit_gain[0]
    ring = Ring(sources)

    packed = packed_rows(falling_saved[0], norm_gain, route_ids[:, 0], route_gates[:, 0], sources)
    all_packed = ring.gather(packed)
    moved_cot, moved_rise = passed_along((falling_cot[0], rising_prev[0]), "pipe", 1)
    own = (w_gate[0, 0], w_up[0, 0], w_down[0, 0])
    weights = own + tuple(lax.ppermute(own, "ep", ring.swap))

    at_start = section_index == 0
    cot_in = jnp.where(at_start, entering[1], moved_cot)
    all_cot = ring.gather(cot_in)
    rise_in = jnp.where(at_start, entering[0], moved_rise)
    rise_wide = rise_in.astype(jnp.float32)
    all_rise = ring.gather(normed(rise_wide, norm_row).astype(jnp.bfloat16))

    cotangent = cot_in.astype(jnp.float32)
    head_rise = jnp.take(exit_list[0], section_index).astype(jnp.float32)
    head_fall = jnp.take(exit_list[1], sections - 1 - section_index).astype(jnp.float32)
    fall_wide = falling_saved[0].astype(jnp.float32)

    made_fall = run_groups("backward", names, all_packed, all_cot, weights, sources)
    grad_parts = ring.scatter_sum(made_fall)
    norm_grad = grad_parts[0] + grad_parts[1] + grad_parts[2]
    made_rise = run_groups("forward", names, all_packed, all_rise, weights, sources)
    rise_parts = ring.scatter_sum(made_rise)
    layer_out = rise_wide + (rise_parts[0] + rise_parts[1] + rise_parts[2])

    rise_diff = normed(rise_wide, exit_row) - targets[0].astype(jnp.float32)
    loss_rise = head_rise * 0.5 * jnp.mean(rise_diff * rise_diff, axis=-1)
    fall_diff = normed(fall_wide, exit_row) - targets[1].astype(jnp.float32)
    fall_total = cotangent + norm_pullback(fall_wide, norm_row, norm_grad)
    fall_total = fall_total + head_fall * norm_pullback(fall_wide, exit_row, fall_diff)
    loss_fall = head_fall * 0.5 * jnp.mean(fall_diff * fall_diff, axis=-1)
    exit_loss = jnp.stack([loss_rise, loss_fall])[:, None, :]
    return (layer_out.astype(jnp.bfloat16)[None], fall_total.astype(jnp.bfloat16)[None], exit_loss)


def solution(mesh):
    placed = (
        P(None, "ep", None),
        P("pipe", "ep", None),
        P("pipe", "ep", None),
        P("pipe", "ep", None),
        P(None, "ep", None),
        P("pipe", None),
        P("pipe", None),
        P("pipe", "ep", None, None),
        P("pipe", "ep", None, None),
        P("pipe", "ep", None, None),
        P(None, "pipe", "ep", None),
        P(None, "pipe", "ep", None),
        P(),
    )
    return jax.shard_map(
        local,
        mesh=mesh,
        in_specs=placed,
        out_specs=(P("pipe", "ep", None), P("pipe", "ep", None), P(None, "pipe", "ep")),
        check_vma=False,
    )
```

time: 436 us -> 287 us (0.66)
  waiting for transfers between devices: 266 us -> 108 us
  Pallas kernels: 0 us -> 102 us
  matrix products: 83.3 us -> 0 us
  starting transfers between devices: 9.31 us -> 48.1 us
  blocking collectives: 34.4 us -> 0 us
  between operations: 15.4 us -> 2.58 us
    reduce_scatter x2 -> x0, waiting for transfers between devices: 129 us -> none  [scattered(): lax.psum_scatter(block, 'ep', scatter_dimension=0, axis_index_groups=grou...]
    all_gather x3 -> x0, waiting for transfers between devices: 121 us -> none  [gathered(): return lax.all_gather(block, 'ep', axis_index_groups=groups, tiled=True)]
    ppermute x3 -> x43, waiting for transfers between devices: 0.01 us -> 107 us  [the longest x40 107 us: pass_on(): return lax.ppermute(block, 'ep', self.routes[way])]
    pallas_call x0 -> x9, Pallas kernels: none -> 102 us  [the longest x8 99.8 us: expert_call(): pl.pallas_call(functools.partial(body, parts, experts, width, tile), out_...]
    dot_general x12 -> x0, matrix products: 83.3 us -> none  [the longest x2 24.4 us: expert_backward(): lax.dot_general(gate_grad, gate_weight, contract, preferred_element_type=...]
    ppermute x3 -> x43, starting transfers between devices: 0.65 us -> 41.1 us  [the longest x40 41.1 us: pass_on(): return lax.ppermute(block, 'ep', self.routes[way])]
    all_gather x1 -> x0, blocking collectives: 34.4 us -> none  [gathered(): return lax.all_gather(block, 'ep', axis_index_groups=groups, tiled=True)]
    ppermute x2, waiting for transfers between devices: 15.9 us -> 0.24 us  [passed_along(): return lax.ppermute(block, axis, route)]
  transfers between devices with their start and end apart: 10 -> 45, of which waited for: 7 -> 26; matrix products, arithmetic and copies ran while one was open for 12% -> 7% of each run, Pallas kernels for 0% -> 32%
where the time goes in v2:
time: 287 us
  waiting for transfers between devices  108 us (38%)
  Pallas kernels  102 us (36%)
  starting transfers between devices  48.1 us (17%)
  local copies, waits for them, and re-layouts  15.2 us (5%)
  other arithmetic  10.5 us (4%)
    ppermute x40, waiting for transfers between devices, pass_on(): return lax.ppermute(block, 'ep', self.routes[way])  107 us
    pallas_call x8, Pallas kernels, expert_call(): pl.pallas_call(functools.partial(body, parts, experts, width, tile), out_...  99.8 us
    ppermute x40, starting transfers between devices, pass_on(): return lax.ppermute(block, 'ep', self.routes[way])  41.1 us
    ppermute x2, starting transfers between devices, passed_along(): return lax.ppermute(block, axis, route)  7.06 us
  transfers between devices with their start and end apart: 45, of which 26 were waited for; matrix products, arithmetic and copies ran while one was open for 7% of the time, Pallas kernels for 32%

profile of v2, /device:TPU:0, one launch (start us, length us, event | category | flops | bytes accessed | tf_op | source)
XLA Modules:
  0.0 286.6 jit_solution(13997489363468990014)
XLA Ops:
  0.7 5.8 %collective-permute-start.28 = (bf16[96,2048]{1,0:T(8,128)(2,1)}, bf16[96,2048]{1,0:T(8,128)(2,1)}, u32[]{:S(2)}, u32[]{:S(2)}) collective-permute-start(bf16[96,2048]{1,0:T(8,128)(2,1)} %bitcast.84), channel_id=1, source_target_pairs={{0,16},{1,17},{2,18},{3,19},{4,20},{5,21},{6,22},{7,23},{8,24},{9,... | collective-permute-start | bytes 1179656 | tf_op jit(solution)/shard_map/ppermute | solution.py:17
  6.4 1.5 copy.16
  7.9 1.5 copy.17
  9.3 2.7 shard_map.148.refs_0_
  12.0 1.6 collective-permute-start.1
  14.3 1.0 bitcast_select_fusion.refs_3_
  15.4 1.6 collective-permute-start.29
  17.4 7.4 %collective-permute-done.1.refs_1_ = bf16[96,2176]{1,0:T(8,128)(2,1)S(1)} collective-permute-done((bf16[96,2176]{1,0:T(8,128)(2,1)}, bf16[96,2176]{1,0:T(8,128)(2,1)S(1)}, u32[]{:S(2)}, u32[]{:S(2)}) %collective-permute-start.1) | collective-permute-done | bytes 417824 | tf_op jit(solution)/shard_map/ppermute | solution.py:255
  24.8 1.7 collective-permute-done.2.refs_2_
  26.5 5.3 %collective-permute-done.29.refs_4_ = bf16[96,2048]{1,0:T(8,128)(2,1)S(1)} collective-permute-done((bf16[96,2048]{1,0:T(8,128)(2,1)S(1)}, bf16[96,2048]{1,0:T(8,128)(2,1)S(1)}, u32[]{:S(2)}, u32[]{:S(2)}) %collective-permute-start.29) | collective-permute-done | bytes 393248 | tf_op jit(solution)/shard_map/ppermute | solution.py:255
  31.8 1.6 collective-permute-start.8
  33.8 8.4 %collective-permute-done.8.refs_0_ = bf16[96,2176]{1,0:T(8,128)(2,1)S(1)} collective-permute-done((bf16[96,2176]{1,0:T(8,128)(2,1)}, bf16[96,2176]{1,0:T(8,128)(2,1)S(1)}, u32[]{:S(2)}, u32[]{:S(2)}) %collective-permute-start.8) | collective-permute-done | bytes 417824 | tf_op jit(solution)/shard_map/ppermute | solution.py:255
  42.2 1.6 collective-permute-start.31
  44.2 7.2 %collective-permute-done.31.refs_2_ = bf16[96,2048]{1,0:T(8,128)(2,1)} collective-permute-done((bf16[96,2048]{1,0:T(8,128)(2,1)S(1)}, bf16[96,2048]{1,0:T(8,128)(2,1)}, u32[]{:S(2)}, u32[]{:S(2)}) %collective-permute-start.31) | collective-permute-done | bytes 393248 | tf_op jit(solution)/shard_map/ppermute | solution.py:255
  51.5 1.6 collective-permute-start.12
  53.5 7.6 %collective-permute-done.12.refs_0_ = bf16[96,2176]{1,0:T(8,128)(2,1)} collective-permute-done((bf16[96,2176]{1,0:T(8,128)(2,1)S(1)}, bf16[96,2176]{1,0:T(8,128)(2,1)}, u32[]{:S(2)}, u32[]{:S(2)}) %collective-permute-start.12) | collective-permute-done | bytes 417824 | tf_op jit(solution)/shard_map/ppermute | solution.py:255
  61.1 1.6 collective-permute-start.33
  64.1 0.9 slice.91
  65.0 6.3 %collective-permute-done.33.refs_2_ = bf16[96,2048]{1,0:T(8,128)(2,1)} collective-permute-done((bf16[96,2048]{1,0:T(8,128)(2,1)}, bf16[96,2048]{1,0:T(8,128)(2,1)}, u32[]{:S(2)}, u32[]{:S(2)}) %collective-permute-start.33) | collective-permute-done | bytes 393248 | tf_op jit(solution)/shard_map/ppermute | solution.py:255
  71.4 1.6 collective-permute-start.16
  76.2 2.1 collective-permute-done.16.refs_0_
  78.3 1.6 collective-permute-start.35
  80.4 3.6 %collective-permute-done.35.refs_2_ = bf16[48,2048]{1,0:T(8,128)(2,1)S(1)} collective-permute-done((bf16[48,2048]{1,0:T(8,128)(2,1)S(1)}, bf16[48,2048]{1,0:T(8,128)(2,1)S(1)}, u32[]{:S(2)}, u32[]{:S(2)}) %collective-permute-start.35) | collective-permute-done | bytes 196640 | tf_op jit(solution)/shard_map/ppermute | solution.py:255
  84.0 1.3 collective-permute-start
  86.3 12.7 %shard_map.156 = (bf16[48,2048]{1,0:T(8,128)(2,1)}, bf16[48,2048]{1,0:T(8,128)(2,1)}) custom-call(s32[2]{0:T(128)} %pad_add_fusion.names_ref, bf16[48,2176]{1,0:T(8,128)(2,1)} %copy-done.9, bf16[48,2176]{1,0:T(8,128)(2,1)} %copy-done.10, bf16[48,2048]{1,0:T(8,128)(2,1)} %copy-done.30, bf16[48,2048]{1,0:T(8,128)(2,1)} %copy-done.32, ...), custom_call_target="tpu_custom_call" | custom-call | flops 2013265920 | bytes 12582912 | tf_op jit(solution)/shard_map/pallas_call | solution.py:230
  99.1 1.6 collective-permute-start.37
  100.7 14.1 %shard_map.155 = (bf16[96,2048]{1,0:T(8,128)(2,1)}, bf16[96,2048]{1,0:T(8,128)(2,1)}) custom-call(s32[2]{0:T(128)} %pad_add_fusion.names_ref, bf16[96,2176]{1,0:T(8,128)(2,1)} %collective-permute-done.12.refs_0_, bf16[96,2176]{1,0:T(8,128)(2,1)} %collective-permute-done.13.refs_1_, bf16[96,2048]{1,0:T(8,128)(2,1)} %collective-permute-done.33.refs_2_, ...), custom_call_target="tpu_custom_call" | custom-call | flops 4026531840 | bytes 12582912 | tf_op jit(solution)/shard_map/pallas_call | solution.py:230
  117.3 15.6 %shard_map.153 = (bf16[96,2048]{1,0:T(8,128)(2,1)}, bf16[96,2048]{1,0:T(8,128)(2,1)}, bf16[96,2048]{1,0:T(8,128)(2,1)}) custom-call(s32[2]{0:T(128)} %pad_add_fusion.names_ref, bf16[96,2176]{1,0:T(8,128)(2,1)} %shard_map.148.refs_0_, bf16[96,2176]{1,0:T(8,128)(2,1)} %copy-done.14, bf16[96,2176]{1,0:T(8,128)(2,1)} %collective-permute-done.2.refs_2_, ...), custom_call_target="tpu_custom_call" | custom-call | flops 6039797760 | bytes 12582912 | tf_op jit(solution)/shard_map/pallas_call | solution.py:230
  132.9 14.2 %shard_map.154 = (bf16[96,2048]{1,0:T(8,128)(2,1)}, bf16[96,2048]{1,0:T(8,128)(2,1)}) custom-call(s32[2]{0:T(128)} %pad_add_fusion.names_ref, bf16[96,2176]{1,0:T(8,128)(2,1)} %copy-done.12, bf16[96,2176]{1,0:T(8,128)(2,1)} %copy-done.13, bf16[96,2048]{1,0:T(8,128)(2,1)} %collective-permute-done.31.refs_2_, ...), custom_call_target="tpu_custom_call" | custom-call | flops 4026531840 | bytes 12582912 | tf_op jit(solution)/shard_map/pallas_call | solution.py:230
  147.3 1.6 collective-permute-start.38
  149.5 8.4 %collective-permute-done.38 = bf16[96,2048]{1,0:T(8,128)(2,1)S(1)} collective-permute-done((bf16[96,2048]{1,0:T(8,128)(2,1)S(1)}, bf16[96,2048]{1,0:T(8,128)(2,1)S(1)}, u32[]{:S(2)}, u32[]{:S(2)}) %collective-permute-start.38) | collective-permute-done | bytes 393248 | tf_op jit(solution)/shard_map/ppermute | solution.py:255
  158.0 1.6 collective-permute-start.39
  160.3 7.4 %collective-permute-done.39 = bf16[96,2048]{1,0:T(8,128)(2,1)S(1)} collective-permute-done((bf16[96,2048]{1,0:T(8,128)(2,1)S(1)}, bf16[96,2048]{1,0:T(8,128)(2,1)S(1)}, u32[]{:S(2)}, u32[]{:S(2)}) %collective-permute-start.39) | collective-permute-done | bytes 393248 | tf_op jit(solution)/shard_map/ppermute | solution.py:255
  167.8 1.6 collective-permute-start.40
  170.3 8.7 %collective-permute-done.40 = bf16[96,2048]{1,0:T(8,128)(2,1)S(1)} collective-permute-done((bf16[96,2048]{1,0:T(8,128)(2,1)S(1)}, bf16[96,2048]{1,0:T(8,128)(2,1)S(1)}, u32[]{:S(2)}, u32[]{:S(2)}) %collective-permute-start.40) | collective-permute-done | bytes 393248 | tf_op jit(solution)/shard_map/ppermute | solution.py:255
  179.0 1.3 collective-permute-done.44
  180.3 1.4 multiply_reduce_fusion
  181.7 1.5 collective-permute-start.3
  185.5 1.3 constant_dynamic-slice_fusion
  188.2 3.2 %collective-permute-done.3.refs_4_ = bf16[96,2048]{1,0:T(8,128)(2,1)S(1)} collective-permute-done((bf16[96,2048]{1,0:T(8,128)(2,1)S(1)}, bf16[96,2048]{1,0:T(8,128)(2,1)S(1)}, u32[]{:S(2)}, u32[]{:S(2)}) %collective-permute-start.3) | collective-permute-done | bytes 393248 | tf_op jit(solution)/shard_map/ppermute | solution.py:255
  191.4 1.5 collective-permute-start.10
  194.8 4.4 %collective-permute-done.10.refs_2_ = bf16[96,2048]{1,0:T(8,128)(2,1)S(1)} collective-permute-done((bf16[96,2048]{1,0:T(8,128)(2,1)S(1)}, bf16[96,2048]{1,0:T(8,128)(2,1)S(1)}, u32[]{:S(2)}, u32[]{:S(2)}) %collective-permute-start.10) | collective-permute-done | bytes 393248 | tf_op jit(solution)/shard_map/ppermute | solution.py:255
  199.2 1.5 collective-permute-start.14
  202.0 12.1 %shard_map.149 = (bf16[96,2048]{1,0:T(8,128)(2,1)}, bf16[96,2048]{1,0:T(8,128)(2,1)}, bf16[96,2048]{1,0:T(8,128)(2,1)}) custom-call(s32[2]{0:T(128)} %pad_add_fusion.names_ref, bf16[96,2176]{1,0:T(8,128)(2,1)} %shard_map.148.refs_0_, bf16[96,2176]{1,0:T(8,128)(2,1)} %copy-done.14, bf16[96,2176]{1,0:T(8,128)(2,1)} %collective-permute-done.2.refs_2_, ...), custom_call_target="tpu_custom_call" | custom-call | flops 3623878656 | bytes 12582912 | tf_op jit(solution)/shard_map/pallas_call | solution.py:230
  214.2 1.5 collective-permute-start.18
  216.3 10.7 %shard_map.150 = (bf16[96,2048]{1,0:T(8,128)(2,1)}, bf16[96,2048]{1,0:T(8,128)(2,1)}) custom-call(s32[2]{0:T(128)} %pad_add_fusion.names_ref, bf16[96,2176]{1,0:T(8,128)(2,1)} %copy-done.12, bf16[96,2176]{1,0:T(8,128)(2,1)} %copy-done.13, bf16[96,2048]{1,0:T(8,128)(2,1)} %copy-done.15, bf16[96,2048]{1,0:T(8,128)(2,1)} %copy-done.16, ...), custom_call_target="tpu_custom_call" | custom-call | flops 2415919104 | bytes 12582912 | tf_op jit(solution)/shard_map/pallas_call | solution.py:230
  228.4 9.6 %shard_map.152 = (bf16[48,2048]{1,0:T(8,128)(2,1)}, bf16[48,2048]{1,0:T(8,128)(2,1)}) custom-call(s32[2]{0:T(128)} %pad_add_fusion.names_ref, bf16[48,2176]{1,0:T(8,128)(2,1)} %copy-done.9, bf16[48,2176]{1,0:T(8,128)(2,1)} %copy-done.10, bf16[48,2048]{1,0:T(8,128)(2,1)} %copy-done.31, bf16[48,2048]{1,0:T(8,128)(2,1)} %copy-done.33, ...), custom_call_target="tpu_custom_call" | custom-call | flops 1207959552 | bytes 12582912 | tf_op jit(solution)/shard_map/pallas_call | solution.py:230
  238.1 1.7 collective-permute-start.20
  239.8 10.7 %shard_map.151 = (bf16[96,2048]{1,0:T(8,128)(2,1)}, bf16[96,2048]{1,0:T(8,128)(2,1)}) custom-call(s32[2]{0:T(128)} %pad_add_fusion.names_ref, bf16[96,2176]{1,0:T(8,128)(2,1)} %collective-permute-done.12.refs_0_, bf16[96,2176]{1,0:T(8,128)(2,1)} %collective-permute-done.13.refs_1_, bf16[96,2048]{1,0:T(8,128)(2,1)} %copy-done.7, bf16[96,2048]{1,0:T(8,128)(2,1)} %copy-done.8, ...), custom_call_target="tpu_custom_call" | custom-call | flops 2415919104 | bytes 12582912 | tf_op jit(solution)/shard_map/pallas_call | solution.py:230
  250.5 1.0 slice.66
  251.5 1.0 slice.67
  253.2 1.0 add_convert_fusion.11
  254.2 1.5 collective-permute-start.21
  255.7 3.1 %collective-permute-done.24 = bf16[48,2048]{1,0:T(8,128)(2,1)S(1)} collective-permute-done((bf16[48,2048]{1,0:T(8,128)(2,1)S(1)}, bf16[48,2048]{1,0:T(8,128)(2,1)S(1)}, u32[]{:S(2)}, u32[]{:S(2)}) %collective-permute-start.24) | collective-permute-done | bytes 196640 | tf_op jit(solution)/shard_map/ppermute | solution.py:255
  259.2 6.7 %collective-permute-done.21 = bf16[96,2048]{1,0:T(8,128)(2,1)S(1)} collective-permute-done((bf16[96,2048]{1,0:T(8,128)(2,1)S(1)}, bf16[96,2048]{1,0:T(8,128)(2,1)S(1)}, u32[]{:S(2)}, u32[]{:S(2)}) %collective-permute-start.21) | collective-permute-done | bytes 393248 | tf_op jit(solution)/shard_map/ppermute | solution.py:255
  266.0 1.8 collective-permute-start.22
  267.8 1.0 collective-permute-done.25
  269.0 4.9 %collective-permute-done.22 = bf16[96,2048]{1,0:T(8,128)(2,1)S(1)} collective-permute-done((bf16[96,2048]{1,0:T(8,128)(2,1)S(1)}, bf16[96,2048]{1,0:T(8,128)(2,1)S(1)}, u32[]{:S(2)}, u32[]{:S(2)}) %collective-permute-start.22) | collective-permute-done | bytes 393248 | tf_op jit(solution)/shard_map/ppermute | solution.py:255
  274.0 1.8 collective-permute-start.23
  275.8 1.9 collective-permute-done.26
  277.9 1.4 fusion.18
  279.3 2.5 collective-permute-done.23
  281.8 3.8 %collective-permute-done.27 = bf16[96,2048]{1,0:T(8,128)(2,1)S(1)} collective-permute-done((bf16[96,2048]{1,0:T(8,128)(2,1)S(1)}, bf16[96,2048]{1,0:T(8,128)(2,1)S(1)}, u32[]{:S(2)}, u32[]{:S(2)}) %collective-permute-start.27) | collective-permute-done | bytes 393248 | tf_op jit(solution)/shard_map/ppermute | solution.py:255
  285.6 1.0 fusion.17
  (167 shorter events, 22.8 us)
Async XLA Ops:
  0.6 16.8 %copy-start = (bf16[1,1,2048,512]{3,2,1,0:T(8,128)(2,1)S(1)}, bf16[1,1,2048,512]{3,2,1,0:T(8,128)(2,1)}, u32[]{:S(2)}) copy-start(bf16[1,1,2048,512]{3,2,1,0:T(8,128)(2,1)} %param.20) | copy-start | bytes 6291460
  0.6 73.5 %copy-start.1 = (bf16[1,96,2048]{2,1,0:T(8,128)(2,1)S(1)}, bf16[1,96,2048]{2,1,0:T(8,128)(2,1)}, u32[]{:S(2)}) copy-start(bf16[1,96,2048]{2,1,0:T(8,128)(2,1)} %param.16) | copy-start | bytes 1179652
  0.7 13.7 %collective-permute-start.28 = (bf16[96,2048]{1,0:T(8,128)(2,1)}, bf16[96,2048]{1,0:T(8,128)(2,1)}, u32[]{:S(2)}, u32[]{:S(2)}) collective-permute-start(bf16[96,2048]{1,0:T(8,128)(2,1)} %bitcast.84), channel_id=1, source_target_pairs={{0,16},{1,17},{2,18},{3,19},{4,20},{5,21},{6,22},{7,23},{8,24},{9,... | collective-permute-start | bytes 1179656 | tf_op jit(solution)/shard_map/ppermute | solution.py:17
  12.0 12.8 %collective-permute-start.1 = (bf16[96,2176]{1,0:T(8,128)(2,1)}, bf16[96,2176]{1,0:T(8,128)(2,1)S(1)}, u32[]{:S(2)}, u32[]{:S(2)}) collective-permute-start(bf16[96,2176]{1,0:T(8,128)(2,1)} %shard_map.148.refs_0_), channel_id=1, source_target_pairs={{0,4},{1,5},{4,8},{5,9},{8,12},{9,13},{12,14},{13,15},{14,10},{15,... | collective-permute-start | bytes 1253384 | tf_op jit(solution)/shard_map/ppermute | solution.py:255
  13.6 12.9 %collective-permute-start.2 = (bf16[96,2176]{1,0:T(8,128)(2,1)}, bf16[96,2176]{1,0:T(8,128)(2,1)}, u32[]{:S(2)}, u32[]{:S(2)}) collective-permute-start(bf16[96,2176]{1,0:T(8,128)(2,1)} %shard_map.148.refs_0_), channel_id=1, source_target_pairs={{4,0},{5,1},{8,4},{9,5},{12,8},{13,9},{14,12},{15,13},{10,14},{11,... | collective-permute-start | bytes 1253384 | tf_op jit(solution)/shard_map/ppermute | solution.py:255
  15.4 83.7 %copy-start.4 = (bf16[96,2048]{1,0:T(8,128)(2,1)}, bf16[96,2048]{1,0:T(8,128)(2,1)S(1)}, u32[]{:S(2)}) copy-start(bf16[96,2048]{1,0:T(8,128)(2,1)S(1)} %bitcast_select_fusion.refs_3_) | copy-start | bytes 1179652
  15.4 16.4 %collective-permute-start.29 = (bf16[96,2048]{1,0:T(8,128)(2,1)S(1)}, bf16[96,2048]{1,0:T(8,128)(2,1)S(1)}, u32[]{:S(2)}, u32[]{:S(2)}) collective-permute-start(bf16[96,2048]{1,0:T(8,128)(2,1)S(1)} %bitcast_select_fusion.refs_3_), channel_id=1, source_target_pairs={{0,4},{1,5},{4,8},{5,9},{8,12},{9,13},{12,14},{13,15},{14,10},{15,... | collective-permute-start | bytes 1179656 | tf_op jit(solution)/shard_map/ppermute | solution.py:255
  17.0 16.4 %collective-permute-start.30 = (bf16[96,2048]{1,0:T(8,128)(2,1)S(1)}, bf16[96,2048]{1,0:T(8,128)(2,1)S(1)}, u32[]{:S(2)}, u32[]{:S(2)}) collective-permute-start(bf16[96,2048]{1,0:T(8,128)(2,1)S(1)} %bitcast_select_fusion.refs_3_), channel_id=1, source_target_pairs={{4,0},{5,1},{8,4},{9,5},{12,8},{13,9},{14,12},{15,13},{10,14},{11,... | collective-permute-start | bytes 1179656 | tf_op jit(solution)/shard_map/ppermute | solution.py:255
  17.4 68.1 %collective-permute-start.5 = (bf16[2048,512]{1,0:T(8,128)(2,1)S(1)}, bf16[2048,512]{1,0:T(8,128)(2,1)}, u32[]{:S(2)}, u32[]{:S(2)}) collective-permute-start(bf16[2048,512]{1,0:T(8,128)(2,1)S(1)} %bitcast.57), channel_id=1, source_target_pairs={{0,1},{1,0},{2,3},{3,2},{4,5},{5,4},{6,7},{7,6},{8,9},{9,8},{10,11... | collective-permute-start | bytes 6291464 | tf_op jit(solution)/shard_map/ppermute | solution.py:323
  24.8 60.8 %collective-permute-start.6 = (bf16[2048,512]{1,0:T(8,128)(2,1)}, bf16[2048,512]{1,0:T(8,128)(2,1)}, u32[]{:S(2)}, u32[]{:S(2)}) collective-permute-start(bf16[2048,512]{1,0:T(8,128)(2,1)} %bitcast.58), channel_id=1, source_target_pairs={{0,1},{1,0},{2,3},{3,2},{4,5},{5,4},{6,7},{7,6},{8,9},{9,8},{10,11... | collective-permute-start | bytes 6291464 | tf_op jit(solution)/shard_map/ppermute | solution.py:323
  26.5 59.1 %collective-permute-start.7 = (bf16[512,2048]{1,0:T(8,128)(2,1)}, bf16[512,2048]{1,0:T(8,128)(2,1)}, u32[]{:S(2)}, u32[]{:S(2)}) collective-permute-start(bf16[512,2048]{1,0:T(8,128)(2,1)} %bitcast.67), channel_id=1, source_target_pairs={{0,1},{1,0},{2,3},{3,2},{4,5},{5,4},{6,7},{7,6},{8,9},{9,8},{10,11... | collective-permute-start | bytes 6291464 | tf_op jit(solution)/shard_map/ppermute | solution.py:323
  31.8 30.9 %copy-start.40 = (bf16[96,2048]{1,0:T(8,128)(2,1)}, bf16[96,2048]{1,0:T(8,128)(2,1)S(1)}, u32[]{:S(2)}) copy-start(bf16[96,2048]{1,0:T(8,128)(2,1)S(1)} %collective-permute-done.29.refs_4_) | copy-start | bytes 1179652
  31.8 10.4 %collective-permute-start.8 = (bf16[96,2176]{1,0:T(8,128)(2,1)}, bf16[96,2176]{1,0:T(8,128)(2,1)S(1)}, u32[]{:S(2)}, u32[]{:S(2)}) collective-permute-start(bf16[96,2176]{1,0:T(8,128)(2,1)} %copy-done.14), channel_id=1, source_target_pairs={{0,4},{1,5},{4,8},{5,9},{8,12},{9,13},{12,14},{13,15},{14,10},{15,... | collective-permute-start | bytes 1253384 | tf_op jit(solution)/shard_map/ppermute | solution.py:255
  33.4 29.3 %copy-start.41 = (bf16[96,2048]{1,0:T(8,128)(2,1)}, bf16[96,2048]{1,0:T(8,128)(2,1)S(1)}, u32[]{:S(2)}) copy-start(bf16[96,2048]{1,0:T(8,128)(2,1)S(1)} %collective-permute-done.30.refs_5_) | copy-start | bytes 1179652
  33.4 10.4 %collective-permute-start.9 = (bf16[96,2176]{1,0:T(8,128)(2,1)}, bf16[96,2176]{1,0:T(8,128)(2,1)S(1)}, u32[]{:S(2)}, u32[]{:S(2)}) collective-permute-start(bf16[96,2176]{1,0:T(8,128)(2,1)} %collective-permute-done.2.refs_2_), channel_id=1, source_target_pairs={{4,0},{5,1},{8,4},{9,5},{12,8},{13,9},{14,12},{15,13},{10,14},{11,... | collective-permute-start | bytes 1253384 | tf_op jit(solution)/shard_map/ppermute | solution.py:255
  42.2 56.8 %copy-start.12 = (bf16[96,2176]{1,0:T(8,128)(2,1)}, bf16[96,2176]{1,0:T(8,128)(2,1)S(1)}, u32[]{:S(2)}) copy-start(bf16[96,2176]{1,0:T(8,128)(2,1)S(1)} %collective-permute-done.8.refs_0_) | copy-start | bytes 1253380
  42.2 9.3 %collective-permute-start.31 = (bf16[96,2048]{1,0:T(8,128)(2,1)S(1)}, bf16[96,2048]{1,0:T(8,128)(2,1)}, u32[]{:S(2)}, u32[]{:S(2)}) collective-permute-start(bf16[96,2048]{1,0:T(8,128)(2,1)S(1)} %collective-permute-done.29.refs_4_), channel_id=1, source_target_pairs={{0,4},{1,5},{4,8},{5,9},{8,12},{9,13},{12,14},{13,15},{14,10},{15,... | collective-permute-start | bytes 1179656 | tf_op jit(solution)/shard_map/ppermute | solution.py:255
  43.8 17.3 %copy-start.13 = (bf16[96,2176]{1,0:T(8,128)(2,1)}, bf16[96,2176]{1,0:T(8,128)(2,1)S(1)}, u32[]{:S(2)}) copy-start(bf16[96,2176]{1,0:T(8,128)(2,1)S(1)} %collective-permute-done.9.refs_1_) | copy-start | bytes 1253380
  43.8 9.3 %collective-permute-start.32 = (bf16[96,2048]{1,0:T(8,128)(2,1)S(1)}, bf16[96,2048]{1,0:T(8,128)(2,1)}, u32[]{:S(2)}, u32[]{:S(2)}) collective-permute-start(bf16[96,2048]{1,0:T(8,128)(2,1)S(1)} %collective-permute-done.30.refs_5_), channel_id=1, source_target_pairs={{4,0},{5,1},{8,4},{9,5},{12,8},{13,9},{14,12},{15,13},{10,14},{11,... | collective-permute-start | bytes 1179656 | tf_op jit(solution)/shard_map/ppermute | solution.py:255
  51.5 9.6 %collective-permute-start.12 = (bf16[96,2176]{1,0:T(8,128)(2,1)S(1)}, bf16[96,2176]{1,0:T(8,128)(2,1)}, u32[]{:S(2)}, u32[]{:S(2)}) collective-permute-start(bf16[96,2176]{1,0:T(8,128)(2,1)S(1)} %collective-permute-done.8.refs_0_), channel_id=1, source_target_pairs={{0,4},{1,5},{4,8},{5,9},{8,12},{9,13},{12,14},{13,15},{14,10},{15,... | collective-permute-start | bytes 1253384 | tf_op jit(solution)/shard_map/ppermute | solution.py:255
  53.0 9.6 %collective-permute-start.13 = (bf16[96,2176]{1,0:T(8,128)(2,1)S(1)}, bf16[96,2176]{1,0:T(8,128)(2,1)}, u32[]{:S(2)}, u32[]{:S(2)}) collective-permute-start(bf16[96,2176]{1,0:T(8,128)(2,1)S(1)} %collective-permute-done.9.refs_1_), channel_id=1, source_target_pairs={{4,0},{5,1},{8,4},{9,5},{12,8},{13,9},{14,12},{15,13},{10,14},{11,... | collective-permute-start | bytes 1253384 | tf_op jit(solution)/shard_map/ppermute | solution.py:255
  61.1 10.3 %collective-permute-start.33 = (bf16[96,2048]{1,0:T(8,128)(2,1)}, bf16[96,2048]{1,0:T(8,128)(2,1)}, u32[]{:S(2)}, u32[]{:S(2)}) collective-permute-start(bf16[96,2048]{1,0:T(8,128)(2,1)} %collective-permute-done.31.refs_2_), channel_id=1, source_target_pairs={{0,4},{1,5},{4,8},{5,9},{8,12},{9,13},{12,14},{13,15},{14,10},{15,... | collective-permute-start | bytes 1179656 | tf_op jit(solution)/shard_map/ppermute | solution.py:255
  62.6 10.4 %collective-permute-start.34 = (bf16[96,2048]{1,0:T(8,128)(2,1)}, bf16[96,2048]{1,0:T(8,128)(2,1)}, u32[]{:S(2)}, u32[]{:S(2)}) collective-permute-start(bf16[96,2048]{1,0:T(8,128)(2,1)} %collective-permute-done.32.refs_3_), channel_id=1, source_target_pairs={{4,0},{5,1},{8,4},{9,5},{12,8},{13,9},{14,12},{15,13},{10,14},{11,... | collective-permute-start | bytes 1179656 | tf_op jit(solution)/shard_map/ppermute | solution.py:255
  71.4 6.9 %collective-permute-start.16 = (bf16[48,2176]{1,0:T(8,128)(2,1)S(1)}, bf16[48,2176]{1,0:T(8,128)(2,1)S(1)}, u32[]{:S(2)}, u32[]{:S(2)}) collective-permute-start(bf16[48,2176]{1,0:T(8,128)(2,1)S(1)} %slice.90), channel_id=1, source_target_pairs={{0,4},{1,5},{4,8},{5,9},{8,12},{9,13},{12,14},{13,15},{14,10},{15,... | collective-permute-start | bytes 626696 | tf_op jit(solution)/shard_map/ppermute | solution.py:255
  73.0 6.9 %collective-permute-start.17 = (bf16[48,2176]{1,0:T(8,128)(2,1)S(1)}, bf16[48,2176]{1,0:T(8,128)(2,1)S(1)}, u32[]{:S(2)}, u32[]{:S(2)}) collective-permute-start(bf16[48,2176]{1,0:T(8,128)(2,1)S(1)} %slice.91), channel_id=1, source_target_pairs={{4,0},{5,1},{8,4},{9,5},{12,8},{13,9},{14,12},{15,13},{10,14},{11,... | collective-permute-start | bytes 626696 | tf_op jit(solution)/shard_map/ppermute | solution.py:255
  78.3 5.7 %collective-permute-start.35 = (bf16[48,2048]{1,0:T(8,128)(2,1)S(1)}, bf16[48,2048]{1,0:T(8,128)(2,1)S(1)}, u32[]{:S(2)}, u32[]{:S(2)}) collective-permute-start(bf16[48,2048]{1,0:T(8,128)(2,1)S(1)} %slice.94), channel_id=1, source_target_pairs={{0,4},{1,5},{4,8},{5,9},{8,12},{9,13},{12,14},{13,15},{14,10},{15,... | collective-permute-start | bytes 589832 | tf_op jit(solution)/shard_map/ppermute | solution.py:255
  79.9 5.7 %collective-permute-start.36 = (bf16[48,2048]{1,0:T(8,128)(2,1)S(1)}, bf16[48,2048]{1,0:T(8,128)(2,1)S(1)}, u32[]{:S(2)}, u32[]{:S(2)}) collective-permute-start(bf16[48,2048]{1,0:T(8,128)(2,1)S(1)} %slice.95), channel_id=1, source_target_pairs={{4,0},{5,1},{8,4},{9,5},{12,8},{13,9},{14,12},{15,13},{10,14},{11,... | collective-permute-start | bytes 589832 | tf_op jit(solution)/shard_map/ppermute | solution.py:255
  80.4 99.9 %copy-start.36 = (f32[96]{0:T(128)}, f32[96]{0:T(128)S(1)}, u32[]{:S(2)}) copy-start(f32[96]{0:T(128)S(1)} %fusion.19) | copy-start | bytes 1156
  84.0 86.0 %collective-permute-start = (bf16[96,2048]{1,0:T(8,128)(2,1)}, bf16[96,2048]{1,0:T(8,128)(2,1)S(1)}, u32[]{:S(2)}, u32[]{:S(2)}) collective-permute-start(bf16[96,2048]{1,0:T(8,128)(2,1)} %bitcast.85), channel_id=1, source_target_pairs={{0,16},{1,17},{2,18},{3,19},{4,20},{5,21},{6,22},{7,23},{8,24},{9,... | collective-permute-start | bytes 1179656 | tf_op jit(solution)/shard_map/ppermute | solution.py:17
  99.0 16.7 %copy-start.42 = (bf16[48,2048]{1,0:T(8,128)(2,1)S(1)}, bf16[48,2048]{1,0:T(8,128)(2,1)}, u32[]{:S(2)}) copy-start(bf16[48,2048]{1,0:T(8,128)(2,1)} %get-tuple-element.38) | copy-start | bytes 589828
  99.1 48.1 %collective-permute-start.37 = (bf16[48,2048]{1,0:T(8,128)(2,1)}, bf16[48,2048]{1,0:T(8,128)(2,1)S(1)}, u32[]{:S(2)}, u32[]{:S(2)}) collective-permute-start(bf16[48,2048]{1,0:T(8,128)(2,1)} %get-tuple-element.34), channel_id=1, source_target_pairs={{0,4},{1,5},{4,8},{5,9},{8,12},{9,13},{12,14},{13,15},{14,10},{15,... | collective-permute-start | bytes 589832 | tf_op jit(solution)/shard_map/ppermute | solution.py:255
  115.7 33.2 %collective-permute-start.41 = (bf16[48,2048]{1,0:T(8,128)(2,1)S(1)}, bf16[48,2048]{1,0:T(8,128)(2,1)S(1)}, u32[]{:S(2)}, u32[]{:S(2)}) collective-permute-start(bf16[48,2048]{1,0:T(8,128)(2,1)S(1)} %copy-done.42), channel_id=1, source_target_pairs={{4,0},{5,1},{8,4},{9,5},{12,8},{13,9},{14,12},{15,13},{10,14},{11,... | collective-permute-start | bytes 589832 | tf_op jit(solution)/shard_map/ppermute | solution.py:255
  147.3 20.4 %copy-start.25 = (bf16[96,2048]{1,0:T(8,128)(2,1)S(1)}, bf16[96,2048]{1,0:T(8,128)(2,1)}, u32[]{:S(2)}) copy-start(bf16[96,2048]{1,0:T(8,128)(2,1)} %get-tuple-element.31) | copy-start | bytes 1179652
  147.3 10.6 %collective-permute-start.38 = (bf16[96,2048]{1,0:T(8,128)(2,1)S(1)}, bf16[96,2048]{1,0:T(8,128)(2,1)S(1)}, u32[]{:S(2)}, u32[]{:S(2)}) collective-permute-start(bf16[96,2048]{1,0:T(8,128)(2,1)S(1)} %pad_maximum_fusion.2), channel_id=1, source_target_pairs={{0,4},{1,5},{4,8},{5,9},{8,12},{9,13},{12,14},{13,15},{14,10},{15,... | collective-permute-start | bytes 1179656 | tf_op jit(solution)/shard_map/ppermute | solution.py:255
  149.0 20.4 %copy-start.24 = (bf16[96,2048]{1,0:T(8,128)(2,1)S(1)}, bf16[96,2048]{1,0:T(8,128)(2,1)}, u32[]{:S(2)}) copy-start(bf16[96,2048]{1,0:T(8,128)(2,1)} %get-tuple-element.35) | copy-start | bytes 1179652
  149.0 10.6 %collective-permute-start.42 = (bf16[96,2048]{1,0:T(8,128)(2,1)S(1)}, bf16[96,2048]{1,0:T(8,128)(2,1)S(1)}, u32[]{:S(2)}, u32[]{:S(2)}) collective-permute-start(bf16[96,2048]{1,0:T(8,128)(2,1)S(1)} %pad_maximum_fusion.3), channel_id=1, source_target_pairs={{4,0},{5,1},{8,4},{9,5},{12,8},{13,9},{14,12},{15,13},{10,14},{11,... | collective-permute-start | bytes 1179656 | tf_op jit(solution)/shard_map/ppermute | solution.py:255
  158.0 9.7 %collective-permute-start.39 = (bf16[96,2048]{1,0:T(8,128)(2,1)S(1)}, bf16[96,2048]{1,0:T(8,128)(2,1)S(1)}, u32[]{:S(2)}, u32[]{:S(2)}) collective-permute-start(bf16[96,2048]{1,0:T(8,128)(2,1)S(1)} %add_convert_fusion.3), channel_id=1, source_target_pairs={{0,4},{1,5},{4,8},{5,9},{8,12},{9,13},{12,14},{13,15},{14,10},{15,... | collective-permute-start | bytes 1179656 | tf_op jit(solution)/shard_map/ppermute | solution.py:255
  159.6 20.6 %copy-start.2 = (bf16[2,96,2048]{2,1,0:T(8,128)(2,1)S(1)}, bf16[2,96,2048]{2,1,0:T(8,128)(2,1)}, u32[]{:S(2)}) copy-start(bf16[2,96,2048]{2,1,0:T(8,128)(2,1)} %param.17) | copy-start | bytes 2359300
  159.6 20.6 %copy-start.3 = (bf16[96,2048]{1,0:T(8,128)(2,1)S(1)}, bf16[96,2048]{1,0:T(8,128)(2,1)}, u32[]{:S(2)}) copy-start(bf16[96,2048]{1,0:T(8,128)(2,1)} %get-tuple-element.30) | copy-start | bytes 1179652
  159.6 20.6 %copy-start.34 = (f32[1,2048]{1,0:T(1,128)S(1)}, f32[1,2048]{1,0:T(1,128)}, u32[]{:S(2)}) copy-start(f32[1,2048]{1,0:T(1,128)} %gain_ref.1) | copy-start | bytes 24580
  159.7 20.6 %copy-start.35 = (f32[1,2048]{1,0:T(1,128)S(1)}, f32[1,2048]{1,0:T(1,128)}, u32[]{:S(2)}) copy-start(f32[1,2048]{1,0:T(1,128)} %param.19) | copy-start | bytes 24580
  159.8 9.6 %collective-permute-start.43 = (bf16[96,2048]{1,0:T(8,128)(2,1)S(1)}, bf16[96,2048]{1,0:T(8,128)(2,1)S(1)}, u32[]{:S(2)}, u32[]{:S(2)}) collective-permute-start(bf16[96,2048]{1,0:T(8,128)(2,1)S(1)} %add_convert_fusion.1), channel_id=1, source_target_pairs={{4,0},{5,1},{8,4},{9,5},{12,8},{13,9},{14,12},{15,13},{10,14},{11,... | collective-permute-start | bytes 1179656 | tf_op jit(solution)/shard_map/ppermute | solution.py:255
  167.8 11.2 %collective-permute-start.40 = (bf16[96,2048]{1,0:T(8,128)(2,1)S(1)}, bf16[96,2048]{1,0:T(8,128)(2,1)S(1)}, u32[]{:S(2)}, u32[]{:S(2)}) collective-permute-start(bf16[96,2048]{1,0:T(8,128)(2,1)S(1)} %add_convert_fusion.2), channel_id=1, source_target_pairs={{0,4},{1,5},{4,8},{5,9},{8,12},{9,13},{12,14},{13,15},{14,10},{15,... | collective-permute-start | bytes 1179656 | tf_op jit(solution)/shard_map/ppermute | solution.py:255
  169.5 10.7 %collective-permute-start.44 = (bf16[96,2048]{1,0:T(8,128)(2,1)S(1)}, bf16[96,2048]{1,0:T(8,128)(2,1)S(1)}, u32[]{:S(2)}, u32[]{:S(2)}) collective-permute-start(bf16[96,2048]{1,0:T(8,128)(2,1)S(1)} %add_convert_fusion), channel_id=1, source_target_pairs={{4,0},{5,1},{8,4},{9,5},{12,8},{13,9},{14,12},{15,13},{10,14},{11,... | collective-permute-start | bytes 1179656 | tf_op jit(solution)/shard_map/ppermute | solution.py:255
  181.7 20.3 %copy-start.6 = (bf16[96,2048]{1,0:T(8,128)(2,1)}, bf16[96,2048]{1,0:T(8,128)(2,1)S(1)}, u32[]{:S(2)}) copy-start(bf16[96,2048]{1,0:T(8,128)(2,1)S(1)} %get-tuple-element.72.refs_3_) | copy-start | bytes 1179652
  181.7 9.7 %collective-permute-start.3 = (bf16[96,2048]{1,0:T(8,128)(2,1)S(1)}, bf16[96,2048]{1,0:T(8,128)(2,1)S(1)}, u32[]{:S(2)}, u32[]{:S(2)}) collective-permute-start(bf16[96,2048]{1,0:T(8,128)(2,1)S(1)} %get-tuple-element.72.refs_3_), channel_id=1, source_target_pairs={{0,4},{1,5},{4,8},{5,9},{8,12},{9,13},{12,14},{13,15},{14,10},{15,... | collective-permute-start | bytes 1179656 | tf_op jit(solution)/shard_map/ppermute | solution.py:255
  183.2 9.6 %collective-permute-start.4 = (bf16[96,2048]{1,0:T(8,128)(2,1)S(1)}, bf16[96,2048]{1,0:T(8,128)(2,1)}, u32[]{:S(2)}, u32[]{:S(2)}) collective-permute-start(bf16[96,2048]{1,0:T(8,128)(2,1)S(1)} %get-tuple-element.72.refs_3_), channel_id=1, source_target_pairs={{4,0},{5,1},{8,4},{9,5},{12,8},{13,9},{14,12},{15,13},{10,14},{11,... | collective-permute-start | bytes 1179656 | tf_op jit(solution)/shard_map/ppermute | solution.py:255
  191.4 7.8 %collective-permute-start.10 = (bf16[96,2048]{1,0:T(8,128)(2,1)S(1)}, bf16[96,2048]{1,0:T(8,128)(2,1)S(1)}, u32[]{:S(2)}, u32[]{:S(2)}) collective-permute-start(bf16[96,2048]{1,0:T(8,128)(2,1)S(1)} %collective-permute-done.3.refs_4_), channel_id=1, source_target_pairs={{0,4},{1,5},{4,8},{5,9},{8,12},{9,13},{12,14},{13,15},{14,10},{15,... | collective-permute-start | bytes 1179656 | tf_op jit(solution)/shard_map/ppermute | solution.py:255
  192.8 8.0 %collective-permute-start.11 = (bf16[96,2048]{1,0:T(8,128)(2,1)}, bf16[96,2048]{1,0:T(8,128)(2,1)S(1)}, u32[]{:S(2)}, u32[]{:S(2)}) collective-permute-start(bf16[96,2048]{1,0:T(8,128)(2,1)} %collective-permute-done.4.refs_5_), channel_id=1, source_target_pairs={{4,0},{5,1},{8,4},{9,5},{12,8},{13,9},{14,12},{15,13},{10,14},{11,... | collective-permute-start | bytes 1179656 | tf_op jit(solution)/shard_map/ppermute | solution.py:255
  199.2 15.0 %collective-permute-start.14 = (bf16[96,2048]{1,0:T(8,128)(2,1)S(1)}, bf16[96,2048]{1,0:T(8,128)(2,1)S(1)}, u32[]{:S(2)}, u32[]{:S(2)}) collective-permute-start(bf16[96,2048]{1,0:T(8,128)(2,1)S(1)} %collective-permute-done.10.refs_2_), channel_id=1, source_target_pairs={{0,4},{1,5},{4,8},{5,9},{8,12},{9,13},{12,14},{13,15},{14,10},{15,... | collective-permute-start | bytes 1179656 | tf_op jit(solution)/shard_map/ppermute | solution.py:255
  200.8 14.9 %collective-permute-start.15 = (bf16[96,2048]{1,0:T(8,128)(2,1)S(1)}, bf16[96,2048]{1,0:T(8,128)(2,1)S(1)}, u32[]{:S(2)}, u32[]{:S(2)}) collective-permute-start(bf16[96,2048]{1,0:T(8,128)(2,1)S(1)} %collective-permute-done.11.refs_3_), channel_id=1, source_target_pairs={{4,0},{5,1},{8,4},{9,5},{12,8},{13,9},{14,12},{15,13},{10,14},{11,... | collective-permute-start | bytes 1179656 | tf_op jit(solution)/shard_map/ppermute | solution.py:255
  214.2 12.9 %collective-permute-start.18 = (bf16[48,2048]{1,0:T(8,128)(2,1)S(1)}, bf16[48,2048]{1,0:T(8,128)(2,1)S(1)}, u32[]{:S(2)}, u32[]{:S(2)}) collective-permute-start(bf16[48,2048]{1,0:T(8,128)(2,1)S(1)} %slice.92), channel_id=1, source_target_pairs={{0,4},{1,5},{4,8},{5,9},{8,12},{9,13},{12,14},{13,15},{14,10},{15,... | collective-permute-start | bytes 589832 | tf_op jit(solution)/shard_map/ppermute | solution.py:255
  215.7 11.4 %collective-permute-start.19 = (bf16[48,2048]{1,0:T(8,128)(2,1)S(1)}, bf16[48,2048]{1,0:T(8,128)(2,1)S(1)}, u32[]{:S(2)}, u32[]{:S(2)}) collective-permute-start(bf16[48,2048]{1,0:T(8,128)(2,1)S(1)} %slice.93), channel_id=1, source_target_pairs={{4,0},{5,1},{8,4},{9,5},{12,8},{13,9},{14,12},{15,13},{10,14},{11,... | collective-permute-start | bytes 589832 | tf_op jit(solution)/shard_map/ppermute | solution.py:255
  238.1 15.1 %collective-permute-start.20 = (bf16[48,2048]{1,0:T(8,128)(2,1)}, bf16[48,2048]{1,0:T(8,128)(2,1)S(1)}, u32[]{:S(2)}, u32[]{:S(2)}) collective-permute-start(bf16[48,2048]{1,0:T(8,128)(2,1)} %get-tuple-element.25), channel_id=1, source_target_pairs={{0,4},{1,5},{4,8},{5,9},{8,12},{9,13},{12,14},{13,15},{14,10},{15,... | collective-permute-start | bytes 589832 | tf_op jit(solution)/shard_map/ppermute | solution.py:255
  251.5 17.3 %copy-start.22 = (bf16[96,2048]{1,0:T(8,128)(2,1)S(1)}, bf16[96,2048]{1,0:T(8,128)(2,1)}, u32[]{:S(2)}) copy-start(bf16[96,2048]{1,0:T(8,128)(2,1)} %get-tuple-element.27) | copy-start | bytes 1179652
  252.6 6.2 %collective-permute-start.24 = (bf16[48,2048]{1,0:T(8,128)(2,1)S(1)}, bf16[48,2048]{1,0:T(8,128)(2,1)S(1)}, u32[]{:S(2)}, u32[]{:S(2)}) collective-permute-start(bf16[48,2048]{1,0:T(8,128)(2,1)S(1)} %copy-done.43), channel_id=1, source_target_pairs={{4,0},{5,1},{8,4},{9,5},{12,8},{13,9},{14,12},{15,13},{10,14},{11,... | collective-permute-start | bytes 589832 | tf_op jit(solution)/shard_map/ppermute | solution.py:255
  254.2 19.7 %copy-start.21 = (bf16[96,2048]{1,0:T(8,128)(2,1)S(1)}, bf16[96,2048]{1,0:T(8,128)(2,1)}, u32[]{:S(2)}) copy-start(bf16[96,2048]{1,0:T(8,128)(2,1)} %get-tuple-element.22) | copy-start | bytes 1179652
  254.2 11.7 %collective-permute-start.21 = (bf16[96,2048]{1,0:T(8,128)(2,1)S(1)}, bf16[96,2048]{1,0:T(8,128)(2,1)S(1)}, u32[]{:S(2)}, u32[]{:S(2)}) collective-permute-start(bf16[96,2048]{1,0:T(8,128)(2,1)S(1)} %pad_maximum_fusion), channel_id=1, source_target_pairs={{0,4},{1,5},{4,8},{5,9},{8,12},{9,13},{12,14},{13,15},{14,10},{15,... | collective-permute-start | bytes 1179656 | tf_op jit(solution)/shard_map/ppermute | solution.py:255
  258.8 18.8 %copy-start.20 = (bf16[96,2048]{1,0:T(8,128)(2,1)S(1)}, bf16[96,2048]{1,0:T(8,128)(2,1)}, u32[]{:S(2)}) copy-start(bf16[96,2048]{1,0:T(8,128)(2,1)} %get-tuple-element.26) | copy-start | bytes 1179652
  258.9 9.9 %collective-permute-start.25 = (bf16[96,2048]{1,0:T(8,128)(2,1)S(1)}, bf16[96,2048]{1,0:T(8,128)(2,1)S(1)}, u32[]{:S(2)}, u32[]{:S(2)}) collective-permute-start(bf16[96,2048]{1,0:T(8,128)(2,1)S(1)} %pad_maximum_fusion.1), channel_id=1, source_target_pairs={{4,0},{5,1},{8,4},{9,5},{12,8},{13,9},{14,12},{15,13},{10,14},{11,... | collective-permute-start | bytes 1179656 | tf_op jit(solution)/shard_map/ppermute | solution.py:255
  266.0 7.8 %collective-permute-start.22 = (bf16[96,2048]{1,0:T(8,128)(2,1)S(1)}, bf16[96,2048]{1,0:T(8,128)(2,1)S(1)}, u32[]{:S(2)}, u32[]{:S(2)}) collective-permute-start(bf16[96,2048]{1,0:T(8,128)(2,1)S(1)} %add_convert_fusion.7), channel_id=1, source_target_pairs={{0,4},{1,5},{4,8},{5,9},{8,12},{9,13},{12,14},{13,15},{14,10},{15,... | collective-permute-start | bytes 1179656 | tf_op jit(solution)/shard_map/ppermute | solution.py:255
  268.9 8.7 %collective-permute-start.26 = (bf16[96,2048]{1,0:T(8,128)(2,1)S(1)}, bf16[96,2048]{1,0:T(8,128)(2,1)S(1)}, u32[]{:S(2)}, u32[]{:S(2)}) collective-permute-start(bf16[96,2048]{1,0:T(8,128)(2,1)S(1)} %add_convert_fusion.5), channel_id=1, source_target_pairs={{4,0},{5,1},{8,4},{9,5},{12,8},{13,9},{14,12},{15,13},{10,14},{11,... | collective-permute-start | bytes 1179656 | tf_op jit(solution)/shard_map/ppermute | solution.py:255
  274.0 7.8 %collective-permute-start.23 = (bf16[96,2048]{1,0:T(8,128)(2,1)S(1)}, bf16[96,2048]{1,0:T(8,128)(2,1)S(1)}, u32[]{:S(2)}, u32[]{:S(2)}) collective-permute-start(bf16[96,2048]{1,0:T(8,128)(2,1)S(1)} %add_convert_fusion.6), channel_id=1, source_target_pairs={{0,4},{1,5},{4,8},{5,9},{8,12},{9,13},{12,14},{13,15},{14,10},{15,... | collective-permute-start | bytes 1179656 | tf_op jit(solution)/shard_map/ppermute | solution.py:255
  277.8 7.8 %collective-permute-start.27 = (bf16[96,2048]{1,0:T(8,128)(2,1)S(1)}, bf16[96,2048]{1,0:T(8,128)(2,1)S(1)}, u32[]{:S(2)}, u32[]{:S(2)}) collective-permute-start(bf16[96,2048]{1,0:T(8,128)(2,1)S(1)} %add_convert_fusion.4), channel_id=1, source_target_pairs={{4,0},{5,1},{8,4},{9,5},{12,8},{13,9},{14,12},{15,13},{10,14},{11,... | collective-permute-start | bytes 1179656 | tf_op jit(solution)/shard_map/ppermute | solution.py:255
  (25 other events, 244.7 us)

commit v3 on v2

v3 whole, which is shorter than its diff:
```python
import functools
import jax
import jax.numpy as jnp
from jax import lax
from jax.experimental import pallas as pl
from jax.experimental.pallas import tpu as pltpu
from jax.sharding import PartitionSpec as P

EPSILON = 1e-06
VMEM_LIMIT = 56 * 1024 * 1024
NT = (((1,), (1,)), ((), ()))


def passed_along(block, axis, distance):
    devices = range(lax.axis_size(axis))
    route = [(i - distance, i) for i in devices if i - distance in devices]
    return lax.ppermute(block, axis, route)


def normed(values, gain_row):
    return (
        values * lax.rsqrt(jnp.mean(values * values, axis=-1, keepdims=True) + EPSILON) * gain_row
    )


def norm_pullback(values, gain_row, upstream):
    _, pullback = jax.vjp(lambda argument: normed(argument, gain_row), values)
    return pullback(upstream)[0]


def pack_kernel(experts, rows_ref, ids_ref, gates_ref, out_ref):
    width = rows_ref.shape[1]
    out_ref[:, :width] = rows_ref[...]
    count, extra = rows_ref.shape[0], out_ref.shape[1] - width
    lane = lax.broadcasted_iota(jnp.int32, (count, extra), 1)
    table = jnp.zeros((count, extra), jnp.float32)
    for m in range(2):
        for k in range(ids_ref.shape[2]):
            place = ids_ref[m, :, k : k + 1] + 2 * m * experts
            gate = gates_ref[m, :, k : k + 1]
            high = gate.astype(jnp.bfloat16).astype(jnp.float32)
            table = jnp.where(lane == place, high, table)
            table = jnp.where(lane == place + experts, gate - high, table)
    out_ref[:, width:] = table.astype(jnp.bfloat16)


def packed_rows(rows, ids, gates, experts):
    count, width = rows.shape
    extra = -(-4 * experts // 128) * 128
    return pl.pallas_call(
        functools.partial(pack_kernel, experts),
        out_shape=jax.ShapeDtypeStruct((count, width + extra), jnp.bfloat16),
        compiler_params=pltpu.CompilerParams(vmem_limit_bytes=VMEM_LIMIT // 4),
        cost_estimate=pl.CostEstimate(flops=0, bytes_accessed=count * width * 8, transcendentals=0),
    )(rows, ids, gates)


def gate_column(table, micro, experts, expert):
    lane = lax.broadcasted_iota(jnp.int32, table.shape, 1)
    place = 2 * micro * experts + expert
    chosen = (lane == place) | (lane == place + experts)
    return jnp.sum(jnp.where(chosen, table, 0.0), axis=1, keepdims=True)


def start_all(copies):
    for copy in copies:
        copy.start()


def wait_all(copies):
    for copy in copies:
        copy.wait()


def block_copies(sources, target, sems, columns=None):
    copies, start = [], 0
    for i, source in enumerate(sources):
        count = source.shape[0]
        view = source if columns is None else source.at[:, columns]
        copies.append(
            pltpu.make_async_copy(view, target.at[pl.ds(start, count)], sems.at[i])
        )
        start += count
    return copies


def write_tiles(tile, outs, columns):
    start = 0
    for out in outs:
        count = out.shape[0]
        out[:, columns] = tile[start : start + count].astype(out.dtype)
        start += count


def weight_stages(weights, targets, sems, tile, with_down):
    inner = targets[0].shape[2]
    per = inner // tile
    stages, used = [], 0
    for e in range(2):
        for f in range(per):
            part = pl.ds(f * tile, tile)
            views = [(i, (slice(None), part)) for i in range(2)]
            if with_down:
                views.append((2, (part, slice(None))))
            copies = []
            for i, view in views:
                source, target = weights[3 * e + i], targets[i].at[e]
                copies.append(
                    pltpu.make_async_copy(source.at[view], target.at[view], sems.at[used])
                )
                used += 1
            stages.append(copies)
    return stages, used


def forward_kernel(parts, experts, width, tile, names_ref, *refs):
    packed, rows = refs[:parts], refs[parts : 2 * parts]
    weights = refs[2 * parts : 2 * parts + 6]
    outs = refs[2 * parts + 6 : 3 * parts + 6]
    (table, held, hidden, gate_w, up_w, down_w, table_sem, row_sem, weight_sem) = refs[
        3 * parts + 6 :
    ]
    extra = table.shape[1]
    inner = gate_w.shape[2]
    first_copies = block_copies(rows, held, row_sem)
    first_copies += block_copies(packed, table, table_sem, pl.ds(width, extra))
    stages, used = weight_stages(weights, (gate_w, up_w, down_w), weight_sem, tile, False)
    down_copies = [
        pltpu.make_async_copy(weights[3 * e + 2], down_w.at[e], weight_sem.at[used + e])
        for e in range(2)
    ]
    stages.append(down_copies)
    start_all(first_copies + stages[0] + stages[1])
    wait_all(first_copies)
    per = inner // tile
    for stage in range(2 * per):
        e, f = divmod(stage, per)
        wait_all(stages[stage])
        if stage + 2 < len(stages):
            start_all(stages[stage + 2])
        columns = pl.ds(f * tile, tile)
        gate = gate_column(table[...].astype(jnp.float32), 0, experts, names_ref[e])
        first = jnp.dot(held[...], gate_w[e, :, columns], preferred_element_type=jnp.float32)
        second = jnp.dot(held[...], up_w[e, :, columns], preferred_element_type=jnp.float32)
        made = gate * (jax.nn.silu(first) * second)
        hidden[:, pl.ds(stage * tile, tile)] = made.astype(jnp.bfloat16)
    wait_all(down_copies)

    @pl.loop(0, width // tile)
    def _(n):
        columns = pl.ds(pl.multiple_of(n * tile, tile), tile)
        total = jnp.dot(
            hidden[:, :inner], down_w[0, :, columns], preferred_element_type=jnp.float32
        ) + jnp.dot(hidden[:, inner:], down_w[1, :, columns], preferred_element_type=jnp.float32)
        write_tiles(total, outs, columns)


def backward_kernel(parts, experts, width, tile, names_ref, *refs):
    packed, rows = refs[:parts], refs[parts : 2 * parts]
    weights = refs[2 * parts : 2 * parts + 6]
    outs = refs[2 * parts + 6 : 3 * parts + 6]
    (cot, held, slot, grads, gate_w, up_w, down_w, cot_sem, row_sem, weight_sem) = refs[
        3 * parts + 6 :
    ]
    inner = gate_w.shape[2]
    first_copies = block_copies(rows, held, row_sem) + block_copies(packed, cot, cot_sem)
    stages, _ = weight_stages(weights, (gate_w, up_w, down_w), weight_sem, tile, True)
    start_all(first_copies + stages[0] + stages[1])
    wait_all(first_copies)
    per = inner // tile
    for stage in range(2 * per):
        e, f = divmod(stage, per)
        if f == 0:
            table = cot[:, width:].astype(jnp.float32)
            gate = gate_column(table, 1, experts, names_ref[e])
            slot[...] = (gate * cot[:, :width].astype(jnp.float32)).astype(jnp.bfloat16)
        wait_all(stages[stage])
        if stage + 2 < len(stages):
            start_all(stages[stage + 2])
        columns = pl.ds(f * tile, tile)
        first = jnp.dot(held[...], gate_w[e, :, columns], preferred_element_type=jnp.float32)
        second = jnp.dot(held[...], up_w[e, :, columns], preferred_element_type=jnp.float32)
        back = lax.dot_general(
            slot[...], down_w[e, columns, :], NT, preferred_element_type=jnp.float32
        )
        sigmoid_part = jax.nn.sigmoid(first)
        gate_grad = back * second * sigmoid_part * (1.0 + first * (1.0 - sigmoid_part))
        second_grad = back * (first * sigmoid_part)
        grads[2 * e, :, columns] = gate_grad.astype(jnp.bfloat16)
        grads[2 * e + 1, :, columns] = second_grad.astype(jnp.bfloat16)

    @pl.loop(0, width // tile)
    def _(n):
        columns = pl.ds(pl.multiple_of(n * tile, tile), tile)
        total = None
        for e in range(2):
            for i, weight in enumerate((gate_w, up_w)):
                term = lax.dot_general(
                    grads[2 * e + i], weight[e, columns, :], NT, preferred_element_type=jnp.float32
                )
                total = term if total is None else total + term
        write_tiles(total, outs, columns)


def expert_call(kind, names, packed, rows, weights, experts):
    parts = len(rows)
    counts = [block.shape[0] for block in rows]
    total = sum(counts)
    width = rows[0].shape[1]
    full = packed[0].shape[1]
    inner = weights[0].shape[1]
    tile = 256
    hbm = pl.BlockSpec(memory_space=pl.ANY)
    weight_scratch = [
        pltpu.VMEM((2, width, inner), jnp.bfloat16),
        pltpu.VMEM((2, width, inner), jnp.bfloat16),
        pltpu.VMEM((2, inner, width), jnp.bfloat16),
    ]
    sems = [pltpu.SemaphoreType.DMA((parts,)), pltpu.SemaphoreType.DMA((parts,))]
    sems += [pltpu.SemaphoreType.DMA((6 * (inner // tile),))]
    if kind == "forward":
        body = forward_kernel
        scratch = [
            pltpu.VMEM((total, full - width), jnp.bfloat16),
            pltpu.VMEM((total, width), jnp.bfloat16),
            pltpu.VMEM((total, 2 * inner), jnp.bfloat16),
        ]
        products, fixed = 6, 8.5e-6
    else:
        body = backward_kernel
        scratch = [
            pltpu.VMEM((total, full), jnp.bfloat16),
            pltpu.VMEM((total, width), jnp.bfloat16),
            pltpu.VMEM((total, width), jnp.bfloat16),
            pltpu.VMEM((4, total, inner), jnp.bfloat16),
        ]
        products, fixed = 10, 11e-6
    out = pl.pallas_call(
        functools.partial(body, parts, experts, width, tile),
        out_shape=[jax.ShapeDtypeStruct((count, width), jnp.bfloat16) for count in counts],
        in_specs=[pl.BlockSpec(memory_space=pltpu.SMEM)] + [hbm] * (2 * parts + 6),
        scratch_shapes=scratch + weight_scratch + sems,
        compiler_params=pltpu.CompilerParams(vmem_limit_bytes=VMEM_LIMIT),
        cost_estimate=pl.CostEstimate(
            flops=2 * products * total * width * inner + int(fixed * 1.1e15),
            bytes_accessed=12 * width * inner,
            transcendentals=2 * total * inner,
        ),
    )(names, *packed, *rows, *weights)
    return list(out)


def added(first, second):
    return (first.astype(jnp.float32) + second.astype(jnp.float32)).astype(jnp.bfloat16)


class Section:
    def __init__(self, sources, names):
        self.sources = sources
        self.names = names
        self.chips = sources // 2
        self.far = self.chips // 2
        order = list(range(0, self.chips, 2)) + list(range(1, self.chips, 2))[::-1]
        following = {order[i]: order[(i + 1) % self.chips] for i in range(self.chips)}
        pairs = [(2 * a + core, 2 * b + core) for a, b in following.items() for core in range(2)]
        self.routes = (pairs, [(b, a) for a, b in pairs])
        self.swap = [(i, i ^ 1) for i in range(sources)]
        self.held, self.made, self.sums, self.weights = {}, {}, {}, None

    def pass_on(self, block, way):
        return lax.ppermute(block, "ep", self.routes[way])

    def gather(self, name, distance):
        held = self.held[name]
        behind, ahead = held[distance - 1][0], held[distance - 1][-1]
        if distance == self.far:
            half = behind.shape[0] // 2
            behind, ahead = behind[:half], ahead[half:]
        held[distance] = [self.pass_on(behind, 0), self.pass_on(ahead, 1)]

    def work(self, kind, distances):
        rows = self.held["fall" if kind == "backward" else "rise"]
        packed = [block for d in distances for block in self.held["cot"][d]]
        blocks = [block for d in distances for block in rows[d]]
        outs = expert_call(kind, self.names, packed, blocks, self.weights, self.sources)
        made = self.made.setdefault(kind, {})
        for d in distances:
            count = len(rows[d])
            made[d], outs = outs[:count], outs[count:]

    def scatter(self, kind, step):
        distance = self.far + 1 - step
        behind, ahead = self.made[kind][distance]
        if step == 1:
            forth, back = behind, ahead
        else:
            moved_forth, moved_back = self.sums[kind]
            if step == 2:
                half = moved_forth.shape[0]
                forth = jnp.concatenate([added(ahead[:half], moved_forth), ahead[half:]])
                back = jnp.concatenate([behind[:half], added(behind[half:], moved_back)])
            else:
                forth, back = added(ahead, moved_forth), added(behind, moved_back)
        self.sums[kind] = [self.pass_on(forth, 0), self.pass_on(back, 1)]
        del self.made[kind][distance]

    def total(self, kind):
        pieces = self.made[kind][0] + self.sums[kind]
        return sum(piece.astype(jnp.float32) for piece in pieces)

    def fence(self, *others):
        state = (self.held, self.made, self.sums, others)
        state = lax.optimization_barrier(state)
        self.held, self.made, self.sums, others = state
        return others

    def fence_weights(self):
        state = (self.held, self.weights)
        self.held, self.weights = lax.optimization_barrier(state)


def local(
    entering,
    rising_prev,
    falling_cot,
    falling_saved,
    targets,
    norm_gain,
    exit_gain,
    w_gate,
    w_up,
    w_down,
    route_ids,
    route_gates,
    exit_list,
):
    section_index = lax.axis_index("pipe")
    sections = lax.axis_size("pipe")
    sources = lax.axis_size("ep")
    here = lax.axis_index("ep")
    names = jnp.stack([here, here + 1 - 2 * (here % 2)]).astype(jnp.int32)
    norm_row = norm_gain[0]
    exit_row = exit_gain[0]
    ring = Section(sources, names)
    far = ring.far
    planned = far == 4

    fall_wide = falling_saved[0].astype(jnp.float32)
    fall_normal = normed(fall_wide, norm_row).astype(jnp.bfloat16)
    fall_normal, leaving_cot, leaving_rise = lax.optimization_barrier(
        (fall_normal, falling_cot[0], rising_prev[0])
    )
    ring.held["fall"] = {0: [fall_normal]}
    ring.gather("fall", 1)
    moved_cot = passed_along(leaving_cot, "pipe", 1)
    moved_rise = passed_along(leaving_rise, "pipe", 1)
    own = (w_gate[0, 0], w_up[0, 0], w_down[0, 0])
    ring.weights = own + tuple(lax.ppermute(own, "ep", ring.swap))

    at_start = section_index == 0
    cot_in = jnp.where(at_start, entering[1], moved_cot)
    rise_in = jnp.where(at_start, entering[0], moved_rise)
    rise_wide = rise_in.astype(jnp.float32)
    ring.held["cot"] = {0: [packed_rows(cot_in, route_ids[:, 0], route_gates[:, 0], sources)]}
    ring.held["rise"] = {}
    rise_normal = normed(rise_wide, norm_row).astype(jnp.bfloat16)

    def exit_heads(rise_in, cot_in):
        rise_wide = rise_in.astype(jnp.float32)
        head_rise = jnp.take(exit_list[0], section_index).astype(jnp.float32)
        head_fall = jnp.take(exit_list[1], sections - 1 - section_index).astype(jnp.float32)
        rise_diff = normed(rise_wide, exit_row) - targets[0].astype(jnp.float32)
        loss_rise = head_rise * 0.5 * jnp.mean(rise_diff * rise_diff, axis=-1)
        fall_diff = normed(fall_wide, exit_row) - targets[1].astype(jnp.float32)
        loss_fall = head_fall * 0.5 * jnp.mean(fall_diff * fall_diff, axis=-1)
        kept = cot_in.astype(jnp.float32)
        kept = kept + head_fall * norm_pullback(fall_wide, exit_row, fall_diff)
        return kept, jnp.stack([loss_rise, loss_fall])[:, None, :]

    def falling(kept):
        return kept + norm_pullback(fall_wide, norm_row, ring.total("backward"))

    if planned:
        (cot_in,) = ring.fence(cot_in)
        ring.gather("fall", 2)
        ring.gather("cot", 1)
        ring.fence_weights()
        ring.gather("fall", 3)
        ring.gather("cot", 2)
        kept, exit_loss = exit_heads(rise_in, cot_in)
        rise_normal, kept, exit_loss = ring.fence(rise_normal, kept, exit_loss)
        ring.held["rise"] = {0: [rise_normal]}
        ring.gather("fall", 4)
        ring.gather("cot", 3)
        ring.gather("rise", 1)
        ring.work("backward", [0, 1, 2])
        ring.fence()
        ring.gather("cot", 4)
        ring.gather("rise", 2)
        ring.work("forward", [0, 1])
        ring.fence()
        ring.gather("rise", 3)
        ring.work("backward", [3, 4])
        ring.fence()
        ring.gather("rise", 4)
        ring.scatter("backward", 1)
        ring.fence()
        ring.scatter("backward", 2)
        ring.work("forward", [2, 3, 4])
        ring.fence()
        ring.scatter("backward", 3)
        ring.scatter("forward", 1)
        ring.fence()
        ring.scatter("backward", 4)
        ring.scatter("forward", 2)
        ring.fence()
        ring.scatter("forward", 3)
        fall_total = falling(kept).astype(jnp.bfloat16)
        (fall_total,) = ring.fence(fall_total)
        ring.scatter("forward", 4)
    else:
        kept, exit_loss = exit_heads(rise_in, cot_in)
        ring.held["rise"] = {0: [rise_normal]}
        for name in ("fall", "cot", "rise"):
            for distance in range(1 if name != "fall" else 2, far + 1):
                ring.gather(name, distance)
        for kind in ("backward", "forward"):
            ring.work(kind, [0, 1])
            for distance in range(2, far + 1):
                ring.work(kind, [distance])
            for step in range(1, far + 1):
                ring.scatter(kind, step)
        fall_total = falling(kept).astype(jnp.bfloat16)
    layer_out = (rise_wide + ring.total("forward")).astype(jnp.bfloat16)
    return (layer_out[None], fall_total[None], exit_loss)


def solution(mesh):
    placed = (
        P(None, "ep", None),
        P("pipe", "ep", None),
        P("pipe", "ep", None),
        P("pipe", "ep", None),
        P(None, "ep", None),
        P("pipe", None),
        P("pipe", None),
        P("pipe", "ep", None, None),
        P("pipe", "ep", None, None),
        P("pipe", "ep", None, None),
        P(None, "pipe", "ep", None),
        P(None, "pipe", "ep", None),
        P(),
    )
    return jax.shard_map(
        local,
        mesh=mesh,
        in_specs=placed,
        out_specs=(P("pipe", "ep", None), P("pipe", "ep", None), P(None, "pipe", "ep")),
        check_vma=False,
    )
```

time: 287 us -> 215 us (0.75)
  Pallas kernels: 102 us -> 60.4 us
  waiting for transfers between devices: 108 us -> 81 us
  local copies, waits for them, and re-layouts: 15.2 us -> 5.66 us
  starting transfers between devices: 48.1 us -> 54.3 us
    pallas_call x8 -> x4, Pallas kernels: 99.8 us -> 59.7 us  [expert_call(): pl.pallas_call(functools.partial(body, parts, experts, width, tile), out_...]
    ppermute x40, waiting for transfers between devices: 107 us -> 77.4 us  [pass_on(): return lax.ppermute(block, 'ep', self.routes[way])]
    slice x11, local copies, waits for them, and re-layouts: 8.23 us -> 1.84 us  [the longest x2 0.96 us: scatter(): back = jnp.concatenate([behind[:half], added(behind[half:], moved_back)])]
    ppermute x40, starting transfers between devices: 41.1 us -> 45.2 us  [pass_on(): return lax.ppermute(block, 'ep', self.routes[way])]
    ppermute x2, waiting for transfers between devices: 0.24 us -> 3.5 us  [passed_along(): return lax.ppermute(block, axis, route)]
  transfers between devices with their start and end apart: 45 -> 45, of which waited for: 26 -> 22; matrix products, arithmetic and copies ran while one was open for 7% -> 4% of each run, Pallas kernels for 32% -> 28%
where the time goes in v3:
time: 215 us
  waiting for transfers between devices  81 us (38%)
  Pallas kernels  60.4 us (28%)
  starting transfers between devices  54.3 us (25%)
  other arithmetic  10.5 us (5%)
  local copies, waits for them, and re-layouts  5.66 us (3%)
  between operations  2.86 us (1%)
    ppermute x40, waiting for transfers between devices, pass_on(): return lax.ppermute(block, 'ep', self.routes[way])  77.4 us
    pallas_call x4, Pallas kernels, expert_call(): pl.pallas_call(functools.partial(body, parts, experts, width, tile), out_...  59.7 us
    ppermute x40, starting transfers between devices, pass_on(): return lax.ppermute(block, 'ep', self.routes[way])  45.2 us
    ppermute x2, starting transfers between devices, passed_along(): return lax.ppermute(block, axis, route)  8.6 us
  transfers between devices with their start and end apart: 45, of which 22 were waited for; matrix products, arithmetic and copies ran while one was open for 4% of the time, Pallas kernels for 28%

profile of v3, /device:TPU:0, one launch (start us, length us, event | category | flops | bytes accessed | tf_op | source)
XLA Modules:
  0.0 214.7 jit_solution(15138561274008596577)
XLA Ops:
  0.6 1.2 fusion.16
  2.0 1.2 fusion.4.refs_5_
  3.2 4.9 %collective-permute-start.1 = (bf16[96,2048]{1,0:T(8,128)(2,1)}, bf16[96,2048]{1,0:T(8,128)(2,1)S(1)}, u32[]{:S(2)}, u32[]{:S(2)}) collective-permute-start(bf16[96,2048]{1,0:T(8,128)(2,1)} %bitcast.74), channel_id=1, source_target_pairs={{0,16},{1,17},{2,18},{3,19},{4,20},{5,21},{6,22},{7,23},{8,24},{9,... | collective-permute-start | bytes 1179656 | tf_op jit(solution)/shard_map/ppermute | solution.py:17
  8.1 1.6 collective-permute-start.2
  10.2 0.8 copy.16
  11.0 0.8 copy.17
  11.9 0.8 fusion.21
  15.1 1.6 collective-permute-done.1
  16.7 1.5 collective-permute-start.3
  18.8 3.7 %collective-permute-start = (bf16[96,2048]{1,0:T(8,128)(2,1)}, bf16[96,2048]{1,0:T(8,128)(2,1)S(1)}, u32[]{:S(2)}, u32[]{:S(2)}) collective-permute-start(bf16[96,2048]{1,0:T(8,128)(2,1)} %bitcast.75), channel_id=1, source_target_pairs={{0,16},{1,17},{2,18},{3,19},{4,20},{5,21},{6,22},{7,23},{8,24},{9,... | collective-permute-start | bytes 1179656 | tf_op jit(solution)/shard_map/ppermute | solution.py:17
  22.6 1.1 bitcast_select_fusion.rows_ref
  23.6 0.7 shard_map.148.refs_0_
  24.4 2.3 %collective-permute-done.3.refs_7_ = bf16[96,2048]{1,0:T(8,128)(2,1)S(1)} collective-permute-done((bf16[96,2048]{1,0:T(8,128)(2,1)S(1)}, bf16[96,2048]{1,0:T(8,128)(2,1)S(1)}, u32[]{:S(2)}, u32[]{:S(2)}) %collective-permute-start.3) | collective-permute-done | bytes 393248 | tf_op jit(solution)/shard_map/ppermute | solution.py:271
  26.7 1.6 collective-permute-start.6
  28.3 1.9 collective-permute-done
  30.2 1.6 collective-permute-start.7
  32.7 3.5 %collective-permute-done.6.refs_8_ = bf16[96,2048]{1,0:T(8,128)(2,1)S(1)} collective-permute-done((bf16[96,2048]{1,0:T(8,128)(2,1)}, bf16[96,2048]{1,0:T(8,128)(2,1)S(1)}, u32[]{:S(2)}, u32[]{:S(2)}) %collective-permute-start.6) | collective-permute-done | bytes 393248 | tf_op jit(solution)/shard_map/ppermute | solution.py:271
  36.2 1.6 collective-permute-start.4
  37.8 1.7 collective-permute-done.7.refs_9_
  39.4 1.6 collective-permute-start.5
  41.6 3.3 %collective-permute-done.4.refs_1_ = bf16[96,2176]{1,0:T(8,128)(2,1)S(1)} collective-permute-done((bf16[96,2176]{1,0:T(8,128)(2,1)S(1)}, bf16[96,2176]{1,0:T(8,128)(2,1)S(1)}, u32[]{:S(2)}, u32[]{:S(2)}) %collective-permute-start.4) | collective-permute-done | bytes 417824 | tf_op jit(solution)/shard_map/ppermute | solution.py:271
  45.0 4.0 %collective-permute-done.5.refs_2_ = bf16[96,2176]{1,0:T(8,128)(2,1)S(1)} collective-permute-done((bf16[96,2176]{1,0:T(8,128)(2,1)S(1)}, bf16[96,2176]{1,0:T(8,128)(2,1)S(1)}, u32[]{:S(2)}, u32[]{:S(2)}) %collective-permute-start.5) | collective-permute-done | bytes 417824 | tf_op jit(solution)/shard_map/ppermute | solution.py:271
  49.0 2.0 collective-permute-start.12
  51.1 2.0 collective-permute-start.14
  53.5 10.6 %collective-permute-done.13.refs_4_ = bf16[96,2048]{1,0:T(8,128)(2,1)S(1)} collective-permute-done((bf16[96,2048]{1,0:T(8,128)(2,1)S(1)}, bf16[96,2048]{1,0:T(8,128)(2,1)S(1)}, u32[]{:S(2)}, u32[]{:S(2)}) %collective-permute-start.13) | collective-permute-done | bytes 393248 | tf_op jit(solution)/shard_map/ppermute | solution.py:271
  64.1 1.2 collective-permute-done.14.refs_5_
  65.5 0.7 copy-done.27
  67.5 1.6 collective-permute-start.19
  69.5 1.6 collective-permute-start.15
  71.6 2.6 %collective-permute-done.17.refs_6_ = bf16[48,2048]{1,0:T(8,128)(2,1)S(1)} collective-permute-done((bf16[48,2048]{1,0:T(8,128)(2,1)S(1)}, bf16[48,2048]{1,0:T(8,128)(2,1)S(1)}, u32[]{:S(2)}, u32[]{:S(2)}) %collective-permute-start.17) | collective-permute-done | bytes 196640 | tf_op jit(solution)/shard_map/ppermute | solution.py:271
  74.2 1.8 collective-permute-start.18
  76.0 21.2 %shard_map.149 = (bf16[96,2048]{1,0:T(8,128)(2,1)}, bf16[96,2048]{1,0:T(8,128)(2,1)}, bf16[96,2048]{1,0:T(8,128)(2,1)}, bf16[96,2048]{1,0:T(8,128)(2,1)}, bf16[96,2048]{1,0:T(8,128)(2,1)}) custom-call(s32[2]{0:T(128)} %pad_add_fusion.names_ref, bf16[96,2176]{1,0:T(8,128)(2,1)} %copy-done, bf16[96,2176]{1,0:T(8,128)(2,1)} %copy-done.29, ...), custom_call_target="tpu_custom_call" | custom-call | flops 22166329344 | bytes 12582912 | tf_op jit(solution)/shard_map/pallas_call | solution.py:238
  97.6 1.9 collective-permute-start.22
  99.7 1.8 collective-permute-start.24
  101.5 10.7 %shard_map.150 = (bf16[96,2048]{1,0:T(8,128)(2,1)}, bf16[96,2048]{1,0:T(8,128)(2,1)}, bf16[96,2048]{1,0:T(8,128)(2,1)}) custom-call(s32[2]{0:T(128)} %pad_add_fusion.names_ref, bf16[96,2176]{1,0:T(8,128)(2,1)} %copy-done, bf16[96,2176]{1,0:T(8,128)(2,1)} %copy-done.29, bf16[96,2176]{1,0:T(8,128)(2,1)} %copy-done.30, bf16[96,2048]{1,0:T(8,128)(2,1)} %copy-done.5, ...), custom_call_target="tpu_custom_call" | custom-call | flops 12973878272 | bytes 12582912 | tf_op jit(solution)/shard_map/pallas_call | solution.py:238
  112.6 1.8 collective-permute-start.26
  114.4 15.0 %shard_map.151 = (bf16[96,2048]{1,0:T(8,128)(2,1)}, bf16[96,2048]{1,0:T(8,128)(2,1)}, bf16[48,2048]{1,0:T(8,128)(2,1)}, bf16[48,2048]{1,0:T(8,128)(2,1)}) custom-call(s32[2]{0:T(128)} %pad_add_fusion.names_ref, bf16[96,2176]{1,0:T(8,128)(2,1)} %copy-done.20, bf16[96,2176]{1,0:T(8,128)(2,1)} %copy-done.21, bf16[48,2176]{1,0:T(8,128)(2,1)} %copy-done.38, ...), custom_call_target="tpu_custom_call" | custom-call | flops 18139797504 | bytes 12582912 | tf_op jit(solution)/shard_map/pallas_call | solution.py:238
  129.8 1.8 collective-permute-start.28
  131.9 1.7 collective-permute-start.30
  133.6 3.6 %collective-permute-done.27.refs_10_ = bf16[48,2048]{1,0:T(8,128)(2,1)S(1)} collective-permute-done((bf16[48,2048]{1,0:T(8,128)(2,1)S(1)}, bf16[48,2048]{1,0:T(8,128)(2,1)S(1)}, u32[]{:S(2)}, u32[]{:S(2)}) %collective-permute-start.27) | collective-permute-done | bytes 196640 | tf_op jit(solution)/shard_map/ppermute | solution.py:271
  137.3 3.5 %collective-permute-done.29 = bf16[48,2048]{1,0:T(8,128)(2,1)S(1)} collective-permute-done((bf16[48,2048]{1,0:T(8,128)(2,1)}, bf16[48,2048]{1,0:T(8,128)(2,1)S(1)}, u32[]{:S(2)}, u32[]{:S(2)}) %collective-permute-start.29) | collective-permute-done | bytes 196640 | tf_op jit(solution)/shard_map/ppermute | solution.py:271
  140.8 0.9 slice.74
  141.7 1.0 add_convert_fusion.10
  142.7 1.6 collective-permute-start.32
  145.0 12.8 %shard_map.152 = (bf16[96,2048]{1,0:T(8,128)(2,1)}, bf16[96,2048]{1,0:T(8,128)(2,1)}, bf16[96,2048]{1,0:T(8,128)(2,1)}, bf16[96,2048]{1,0:T(8,128)(2,1)}, bf16[4...) custom-call(s32[2]{0:T(128)} %pad_add_fusion.names_ref, bf16[96,2176]{1,0:T(8,128)(2,1)} %copy-done.27, ...), custom_call_target="tpu_custom_call" | custom-call | flops 15389797376 | bytes 12582912 | tf_op jit(solution)/shard_map/pallas_call | solution.py:238
  158.0 1.6 collective-permute-start.34
  160.8 1.5 collective-permute-start.36
  162.3 13.8 %collective-permute-done.35 = bf16[48,2048]{1,0:T(8,128)(2,1)S(1)} collective-permute-done((bf16[48,2048]{1,0:T(8,128)(2,1)S(1)}, bf16[48,2048]{1,0:T(8,128)(2,1)S(1)}, u32[]{:S(2)}, u32[]{:S(2)}) %collective-permute-start.35) | collective-permute-done | bytes 196640 | tf_op jit(solution)/shard_map/ppermute | solution.py:271
  176.2 1.5 collective-permute-start.40
  178.6 1.5 collective-permute-start.38
  180.8 6.6 %collective-permute-done.40 = bf16[96,2048]{1,0:T(8,128)(2,1)S(1)} collective-permute-done((bf16[96,2048]{1,0:T(8,128)(2,1)S(1)}, bf16[96,2048]{1,0:T(8,128)(2,1)S(1)}, u32[]{:S(2)}, u32[]{:S(2)}) %collective-permute-start.40) | collective-permute-done | bytes 393248 | tf_op jit(solution)/shard_map/ppermute | solution.py:271
  187.4 1.4 collective-permute-done.39
  188.8 3.5 %collective-permute-done.38 = bf16[96,2048]{1,0:T(8,128)(2,1)S(1)} collective-permute-done((bf16[96,2048]{1,0:T(8,128)(2,1)S(1)}, bf16[96,2048]{1,0:T(8,128)(2,1)S(1)}, u32[]{:S(2)}, u32[]{:S(2)}) %collective-permute-start.38) | collective-permute-done | bytes 393248 | tf_op jit(solution)/shard_map/ppermute | solution.py:271
  192.3 3.2 %collective-permute-done.37 = bf16[96,2048]{1,0:T(8,128)(2,1)S(1)} collective-permute-done((bf16[96,2048]{1,0:T(8,128)(2,1)S(1)}, bf16[96,2048]{1,0:T(8,128)(2,1)S(1)}, u32[]{:S(2)}, u32[]{:S(2)}) %collective-permute-start.37) | collective-permute-done | bytes 393248 | tf_op jit(solution)/shard_map/ppermute | solution.py:271
  195.5 0.8 collective-permute-start.42
  196.5 1.3 collective-permute-start.41
  198.2 1.1 fusion.15
  199.3 4.1 %collective-permute-done.42 = bf16[96,2048]{1,0:T(8,128)(2,1)S(1)} collective-permute-done((bf16[96,2048]{1,0:T(8,128)(2,1)S(1)}, bf16[96,2048]{1,0:T(8,128)(2,1)S(1)}, u32[]{:S(2)}, u32[]{:S(2)}) %collective-permute-start.42) | collective-permute-done | bytes 393248 | tf_op jit(solution)/shard_map/ppermute | solution.py:271
  203.4 0.9 collective-permute-done.41
  204.4 1.3 collective-permute-start.43
  205.8 0.8 collective-permute-start.44
  206.7 5.6 %collective-permute-done.43 = bf16[96,2048]{1,0:T(8,128)(2,1)S(1)} collective-permute-done((bf16[96,2048]{1,0:T(8,128)(2,1)S(1)}, bf16[96,2048]{1,0:T(8,128)(2,1)S(1)}, u32[]{:S(2)}, u32[]{:S(2)}) %collective-permute-start.43) | collective-permute-done | bytes 393248 | tf_op jit(solution)/shard_map/ppermute | solution.py:271
  212.2 1.4 collective-permute-done.44
  213.7 1.0 fusion.19
  (170 shorter events, 12.4 us)
Async XLA Ops:
  0.6 31.1 %copy-start.4 = (bf16[2,96,2048]{2,1,0:T(8,128)(2,1)S(1)}, bf16[2,96,2048]{2,1,0:T(8,128)(2,1)}, u32[]{:S(2)}) copy-start(bf16[2,96,2048]{2,1,0:T(8,128)(2,1)} %param.13) | copy-start | bytes 2359300
  1.9 30.1 %copy-start.1 = (bf16[1,96,2048]{2,1,0:T(8,128)(2,1)S(1)}, bf16[1,96,2048]{2,1,0:T(8,128)(2,1)}, u32[]{:S(2)}) copy-start(bf16[1,96,2048]{2,1,0:T(8,128)(2,1)} %param.16) | copy-start | bytes 1179652
  1.9 30.1 %copy-start.2 = (bf16[2,96,2048]{2,1,0:T(8,128)(2,1)S(1)}, bf16[2,96,2048]{2,1,0:T(8,128)(2,1)}, u32[]{:S(2)}) copy-start(bf16[2,96,2048]{2,1,0:T(8,128)(2,1)} %param.17) | copy-start | bytes 2359300
  1.9 30.1 %copy-start.19 = (f32[1,2048]{1,0:T(1,128)S(1)}, f32[1,2048]{1,0:T(1,128)}, u32[]{:S(2)}) copy-start(f32[1,2048]{1,0:T(1,128)} %param.18) | copy-start | bytes 24580
  1.9 30.1 %copy-start.26 = (f32[1,2048]{1,0:T(1,128)S(1)}, f32[1,2048]{1,0:T(1,128)}, u32[]{:S(2)}) copy-start(f32[1,2048]{1,0:T(1,128)} %param.19) | copy-start | bytes 24580
  3.2 27.0 %copy-start.9 = (bf16[96,2048]{1,0:T(8,128)(2,1)}, bf16[96,2048]{1,0:T(8,128)(2,1)S(1)}, u32[]{:S(2)}) copy-start(bf16[96,2048]{1,0:T(8,128)(2,1)S(1)} %fusion.4.refs_5_) | copy-start | bytes 1179652
  3.2 13.5 %collective-permute-start.1 = (bf16[96,2048]{1,0:T(8,128)(2,1)}, bf16[96,2048]{1,0:T(8,128)(2,1)S(1)}, u32[]{:S(2)}, u32[]{:S(2)}) collective-permute-start(bf16[96,2048]{1,0:T(8,128)(2,1)} %bitcast.74), channel_id=1, source_target_pairs={{0,16},{1,17},{2,18},{3,19},{4,20},{5,21},{6,22},{7,23},{8,24},{9,... | collective-permute-start | bytes 1179656 | tf_op jit(solution)/shard_map/ppermute | solution.py:17
  8.1 10.7 %collective-permute-start.2 = (bf16[96,2048]{1,0:T(8,128)(2,1)S(1)}, bf16[96,2048]{1,0:T(8,128)(2,1)}, u32[]{:S(2)}, u32[]{:S(2)}) collective-permute-start(bf16[96,2048]{1,0:T(8,128)(2,1)S(1)} %fusion.4.refs_5_), channel_id=1, source_target_pairs={{0,4},{1,5},{4,8},{5,9},{8,12},{9,13},{12,14},{13,15},{14,10},{15,... | collective-permute-start | bytes 1179656 | tf_op jit(solution)/shard_map/ppermute | solution.py:271
  9.7 39.2 %collective-permute-start.10 = (bf16[512,2048]{1,0:T(8,128)(2,1)}, bf16[512,2048]{1,0:T(8,128)(2,1)}, u32[]{:S(2)}, u32[]{:S(2)}) collective-permute-start(bf16[512,2048]{1,0:T(8,128)(2,1)} %bitcast.69), channel_id=1, source_target_pairs={{0,1},{1,0},{2,3},{3,2},{4,5},{5,4},{6,7},{7,6},{8,9},{9,8},{10,11... | collective-permute-start | bytes 6291464 | tf_op jit(solution)/shard_map/ppermute | solution.py:358
  9.7 39.2 %collective-permute-start.8 = (bf16[2048,512]{1,0:T(8,128)(2,1)}, bf16[2048,512]{1,0:T(8,128)(2,1)}, u32[]{:S(2)}, u32[]{:S(2)}) collective-permute-start(bf16[2048,512]{1,0:T(8,128)(2,1)} %bitcast.59), channel_id=1, source_target_pairs={{0,1},{1,0},{2,3},{3,2},{4,5},{5,4},{6,7},{7,6},{8,9},{9,8},{10,11... | collective-permute-start | bytes 6291464 | tf_op jit(solution)/shard_map/ppermute | solution.py:358
  10.2 38.7 %collective-permute-start.9 = (bf16[2048,512]{1,0:T(8,128)(2,1)}, bf16[2048,512]{1,0:T(8,128)(2,1)}, u32[]{:S(2)}, u32[]{:S(2)}) collective-permute-start(bf16[2048,512]{1,0:T(8,128)(2,1)} %bitcast.64), channel_id=1, source_target_pairs={{0,1},{1,0},{2,3},{3,2},{4,5},{5,4},{6,7},{7,6},{8,9},{9,8},{10,11... | collective-permute-start | bytes 6291464 | tf_op jit(solution)/shard_map/ppermute | solution.py:358
  16.7 10.0 %collective-permute-start.3 = (bf16[96,2048]{1,0:T(8,128)(2,1)S(1)}, bf16[96,2048]{1,0:T(8,128)(2,1)S(1)}, u32[]{:S(2)}, u32[]{:S(2)}) collective-permute-start(bf16[96,2048]{1,0:T(8,128)(2,1)S(1)} %fusion.4.refs_5_), channel_id=1, source_target_pairs={{4,0},{5,1},{8,4},{9,5},{12,8},{13,9},{14,12},{15,13},{10,14},{11,... | collective-permute-start | bytes 1179656 | tf_op jit(solution)/shard_map/ppermute | solution.py:271
  18.8 11.3 %collective-permute-start = (bf16[96,2048]{1,0:T(8,128)(2,1)}, bf16[96,2048]{1,0:T(8,128)(2,1)S(1)}, u32[]{:S(2)}, u32[]{:S(2)}) collective-permute-start(bf16[96,2048]{1,0:T(8,128)(2,1)} %bitcast.75), channel_id=1, source_target_pairs={{0,16},{1,17},{2,18},{3,19},{4,20},{5,21},{6,22},{7,23},{8,24},{9,... | collective-permute-start | bytes 1179656 | tf_op jit(solution)/shard_map/ppermute | solution.py:17
  24.4 29.1 %copy-start = (bf16[96,2176]{1,0:T(8,128)(2,1)}, bf16[96,2176]{1,0:T(8,128)(2,1)S(1)}, u32[]{:S(2)}) copy-start(bf16[96,2176]{1,0:T(8,128)(2,1)S(1)} %shard_map.148.refs_0_) | copy-start | bytes 1253380
  26.7 26.8 %copy-start.31 = (bf16[96,2048]{1,0:T(8,128)(2,1)}, bf16[96,2048]{1,0:T(8,128)(2,1)S(1)}, u32[]{:S(2)}) copy-start(bf16[96,2048]{1,0:T(8,128)(2,1)S(1)} %collective-permute-done.3.refs_7_) | copy-start | bytes 1179652
  26.7 9.5 %collective-permute-start.6 = (bf16[96,2048]{1,0:T(8,128)(2,1)}, bf16[96,2048]{1,0:T(8,128)(2,1)S(1)}, u32[]{:S(2)}, u32[]{:S(2)}) collective-permute-start(bf16[96,2048]{1,0:T(8,128)(2,1)} %collective-permute-done.2.refs_6_), channel_id=1, source_target_pairs={{0,4},{1,5},{4,8},{5,9},{8,12},{9,13},{12,14},{13,15},{14,10},{15,... | collective-permute-start | bytes 1179656 | tf_op jit(solution)/shard_map/ppermute | solution.py:271
  30.2 9.3 %collective-permute-start.7 = (bf16[96,2048]{1,0:T(8,128)(2,1)S(1)}, bf16[96,2048]{1,0:T(8,128)(2,1)S(1)}, u32[]{:S(2)}, u32[]{:S(2)}) collective-permute-start(bf16[96,2048]{1,0:T(8,128)(2,1)S(1)} %collective-permute-done.3.refs_7_), channel_id=1, source_target_pairs={{4,0},{5,1},{8,4},{9,5},{12,8},{13,9},{14,12},{15,13},{10,14},{11,... | collective-permute-start | bytes 1179656 | tf_op jit(solution)/shard_map/ppermute | solution.py:271
  32.7 64.5 %copy-start.5 = (bf16[96,2048]{1,0:T(8,128)(2,1)}, bf16[96,2048]{1,0:T(8,128)(2,1)S(1)}, u32[]{:S(2)}) copy-start(bf16[96,2048]{1,0:T(8,128)(2,1)S(1)} %get-tuple-element.240.refs_3_) | copy-start | bytes 1179652
  36.2 29.2 %copy-start.32 = (bf16[96,2048]{1,0:T(8,128)(2,1)}, bf16[96,2048]{1,0:T(8,128)(2,1)S(1)}, u32[]{:S(2)}) copy-start(bf16[96,2048]{1,0:T(8,128)(2,1)S(1)} %collective-permute-done.6.refs_8_) | copy-start | bytes 1179652
  36.2 8.7 %collective-permute-start.4 = (bf16[96,2176]{1,0:T(8,128)(2,1)S(1)}, bf16[96,2176]{1,0:T(8,128)(2,1)S(1)}, u32[]{:S(2)}, u32[]{:S(2)}) collective-permute-start(bf16[96,2176]{1,0:T(8,128)(2,1)S(1)} %shard_map.148.refs_0_), channel_id=1, source_target_pairs={{0,4},{1,5},{4,8},{5,9},{8,12},{9,13},{12,14},{13,15},{14,10},{15,... | collective-permute-start | bytes 1253384 | tf_op jit(solution)/shard_map/ppermute | solution.py:271
  39.4 26.0 %copy-start.33 = (bf16[96,2048]{1,0:T(8,128)(2,1)}, bf16[96,2048]{1,0:T(8,128)(2,1)S(1)}, u32[]{:S(2)}) copy-start(bf16[96,2048]{1,0:T(8,128)(2,1)S(1)} %collective-permute-done.7.refs_9_) | copy-start | bytes 1179652
  39.4 9.5 %collective-permute-start.5 = (bf16[96,2176]{1,0:T(8,128)(2,1)S(1)}, bf16[96,2176]{1,0:T(8,128)(2,1)S(1)}, u32[]{:S(2)}, u32[]{:S(2)}) collective-permute-start(bf16[96,2176]{1,0:T(8,128)(2,1)S(1)} %shard_map.148.refs_0_), channel_id=1, source_target_pairs={{4,0},{5,1},{8,4},{9,5},{12,8},{13,9},{14,12},{15,13},{10,14},{11,... | collective-permute-start | bytes 1253384 | tf_op jit(solution)/shard_map/ppermute | solution.py:271
  45.0 20.5 %copy-start.29 = (bf16[96,2176]{1,0:T(8,128)(2,1)}, bf16[96,2176]{1,0:T(8,128)(2,1)S(1)}, u32[]{:S(2)}) copy-start(bf16[96,2176]{1,0:T(8,128)(2,1)S(1)} %collective-permute-done.4.refs_1_) | copy-start | bytes 1253380
  49.0 16.4 %collective-permute-start.11 = (bf16[96,2176]{1,0:T(8,128)(2,1)S(1)}, bf16[96,2176]{1,0:T(8,128)(2,1)S(1)}, u32[]{:S(2)}, u32[]{:S(2)}) collective-permute-start(bf16[96,2176]{1,0:T(8,128)(2,1)S(1)} %collective-permute-done.4.refs_1_), channel_id=1, source_target_pairs={{0,4},{1,5},{4,8},{5,9},{8,12},{9,13},{12,14},{13,15},{14,10},{15,... | collective-permute-start | bytes 1253384 | tf_op jit(solution)/shard_map/ppermute | solution.py:271
  49.0 16.4 %collective-permute-start.12 = (bf16[96,2176]{1,0:T(8,128)(2,1)S(1)}, bf16[96,2176]{1,0:T(8,128)(2,1)S(1)}, u32[]{:S(2)}, u32[]{:S(2)}) collective-permute-start(bf16[96,2176]{1,0:T(8,128)(2,1)S(1)} %collective-permute-done.5.refs_2_), channel_id=1, source_target_pairs={{4,0},{5,1},{8,4},{9,5},{12,8},{13,9},{14,12},{15,13},{10,14},{11,... | collective-permute-start | bytes 1253384 | tf_op jit(solution)/shard_map/ppermute | solution.py:271
  51.1 13.1 %collective-permute-start.13 = (bf16[96,2048]{1,0:T(8,128)(2,1)S(1)}, bf16[96,2048]{1,0:T(8,128)(2,1)S(1)}, u32[]{:S(2)}, u32[]{:S(2)}) collective-permute-start(bf16[96,2048]{1,0:T(8,128)(2,1)S(1)} %collective-permute-done.6.refs_8_), channel_id=1, source_target_pairs={{0,4},{1,5},{4,8},{5,9},{8,12},{9,13},{12,14},{13,15},{14,10},{15,... | collective-permute-start | bytes 1179656 | tf_op jit(solution)/shard_map/ppermute | solution.py:271
  51.1 14.3 %collective-permute-start.14 = (bf16[96,2048]{1,0:T(8,128)(2,1)S(1)}, bf16[96,2048]{1,0:T(8,128)(2,1)S(1)}, u32[]{:S(2)}, u32[]{:S(2)}) collective-permute-start(bf16[96,2048]{1,0:T(8,128)(2,1)S(1)} %collective-permute-done.7.refs_9_), channel_id=1, source_target_pairs={{4,0},{5,1},{8,4},{9,5},{12,8},{13,9},{14,12},{15,13},{10,14},{11,... | collective-permute-start | bytes 1179656 | tf_op jit(solution)/shard_map/ppermute | solution.py:271
  65.4 31.8 %copy-start.23 = (bf16[96,2048]{1,0:T(8,128)(2,1)}, bf16[96,2048]{1,0:T(8,128)(2,1)S(1)}, u32[]{:S(2)}) copy-start(bf16[96,2048]{1,0:T(8,128)(2,1)S(1)} %collective-permute-done.14.refs_5_) | copy-start | bytes 1179652
  66.3 7.8 %collective-permute-start.17 = (bf16[48,2048]{1,0:T(8,128)(2,1)S(1)}, bf16[48,2048]{1,0:T(8,128)(2,1)S(1)}, u32[]{:S(2)}, u32[]{:S(2)}) collective-permute-start(bf16[48,2048]{1,0:T(8,128)(2,1)S(1)} %slice.66), channel_id=1, source_target_pairs={{0,4},{1,5},{4,8},{5,9},{8,12},{9,13},{12,14},{13,15},{14,10},{15,... | collective-permute-start | bytes 589832 | tf_op jit(solution)/shard_map/ppermute | solution.py:271
  67.5 29.7 %collective-permute-start.19 = (bf16[96,2048]{1,0:T(8,128)(2,1)S(1)}, bf16[96,2048]{1,0:T(8,128)(2,1)S(1)}, u32[]{:S(2)}, u32[]{:S(2)}) collective-permute-start(bf16[96,2048]{1,0:T(8,128)(2,1)S(1)} %get-tuple-element.240.refs_3_), channel_id=1, source_target_pairs={{0,4},{1,5},{4,8},{5,9},{8,12},{9,13},{12,14},{13,15},{14,10},{15,... | collective-permute-start | bytes 1179656 | tf_op jit(solution)/shard_map/ppermute | solution.py:271
  69.1 28.2 %collective-permute-start.20 = (bf16[96,2048]{1,0:T(8,128)(2,1)S(1)}, bf16[96,2048]{1,0:T(8,128)(2,1)S(1)}, u32[]{:S(2)}, u32[]{:S(2)}) collective-permute-start(bf16[96,2048]{1,0:T(8,128)(2,1)S(1)} %get-tuple-element.240.refs_3_), channel_id=1, source_target_pairs={{4,0},{5,1},{8,4},{9,5},{12,8},{13,9},{14,12},{15,13},{10,14},{11,... | collective-permute-start | bytes 1179656 | tf_op jit(solution)/shard_map/ppermute | solution.py:271
  69.5 27.7 %collective-permute-start.15 = (bf16[96,2176]{1,0:T(8,128)(2,1)}, bf16[96,2176]{1,0:T(8,128)(2,1)S(1)}, u32[]{:S(2)}, u32[]{:S(2)}) collective-permute-start(bf16[96,2176]{1,0:T(8,128)(2,1)} %copy-done.27), channel_id=1, source_target_pairs={{0,4},{1,5},{4,8},{5,9},{8,12},{9,13},{12,14},{13,15},{14,10},{15,... | collective-permute-start | bytes 1253384 | tf_op jit(solution)/shard_map/ppermute | solution.py:271
  71.1 26.2 %collective-permute-start.16 = (bf16[96,2176]{1,0:T(8,128)(2,1)}, bf16[96,2176]{1,0:T(8,128)(2,1)S(1)}, u32[]{:S(2)}, u32[]{:S(2)}) collective-permute-start(bf16[96,2176]{1,0:T(8,128)(2,1)} %copy-done.28), channel_id=1, source_target_pairs={{4,0},{5,1},{8,4},{9,5},{12,8},{13,9},{14,12},{15,13},{10,14},{11,... | collective-permute-start | bytes 1253384 | tf_op jit(solution)/shard_map/ppermute | solution.py:271
  74.2 23.0 %copy-start.40 = (bf16[48,2048]{1,0:T(8,128)(2,1)}, bf16[48,2048]{1,0:T(8,128)(2,1)S(1)}, u32[]{:S(2)}) copy-start(bf16[48,2048]{1,0:T(8,128)(2,1)S(1)} %collective-permute-done.17.refs_6_) | copy-start | bytes 589828
  74.2 23.0 %collective-permute-start.18 = (bf16[48,2048]{1,0:T(8,128)(2,1)S(1)}, bf16[48,2048]{1,0:T(8,128)(2,1)S(1)}, u32[]{:S(2)}, u32[]{:S(2)}) collective-permute-start(bf16[48,2048]{1,0:T(8,128)(2,1)S(1)} %slice.67), channel_id=1, source_target_pairs={{4,0},{5,1},{8,4},{9,5},{12,8},{13,9},{14,12},{15,13},{10,14},{11,... | collective-permute-start | bytes 589832 | tf_op jit(solution)/shard_map/ppermute | solution.py:271
  97.3 14.9 %collective-permute-start.21 = (bf16[48,2176]{1,0:T(8,128)(2,1)S(1)}, bf16[48,2176]{1,0:T(8,128)(2,1)S(1)}, u32[]{:S(2)}, u32[]{:S(2)}) collective-permute-start(bf16[48,2176]{1,0:T(8,128)(2,1)S(1)} %slice.68), channel_id=1, source_target_pairs={{0,4},{1,5},{4,8},{5,9},{8,12},{9,13},{12,14},{13,15},{14,10},{15,... | collective-permute-start | bytes 626696 | tf_op jit(solution)/shard_map/ppermute | solution.py:271
  97.6 14.6 %collective-permute-start.22 = (bf16[48,2176]{1,0:T(8,128)(2,1)S(1)}, bf16[48,2176]{1,0:T(8,128)(2,1)S(1)}, u32[]{:S(2)}, u32[]{:S(2)}) collective-permute-start(bf16[48,2176]{1,0:T(8,128)(2,1)S(1)} %slice.69), channel_id=1, source_target_pairs={{4,0},{5,1},{8,4},{9,5},{12,8},{13,9},{14,12},{15,13},{10,14},{11,... | collective-permute-start | bytes 626696 | tf_op jit(solution)/shard_map/ppermute | solution.py:271
  99.5 12.8 %collective-permute-start.23 = (bf16[96,2048]{1,0:T(8,128)(2,1)S(1)}, bf16[96,2048]{1,0:T(8,128)(2,1)S(1)}, u32[]{:S(2)}, u32[]{:S(2)}) collective-permute-start(bf16[96,2048]{1,0:T(8,128)(2,1)S(1)} %collective-permute-done.19.refs_4_), channel_id=1, source_target_pairs={{0,4},{1,5},{4,8},{5,9},{8,12},{9,13},{12,14},{13,15},{14,10},{15,... | collective-permute-start | bytes 1179656 | tf_op jit(solution)/shard_map/ppermute | solution.py:271
  99.7 12.6 %collective-permute-start.24 = (bf16[96,2048]{1,0:T(8,128)(2,1)S(1)}, bf16[96,2048]{1,0:T(8,128)(2,1)S(1)}, u32[]{:S(2)}, u32[]{:S(2)}) collective-permute-start(bf16[96,2048]{1,0:T(8,128)(2,1)S(1)} %collective-permute-done.20.refs_5_), channel_id=1, source_target_pairs={{4,0},{5,1},{8,4},{9,5},{12,8},{13,9},{14,12},{15,13},{10,14},{11,... | collective-permute-start | bytes 1179656 | tf_op jit(solution)/shard_map/ppermute | solution.py:271
  112.3 17.1 %collective-permute-start.25 = (bf16[96,2048]{1,0:T(8,128)(2,1)S(1)}, bf16[96,2048]{1,0:T(8,128)(2,1)S(1)}, u32[]{:S(2)}, u32[]{:S(2)}) collective-permute-start(bf16[96,2048]{1,0:T(8,128)(2,1)S(1)} %collective-permute-done.23.refs_6_), channel_id=1, source_target_pairs={{0,4},{1,5},{4,8},{5,9},{8,12},{9,13},{12,14},{13,15},{14,10},{15,... | collective-permute-start | bytes 1179656 | tf_op jit(solution)/shard_map/ppermute | solution.py:271
  112.6 16.8 %collective-permute-start.26 = (bf16[96,2048]{1,0:T(8,128)(2,1)S(1)}, bf16[96,2048]{1,0:T(8,128)(2,1)S(1)}, u32[]{:S(2)}, u32[]{:S(2)}) collective-permute-start(bf16[96,2048]{1,0:T(8,128)(2,1)S(1)} %collective-permute-done.24.refs_7_), channel_id=1, source_target_pairs={{4,0},{5,1},{8,4},{9,5},{12,8},{13,9},{14,12},{15,13},{10,14},{11,... | collective-permute-start | bytes 1179656 | tf_op jit(solution)/shard_map/ppermute | solution.py:271
  129.5 7.8 %collective-permute-start.27 = (bf16[48,2048]{1,0:T(8,128)(2,1)S(1)}, bf16[48,2048]{1,0:T(8,128)(2,1)S(1)}, u32[]{:S(2)}, u32[]{:S(2)}) collective-permute-start(bf16[48,2048]{1,0:T(8,128)(2,1)S(1)} %slice.70), channel_id=1, source_target_pairs={{0,4},{1,5},{4,8},{5,9},{8,12},{9,13},{12,14},{13,15},{14,10},{15,... | collective-permute-start | bytes 589832 | tf_op jit(solution)/shard_map/ppermute | solution.py:271
  129.8 7.4 %collective-permute-start.28 = (bf16[48,2048]{1,0:T(8,128)(2,1)S(1)}, bf16[48,2048]{1,0:T(8,128)(2,1)S(1)}, u32[]{:S(2)}, u32[]{:S(2)}) collective-permute-start(bf16[48,2048]{1,0:T(8,128)(2,1)S(1)} %slice.71), channel_id=1, source_target_pairs={{4,0},{5,1},{8,4},{9,5},{12,8},{13,9},{14,12},{15,13},{10,14},{11,... | collective-permute-start | bytes 589832 | tf_op jit(solution)/shard_map/ppermute | solution.py:271
  131.6 9.1 %collective-permute-start.29 = (bf16[48,2048]{1,0:T(8,128)(2,1)}, bf16[48,2048]{1,0:T(8,128)(2,1)S(1)}, u32[]{:S(2)}, u32[]{:S(2)}) collective-permute-start(bf16[48,2048]{1,0:T(8,128)(2,1)} %get-tuple-element.295), channel_id=1, source_target_pairs={{0,4},{1,5},{4,8},{5,9},{8,12},{9,13},{12,14},{13,15},{14,10},{15,... | collective-permute-start | bytes 589832 | tf_op jit(solution)/shard_map/ppermute | solution.py:271
  131.9 8.9 %collective-permute-start.30 = (bf16[48,2048]{1,0:T(8,128)(2,1)}, bf16[48,2048]{1,0:T(8,128)(2,1)S(1)}, u32[]{:S(2)}, u32[]{:S(2)}) collective-permute-start(bf16[48,2048]{1,0:T(8,128)(2,1)} %get-tuple-element.296), channel_id=1, source_target_pairs={{4,0},{5,1},{8,4},{9,5},{12,8},{13,9},{14,12},{15,13},{10,14},{11,... | collective-permute-start | bytes 589832 | tf_op jit(solution)/shard_map/ppermute | solution.py:271
  142.7 15.2 %collective-permute-start.32 = (bf16[96,2048]{1,0:T(8,128)(2,1)S(1)}, bf16[96,2048]{1,0:T(8,128)(2,1)S(1)}, u32[]{:S(2)}, u32[]{:S(2)}) collective-permute-start(bf16[96,2048]{1,0:T(8,128)(2,1)S(1)} %pad_maximum_fusion.1), channel_id=1, source_target_pairs={{4,0},{5,1},{8,4},{9,5},{12,8},{13,9},{14,12},{15,13},{10,14},{11,... | collective-permute-start | bytes 1179656 | tf_op jit(solution)/shard_map/ppermute | solution.py:271
  144.5 13.4 %collective-permute-start.31 = (bf16[96,2048]{1,0:T(8,128)(2,1)S(1)}, bf16[96,2048]{1,0:T(8,128)(2,1)S(1)}, u32[]{:S(2)}, u32[]{:S(2)}) collective-permute-start(bf16[96,2048]{1,0:T(8,128)(2,1)S(1)} %pad_maximum_fusion), channel_id=1, source_target_pairs={{0,4},{1,5},{4,8},{5,9},{8,12},{9,13},{12,14},{13,15},{14,10},{15,... | collective-permute-start | bytes 1179656 | tf_op jit(solution)/shard_map/ppermute | solution.py:271
  157.9 19.9 %copy-start.6 = (bf16[96,2048]{1,0:T(8,128)(2,1)S(1)}, bf16[96,2048]{1,0:T(8,128)(2,1)}, u32[]{:S(2)}) copy-start(bf16[96,2048]{1,0:T(8,128)(2,1)} %get-tuple-element.353) | copy-start | bytes 1179652
  158.0 20.5 %copy-start.13 = (bf16[96,2048]{1,0:T(8,128)(2,1)S(1)}, bf16[96,2048]{1,0:T(8,128)(2,1)}, u32[]{:S(2)}) copy-start(bf16[96,2048]{1,0:T(8,128)(2,1)} %get-tuple-element.351) | copy-start | bytes 1179652
  158.0 18.0 %collective-permute-start.34 = (bf16[96,2048]{1,0:T(8,128)(2,1)S(1)}, bf16[96,2048]{1,0:T(8,128)(2,1)S(1)}, u32[]{:S(2)}, u32[]{:S(2)}) collective-permute-start(bf16[96,2048]{1,0:T(8,128)(2,1)S(1)} %add_convert_fusion.6), channel_id=1, source_target_pairs={{4,0},{5,1},{8,4},{9,5},{12,8},{13,9},{14,12},{15,13},{10,14},{11,... | collective-permute-start | bytes 1179656 | tf_op jit(solution)/shard_map/ppermute | solution.py:271
  159.8 16.3 %collective-permute-start.33 = (bf16[96,2048]{1,0:T(8,128)(2,1)S(1)}, bf16[96,2048]{1,0:T(8,128)(2,1)S(1)}, u32[]{:S(2)}, u32[]{:S(2)}) collective-permute-start(bf16[96,2048]{1,0:T(8,128)(2,1)S(1)} %add_convert_fusion.7), channel_id=1, source_target_pairs={{0,4},{1,5},{4,8},{5,9},{8,12},{9,13},{12,14},{13,15},{14,10},{15,... | collective-permute-start | bytes 1179656 | tf_op jit(solution)/shard_map/ppermute | solution.py:271
  160.3 15.8 %collective-permute-start.35 = (bf16[48,2048]{1,0:T(8,128)(2,1)S(1)}, bf16[48,2048]{1,0:T(8,128)(2,1)S(1)}, u32[]{:S(2)}, u32[]{:S(2)}) collective-permute-start(bf16[48,2048]{1,0:T(8,128)(2,1)S(1)} %copy-done.45), channel_id=1, source_target_pairs={{0,4},{1,5},{4,8},{5,9},{8,12},{9,13},{12,14},{13,15},{14,10},{15,... | collective-permute-start | bytes 589832 | tf_op jit(solution)/shard_map/ppermute | solution.py:271
  160.8 15.3 %collective-permute-start.36 = (bf16[48,2048]{1,0:T(8,128)(2,1)S(1)}, bf16[48,2048]{1,0:T(8,128)(2,1)S(1)}, u32[]{:S(2)}, u32[]{:S(2)}) collective-permute-start(bf16[48,2048]{1,0:T(8,128)(2,1)S(1)} %copy-done.44), channel_id=1, source_target_pairs={{4,0},{5,1},{8,4},{9,5},{12,8},{13,9},{14,12},{15,13},{10,14},{11,... | collective-permute-start | bytes 589832 | tf_op jit(solution)/shard_map/ppermute | solution.py:271
  176.2 19.2 %copy-start.17 = (bf16[96,2048]{1,0:T(8,128)(2,1)S(1)}, bf16[96,2048]{1,0:T(8,128)(2,1)}, u32[]{:S(2)}) copy-start(bf16[96,2048]{1,0:T(8,128)(2,1)} %get-tuple-element.365) | copy-start | bytes 1179652
  176.2 11.2 %collective-permute-start.40 = (bf16[96,2048]{1,0:T(8,128)(2,1)S(1)}, bf16[96,2048]{1,0:T(8,128)(2,1)S(1)}, u32[]{:S(2)}, u32[]{:S(2)}) collective-permute-start(bf16[96,2048]{1,0:T(8,128)(2,1)S(1)} %pad_maximum_fusion.3), channel_id=1, source_target_pairs={{4,0},{5,1},{8,4},{9,5},{12,8},{13,9},{14,12},{15,13},{10,14},{11,... | collective-permute-start | bytes 1179656 | tf_op jit(solution)/shard_map/ppermute | solution.py:271
  177.8 18.5 %copy-start.16 = (bf16[96,2048]{1,0:T(8,128)(2,1)S(1)}, bf16[96,2048]{1,0:T(8,128)(2,1)}, u32[]{:S(2)}) copy-start(bf16[96,2048]{1,0:T(8,128)(2,1)} %get-tuple-element.363) | copy-start | bytes 1179652
  177.9 19.9 %copy-start.3 = (bf16[96,2048]{1,0:T(8,128)(2,1)S(1)}, bf16[96,2048]{1,0:T(8,128)(2,1)}, u32[]{:S(2)}) copy-start(bf16[96,2048]{1,0:T(8,128)(2,1)} %get-tuple-element.357) | copy-start | bytes 1179652
  177.9 10.9 %collective-permute-start.39 = (bf16[96,2048]{1,0:T(8,128)(2,1)S(1)}, bf16[96,2048]{1,0:T(8,128)(2,1)S(1)}, u32[]{:S(2)}, u32[]{:S(2)}) collective-permute-start(bf16[96,2048]{1,0:T(8,128)(2,1)S(1)} %pad_maximum_fusion.2), channel_id=1, source_target_pairs={{0,4},{1,5},{4,8},{5,9},{8,12},{9,13},{12,14},{13,15},{14,10},{15,... | collective-permute-start | bytes 1179656 | tf_op jit(solution)/shard_map/ppermute | solution.py:271
  178.6 13.7 %collective-permute-start.38 = (bf16[96,2048]{1,0:T(8,128)(2,1)S(1)}, bf16[96,2048]{1,0:T(8,128)(2,1)S(1)}, u32[]{:S(2)}, u32[]{:S(2)}) collective-permute-start(bf16[96,2048]{1,0:T(8,128)(2,1)S(1)} %add_convert_fusion.4), channel_id=1, source_target_pairs={{4,0},{5,1},{8,4},{9,5},{12,8},{13,9},{14,12},{15,13},{10,14},{11,... | collective-permute-start | bytes 1179656 | tf_op jit(solution)/shard_map/ppermute | solution.py:271
  180.2 15.2 %collective-permute-start.37 = (bf16[96,2048]{1,0:T(8,128)(2,1)S(1)}, bf16[96,2048]{1,0:T(8,128)(2,1)S(1)}, u32[]{:S(2)}, u32[]{:S(2)}) collective-permute-start(bf16[96,2048]{1,0:T(8,128)(2,1)S(1)} %add_convert_fusion.5), channel_id=1, source_target_pairs={{0,4},{1,5},{4,8},{5,9},{8,12},{9,13},{12,14},{13,15},{14,10},{15,... | collective-permute-start | bytes 1179656 | tf_op jit(solution)/shard_map/ppermute | solution.py:271
  195.5 7.8 %collective-permute-start.42 = (bf16[96,2048]{1,0:T(8,128)(2,1)S(1)}, bf16[96,2048]{1,0:T(8,128)(2,1)S(1)}, u32[]{:S(2)}, u32[]{:S(2)}) collective-permute-start(bf16[96,2048]{1,0:T(8,128)(2,1)S(1)} %add_convert_fusion.2), channel_id=1, source_target_pairs={{4,0},{5,1},{8,4},{9,5},{12,8},{13,9},{14,12},{15,13},{10,14},{11,... | collective-permute-start | bytes 1179656 | tf_op jit(solution)/shard_map/ppermute | solution.py:271
  196.5 7.8 %collective-permute-start.41 = (bf16[96,2048]{1,0:T(8,128)(2,1)S(1)}, bf16[96,2048]{1,0:T(8,128)(2,1)S(1)}, u32[]{:S(2)}, u32[]{:S(2)}) collective-permute-start(bf16[96,2048]{1,0:T(8,128)(2,1)S(1)} %add_convert_fusion.3), channel_id=1, source_target_pairs={{0,4},{1,5},{4,8},{5,9},{8,12},{9,13},{12,14},{13,15},{14,10},{15,... | collective-permute-start | bytes 1179656 | tf_op jit(solution)/shard_map/ppermute | solution.py:271
  204.4 7.8 %collective-permute-start.43 = (bf16[96,2048]{1,0:T(8,128)(2,1)S(1)}, bf16[96,2048]{1,0:T(8,128)(2,1)S(1)}, u32[]{:S(2)}, u32[]{:S(2)}) collective-permute-start(bf16[96,2048]{1,0:T(8,128)(2,1)S(1)} %add_convert_fusion.1), channel_id=1, source_target_pairs={{0,4},{1,5},{4,8},{5,9},{8,12},{9,13},{12,14},{13,15},{14,10},{15,... | collective-permute-start | bytes 1179656 | tf_op jit(solution)/shard_map/ppermute | solution.py:271
  205.8 7.8 %collective-permute-start.44 = (bf16[96,2048]{1,0:T(8,128)(2,1)S(1)}, bf16[96,2048]{1,0:T(8,128)(2,1)S(1)}, u32[]{:S(2)}, u32[]{:S(2)}) collective-permute-start(bf16[96,2048]{1,0:T(8,128)(2,1)S(1)} %add_convert_fusion), channel_id=1, source_target_pairs={{4,0},{5,1},{8,4},{9,5},{12,8},{13,9},{14,12},{15,13},{10,14},{11,... | collective-permute-start | bytes 1179656 | tf_op jit(solution)/shard_map/ppermute | solution.py:271
  (27 other events, 259.0 us)

commit v4 on v3

--- a/solution.py
+++ b/solution.py
@@ -254,6 +254,17 @@
     return (first.astype(jnp.float32) + second.astype(jnp.float32)).astype(jnp.bfloat16)
 
 
+def joined(block, moved, way):
+    if moved is None:
+        return block
+    half = moved.shape[0]
+    if half == block.shape[0]:
+        return added(block, moved)
+    if way == 0:
+        return jnp.concatenate([added(block[:half], moved), block[half:]])
+    return jnp.concatenate([block[:half], added(block[half:], moved)])
+
+
 class Section:
     def __init__(self, sources, names):
         self.sources = sources
@@ -270,9 +281,12 @@
     def pass_on(self, block, way):
         return lax.ppermute(block, "ep", self.routes[way])
 
-    def gather(self, name, distance):
+    def gather(self, name, distance, way=None):
         held = self.held[name]
         behind, ahead = held[distance - 1][0], held[distance - 1][-1]
+        if distance == self.far and way is not None:
+            held[distance] = [self.pass_on((behind, ahead)[way], way)]
+            return
         if distance == self.far:
             half = behind.shape[0] // 2
             behind, ahead = behind[:half], ahead[half:]
@@ -288,21 +302,21 @@
             count = len(rows[d])
             made[d], outs = outs[:count], outs[count:]
 
-    def scatter(self, kind, step):
+    def scatter(self, kind, step, way=None):
         distance = self.far + 1 - step
-        behind, ahead = self.made[kind][distance]
-        if step == 1:
-            forth, back = behind, ahead
-        else:
-            moved_forth, moved_back = self.sums[kind]
-            if step == 2:
-                half = moved_forth.shape[0]
-                forth = jnp.concatenate([added(ahead[:half], moved_forth), ahead[half:]])
-                back = jnp.concatenate([behind[:half], added(behind[half:], moved_back)])
+        pieces = self.made[kind].pop(distance)
+        if step == 1 and len(pieces) == 1:
+            half = pieces[0].shape[0] // 2
+            if way is None:
+                pieces = [pieces[0][:half], pieces[0][half:]]
             else:
-                forth, back = added(ahead, moved_forth), added(behind, moved_back)
-        self.sums[kind] = [self.pass_on(forth, 0), self.pass_on(back, 1)]
-        del self.made[kind][distance]
+                pieces = [pieces[0] if way == i else None for i in range(2)]
+        elif step > 1:
+            moved = self.sums[kind]
+            pieces = [joined(pieces[1 - i], moved[i], i) for i in range(2)]
+        self.sums[kind] = [
+            None if piece is None else self.pass_on(piece, i) for i, piece in enumerate(pieces)
+        ]
 
     def total(self, kind):
         pieces = self.made[kind][0] + self.sums[kind]
@@ -313,10 +327,6 @@
         state = lax.optimization_barrier(state)
         self.held, self.made, self.sums, others = state
         return others
-
-    def fence_weights(self):
-        state = (self.held, self.weights)
-        self.held, self.weights = lax.optimization_barrier(state)
 
 
 def local(
@@ -355,20 +365,21 @@
     moved_cot = passed_along(leaving_cot, "pipe", 1)
     moved_rise = passed_along(leaving_rise, "pipe", 1)
     own = (w_gate[0, 0], w_up[0, 0], w_down[0, 0])
-    ring.weights = own + tuple(lax.ppermute(own, "ep", ring.swap))
+
+    def swapped(weight):
+        return lax.ppermute(weight, "ep", ring.swap)
 
     at_start = section_index == 0
     cot_in = jnp.where(at_start, entering[1], moved_cot)
     rise_in = jnp.where(at_start, entering[0], moved_rise)
-    rise_wide = rise_in.astype(jnp.float32)
     ring.held["cot"] = {0: [packed_rows(cot_in, route_ids[:, 0], route_gates[:, 0], sources)]}
     ring.held["rise"] = {}
-    rise_normal = normed(rise_wide, norm_row).astype(jnp.bfloat16)
-
-    def exit_heads(rise_in, cot_in):
+
+    head_rise = jnp.take(exit_list[0], section_index).astype(jnp.float32)
+    head_fall = jnp.take(exit_list[1], sections - 1 - section_index).astype(jnp.float32)
+
+    def exit_heads(rise_in, cot_in, head_rise, head_fall):
         rise_wide = rise_in.astype(jnp.float32)
-        head_rise = jnp.take(exit_list[0], section_index).astype(jnp.float32)
-        head_fall = jnp.take(exit_list[1], sections - 1 - section_index).astype(jnp.float32)
         rise_diff = normed(rise_wide, exit_row) - targets[0].astype(jnp.float32)
         loss_rise = head_rise * 0.5 * jnp.mean(rise_diff * rise_diff, axis=-1)
         fall_diff = normed(fall_wide, exit_row) - targets[1].astype(jnp.float32)
@@ -381,32 +392,44 @@
         return kept + norm_pullback(fall_wide, norm_row, ring.total("backward"))
 
     if planned:
-        (cot_in,) = ring.fence(cot_in)
+        own_gate, own_up, own_down = own
+        other_down = swapped(own_down)
+        cot_in, rise_in, own_gate, own_up, other_down = ring.fence(
+            cot_in, rise_in, own_gate, own_up, other_down
+        )
+        heads, ring.names = lax.optimization_barrier(((head_rise, head_fall), names))
         ring.gather("fall", 2)
         ring.gather("cot", 1)
-        ring.fence_weights()
+        other_gate = swapped(own_gate)
+        rise_normal = normed(rise_in.astype(jnp.float32), norm_row).astype(jnp.bfloat16)
+        rise_normal, own_up, other_gate, heads, ring.names = ring.fence(
+            rise_normal, own_up, other_gate, heads, ring.names
+        )
         ring.gather("fall", 3)
         ring.gather("cot", 2)
-        kept, exit_loss = exit_heads(rise_in, cot_in)
-        rise_normal, kept, exit_loss = ring.fence(rise_normal, kept, exit_loss)
+        other_up = swapped(own_up)
+        kept, exit_loss = exit_heads(rise_in, cot_in, *heads)
+        kept, exit_loss, other_up = ring.fence(kept, exit_loss, other_up)
+        ring.weights = own + (other_gate, other_up, other_down)
         ring.held["rise"] = {0: [rise_normal]}
-        ring.gather("fall", 4)
         ring.gather("cot", 3)
         ring.gather("rise", 1)
-        ring.work("backward", [0, 1, 2])
-        ring.fence()
-        ring.gather("cot", 4)
+        ring.work("backward", [0, 1])
+        ring.fence()
+        ring.gather("fall", 4, 0)
+        ring.gather("cot", 4, 1)
         ring.gather("rise", 2)
-        ring.work("forward", [0, 1])
+        ring.work("backward", [2, 3])
         ring.fence()
         ring.gather("rise", 3)
-        ring.work("backward", [3, 4])
-        ring.fence()
-        ring.gather("rise", 4)
-        ring.scatter("backward", 1)
+        ring.work("backward", [4])
+        ring.fence()
+        ring.gather("rise", 4, 0)
+        ring.scatter("backward", 1, 1)
+        ring.work("forward", [0, 1, 2])
         ring.fence()
         ring.scatter("backward", 2)
-        ring.work("forward", [2, 3, 4])
+        ring.work("forward", [3, 4])
         ring.fence()
         ring.scatter("backward", 3)
         ring.scatter("forward", 1)
@@ -419,7 +442,9 @@
         (fall_total,) = ring.fence(fall_total)
         ring.scatter("forward", 4)
     else:
-        kept, exit_loss = exit_heads(rise_in, cot_in)
+        ring.weights = own + tuple(swapped(own))
+        kept, exit_loss = exit_heads(rise_in, cot_in, head_rise, head_fall)
+        rise_normal = normed(rise_in.astype(jnp.float32), norm_row).astype(jnp.bfloat16)
         ring.held["rise"] = {0: [rise_normal]}
         for name in ("fall", "cot", "rise"):
             for distance in range(1 if name != "fall" else 2, far + 1):
@@ -431,7 +456,7 @@
             for step in range(1, far + 1):
                 ring.scatter(kind, step)
         fall_total = falling(kept).astype(jnp.bfloat16)
-    layer_out = (rise_wide + ring.total("forward")).astype(jnp.bfloat16)
+    layer_out = (rise_in.astype(jnp.float32) + ring.total("forward")).astype(jnp.bfloat16)
     return (layer_out[None], fall_total[None], exit_loss)
 
 

time: 215 us -> 214 us (level)
  starting transfers between devices: 54.3 us -> 44.5 us
  Pallas kernels: 60.4 us -> 68.9 us
  waiting for transfers between devices: 81 us -> 83.5 us
    ppermute x2, waiting for transfers between devices: 3.5 us -> 12.7 us  [passed_along(): return lax.ppermute(block, axis, route)]
    pallas_call x4 -> x5, Pallas kernels: 59.7 us -> 68.2 us  [expert_call(): pl.pallas_call(functools.partial(body, parts, experts, width, tile), out_...]
    ppermute x40 -> x36, starting transfers between devices: 45.2 us -> 37.9 us  [pass_on(): return lax.ppermute(block, 'ep', self.routes[way])]
    ppermute x40 -> x36, waiting for transfers between devices: 77.4 us -> 70.8 us  [pass_on(): return lax.ppermute(block, 'ep', self.routes[way])]
    ppermute x2, starting transfers between devices: 8.6 us -> 5.88 us  [passed_along(): return lax.ppermute(block, axis, route)]
  transfers between devices with their start and end apart: 45 -> 41, of which waited for: 22 -> 16; matrix products, arithmetic and copies ran while one was open for 4% -> 5% of each run, Pallas kernels for 28% -> 32%
where the time goes in v4:
time: 214 us; the launch traced here: 213 us
  waiting for transfers between devices  83.5 us (39%)
  Pallas kernels  68.9 us (32%)
  starting transfers between devices  44.5 us (21%)
  other arithmetic  9.53 us (4%)
  local copies, waits for them, and re-layouts  4.07 us (2%)
  between operations  2.87 us (1%)
    ppermute x36, waiting for transfers between devices, pass_on(): return lax.ppermute(block, 'ep', self.routes[way])  70.8 us
    pallas_call x5, Pallas kernels, expert_call(): pl.pallas_call(functools.partial(body, parts, experts, width, tile), out_...  68.2 us
    ppermute x36, starting transfers between devices, pass_on(): return lax.ppermute(block, 'ep', self.routes[way])  37.9 us
    ppermute x2, waiting for transfers between devices, passed_along(): return lax.ppermute(block, axis, route)  12.7 us
    ppermute x2, starting transfers between devices, passed_along(): return lax.ppermute(block, axis, route)  5.88 us
  transfers between devices with their start and end apart: 41, of which 16 were waited for; matrix products, arithmetic and copies ran while one was open for 5% of the time, Pallas kernels for 32%

profile of v4, /device:TPU:0, one launch (start us, length us, event | category | flops | bytes accessed | tf_op | source)
XLA Modules:
  0.0 213.4 jit_solution(16804694548037935597)
XLA Ops:
  0.6 0.5 collective-permute-start.4
  1.1 1.2 fusion.16
  2.3 1.2 fusion.4.refs_3_
  3.6 4.6 %collective-permute-start = (bf16[96,2048]{1,0:T(8,128)(2,1)}, bf16[96,2048]{1,0:T(8,128)(2,1)S(1)}, u32[]{:S(2)}, u32[]{:S(2)}) collective-permute-start(bf16[96,2048]{1,0:T(8,128)(2,1)} %bitcast.64), channel_id=1, source_target_pairs={{0,16},{1,17},{2,18},{3,19},{4,20},{5,21},{6,22},{7,23},{8,24},{9,... | collective-permute-start | bytes 1179656 | tf_op jit(solution)/shard_map/ppermute | solution.py:17
  8.2 1.3 collective-permute-start.3
  9.5 1.6 collective-permute-start.2
  11.1 0.5 collective-permute-start.1
  11.6 0.8 copy.16
  12.4 0.8 copy.17
  13.2 4.7 %collective-permute-done = bf16[96,2048]{1,0:T(8,128)(2,1)S(1)} collective-permute-done((bf16[96,2048]{1,0:T(8,128)(2,1)}, bf16[96,2048]{1,0:T(8,128)(2,1)S(1)}, u32[]{:S(2)}, u32[]{:S(2)}) %collective-permute-start) | collective-permute-done | bytes 393248 | tf_op jit(solution)/shard_map/ppermute | solution.py:17
  17.9 8.0 %collective-permute-done.3 = bf16[96,2048]{1,0:T(8,128)(2,1)S(1)} collective-permute-done((bf16[96,2048]{1,0:T(8,128)(2,1)}, bf16[96,2048]{1,0:T(8,128)(2,1)S(1)}, u32[]{:S(2)}, u32[]{:S(2)}) %collective-permute-start.3) | collective-permute-done | bytes 393248 | tf_op jit(solution)/shard_map/ppermute | solution.py:17
  25.9 1.2 bitcast_select_fusion
  27.1 0.7 shard_map.148.refs_0_
  28.0 0.6 constant_dynamic-slice_fusion.1
  29.3 0.6 constant_dynamic-slice_fusion
  30.5 0.7 pad_add_fusion.names_ref
  31.2 1.5 collective-permute-start.6
  32.7 0.5 collective-permute-start.5
  33.2 1.6 collective-permute-start.7
  35.5 0.6 multiply_reduce_fusion
  36.1 16.7 %collective-permute-done.7.refs_4_ = bf16[96,2048]{1,0:T(8,128)(2,1)S(1)} collective-permute-done((bf16[96,2048]{1,0:T(8,128)(2,1)}, bf16[96,2048]{1,0:T(8,128)(2,1)S(1)}, u32[]{:S(2)}, u32[]{:S(2)}) %collective-permute-start.7) | collective-permute-done | bytes 393248 | tf_op jit(solution)/shard_map/ppermute | solution.py:282
  53.0 0.7 copy-done.22
  54.0 0.5 collective-permute-start.12
  54.6 1.5 collective-permute-start.13
  56.1 0.5 collective-permute-start.10
  56.6 1.5 collective-permute-start.11
  58.1 0.6 maximum_bitcast_fusion
  59.1 7.2 %collective-permute-done.12.refs_6_ = bf16[96,2048]{1,0:T(8,128)(2,1)S(1)} collective-permute-done((bf16[96,2048]{1,0:T(8,128)(2,1)}, bf16[96,2048]{1,0:T(8,128)(2,1)S(1)}, u32[]{:S(2)}, u32[]{:S(2)}) %collective-permute-start.12) | collective-permute-done | bytes 393248 | tf_op jit(solution)/shard_map/ppermute | solution.py:282
  66.3 1.6 collective-permute-start.18
  68.4 6.9 %collective-permute-done.10.refs_0_.refs_3_ = bf16[96,2176]{1,0:T(8,128)(2,1)S(1)} collective-permute-done((bf16[96,2176]{1,0:T(8,128)(2,1)}, bf16[96,2176]{1,0:T(8,128)(2,1)S(1)}, u32[]{:S(2)}, u32[]{:S(2)}) %collective-permute-start.10) | collective-permute-done | bytes 417824 | tf_op jit(solution)/shard_map/ppermute | solution.py:282
  75.3 0.5 collective-permute-done.11.refs_1_.refs_4_
  75.8 1.6 collective-permute-start.15
  77.8 15.0 %shard_map.149 = (bf16[96,2048]{1,0:T(8,128)(2,1)}, bf16[96,2048]{1,0:T(8,128)(2,1)}, bf16[96,2048]{1,0:T(8,128)(2,1)}) custom-call(s32[2]{0:T(128)} %pad_add_fusion.names_ref, bf16[96,2176]{1,0:T(8,128)(2,1)} %copy-done, bf16[96,2176]{1,0:T(8,128)(2,1)} %copy-done.23, bf16[96,2176]{1,0:T(8,128)(2,1)} %copy-done.22, bf16[96,2048]{1,0:T(8,128)(2,1)} %copy-done.8, ...), custom_call_target="tpu_custom_call" | custom-call | flops 18139797504 | bytes 12582912 | tf_op jit(solution)/shard_map/pallas_call | solution.py:238
  92.9 1.6 collective-permute-start.21
  95.0 1.6 collective-permute-start.20
  97.1 17.9 %shard_map.150 = (bf16[96,2048]{1,0:T(8,128)(2,1)}, bf16[96,2048]{1,0:T(8,128)(2,1)}, bf16[96,2048]{1,0:T(8,128)(2,1)}, bf16[96,2048]{1,0:T(8,128)(2,1)}) custom-call(s32[2]{0:T(128)} %pad_add_fusion.names_ref, bf16[96,2176]{1,0:T(8,128)(2,1)} %copy-done.24, bf16[96,2176]{1,0:T(8,128)(2,1)} %copy-done.25, bf16[96,2176]{1,0:T(8,128)(2,1)} %copy-done.26, ...), custom_call_target="tpu_custom_call" | custom-call | flops 20153063424 | bytes 12582912 | tf_op jit(solution)/shard_map/pallas_call | solution.py:238
  115.1 1.6 collective-permute-start.23
  117.2 11.7 %shard_map.151 = bf16[96,2048]{1,0:T(8,128)(2,1)} custom-call(s32[2]{0:T(128)} %pad_add_fusion.names_ref, bf16[96,2176]{1,0:T(8,128)(2,1)} %copy-done.28, bf16[96,2048]{1,0:T(8,128)(2,1)} %copy-done.41, bf16[2048,512]{1,0:T(8,128)(2,1)} %bitcast.9.refs_6_.refs_8_.refs_2_.refs_10_, bf16[2048,512]{1,0:T(8,128)(2,1)} %bitcast.10.refs_7_.refs_9_.refs_3_.refs_11_, ...), custom_call_target="tpu_custom_call" | custom-call | flops 14113265664 | bytes 12582912 | tf_op jit(solution)/shard_map/pallas_call | solution.py:238
  129.0 1.6 collective-permute-start.26
  131.1 12.8 %shard_map.152 = (bf16[96,2048]{1,0:T(8,128)(2,1)}, bf16[96,2048]{1,0:T(8,128)(2,1)}, bf16[96,2048]{1,0:T(8,128)(2,1)}, bf16[96,2048]{1,0:T(8,128)(2,1)}, bf16[96,2048]{1,0:T(8,128)(2,1)}) custom-call(s32[2]{0:T(128)} %pad_add_fusion.names_ref, bf16[96,2176]{1,0:T(8,128)(2,1)} %copy-done, bf16[96,2176]{1,0:T(8,128)(2,1)} %copy-done.23, ...), custom_call_target="tpu_custom_call" | custom-call | flops 15389797376 | bytes 12582912 | tf_op jit(solution)/shard_map/pallas_call | solution.py:238
  144.1 1.6 collective-permute-start.28
  145.6 0.5 collective-permute-start.27
  146.2 10.7 %shard_map.153 = (bf16[96,2048]{1,0:T(8,128)(2,1)}, bf16[96,2048]{1,0:T(8,128)(2,1)}, bf16[96,2048]{1,0:T(8,128)(2,1)}) custom-call(s32[2]{0:T(128)} %pad_add_fusion.names_ref, bf16[96,2176]{1,0:T(8,128)(2,1)} %copy-done.26, bf16[96,2176]{1,0:T(8,128)(2,1)} %copy-done.27, bf16[96,2176]{1,0:T(8,128)(2,1)} %copy-done.28, bf16[96,2048]{1,0:T(8,128)(2,1)} %copy-done.38, ...), custom_call_target="tpu_custom_call" | custom-call | flops 12973878272 | bytes 12582912 | tf_op jit(solution)/shard_map/pallas_call | solution.py:238
  157.1 1.6 collective-permute-start.30
  158.8 0.6 collective-permute-start.29
  159.4 1.6 collective-permute-start.32
  160.9 0.5 collective-permute-start.31
  161.5 7.9 %collective-permute-done.32 = bf16[48,2048]{1,0:T(8,128)(2,1)S(1)} collective-permute-done((bf16[48,2048]{1,0:T(8,128)(2,1)S(1)}, bf16[48,2048]{1,0:T(8,128)(2,1)S(1)}, u32[]{:S(2)}, u32[]{:S(2)}) %collective-permute-start.32) | collective-permute-done | bytes 196640 | tf_op jit(solution)/shard_map/ppermute | solution.py:282
  169.4 1.9 collective-permute-done.31
  171.6 1.6 collective-permute-start.34
  173.9 1.6 collective-permute-start.36
  176.0 3.6 %collective-permute-done.34 = bf16[96,2048]{1,0:T(8,128)(2,1)S(1)} collective-permute-done((bf16[96,2048]{1,0:T(8,128)(2,1)S(1)}, bf16[96,2048]{1,0:T(8,128)(2,1)S(1)}, u32[]{:S(2)}, u32[]{:S(2)}) %collective-permute-start.34) | collective-permute-done | bytes 393248 | tf_op jit(solution)/shard_map/ppermute | solution.py:282
  179.7 1.7 collective-permute-done.33
  181.4 6.2 %collective-permute-done.36 = bf16[96,2048]{1,0:T(8,128)(2,1)S(1)} collective-permute-done((bf16[96,2048]{1,0:T(8,128)(2,1)S(1)}, bf16[96,2048]{1,0:T(8,128)(2,1)S(1)}, u32[]{:S(2)}, u32[]{:S(2)}) %collective-permute-start.36) | collective-permute-done | bytes 393248 | tf_op jit(solution)/shard_map/ppermute | solution.py:282
  187.6 2.0 collective-permute-done.35
  189.7 2.6 %collective-permute-start.38 = (bf16[96,2048]{1,0:T(8,128)(2,1)S(1)}, bf16[96,2048]{1,0:T(8,128)(2,1)S(1)}, u32[]{:S(2)}, u32[]{:S(2)}) collective-permute-start(bf16[96,2048]{1,0:T(8,128)(2,1)S(1)} %add_convert_fusion.2), channel_id=1, source_target_pairs={{4,0},{5,1},{8,4},{9,5},{12,8},{13,9},{14,12},{15,13},{10,14},{11,... | collective-permute-start | bytes 1179656 | tf_op jit(solution)/shard_map/ppermute | solution.py:282
  192.9 1.1 fusion.15
  194.0 6.9 %collective-permute-done.38 = bf16[96,2048]{1,0:T(8,128)(2,1)S(1)} collective-permute-done((bf16[96,2048]{1,0:T(8,128)(2,1)S(1)}, bf16[96,2048]{1,0:T(8,128)(2,1)S(1)}, u32[]{:S(2)}, u32[]{:S(2)}) %collective-permute-start.38) | collective-permute-done | bytes 393248 | tf_op jit(solution)/shard_map/ppermute | solution.py:282
  200.9 1.8 collective-permute-done.37
  202.8 1.6 collective-permute-start.40
  204.5 0.5 collective-permute-start.39
  205.1 5.6 %collective-permute-done.40 = bf16[96,2048]{1,0:T(8,128)(2,1)S(1)} collective-permute-done((bf16[96,2048]{1,0:T(8,128)(2,1)S(1)}, bf16[96,2048]{1,0:T(8,128)(2,1)S(1)}, u32[]{:S(2)}, u32[]{:S(2)}) %collective-permute-start.40) | collective-permute-done | bytes 393248 | tf_op jit(solution)/shard_map/ppermute | solution.py:282
  210.6 1.7 collective-permute-done.39
  212.4 1.0 fusion.19
  (145 shorter events, 7.1 us)
Async XLA Ops:
  0.6 27.3 %collective-permute-start.4 = (bf16[512,2048]{1,0:T(8,128)(2,1)}, bf16[512,2048]{1,0:T(8,128)(2,1)}, u32[]{:S(2)}, u32[]{:S(2)}) collective-permute-start(bf16[512,2048]{1,0:T(8,128)(2,1)} %bitcast.58), channel_id=1, source_target_pairs={{0,1},{1,0},{2,3},{3,2},{4,5},{5,4},{6,7},{7,6},{8,9},{9,8},{10,11... | collective-permute-start | bytes 6291464 | tf_op jit(solution)/shard_map/ppermute | solution.py:370
  2.3 25.7 %copy-start.21 = (s32[2,2]{1,0:T(2,128)S(1)}, s32[2,2]{1,0:T(2,128)}, u32[]{:S(2)}) copy-start(s32[2,2]{1,0:T(2,128)} %param.25) | copy-start | bytes 52
  3.5 32.6 %copy-start.8 = (bf16[96,2048]{1,0:T(8,128)(2,1)}, bf16[96,2048]{1,0:T(8,128)(2,1)S(1)}, u32[]{:S(2)}) copy-start(bf16[96,2048]{1,0:T(8,128)(2,1)S(1)} %fusion.4.refs_3_) | copy-start | bytes 1179652
  3.5 31.9 %copy-start.1 = (bf16[1,96,2048]{2,1,0:T(8,128)(2,1)S(1)}, bf16[1,96,2048]{2,1,0:T(8,128)(2,1)}, u32[]{:S(2)}) copy-start(bf16[1,96,2048]{2,1,0:T(8,128)(2,1)} %param.16) | copy-start | bytes 1179652
  3.5 31.9 %copy-start.2 = (bf16[2,96,2048]{2,1,0:T(8,128)(2,1)S(1)}, bf16[2,96,2048]{2,1,0:T(8,128)(2,1)}, u32[]{:S(2)}) copy-start(bf16[2,96,2048]{2,1,0:T(8,128)(2,1)} %param.17) | copy-start | bytes 2359300
  3.6 31.9 %copy-start.19 = (f32[1,2048]{1,0:T(1,128)S(1)}, f32[1,2048]{1,0:T(1,128)}, u32[]{:S(2)}) copy-start(f32[1,2048]{1,0:T(1,128)} %param.18) | copy-start | bytes 24580
  3.6 31.9 %copy-start.20 = (f32[1,2048]{1,0:T(1,128)S(1)}, f32[1,2048]{1,0:T(1,128)}, u32[]{:S(2)}) copy-start(f32[1,2048]{1,0:T(1,128)} %param.19) | copy-start | bytes 24580
  3.6 14.3 %collective-permute-start = (bf16[96,2048]{1,0:T(8,128)(2,1)}, bf16[96,2048]{1,0:T(8,128)(2,1)S(1)}, u32[]{:S(2)}, u32[]{:S(2)}) collective-permute-start(bf16[96,2048]{1,0:T(8,128)(2,1)} %bitcast.64), channel_id=1, source_target_pairs={{0,16},{1,17},{2,18},{3,19},{4,20},{5,21},{6,22},{7,23},{8,24},{9,... | collective-permute-start | bytes 1179656 | tf_op jit(solution)/shard_map/ppermute | solution.py:17
  8.2 17.7 %collective-permute-start.3 = (bf16[96,2048]{1,0:T(8,128)(2,1)}, bf16[96,2048]{1,0:T(8,128)(2,1)S(1)}, u32[]{:S(2)}, u32[]{:S(2)}) collective-permute-start(bf16[96,2048]{1,0:T(8,128)(2,1)} %bitcast.65), channel_id=1, source_target_pairs={{0,16},{1,17},{2,18},{3,19},{4,20},{5,21},{6,22},{7,23},{8,24},{9,... | collective-permute-start | bytes 1179656 | tf_op jit(solution)/shard_map/ppermute | solution.py:17
  9.5 18.4 %collective-permute-start.2 = (bf16[96,2048]{1,0:T(8,128)(2,1)S(1)}, bf16[96,2048]{1,0:T(8,128)(2,1)}, u32[]{:S(2)}, u32[]{:S(2)}) collective-permute-start(bf16[96,2048]{1,0:T(8,128)(2,1)S(1)} %fusion.4.refs_3_), channel_id=1, source_target_pairs={{4,0},{5,1},{8,4},{9,5},{12,8},{13,9},{14,12},{15,13},{10,14},{11,... | collective-permute-start | bytes 1179656 | tf_op jit(solution)/shard_map/ppermute | solution.py:282
  11.1 16.8 %collective-permute-start.1 = (bf16[96,2048]{1,0:T(8,128)(2,1)S(1)}, bf16[96,2048]{1,0:T(8,128)(2,1)}, u32[]{:S(2)}, u32[]{:S(2)}) collective-permute-start(bf16[96,2048]{1,0:T(8,128)(2,1)S(1)} %fusion.4.refs_3_), channel_id=1, source_target_pairs={{0,4},{1,5},{4,8},{5,9},{8,12},{9,13},{12,14},{13,15},{14,10},{15,... | collective-permute-start | bytes 1179656 | tf_op jit(solution)/shard_map/ppermute | solution.py:282
  27.9 31.2 %copy-start = (bf16[96,2176]{1,0:T(8,128)(2,1)}, bf16[96,2176]{1,0:T(8,128)(2,1)S(1)}, u32[]{:S(2)}) copy-start(bf16[96,2176]{1,0:T(8,128)(2,1)S(1)} %shard_map.148.refs_0_) | copy-start | bytes 1253380
  27.9 25.0 %collective-permute-start.9 = (bf16[2048,512]{1,0:T(8,128)(2,1)}, bf16[2048,512]{1,0:T(8,128)(2,1)}, u32[]{:S(2)}, u32[]{:S(2)}) collective-permute-start(bf16[2048,512]{1,0:T(8,128)(2,1)} %bitcast.9.refs_6_.refs_8_.refs_2_.refs_10_), channel_id=1, source_target_pairs={{0,1},{1,0},{2,3},{3,2},{4,5},{5,4},{6,7},{7,6},{8,9},{9,8},{10,11... | collective-permute-start | bytes 6291464 | tf_op jit(solution)/shard_map/ppermute | solution.py:370
  31.2 21.7 %collective-permute-start.6 = (bf16[96,2176]{1,0:T(8,128)(2,1)S(1)}, bf16[96,2176]{1,0:T(8,128)(2,1)S(1)}, u32[]{:S(2)}, u32[]{:S(2)}) collective-permute-start(bf16[96,2176]{1,0:T(8,128)(2,1)S(1)} %shard_map.148.refs_0_), channel_id=1, source_target_pairs={{4,0},{5,1},{8,4},{9,5},{12,8},{13,9},{14,12},{15,13},{10,14},{11,... | collective-permute-start | bytes 1253384 | tf_op jit(solution)/shard_map/ppermute | solution.py:282
  32.7 20.2 %collective-permute-start.5 = (bf16[96,2176]{1,0:T(8,128)(2,1)S(1)}, bf16[96,2176]{1,0:T(8,128)(2,1)S(1)}, u32[]{:S(2)}, u32[]{:S(2)}) collective-permute-start(bf16[96,2176]{1,0:T(8,128)(2,1)S(1)} %shard_map.148.refs_0_), channel_id=1, source_target_pairs={{0,4},{1,5},{4,8},{5,9},{8,12},{9,13},{12,14},{13,15},{14,10},{15,... | collective-permute-start | bytes 1253384 | tf_op jit(solution)/shard_map/ppermute | solution.py:282
  33.2 19.6 %collective-permute-start.7 = (bf16[96,2048]{1,0:T(8,128)(2,1)}, bf16[96,2048]{1,0:T(8,128)(2,1)S(1)}, u32[]{:S(2)}, u32[]{:S(2)}) collective-permute-start(bf16[96,2048]{1,0:T(8,128)(2,1)} %collective-permute-done.1.refs_4_), channel_id=1, source_target_pairs={{0,4},{1,5},{4,8},{5,9},{8,12},{9,13},{12,14},{13,15},{14,10},{15,... | collective-permute-start | bytes 1179656 | tf_op jit(solution)/shard_map/ppermute | solution.py:282
  34.8 18.1 %collective-permute-start.8 = (bf16[96,2048]{1,0:T(8,128)(2,1)}, bf16[96,2048]{1,0:T(8,128)(2,1)S(1)}, u32[]{:S(2)}, u32[]{:S(2)}) collective-permute-start(bf16[96,2048]{1,0:T(8,128)(2,1)} %collective-permute-done.2.refs_5_), channel_id=1, source_target_pairs={{4,0},{5,1},{8,4},{9,5},{12,8},{13,9},{14,12},{15,13},{10,14},{11,... | collective-permute-start | bytes 1179656 | tf_op jit(solution)/shard_map/ppermute | solution.py:282
  36.1 56.7 %copy-start.4 = (bf16[96,2048]{1,0:T(8,128)(2,1)}, bf16[96,2048]{1,0:T(8,128)(2,1)S(1)}, u32[]{:S(2)}) copy-start(bf16[96,2048]{1,0:T(8,128)(2,1)S(1)} %get-tuple-element.282.refs_5_) | copy-start | bytes 1179652
  52.9 22.9 %collective-permute-start.14 = (bf16[2048,512]{1,0:T(8,128)(2,1)}, bf16[2048,512]{1,0:T(8,128)(2,1)}, u32[]{:S(2)}, u32[]{:S(2)}) collective-permute-start(bf16[2048,512]{1,0:T(8,128)(2,1)} %bitcast.10.refs_7_.refs_9_.refs_3_.refs_11_), channel_id=1, source_target_pairs={{0,1},{1,0},{2,3},{3,2},{4,5},{5,4},{6,7},{7,6},{8,9},{9,8},{10,11... | collective-permute-start | bytes 6291464 | tf_op jit(solution)/shard_map/ppermute | solution.py:370
  54.0 12.3 %collective-permute-start.12 = (bf16[96,2048]{1,0:T(8,128)(2,1)}, bf16[96,2048]{1,0:T(8,128)(2,1)S(1)}, u32[]{:S(2)}, u32[]{:S(2)}) collective-permute-start(bf16[96,2048]{1,0:T(8,128)(2,1)} %copy-done.29), channel_id=1, source_target_pairs={{0,4},{1,5},{4,8},{5,9},{8,12},{9,13},{12,14},{13,15},{14,10},{15,... | collective-permute-start | bytes 1179656 | tf_op jit(solution)/shard_map/ppermute | solution.py:282
  54.6 13.3 %collective-permute-start.13 = (bf16[96,2048]{1,0:T(8,128)(2,1)}, bf16[96,2048]{1,0:T(8,128)(2,1)S(1)}, u32[]{:S(2)}, u32[]{:S(2)}) collective-permute-start(bf16[96,2048]{1,0:T(8,128)(2,1)} %copy-done.30), channel_id=1, source_target_pairs={{4,0},{5,1},{8,4},{9,5},{12,8},{13,9},{14,12},{15,13},{10,14},{11,... | collective-permute-start | bytes 1179656 | tf_op jit(solution)/shard_map/ppermute | solution.py:282
  56.1 19.2 %collective-permute-start.10 = (bf16[96,2176]{1,0:T(8,128)(2,1)}, bf16[96,2176]{1,0:T(8,128)(2,1)S(1)}, u32[]{:S(2)}, u32[]{:S(2)}) collective-permute-start(bf16[96,2176]{1,0:T(8,128)(2,1)} %copy-done.23), channel_id=1, source_target_pairs={{0,4},{1,5},{4,8},{5,9},{8,12},{9,13},{12,14},{13,15},{14,10},{15,... | collective-permute-start | bytes 1253384 | tf_op jit(solution)/shard_map/ppermute | solution.py:282
  56.6 19.2 %collective-permute-start.11 = (bf16[96,2176]{1,0:T(8,128)(2,1)}, bf16[96,2176]{1,0:T(8,128)(2,1)S(1)}, u32[]{:S(2)}, u32[]{:S(2)}) collective-permute-start(bf16[96,2176]{1,0:T(8,128)(2,1)} %copy-done.22), channel_id=1, source_target_pairs={{4,0},{5,1},{8,4},{9,5},{12,8},{13,9},{14,12},{15,13},{10,14},{11,... | collective-permute-start | bytes 1253384 | tf_op jit(solution)/shard_map/ppermute | solution.py:282
  66.3 28.7 %copy-start.33 = (bf16[96,2048]{1,0:T(8,128)(2,1)}, bf16[96,2048]{1,0:T(8,128)(2,1)S(1)}, u32[]{:S(2)}) copy-start(bf16[96,2048]{1,0:T(8,128)(2,1)S(1)} %collective-permute-done.12.refs_6_) | copy-start | bytes 1179652
  66.3 26.5 %collective-permute-start.18 = (bf16[96,2048]{1,0:T(8,128)(2,1)S(1)}, bf16[96,2048]{1,0:T(8,128)(2,1)S(1)}, u32[]{:S(2)}, u32[]{:S(2)}) collective-permute-start(bf16[96,2048]{1,0:T(8,128)(2,1)S(1)} %get-tuple-element.282.refs_5_), channel_id=1, source_target_pairs={{4,0},{5,1},{8,4},{9,5},{12,8},{13,9},{14,12},{15,13},{10,14},{11,... | collective-permute-start | bytes 1179656 | tf_op jit(solution)/shard_map/ppermute | solution.py:282
  67.9 24.9 %copy-start.34 = (bf16[96,2048]{1,0:T(8,128)(2,1)}, bf16[96,2048]{1,0:T(8,128)(2,1)S(1)}, u32[]{:S(2)}) copy-start(bf16[96,2048]{1,0:T(8,128)(2,1)S(1)} %collective-permute-done.13.refs_7_) | copy-start | bytes 1179652
  67.9 25.0 %collective-permute-start.17 = (bf16[96,2048]{1,0:T(8,128)(2,1)S(1)}, bf16[96,2048]{1,0:T(8,128)(2,1)S(1)}, u32[]{:S(2)}, u32[]{:S(2)}) collective-permute-start(bf16[96,2048]{1,0:T(8,128)(2,1)S(1)} %get-tuple-element.282.refs_5_), channel_id=1, source_target_pairs={{0,4},{1,5},{4,8},{5,9},{8,12},{9,13},{12,14},{13,15},{14,10},{15,... | collective-permute-start | bytes 1179656 | tf_op jit(solution)/shard_map/ppermute | solution.py:282
  75.3 17.6 %copy-start.24 = (bf16[96,2176]{1,0:T(8,128)(2,1)}, bf16[96,2176]{1,0:T(8,128)(2,1)S(1)}, u32[]{:S(2)}) copy-start(bf16[96,2176]{1,0:T(8,128)(2,1)S(1)} %collective-permute-done.10.refs_0_.refs_3_) | copy-start | bytes 1253380
  75.8 17.1 %copy-start.25 = (bf16[96,2176]{1,0:T(8,128)(2,1)}, bf16[96,2176]{1,0:T(8,128)(2,1)S(1)}, u32[]{:S(2)}) copy-start(bf16[96,2176]{1,0:T(8,128)(2,1)S(1)} %collective-permute-done.11.refs_1_.refs_4_) | copy-start | bytes 1253380
  75.8 17.1 %collective-permute-start.15 = (bf16[96,2176]{1,0:T(8,128)(2,1)S(1)}, bf16[96,2176]{1,0:T(8,128)(2,1)S(1)}, u32[]{:S(2)}, u32[]{:S(2)}) collective-permute-start(bf16[96,2176]{1,0:T(8,128)(2,1)S(1)} %collective-permute-done.10.refs_0_.refs_3_), channel_id=1, source_target_pairs={{0,4},{1,5},{4,8},{5,9},{8,12},{9,13},{12,14},{13,15},{14,10},{15,... | collective-permute-start | bytes 1253384 | tf_op jit(solution)/shard_map/ppermute | solution.py:282
  77.4 15.6 %collective-permute-start.16 = (bf16[96,2176]{1,0:T(8,128)(2,1)S(1)}, bf16[96,2176]{1,0:T(8,128)(2,1)S(1)}, u32[]{:S(2)}, u32[]{:S(2)}) collective-permute-start(bf16[96,2176]{1,0:T(8,128)(2,1)S(1)} %collective-permute-done.11.refs_1_.refs_4_), channel_id=1, source_target_pairs={{4,0},{5,1},{8,4},{9,5},{12,8},{13,9},{14,12},{15,13},{10,14},{11,... | collective-permute-start | bytes 1253384 | tf_op jit(solution)/shard_map/ppermute | solution.py:282
  92.9 22.1 %copy-start.31 = (bf16[96,2048]{1,0:T(8,128)(2,1)}, bf16[96,2048]{1,0:T(8,128)(2,1)S(1)}, u32[]{:S(2)}) copy-start(bf16[96,2048]{1,0:T(8,128)(2,1)S(1)} %collective-permute-done.18.refs_7_) | copy-start | bytes 1179652
  92.9 22.1 %copy-start.32 = (bf16[96,2048]{1,0:T(8,128)(2,1)}, bf16[96,2048]{1,0:T(8,128)(2,1)S(1)}, u32[]{:S(2)}) copy-start(bf16[96,2048]{1,0:T(8,128)(2,1)S(1)} %collective-permute-done.17.refs_6_) | copy-start | bytes 1179652
  92.9 22.1 %collective-permute-start.21 = (bf16[96,2048]{1,0:T(8,128)(2,1)S(1)}, bf16[96,2048]{1,0:T(8,128)(2,1)S(1)}, u32[]{:S(2)}, u32[]{:S(2)}) collective-permute-start(bf16[96,2048]{1,0:T(8,128)(2,1)S(1)} %collective-permute-done.17.refs_6_), channel_id=1, source_target_pairs={{0,4},{1,5},{4,8},{5,9},{8,12},{9,13},{12,14},{13,15},{14,10},{15,... | collective-permute-start | bytes 1179656 | tf_op jit(solution)/shard_map/ppermute | solution.py:282
  94.6 20.5 %collective-permute-start.22 = (bf16[96,2048]{1,0:T(8,128)(2,1)S(1)}, bf16[96,2048]{1,0:T(8,128)(2,1)S(1)}, u32[]{:S(2)}, u32[]{:S(2)}) collective-permute-start(bf16[96,2048]{1,0:T(8,128)(2,1)S(1)} %collective-permute-done.18.refs_7_), channel_id=1, source_target_pairs={{4,0},{5,1},{8,4},{9,5},{12,8},{13,9},{14,12},{15,13},{10,14},{11,... | collective-permute-start | bytes 1179656 | tf_op jit(solution)/shard_map/ppermute | solution.py:282
  95.0 20.0 %collective-permute-start.20 = (bf16[96,2048]{1,0:T(8,128)(2,1)S(1)}, bf16[96,2048]{1,0:T(8,128)(2,1)S(1)}, u32[]{:S(2)}, u32[]{:S(2)}) collective-permute-start(bf16[96,2048]{1,0:T(8,128)(2,1)S(1)} %collective-permute-done.12.refs_6_), channel_id=1, source_target_pairs={{0,4},{1,5},{4,8},{5,9},{8,12},{9,13},{12,14},{13,15},{14,10},{15,... | collective-permute-start | bytes 1179656 | tf_op jit(solution)/shard_map/ppermute | solution.py:282
  96.6 18.5 %collective-permute-start.19 = (bf16[96,2176]{1,0:T(8,128)(2,1)S(1)}, bf16[96,2176]{1,0:T(8,128)(2,1)S(1)}, u32[]{:S(2)}, u32[]{:S(2)}) collective-permute-start(bf16[96,2176]{1,0:T(8,128)(2,1)S(1)} %collective-permute-done.16.refs_3_.refs_1_), channel_id=1, source_target_pairs={{4,0},{5,1},{8,4},{9,5},{12,8},{13,9},{14,12},{15,13},{10,14},{11,... | collective-permute-start | bytes 1253384 | tf_op jit(solution)/shard_map/ppermute | solution.py:282
  115.1 13.9 %collective-permute-start.23 = (bf16[96,2048]{1,0:T(8,128)(2,1)S(1)}, bf16[96,2048]{1,0:T(8,128)(2,1)S(1)}, u32[]{:S(2)}, u32[]{:S(2)}) collective-permute-start(bf16[96,2048]{1,0:T(8,128)(2,1)S(1)} %collective-permute-done.21.refs_8_), channel_id=1, source_target_pairs={{0,4},{1,5},{4,8},{5,9},{8,12},{9,13},{12,14},{13,15},{14,10},{15,... | collective-permute-start | bytes 1179656 | tf_op jit(solution)/shard_map/ppermute | solution.py:282
  116.7 12.3 %collective-permute-start.24 = (bf16[96,2048]{1,0:T(8,128)(2,1)S(1)}, bf16[96,2048]{1,0:T(8,128)(2,1)S(1)}, u32[]{:S(2)}, u32[]{:S(2)}) collective-permute-start(bf16[96,2048]{1,0:T(8,128)(2,1)S(1)} %collective-permute-done.22.refs_9_), channel_id=1, source_target_pairs={{4,0},{5,1},{8,4},{9,5},{12,8},{13,9},{14,12},{15,13},{10,14},{11,... | collective-permute-start | bytes 1179656 | tf_op jit(solution)/shard_map/ppermute | solution.py:282
  128.9 15.0 %copy-start.17 = (bf16[96,2048]{1,0:T(8,128)(2,1)S(1)}, bf16[96,2048]{1,0:T(8,128)(2,1)}, u32[]{:S(2)}) copy-start(bf16[96,2048]{1,0:T(8,128)(2,1)} %get-tuple-element.322) | copy-start | bytes 1179652
  128.9 16.7 %copy-start.35 = (bf16[96,2048]{1,0:T(8,128)(2,1)S(1)}, bf16[96,2048]{1,0:T(8,128)(2,1)}, u32[]{:S(2)}) copy-start(bf16[96,2048]{1,0:T(8,128)(2,1)} %get-tuple-element.321) | copy-start | bytes 1179652
  129.0 14.9 %copy-start.38 = (bf16[96,2048]{1,0:T(8,128)(2,1)}, bf16[96,2048]{1,0:T(8,128)(2,1)S(1)}, u32[]{:S(2)}) copy-start(bf16[96,2048]{1,0:T(8,128)(2,1)S(1)} %collective-permute-done.23.refs_3_) | copy-start | bytes 1179652
  129.0 14.9 %copy-start.39 = (bf16[96,2048]{1,0:T(8,128)(2,1)}, bf16[96,2048]{1,0:T(8,128)(2,1)S(1)}, u32[]{:S(2)}) copy-start(bf16[96,2048]{1,0:T(8,128)(2,1)S(1)} %collective-permute-done.24.refs_4_) | copy-start | bytes 1179652
  129.0 14.9 %collective-permute-start.26 = (bf16[96,2048]{1,0:T(8,128)(2,1)}, bf16[96,2048]{1,0:T(8,128)(2,1)S(1)}, u32[]{:S(2)}, u32[]{:S(2)}) collective-permute-start(bf16[96,2048]{1,0:T(8,128)(2,1)} %shard_map.151), channel_id=1, source_target_pairs={{4,0},{5,1},{8,4},{9,5},{12,8},{13,9},{14,12},{15,13},{10,14},{11,... | collective-permute-start | bytes 1179656 | tf_op jit(solution)/shard_map/ppermute | solution.py:282
  130.6 13.4 %collective-permute-start.25 = (bf16[96,2048]{1,0:T(8,128)(2,1)S(1)}, bf16[96,2048]{1,0:T(8,128)(2,1)S(1)}, u32[]{:S(2)}, u32[]{:S(2)}) collective-permute-start(bf16[96,2048]{1,0:T(8,128)(2,1)S(1)} %collective-permute-done.23.refs_3_), channel_id=1, source_target_pairs={{0,4},{1,5},{4,8},{5,9},{8,12},{9,13},{12,14},{13,15},{14,10},{15,... | collective-permute-start | bytes 1179656 | tf_op jit(solution)/shard_map/ppermute | solution.py:282
  144.1 14.6 %copy-start.15 = (bf16[96,2048]{1,0:T(8,128)(2,1)S(1)}, bf16[96,2048]{1,0:T(8,128)(2,1)}, u32[]{:S(2)}) copy-start(bf16[96,2048]{1,0:T(8,128)(2,1)} %get-tuple-element.334) | copy-start | bytes 1179652
  144.1 12.9 %collective-permute-start.28 = (bf16[96,2048]{1,0:T(8,128)(2,1)S(1)}, bf16[96,2048]{1,0:T(8,128)(2,1)S(1)}, u32[]{:S(2)}, u32[]{:S(2)}) collective-permute-start(bf16[96,2048]{1,0:T(8,128)(2,1)S(1)} %add_convert_fusion.8), channel_id=1, source_target_pairs={{4,0},{5,1},{8,4},{9,5},{12,8},{13,9},{14,12},{15,13},{10,14},{11,... | collective-permute-start | bytes 1179656 | tf_op jit(solution)/shard_map/ppermute | solution.py:282
  145.6 11.3 %collective-permute-start.27 = (bf16[96,2048]{1,0:T(8,128)(2,1)S(1)}, bf16[96,2048]{1,0:T(8,128)(2,1)S(1)}, u32[]{:S(2)}, u32[]{:S(2)}) collective-permute-start(bf16[96,2048]{1,0:T(8,128)(2,1)S(1)} %copy-done.35), channel_id=1, source_target_pairs={{0,4},{1,5},{4,8},{5,9},{8,12},{9,13},{12,14},{13,15},{14,10},{15,... | collective-permute-start | bytes 1179656 | tf_op jit(solution)/shard_map/ppermute | solution.py:282
  157.1 14.2 %collective-permute-start.30 = (bf16[96,2048]{1,0:T(8,128)(2,1)S(1)}, bf16[96,2048]{1,0:T(8,128)(2,1)S(1)}, u32[]{:S(2)}, u32[]{:S(2)}) collective-permute-start(bf16[96,2048]{1,0:T(8,128)(2,1)S(1)} %add_convert_fusion.6), channel_id=1, source_target_pairs={{4,0},{5,1},{8,4},{9,5},{12,8},{13,9},{14,12},{15,13},{10,14},{11,... | collective-permute-start | bytes 1179656 | tf_op jit(solution)/shard_map/ppermute | solution.py:282
  158.8 12.5 %collective-permute-start.29 = (bf16[96,2048]{1,0:T(8,128)(2,1)S(1)}, bf16[96,2048]{1,0:T(8,128)(2,1)S(1)}, u32[]{:S(2)}, u32[]{:S(2)}) collective-permute-start(bf16[96,2048]{1,0:T(8,128)(2,1)S(1)} %add_convert_fusion.7), channel_id=1, source_target_pairs={{0,4},{1,5},{4,8},{5,9},{8,12},{9,13},{12,14},{13,15},{14,10},{15,... | collective-permute-start | bytes 1179656 | tf_op jit(solution)/shard_map/ppermute | solution.py:282
  159.4 10.0 %collective-permute-start.32 = (bf16[48,2048]{1,0:T(8,128)(2,1)S(1)}, bf16[48,2048]{1,0:T(8,128)(2,1)S(1)}, u32[]{:S(2)}, u32[]{:S(2)}) collective-permute-start(bf16[48,2048]{1,0:T(8,128)(2,1)S(1)} %get-tuple-element.404), channel_id=1, source_target_pairs={{4,0},{5,1},{8,4},{9,5},{12,8},{13,9},{14,12},{15,13},{10,14},{11,... | collective-permute-start | bytes 589832 | tf_op jit(solution)/shard_map/ppermute | solution.py:282
  160.9 10.3 %collective-permute-start.31 = (bf16[48,2048]{1,0:T(8,128)(2,1)S(1)}, bf16[48,2048]{1,0:T(8,128)(2,1)S(1)}, u32[]{:S(2)}, u32[]{:S(2)}) collective-permute-start(bf16[48,2048]{1,0:T(8,128)(2,1)S(1)} %get-tuple-element.405), channel_id=1, source_target_pairs={{0,4},{1,5},{4,8},{5,9},{8,12},{9,13},{12,14},{13,15},{14,10},{15,... | collective-permute-start | bytes 589832 | tf_op jit(solution)/shard_map/ppermute | solution.py:282
  171.5 18.1 %copy-start.14 = (bf16[96,2048]{1,0:T(8,128)(2,1)S(1)}, bf16[96,2048]{1,0:T(8,128)(2,1)}, u32[]{:S(2)}) copy-start(bf16[96,2048]{1,0:T(8,128)(2,1)} %get-tuple-element.361) | copy-start | bytes 1179652
  171.6 20.7 %copy-start.13 = (bf16[96,2048]{1,0:T(8,128)(2,1)S(1)}, bf16[96,2048]{1,0:T(8,128)(2,1)}, u32[]{:S(2)}) copy-start(bf16[96,2048]{1,0:T(8,128)(2,1)} %get-tuple-element.359) | copy-start | bytes 1179652
  171.6 8.1 %collective-permute-start.34 = (bf16[96,2048]{1,0:T(8,128)(2,1)S(1)}, bf16[96,2048]{1,0:T(8,128)(2,1)S(1)}, u32[]{:S(2)}, u32[]{:S(2)}) collective-permute-start(bf16[96,2048]{1,0:T(8,128)(2,1)S(1)} %add_convert_fusion.4), channel_id=1, source_target_pairs={{4,0},{5,1},{8,4},{9,5},{12,8},{13,9},{14,12},{15,13},{10,14},{11,... | collective-permute-start | bytes 1179656 | tf_op jit(solution)/shard_map/ppermute | solution.py:282
  173.3 19.2 %copy-start.3 = (bf16[96,2048]{1,0:T(8,128)(2,1)S(1)}, bf16[96,2048]{1,0:T(8,128)(2,1)}, u32[]{:S(2)}) copy-start(bf16[96,2048]{1,0:T(8,128)(2,1)} %get-tuple-element.353) | copy-start | bytes 1179652
  173.4 8.0 %collective-permute-start.33 = (bf16[96,2048]{1,0:T(8,128)(2,1)S(1)}, bf16[96,2048]{1,0:T(8,128)(2,1)S(1)}, u32[]{:S(2)}, u32[]{:S(2)}) collective-permute-start(bf16[96,2048]{1,0:T(8,128)(2,1)S(1)} %add_convert_fusion.5), channel_id=1, source_target_pairs={{0,4},{1,5},{4,8},{5,9},{8,12},{9,13},{12,14},{13,15},{14,10},{15,... | collective-permute-start | bytes 1179656 | tf_op jit(solution)/shard_map/ppermute | solution.py:282
  173.9 13.7 %collective-permute-start.36 = (bf16[96,2048]{1,0:T(8,128)(2,1)S(1)}, bf16[96,2048]{1,0:T(8,128)(2,1)S(1)}, u32[]{:S(2)}, u32[]{:S(2)}) collective-permute-start(bf16[96,2048]{1,0:T(8,128)(2,1)S(1)} %pad_maximum_fusion.1), channel_id=1, source_target_pairs={{4,0},{5,1},{8,4},{9,5},{12,8},{13,9},{14,12},{15,13},{10,14},{11,... | collective-permute-start | bytes 1179656 | tf_op jit(solution)/shard_map/ppermute | solution.py:282
  175.5 14.0 %collective-permute-start.35 = (bf16[96,2048]{1,0:T(8,128)(2,1)S(1)}, bf16[96,2048]{1,0:T(8,128)(2,1)S(1)}, u32[]{:S(2)}, u32[]{:S(2)}) collective-permute-start(bf16[96,2048]{1,0:T(8,128)(2,1)S(1)} %pad_maximum_fusion), channel_id=1, source_target_pairs={{0,4},{1,5},{4,8},{5,9},{8,12},{9,13},{12,14},{13,15},{14,10},{15,... | collective-permute-start | bytes 1179656 | tf_op jit(solution)/shard_map/ppermute | solution.py:282
  189.7 11.2 %collective-permute-start.38 = (bf16[96,2048]{1,0:T(8,128)(2,1)S(1)}, bf16[96,2048]{1,0:T(8,128)(2,1)S(1)}, u32[]{:S(2)}, u32[]{:S(2)}) collective-permute-start(bf16[96,2048]{1,0:T(8,128)(2,1)S(1)} %add_convert_fusion.2), channel_id=1, source_target_pairs={{4,0},{5,1},{8,4},{9,5},{12,8},{13,9},{14,12},{15,13},{10,14},{11,... | collective-permute-start | bytes 1179656 | tf_op jit(solution)/shard_map/ppermute | solution.py:282
  192.4 10.3 %collective-permute-start.37 = (bf16[96,2048]{1,0:T(8,128)(2,1)S(1)}, bf16[96,2048]{1,0:T(8,128)(2,1)S(1)}, u32[]{:S(2)}, u32[]{:S(2)}) collective-permute-start(bf16[96,2048]{1,0:T(8,128)(2,1)S(1)} %add_convert_fusion.3), channel_id=1, source_target_pairs={{0,4},{1,5},{4,8},{5,9},{8,12},{9,13},{12,14},{13,15},{14,10},{15,... | collective-permute-start | bytes 1179656 | tf_op jit(solution)/shard_map/ppermute | solution.py:282
  192.9 19.5 %copy-start.18 = (bf16[96,2048]{1,0:T(8,128)(2,1)S(1)}, bf16[96,2048]{1,0:T(8,128)(2,1)}, u32[]{:S(2)}) copy-start(bf16[96,2048]{1,0:T(8,128)(2,1)} %get-tuple-element.364) | copy-start | bytes 1179652
  202.8 7.8 %collective-permute-start.40 = (bf16[96,2048]{1,0:T(8,128)(2,1)S(1)}, bf16[96,2048]{1,0:T(8,128)(2,1)S(1)}, u32[]{:S(2)}, u32[]{:S(2)}) collective-permute-start(bf16[96,2048]{1,0:T(8,128)(2,1)S(1)} %add_convert_fusion), channel_id=1, source_target_pairs={{4,0},{5,1},{8,4},{9,5},{12,8},{13,9},{14,12},{15,13},{10,14},{11,... | collective-permute-start | bytes 1179656 | tf_op jit(solution)/shard_map/ppermute | solution.py:282
  204.5 7.8 %collective-permute-start.39 = (bf16[96,2048]{1,0:T(8,128)(2,1)S(1)}, bf16[96,2048]{1,0:T(8,128)(2,1)S(1)}, u32[]{:S(2)}, u32[]{:S(2)}) collective-permute-start(bf16[96,2048]{1,0:T(8,128)(2,1)S(1)} %add_convert_fusion.1), channel_id=1, source_target_pairs={{0,4},{1,5},{4,8},{5,9},{8,12},{9,13},{12,14},{13,15},{14,10},{15,... | collective-permute-start | bytes 1179656 | tf_op jit(solution)/shard_map/ppermute | solution.py:282
  (19 other events, 141.3 us)

commit v5 on v4

--- a/solution.py
+++ b/solution.py
@@ -92,25 +92,30 @@
         start += count
 
 
-def weight_stages(weights, targets, sems, tile, with_down):
-    inner = targets[0].shape[2]
-    per = inner // tile
-    stages, used = [], 0
-    for e in range(2):
-        for f in range(per):
-            part = pl.ds(f * tile, tile)
-            views = [(i, (slice(None), part)) for i in range(2)]
-            if with_down:
-                views.append((2, (part, slice(None))))
-            copies = []
-            for i, view in views:
-                source, target = weights[3 * e + i], targets[i].at[e]
-                copies.append(
-                    pltpu.make_async_copy(source.at[view], target.at[view], sems.at[used])
-                )
-                used += 1
-            stages.append(copies)
-    return stages, used
+def in_order(copies):
+    start_all(copies[:2])
+
+    def arrived(i):
+        copies[i].wait()
+        if i + 2 < len(copies):
+            copies[i + 2].start()
+
+    return arrived
+
+
+def matrix_copies(weights, targets, sems):
+    return [
+        pltpu.make_async_copy(weight, target, sems.at[i])
+        for i, (weight, target) in enumerate(zip(weights, targets))
+    ]
+
+
+def dot(first, second):
+    return jnp.dot(first, second, preferred_element_type=jnp.float32)
+
+
+def dot_nt(first, second):
+    return lax.dot_general(first, second, NT, preferred_element_type=jnp.float32)
 
 
 def forward_kernel(parts, experts, width, tile, names_ref, *refs):
@@ -124,70 +129,89 @@
     inner = gate_w.shape[2]
     first_copies = block_copies(rows, held, row_sem)
     first_copies += block_copies(packed, table, table_sem, pl.ds(width, extra))
-    stages, used = weight_stages(weights, (gate_w, up_w, down_w), weight_sem, tile, False)
-    down_copies = [
-        pltpu.make_async_copy(weights[3 * e + 2], down_w.at[e], weight_sem.at[used + e])
-        for e in range(2)
-    ]
-    stages.append(down_copies)
-    start_all(first_copies + stages[0] + stages[1])
+    start_all(first_copies)
+    order = [(0, gate_w, 0), (1, up_w, 0), (3, gate_w, 1), (4, up_w, 1), (2, down_w, 0)]
+    order += [(5, down_w, 1)]
+    arrived = in_order(
+        matrix_copies(
+            [weights[i] for i, _, _ in order], [ref.at[e] for _, ref, e in order], weight_sem
+        )
+    )
     wait_all(first_copies)
-    per = inner // tile
-    for stage in range(2 * per):
-        e, f = divmod(stage, per)
-        wait_all(stages[stage])
-        if stage + 2 < len(stages):
-            start_all(stages[stage + 2])
-        columns = pl.ds(f * tile, tile)
+    for e in range(2):
         gate = gate_column(table[...].astype(jnp.float32), 0, experts, names_ref[e])
-        first = jnp.dot(held[...], gate_w[e, :, columns], preferred_element_type=jnp.float32)
-        second = jnp.dot(held[...], up_w[e, :, columns], preferred_element_type=jnp.float32)
+        arrived(2 * e)
+        first = dot(held[...], gate_w[e])
+        arrived(2 * e + 1)
+        second = dot(held[...], up_w[e])
         made = gate * (jax.nn.silu(first) * second)
-        hidden[:, pl.ds(stage * tile, tile)] = made.astype(jnp.bfloat16)
-    wait_all(down_copies)
+        hidden[:, pl.ds(e * inner, inner)] = made.astype(jnp.bfloat16)
+    arrived(4)
+    arrived(5)
 
     @pl.loop(0, width // tile)
     def _(n):
         columns = pl.ds(pl.multiple_of(n * tile, tile), tile)
-        total = jnp.dot(
-            hidden[:, :inner], down_w[0, :, columns], preferred_element_type=jnp.float32
-        ) + jnp.dot(hidden[:, inner:], down_w[1, :, columns], preferred_element_type=jnp.float32)
+        total = dot(hidden[:, :inner], down_w[0, :, columns])
+        total = total + dot(hidden[:, inner:], down_w[1, :, columns])
         write_tiles(total, outs, columns)
 
 
-def backward_kernel(parts, experts, width, tile, names_ref, *refs):
-    packed, rows = refs[:parts], refs[parts : 2 * parts]
-    weights = refs[2 * parts : 2 * parts + 6]
-    outs = refs[2 * parts + 6 : 3 * parts + 6]
-    (cot, held, slot, grads, gate_w, up_w, down_w, cot_sem, row_sem, weight_sem) = refs[
-        3 * parts + 6 :
+def factor_kernel(parts, *refs):
+    rows, weights, out = refs[:parts], refs[parts : parts + 4], refs[parts + 4]
+    held, gate_w, up_w, row_sem, weight_sem = refs[parts + 5 :]
+    first_copies = block_copies(rows, held, row_sem)
+    start_all(first_copies)
+    targets = [gate_w.at[0], up_w.at[0], gate_w.at[1], up_w.at[1]]
+    arrived = in_order(matrix_copies(weights, targets, weight_sem))
+    wait_all(first_copies)
+    for e in range(2):
+        arrived(2 * e)
+        first = dot(held[...], gate_w[e])
+        arrived(2 * e + 1)
+        second = dot(held[...], up_w[e])
+        sigmoid_part = jax.nn.sigmoid(first)
+        out[2 * e] = (
+            second * sigmoid_part * (1.0 + first * (1.0 - sigmoid_part))
+        ).astype(jnp.bfloat16)
+        out[2 * e + 1] = (first * sigmoid_part).astype(jnp.bfloat16)
+
+
+def backward_kernel(parts, experts, width, tile, start, names_ref, *refs):
+    packed, factors = refs[:parts], refs[parts]
+    weights = refs[parts + 1 : parts + 7]
+    outs = refs[parts + 7 : 2 * parts + 7]
+    (cot, slot, grads, gate_w, up_w, down_w, cot_sem, factor_sem, weight_sem) = refs[
+        2 * parts + 7 :
     ]
-    inner = gate_w.shape[2]
-    first_copies = block_copies(rows, held, row_sem) + block_copies(packed, cot, cot_sem)
-    stages, _ = weight_stages(weights, (gate_w, up_w, down_w), weight_sem, tile, True)
-    start_all(first_copies + stages[0] + stages[1])
+    total_rows = slot.shape[0]
+    first_copies = block_copies(packed, cot, cot_sem)
+    start_all(first_copies)
+    order = [(2, down_w, 0), (5, down_w, 1), (0, gate_w, 0), (1, up_w, 0), (3, gate_w, 1)]
+    order += [(4, up_w, 1)]
+    arrived = in_order(
+        matrix_copies(
+            [weights[i] for i, _, _ in order], [ref.at[e] for _, ref, e in order], weight_sem
+        )
+    )
+    factor_copy = pltpu.make_async_copy(
+        factors.at[:, pl.ds(start, total_rows)], grads, factor_sem
+    )
+    factor_copy.start()
     wait_all(first_copies)
-    per = inner // tile
-    for stage in range(2 * per):
-        e, f = divmod(stage, per)
-        if f == 0:
-            table = cot[:, width:].astype(jnp.float32)
-            gate = gate_column(table, 1, experts, names_ref[e])
-            slot[...] = (gate * cot[:, :width].astype(jnp.float32)).astype(jnp.bfloat16)
-        wait_all(stages[stage])
-        if stage + 2 < len(stages):
-            start_all(stages[stage + 2])
-        columns = pl.ds(f * tile, tile)
-        first = jnp.dot(held[...], gate_w[e, :, columns], preferred_element_type=jnp.float32)
-        second = jnp.dot(held[...], up_w[e, :, columns], preferred_element_type=jnp.float32)
-        back = lax.dot_general(
-            slot[...], down_w[e, columns, :], NT, preferred_element_type=jnp.float32
-        )
-        sigmoid_part = jax.nn.sigmoid(first)
-        gate_grad = back * second * sigmoid_part * (1.0 + first * (1.0 - sigmoid_part))
-        second_grad = back * (first * sigmoid_part)
-        grads[2 * e, :, columns] = gate_grad.astype(jnp.bfloat16)
-        grads[2 * e + 1, :, columns] = second_grad.astype(jnp.bfloat16)
+    for e in range(2):
+        table = cot[:, width:].astype(jnp.float32)
+        gate = gate_column(table, 1, experts, names_ref[e])
+        slot[...] = (gate * cot[:, :width].astype(jnp.float32)).astype(jnp.bfloat16)
+        arrived(e)
+        back = dot_nt(slot[...], down_w[e])
+        if e == 0:
+            factor_copy.wait()
+        for i in range(2):
+            made = back * grads[2 * e + i].astype(jnp.float32)
+            grads[2 * e + i] = made.astype(jnp.bfloat16)
+    for i in range(2, 6):
+        arrived(i)
 
     @pl.loop(0, width // tile)
     def _(n):
@@ -195,58 +219,92 @@
         total = None
         for e in range(2):
             for i, weight in enumerate((gate_w, up_w)):
-                term = lax.dot_general(
-                    grads[2 * e + i], weight[e, columns, :], NT, preferred_element_type=jnp.float32
-                )
+                term = dot_nt(grads[2 * e + i], weight[e, columns, :])
                 total = term if total is None else total + term
         write_tiles(total, outs, columns)
 
 
-def expert_call(kind, names, packed, rows, weights, experts):
+HBM = pl.BlockSpec(memory_space=pl.ANY)
+TILE = 512
+
+
+def weight_scratch(width, inner, with_down=True):
+    shapes = [(2, width, inner), (2, width, inner), (2, inner, width)]
+    return [pltpu.VMEM(shape, jnp.bfloat16) for shape in shapes[: 3 if with_down else 2]]
+
+
+def cost(units, rows, width, inner, fixed):
+    return pl.CostEstimate(
+        flops=2 * units * rows * width * inner + int(fixed * 1.1e15),
+        bytes_accessed=12 * width * inner,
+        transcendentals=2 * rows * inner,
+    )
+
+
+PARAMS = pltpu.CompilerParams(vmem_limit_bytes=VMEM_LIMIT)
+
+
+def forward_call(names, packed, rows, weights, experts):
     parts = len(rows)
     counts = [block.shape[0] for block in rows]
-    total = sum(counts)
-    width = rows[0].shape[1]
-    full = packed[0].shape[1]
-    inner = weights[0].shape[1]
-    tile = 256
-    hbm = pl.BlockSpec(memory_space=pl.ANY)
-    weight_scratch = [
-        pltpu.VMEM((2, width, inner), jnp.bfloat16),
-        pltpu.VMEM((2, width, inner), jnp.bfloat16),
-        pltpu.VMEM((2, inner, width), jnp.bfloat16),
-    ]
-    sems = [pltpu.SemaphoreType.DMA((parts,)), pltpu.SemaphoreType.DMA((parts,))]
-    sems += [pltpu.SemaphoreType.DMA((6 * (inner // tile),))]
-    if kind == "forward":
-        body = forward_kernel
-        scratch = [
+    total, width = sum(counts), rows[0].shape[1]
+    full, inner = packed[0].shape[1], weights[0].shape[1]
+    out = pl.pallas_call(
+        functools.partial(forward_kernel, parts, experts, width, TILE),
+        out_shape=[jax.ShapeDtypeStruct((count, width), jnp.bfloat16) for count in counts],
+        in_specs=[pl.BlockSpec(memory_space=pltpu.SMEM)] + [HBM] * (2 * parts + 6),
+        scratch_shapes=[
             pltpu.VMEM((total, full - width), jnp.bfloat16),
             pltpu.VMEM((total, width), jnp.bfloat16),
             pltpu.VMEM((total, 2 * inner), jnp.bfloat16),
         ]
-        products, fixed = 6, 8.5e-6
-    else:
-        body = backward_kernel
-        scratch = [
+        + weight_scratch(width, inner)
+        + [pltpu.SemaphoreType.DMA((count,)) for count in (parts, parts, 6)],
+        compiler_params=PARAMS,
+        cost_estimate=cost(6, total, width, inner, 6e-6),
+    )(names, *packed, *rows, *weights)
+    return list(out)
+
+
+def factor_call(rows, weights):
+    parts = len(rows)
+    total, width = sum(block.shape[0] for block in rows), rows[0].shape[1]
+    inner = weights[0].shape[1]
+    return pl.pallas_call(
+        functools.partial(factor_kernel, parts),
+        out_shape=jax.ShapeDtypeStruct((4, total, inner), jnp.bfloat16),
+        in_specs=[HBM] * (parts + 4),
+        scratch_shapes=[pltpu.VMEM((total, width), jnp.bfloat16)]
+        + weight_scratch(width, inner, False)
+        + [pltpu.SemaphoreType.DMA((count,)) for count in (parts, 4)],
+        compiler_params=PARAMS,
+        cost_estimate=cost(4, total, width, inner, 5e-6),
+    )(*rows, weights[0], weights[1], weights[3], weights[4])
+
+
+def backward_call(names, packed, factors, start, weights, experts):
+    parts = len(packed)
+    counts = [block.shape[0] for block in packed]
+    total, full = sum(counts), packed[0].shape[1]
+    width, inner = weights[0].shape
+    out = pl.pallas_call(
+        functools.partial(backward_kernel, parts, experts, width, TILE, start),
+        out_shape=[jax.ShapeDtypeStruct((count, width), jnp.bfloat16) for count in counts],
+        in_specs=[pl.BlockSpec(memory_space=pltpu.SMEM)] + [HBM] * (parts + 7),
+        scratch_shapes=[
             pltpu.VMEM((total, full), jnp.bfloat16),
-            pltpu.VMEM((total, width), jnp.bfloat16),
             pltpu.VMEM((total, width), jnp.bfloat16),
             pltpu.VMEM((4, total, inner), jnp.bfloat16),
         ]
-        products, fixed = 10, 11e-6
-    out = pl.pallas_call(
-        functools.partial(body, parts, experts, width, tile),
-        out_shape=[jax.ShapeDtypeStruct((count, width), jnp.bfloat16) for count in counts],
-        in_specs=[pl.BlockSpec(memory_space=pltpu.SMEM)] + [hbm] * (2 * parts + 6),
-        scratch_shapes=scratch + weight_scratch + sems,
-        compiler_params=pltpu.CompilerParams(vmem_limit_bytes=VMEM_LIMIT),
-        cost_estimate=pl.CostEstimate(
-            flops=2 * products * total * width * inner + int(fixed * 1.1e15),
-            bytes_accessed=12 * width * inner,
-            transcendentals=2 * total * inner,
-        ),
-    )(names, *packed, *rows, *weights)
+        + weight_scratch(width, inner)
+        + [
+            pltpu.SemaphoreType.DMA((parts,)),
+            pltpu.SemaphoreType.DMA(()),
+            pltpu.SemaphoreType.DMA((6,)),
+        ],
+        compiler_params=PARAMS,
+        cost_estimate=cost(6, total, width, inner, 6e-6),
+    )(names, *packed, factors, *weights)
     return list(out)
 
 
@@ -276,7 +334,8 @@
         pairs = [(2 * a + core, 2 * b + core) for a, b in following.items() for core in range(2)]
         self.routes = (pairs, [(b, a) for a, b in pairs])
         self.swap = [(i, i ^ 1) for i in range(sources)]
-        self.held, self.made, self.sums, self.weights = {}, {}, {}, None
+        self.held, self.made, self.sums, self.starts = {}, {}, {}, {}
+        self.weights = None
 
     def pass_on(self, block, way):
         return lax.ppermute(block, "ep", self.routes[way])
@@ -292,14 +351,28 @@
             behind, ahead = behind[:half], ahead[half:]
         held[distance] = [self.pass_on(behind, 0), self.pass_on(ahead, 1)]
 
+    def prepare(self, distances):
+        blocks = [block for d in distances for block in self.held["fall"][d]]
+        factors, start = factor_call(blocks, self.weights), 0
+        for d in distances:
+            self.held[f"factors{d}"] = {0: [factors]}
+            self.starts[d] = start
+            start += sum(block.shape[0] for block in self.held["fall"][d])
+
     def work(self, kind, distances):
-        rows = self.held["fall" if kind == "backward" else "rise"]
         packed = [block for d in distances for block in self.held["cot"][d]]
-        blocks = [block for d in distances for block in rows[d]]
-        outs = expert_call(kind, self.names, packed, blocks, self.weights, self.sources)
+        if kind == "backward":
+            factors = self.held[f"factors{distances[0]}"][0][0]
+            start = self.starts[distances[0]]
+            outs = backward_call(
+                self.names, packed, factors, start, self.weights, self.sources
+            )
+        else:
+            blocks = [block for d in distances for block in self.held["rise"][d]]
+            outs = forward_call(self.names, packed, blocks, self.weights, self.sources)
         made = self.made.setdefault(kind, {})
         for d in distances:
-            count = len(rows[d])
+            count = len(self.held["cot"][d])
             made[d], outs = outs[:count], outs[count:]
 
     def scatter(self, kind, step, way=None):
@@ -363,7 +436,6 @@
     ring.held["fall"] = {0: [fall_normal]}
     ring.gather("fall", 1)
     moved_cot = passed_along(leaving_cot, "pipe", 1)
-    moved_rise = passed_along(leaving_rise, "pipe", 1)
     own = (w_gate[0, 0], w_up[0, 0], w_down[0, 0])
 
     def swapped(weight):
@@ -371,7 +443,11 @@
 
     at_start = section_index == 0
     cot_in = jnp.where(at_start, entering[1], moved_cot)
-    rise_in = jnp.where(at_start, entering[0], moved_rise)
+
+    def entered(leaving_rise):
+        moved_rise = passed_along(leaving_rise, "pipe", 1)
+        return jnp.where(at_start, entering[0], moved_rise)
+
     ring.held["cot"] = {0: [packed_rows(cot_in, route_ids[:, 0], route_gates[:, 0], sources)]}
     ring.held["rise"] = {}
 
@@ -392,37 +468,39 @@
         return kept + norm_pullback(fall_wide, norm_row, ring.total("backward"))
 
     if planned:
+        ring.gather("fall", 2)
         own_gate, own_up, own_down = own
-        other_down = swapped(own_down)
-        cot_in, rise_in, own_gate, own_up, other_down = ring.fence(
-            cot_in, rise_in, own_gate, own_up, other_down
-        )
-        heads, ring.names = lax.optimization_barrier(((head_rise, head_fall), names))
-        ring.gather("fall", 2)
-        ring.gather("cot", 1)
         other_gate = swapped(own_gate)
-        rise_normal = normed(rise_in.astype(jnp.float32), norm_row).astype(jnp.bfloat16)
-        rise_normal, own_up, other_gate, heads, ring.names = ring.fence(
-            rise_normal, own_up, other_gate, heads, ring.names
+        heads = (head_rise, head_fall)
+        cot_in, leaving_rise, own_up, own_down, other_gate, heads, ring.names = ring.fence(
+            cot_in, leaving_rise, own_up, own_down, other_gate, heads, names
         )
         ring.gather("fall", 3)
+        ring.gather("cot", 1)
+        rise_in = entered(leaving_rise)
+        rise_in, own_up, own_down = ring.fence(rise_in, own_up, own_down)
+        ring.gather("fall", 4)
         ring.gather("cot", 2)
         other_up = swapped(own_up)
+        rise_normal = normed(rise_in.astype(jnp.float32), norm_row).astype(jnp.bfloat16)
         kept, exit_loss = exit_heads(rise_in, cot_in, *heads)
-        kept, exit_loss, other_up = ring.fence(kept, exit_loss, other_up)
-        ring.weights = own + (other_gate, other_up, other_down)
+        rise_normal, kept, exit_loss, other_up, own_down = ring.fence(
+            rise_normal, kept, exit_loss, other_up, own_down
+        )
         ring.held["rise"] = {0: [rise_normal]}
         ring.gather("cot", 3)
         ring.gather("rise", 1)
-        ring.work("backward", [0, 1])
-        ring.fence()
-        ring.gather("fall", 4, 0)
+        other_down = swapped(own_down)
+        ring.weights = own + (other_gate, other_up, other_down)
+        ring.prepare([0, 1, 2, 3, 4])
+        (other_down,) = ring.fence(other_down)
+        ring.weights = own + (other_gate, other_up, other_down)
         ring.gather("cot", 4, 1)
         ring.gather("rise", 2)
-        ring.work("backward", [2, 3])
+        ring.work("backward", [0, 1, 2])
         ring.fence()
         ring.gather("rise", 3)
-        ring.work("backward", [4])
+        ring.work("backward", [3, 4])
         ring.fence()
         ring.gather("rise", 4, 0)
         ring.scatter("backward", 1, 1)
@@ -442,6 +520,7 @@
         (fall_total,) = ring.fence(fall_total)
         ring.scatter("forward", 4)
     else:
+        rise_in = entered(leaving_rise)
         ring.weights = own + tuple(swapped(own))
         kept, exit_loss = exit_heads(rise_in, cot_in, head_rise, head_fall)
         rise_normal = normed(rise_in.astype(jnp.float32), norm_row).astype(jnp.bfloat16)
@@ -449,10 +528,13 @@
         for name in ("fall", "cot", "rise"):
             for distance in range(1 if name != "fall" else 2, far + 1):
                 ring.gather(name, distance)
+        groups = [[0, 1]] + [[distance] for distance in range(2, far + 1)]
+        for group in groups:
+            ring.prepare(group)
+            ring.work("backward", group)
+        for group in groups:
+            ring.work("forward", group)
         for kind in ("backward", "forward"):
-            ring.work(kind, [0, 1])
-            for distance in range(2, far + 1):
-                ring.work(kind, [distance])
             for step in range(1, far + 1):
                 ring.scatter(kind, step)
         fall_total = falling(kept).astype(jnp.bfloat16)

time: 214 us -> 208 us (0.972)
  Pallas kernels: 68.9 us -> 61.6 us
    ppermute x2, waiting for transfers between devices: 12.7 us -> 3.53 us  [passed_along(): return lax.ppermute(block, axis, route)]
    ppermute x36 -> x37, waiting for transfers between devices: 70.8 us -> 78.5 us  [pass_on(): return lax.ppermute(block, 'ep', self.routes[way])]
    pallas_call x5, Pallas kernels: 68.2 us -> 60.9 us  [the longest x2 26.7 us: backward_call(): pl.pallas_call(functools.partial(backward_kernel, parts, experts, width,...]
    ppermute x36 -> x37, starting transfers between devices: 37.9 us -> 38.7 us  [pass_on(): return lax.ppermute(block, 'ep', self.routes[way])]
  transfers between devices with their start and end apart: 41 -> 42, of which waited for: 16 -> 21; matrix products, arithmetic and copies ran while one was open for 5% -> 6% of each run, Pallas kernels for 32% -> 30%
where the time goes in v5:
time: 208 us; the launch traced here: 207 us
  waiting for transfers between devices  82.1 us (39%)
  Pallas kernels  61.6 us (30%)
  starting transfers between devices  46.6 us (22%)
  other arithmetic  9.37 us (5%)
  local copies, waits for them, and re-layouts  5.07 us (2%)
  between operations  2.7 us (1%)
    ppermute x37, waiting for transfers between devices, pass_on(): return lax.ppermute(block, 'ep', self.routes[way])  78.5 us
    ppermute x37, starting transfers between devices, pass_on(): return lax.ppermute(block, 'ep', self.routes[way])  38.7 us
    pallas_call x2, Pallas kernels, backward_call(): pl.pallas_call(functools.partial(backward_kernel, parts, experts, width,...  26.7 us
    pallas_call x2, Pallas kernels, forward_call(): pl.pallas_call(functools.partial(forward_kernel, parts, experts, width, T...  22.3 us
    pallas_call x1, Pallas kernels, factor_call(): pl.pallas_call(functools.partial(factor_kernel, parts), out_shape=jax.Sha...  11.9 us
    ppermute x2, starting transfers between devices, passed_along(): return lax.ppermute(block, axis, route)  7.21 us
  transfers between devices with their start and end apart: 42, of which 21 were waited for; matrix products, arithmetic and copies ran while one was open for 6% of the time, Pallas kernels for 30%

profile of v5, /device:TPU:0, one launch (start us, length us, event | category | flops | bytes accessed | tf_op | source)
XLA Modules:
  0.0 207.4 jit_solution(4348190881443436410)
XLA Ops:
  1.2 1.2 fusion.16
  2.3 1.2 fusion.4.refs_0_
  3.5 2.6 %collective-permute-start.2 = (bf16[96,2048]{1,0:T(8,128)(2,1)S(1)}, bf16[96,2048]{1,0:T(8,128)(2,1)}, u32[]{:S(2)}, u32[]{:S(2)}) collective-permute-start(bf16[96,2048]{1,0:T(8,128)(2,1)S(1)} %fusion.4.refs_0_), channel_id=1, source_target_pairs={{4,0},{5,1},{8,4},{9,5},{12,8},{13,9},{14,12},{15,13},{10,14},{11,... | collective-permute-start | bytes 1179656 | tf_op jit(solution)/shard_map/ppermute | solution.py:341
  6.3 3.8 %collective-permute-start = (bf16[96,2048]{1,0:T(8,128)(2,1)}, bf16[96,2048]{1,0:T(8,128)(2,1)S(1)}, u32[]{:S(2)}, u32[]{:S(2)}) collective-permute-start(bf16[96,2048]{1,0:T(8,128)(2,1)} %bitcast.69), channel_id=1, source_target_pairs={{0,16},{1,17},{2,18},{3,19},{4,20},{5,21},{6,22},{7,23},{8,24},{9,... | collective-permute-start | bytes 1179656 | tf_op jit(solution)/shard_map/ppermute | solution.py:17
  10.1 0.8 fusion.22
  10.9 0.6 constant_dynamic-slice_fusion
  12.7 0.8 copy.16
  13.5 0.8 copy.17
  14.3 0.7 pad_add_fusion.names_ref
  15.0 1.1 collective-permute-done.2.refs_2_
  16.1 1.7 collective-permute-start.4
  18.1 0.7 collective-permute-done
  18.8 1.0 bitcast_select_fusion.1.rows_ref
  19.8 0.7 shard_map.148.refs_0_
  20.6 6.6 %collective-permute-done.4.refs_4_ = bf16[96,2048]{1,0:T(8,128)(2,1)S(1)} collective-permute-done((bf16[96,2048]{1,0:T(8,128)(2,1)}, bf16[96,2048]{1,0:T(8,128)(2,1)S(1)}, u32[]{:S(2)}, u32[]{:S(2)}) %collective-permute-start.4) | collective-permute-done | bytes 393248 | tf_op jit(solution)/shard_map/ppermute | solution.py:341
  27.1 1.2 collective-permute-done.3.refs_3_
  28.3 3.4 %collective-permute-start.10 = (bf16[96,2048]{1,0:T(8,128)(2,1)S(1)}, bf16[96,2048]{1,0:T(8,128)(2,1)S(1)}, u32[]{:S(2)}, u32[]{:S(2)}) collective-permute-start(bf16[96,2048]{1,0:T(8,128)(2,1)S(1)} %bitcast.70), channel_id=1, source_target_pairs={{0,16},{1,17},{2,18},{3,19},{4,20},{5,21},{6,22},{7,23},{8,24},{9,... | collective-permute-start | bytes 1179656 | tf_op jit(solution)/shard_map/ppermute | solution.py:17
  31.8 1.6 collective-permute-start.7
  34.4 1.5 collective-permute-start.9
  35.9 2.8 %collective-permute-done.10 = bf16[96,2048]{1,0:T(8,128)(2,1)S(1)} collective-permute-done((bf16[96,2048]{1,0:T(8,128)(2,1)S(1)}, bf16[96,2048]{1,0:T(8,128)(2,1)S(1)}, u32[]{:S(2)}, u32[]{:S(2)}) %collective-permute-start.10) | collective-permute-done | bytes 393248 | tf_op jit(solution)/shard_map/ppermute | solution.py:17
  38.8 12.6 %collective-permute-done.8.refs_5_ = bf16[96,2048]{1,0:T(8,128)(2,1)} collective-permute-done((bf16[96,2048]{1,0:T(8,128)(2,1)S(1)}, bf16[96,2048]{1,0:T(8,128)(2,1)}, u32[]{:S(2)}, u32[]{:S(2)}) %collective-permute-start.8) | collective-permute-done | bytes 393248 | tf_op jit(solution)/shard_map/ppermute | solution.py:341
  51.5 0.9 slice.46
  52.4 0.9 slice.47
  53.4 1.6 collective-permute-start.14
  55.9 1.6 collective-permute-start.12
  57.7 0.6 multiply_reduce_fusion
  58.8 0.6 maximum_bitcast_fusion
  59.4 1.7 collective-permute-done.14.refs_8_
  61.1 1.6 collective-permute-done.13.refs_7_
  62.8 8.2 %collective-permute-done.11.refs_3_ = bf16[96,2176]{1,0:T(8,128)(2,1)S(1)} collective-permute-done((bf16[96,2176]{1,0:T(8,128)(2,1)}, bf16[96,2176]{1,0:T(8,128)(2,1)S(1)}, u32[]{:S(2)}, u32[]{:S(2)}) %collective-permute-start.11) | collective-permute-done | bytes 417824 | tf_op jit(solution)/shard_map/ppermute | solution.py:341
  71.1 1.6 collective-permute-start.19
  73.6 1.6 collective-permute-start.17
  75.2 11.9 %shard_map.149.refs_5_.refs_3_ = bf16[4,768,512]{2,1,0:T(8,128)(2,1)} custom-call(bf16[96,2048]{1,0:T(8,128)(2,1)} %copy-done.9, bf16[96,2048]{1,0:T(8,128)(2,1)} %collective-permute-done.1.refs_1_, bf16[96,2048]{1,0:T(8,128)(2,1)} %collective-permute-done.2.refs_2_, bf16[96,2048]{1,0:T(8,128)(2,1)} %copy-done.30, bf16[96,2048]{1,0:T(8,128)(2,1)} %copy-done.29, ...), custom_call_target="tpu_custom_call" | custom-call | flops 11942451200 | bytes 12582912 | tf_op jit(solution)/shard_map/pallas_call | solution.py:273
  87.2 5.6 %collective-permute-done.16.refs_0_ = bf16[96,2176]{1,0:T(8,128)(2,1)S(1)} collective-permute-done((bf16[96,2176]{1,0:T(8,128)(2,1)S(1)}, bf16[96,2176]{1,0:T(8,128)(2,1)S(1)}, u32[]{:S(2)}, u32[]{:S(2)}) %collective-permute-start.16) | collective-permute-done | bytes 417824 | tf_op jit(solution)/shard_map/ppermute | solution.py:341
  93.4 1.6 collective-permute-start.23
  94.9 0.6 collective-permute-start.21
  95.5 14.8 %shard_map.150 = (bf16[96,2048]{1,0:T(8,128)(2,1)}, bf16[96,2048]{1,0:T(8,128)(2,1)}, bf16[96,2048]{1,0:T(8,128)(2,1)}, bf16[96,2048]{1,0:T(8,128)(2,1)}, bf16[96,2048]{1,0:T(8,128)(2,1)}) custom-call(s32[2]{0:T(128)} %pad_add_fusion.names_ref, bf16[96,2176]{1,0:T(8,128)(2,1)} %copy-done, bf16[96,2176]{1,0:T(8,128)(2,1)} %collective-permute-done.6.refs_1_, ...), custom_call_target="tpu_custom_call" | custom-call | flops 12639797248 | bytes 12582912 | tf_op jit(solution)/shard_map/pallas_call | solution.py:290
  110.4 2.0 collective-permute-done.21.refs_2_
  112.8 1.6 collective-permute-start.25
  114.4 11.9 %shard_map.151 = (bf16[96,2048]{1,0:T(8,128)(2,1)}, bf16[96,2048]{1,0:T(8,128)(2,1)}, bf16[96,2048]{1,0:T(8,128)(2,1)}) custom-call(s32[2]{0:T(128)} %pad_add_fusion.names_ref, bf16[96,2176]{1,0:T(8,128)(2,1)} %copy-done.25, bf16[96,2176]{1,0:T(8,128)(2,1)} %copy-done.26, bf16[96,2176]{1,0:T(8,128)(2,1)} %copy-done.27, ...), custom_call_target="tpu_custom_call" | custom-call | flops 10223878144 | bytes 12582912 | tf_op jit(solution)/shard_map/pallas_call | solution.py:290
  126.4 1.6 collective-permute-start.27
  128.5 12.3 %shard_map.152 = (bf16[96,2048]{1,0:T(8,128)(2,1)}, bf16[96,2048]{1,0:T(8,128)(2,1)}, bf16[96,2048]{1,0:T(8,128)(2,1)}, bf16[96,2048]{1,0:T(8,128)(2,1)}, bf16[96,2048]{1,0:T(8,128)(2,1)}) custom-call(s32[2]{0:T(128)} %pad_add_fusion.names_ref, bf16[96,2176]{1,0:T(8,128)(2,1)} %copy-done, bf16[96,2176]{1,0:T(8,128)(2,1)} %collective-permute-done.6.refs_1_, ...), custom_call_target="tpu_custom_call" | custom-call | flops 12639797248 | bytes 12582912 | tf_op jit(solution)/shard_map/pallas_call | solution.py:252
  141.0 1.6 collective-permute-start.29
  143.1 9.9 %shard_map.153 = (bf16[96,2048]{1,0:T(8,128)(2,1)}, bf16[96,2048]{1,0:T(8,128)(2,1)}, bf16[96,2048]{1,0:T(8,128)(2,1)}) custom-call(s32[2]{0:T(128)} %pad_add_fusion.names_ref, bf16[96,2176]{1,0:T(8,128)(2,1)} %copy-done.25, bf16[96,2176]{1,0:T(8,128)(2,1)} %copy-done.26, bf16[96,2176]{1,0:T(8,128)(2,1)} %copy-done.27, bf16[96,2048]{1,0:T(8,128)(2,1)} %copy-done.33, ...), custom_call_target="tpu_custom_call" | custom-call | flops 10223878144 | bytes 12582912 | tf_op jit(solution)/shard_map/pallas_call | solution.py:252
  153.2 1.6 collective-permute-start.31
  155.5 1.6 collective-permute-start.33
  157.6 7.7 %collective-permute-done.33 = bf16[48,2048]{1,0:T(8,128)(2,1)S(1)} collective-permute-done((bf16[48,2048]{1,0:T(8,128)(2,1)S(1)}, bf16[48,2048]{1,0:T(8,128)(2,1)S(1)}, u32[]{:S(2)}, u32[]{:S(2)}) %collective-permute-start.33) | collective-permute-done | bytes 196640 | tf_op jit(solution)/shard_map/ppermute | solution.py:341
  165.3 2.4 %collective-permute-done.32 = bf16[48,2048]{1,0:T(8,128)(2,1)S(1)} collective-permute-done((bf16[48,2048]{1,0:T(8,128)(2,1)S(1)}, bf16[48,2048]{1,0:T(8,128)(2,1)S(1)}, u32[]{:S(2)}, u32[]{:S(2)}) %collective-permute-start.32) | collective-permute-done | bytes 196640 | tf_op jit(solution)/shard_map/ppermute | solution.py:341
  168.0 0.6 collective-permute-start.35
  168.7 1.5 collective-permute-start.34
  170.2 0.6 collective-permute-start.37
  170.9 1.5 collective-permute-start.36
  172.4 5.2 %collective-permute-done.35 = bf16[96,2048]{1,0:T(8,128)(2,1)S(1)} collective-permute-done((bf16[96,2048]{1,0:T(8,128)(2,1)S(1)}, bf16[96,2048]{1,0:T(8,128)(2,1)S(1)}, u32[]{:S(2)}, u32[]{:S(2)}) %collective-permute-start.35) | collective-permute-done | bytes 393248 | tf_op jit(solution)/shard_map/ppermute | solution.py:341
  177.6 1.5 collective-permute-done.34
  179.1 4.3 %collective-permute-done.37 = bf16[96,2048]{1,0:T(8,128)(2,1)S(1)} collective-permute-done((bf16[96,2048]{1,0:T(8,128)(2,1)S(1)}, bf16[96,2048]{1,0:T(8,128)(2,1)S(1)}, u32[]{:S(2)}, u32[]{:S(2)}) %collective-permute-start.37) | collective-permute-done | bytes 393248 | tf_op jit(solution)/shard_map/ppermute | solution.py:341
  183.4 2.4 %collective-permute-done.36 = bf16[96,2048]{1,0:T(8,128)(2,1)S(1)} collective-permute-done((bf16[96,2048]{1,0:T(8,128)(2,1)S(1)}, bf16[96,2048]{1,0:T(8,128)(2,1)S(1)}, u32[]{:S(2)}, u32[]{:S(2)}) %collective-permute-start.36) | collective-permute-done | bytes 393248 | tf_op jit(solution)/shard_map/ppermute | solution.py:341
  185.9 0.6 collective-permute-start.39
  186.5 1.6 collective-permute-start.38
  188.5 1.1 fusion.15
  189.6 7.8 %collective-permute-done.39 = bf16[96,2048]{1,0:T(8,128)(2,1)S(1)} collective-permute-done((bf16[96,2048]{1,0:T(8,128)(2,1)S(1)}, bf16[96,2048]{1,0:T(8,128)(2,1)S(1)}, u32[]{:S(2)}, u32[]{:S(2)}) %collective-permute-start.39) | collective-permute-done | bytes 393248 | tf_op jit(solution)/shard_map/ppermute | solution.py:341
  197.4 0.9 collective-permute-done.38
  198.6 2.1 collective-permute-start.40
  200.6 5.6 %collective-permute-done.41 = bf16[96,2048]{1,0:T(8,128)(2,1)S(1)} collective-permute-done((bf16[96,2048]{1,0:T(8,128)(2,1)S(1)}, bf16[96,2048]{1,0:T(8,128)(2,1)S(1)}, u32[]{:S(2)}, u32[]{:S(2)}) %collective-permute-start.41) | collective-permute-done | bytes 393248 | tf_op jit(solution)/shard_map/ppermute | solution.py:341
  206.4 1.0 fusion.19
  (148 shorter events, 9.2 us)
Async XLA Ops:
  0.6 38.1 %copy-start.4 = (bf16[2,96,2048]{2,1,0:T(8,128)(2,1)S(1)}, bf16[2,96,2048]{2,1,0:T(8,128)(2,1)}, u32[]{:S(2)}) copy-start(bf16[2,96,2048]{2,1,0:T(8,128)(2,1)} %param.13) | copy-start | bytes 2359300
  0.6 27.7 %collective-permute-start.5 = (bf16[2048,512]{1,0:T(8,128)(2,1)}, bf16[2048,512]{1,0:T(8,128)(2,1)}, u32[]{:S(2)}, u32[]{:S(2)}) collective-permute-start(bf16[2048,512]{1,0:T(8,128)(2,1)} %bitcast.58), channel_id=1, source_target_pairs={{0,1},{1,0},{2,3},{3,2},{4,5},{5,4},{6,7},{7,6},{8,9},{9,8},{10,11... | collective-permute-start | bytes 6291464 | tf_op jit(solution)/shard_map/ppermute | solution.py:442
  3.5 32.4 %copy-start.9 = (bf16[96,2048]{1,0:T(8,128)(2,1)}, bf16[96,2048]{1,0:T(8,128)(2,1)S(1)}, u32[]{:S(2)}) copy-start(bf16[96,2048]{1,0:T(8,128)(2,1)S(1)} %fusion.4.refs_0_) | copy-start | bytes 1179652
  3.5 12.5 %collective-permute-start.2 = (bf16[96,2048]{1,0:T(8,128)(2,1)S(1)}, bf16[96,2048]{1,0:T(8,128)(2,1)}, u32[]{:S(2)}, u32[]{:S(2)}) collective-permute-start(bf16[96,2048]{1,0:T(8,128)(2,1)S(1)} %fusion.4.refs_0_), channel_id=1, source_target_pairs={{4,0},{5,1},{8,4},{9,5},{12,8},{13,9},{14,12},{15,13},{10,14},{11,... | collective-permute-start | bytes 1179656 | tf_op jit(solution)/shard_map/ppermute | solution.py:341
  6.2 11.6 %collective-permute-start.1 = (bf16[96,2048]{1,0:T(8,128)(2,1)S(1)}, bf16[96,2048]{1,0:T(8,128)(2,1)}, u32[]{:S(2)}, u32[]{:S(2)}) collective-permute-start(bf16[96,2048]{1,0:T(8,128)(2,1)S(1)} %fusion.4.refs_0_), channel_id=1, source_target_pairs={{0,4},{1,5},{4,8},{5,9},{8,12},{9,13},{12,14},{13,15},{14,10},{15,... | collective-permute-start | bytes 1179656 | tf_op jit(solution)/shard_map/ppermute | solution.py:341
  6.3 12.5 %collective-permute-start = (bf16[96,2048]{1,0:T(8,128)(2,1)}, bf16[96,2048]{1,0:T(8,128)(2,1)S(1)}, u32[]{:S(2)}, u32[]{:S(2)}) collective-permute-start(bf16[96,2048]{1,0:T(8,128)(2,1)} %bitcast.69), channel_id=1, source_target_pairs={{0,16},{1,17},{2,18},{3,19},{4,20},{5,21},{6,22},{7,23},{8,24},{9,... | collective-permute-start | bytes 1179656 | tf_op jit(solution)/shard_map/ppermute | solution.py:17
  15.0 42.7 %copy-start.1 = (bf16[1,96,2048]{2,1,0:T(8,128)(2,1)S(1)}, bf16[1,96,2048]{2,1,0:T(8,128)(2,1)}, u32[]{:S(2)}) copy-start(bf16[1,96,2048]{2,1,0:T(8,128)(2,1)} %param.16) | copy-start | bytes 1179652
  15.0 42.7 %copy-start.2 = (bf16[2,96,2048]{2,1,0:T(8,128)(2,1)S(1)}, bf16[2,96,2048]{2,1,0:T(8,128)(2,1)}, u32[]{:S(2)}) copy-start(bf16[2,96,2048]{2,1,0:T(8,128)(2,1)} %param.17) | copy-start | bytes 2359300
  15.0 42.7 %copy-start.20 = (f32[1,2048]{1,0:T(1,128)S(1)}, f32[1,2048]{1,0:T(1,128)}, u32[]{:S(2)}) copy-start(f32[1,2048]{1,0:T(1,128)} %param.18) | copy-start | bytes 24580
  15.0 42.7 %copy-start.21 = (f32[1,2048]{1,0:T(1,128)S(1)}, f32[1,2048]{1,0:T(1,128)}, u32[]{:S(2)}) copy-start(f32[1,2048]{1,0:T(1,128)} %param.19) | copy-start | bytes 24580
  16.1 11.1 %collective-permute-start.4 = (bf16[96,2048]{1,0:T(8,128)(2,1)}, bf16[96,2048]{1,0:T(8,128)(2,1)S(1)}, u32[]{:S(2)}, u32[]{:S(2)}) collective-permute-start(bf16[96,2048]{1,0:T(8,128)(2,1)} %collective-permute-done.2.refs_2_), channel_id=1, source_target_pairs={{4,0},{5,1},{8,4},{9,5},{12,8},{13,9},{14,12},{15,13},{10,14},{11,... | collective-permute-start | bytes 1179656 | tf_op jit(solution)/shard_map/ppermute | solution.py:341
  17.7 10.6 %collective-permute-start.3 = (bf16[96,2048]{1,0:T(8,128)(2,1)}, bf16[96,2048]{1,0:T(8,128)(2,1)S(1)}, u32[]{:S(2)}, u32[]{:S(2)}) collective-permute-start(bf16[96,2048]{1,0:T(8,128)(2,1)} %collective-permute-done.1.refs_1_), channel_id=1, source_target_pairs={{0,4},{1,5},{4,8},{5,9},{8,12},{9,13},{12,14},{13,15},{14,10},{15,... | collective-permute-start | bytes 1179656 | tf_op jit(solution)/shard_map/ppermute | solution.py:341
  20.6 37.8 %copy-start = (bf16[96,2176]{1,0:T(8,128)(2,1)}, bf16[96,2176]{1,0:T(8,128)(2,1)S(1)}, u32[]{:S(2)}) copy-start(bf16[96,2176]{1,0:T(8,128)(2,1)S(1)} %shard_map.148.refs_0_) | copy-start | bytes 1253380
  27.1 24.2 %copy-start.29 = (bf16[96,2048]{1,0:T(8,128)(2,1)}, bf16[96,2048]{1,0:T(8,128)(2,1)S(1)}, u32[]{:S(2)}) copy-start(bf16[96,2048]{1,0:T(8,128)(2,1)S(1)} %collective-permute-done.4.refs_4_) | copy-start | bytes 1179652
  28.3 23.1 %copy-start.30 = (bf16[96,2048]{1,0:T(8,128)(2,1)}, bf16[96,2048]{1,0:T(8,128)(2,1)S(1)}, u32[]{:S(2)}) copy-start(bf16[96,2048]{1,0:T(8,128)(2,1)S(1)} %collective-permute-done.3.refs_3_) | copy-start | bytes 1179652
  28.3 10.4 %collective-permute-start.10 = (bf16[96,2048]{1,0:T(8,128)(2,1)S(1)}, bf16[96,2048]{1,0:T(8,128)(2,1)S(1)}, u32[]{:S(2)}, u32[]{:S(2)}) collective-permute-start(bf16[96,2048]{1,0:T(8,128)(2,1)S(1)} %bitcast.70), channel_id=1, source_target_pairs={{0,16},{1,17},{2,18},{3,19},{4,20},{5,21},{6,22},{7,23},{8,24},{9,... | collective-permute-start | bytes 1179656 | tf_op jit(solution)/shard_map/ppermute | solution.py:17
  31.8 19.6 %collective-permute-start.7 = (bf16[96,2176]{1,0:T(8,128)(2,1)S(1)}, bf16[96,2176]{1,0:T(8,128)(2,1)}, u32[]{:S(2)}, u32[]{:S(2)}) collective-permute-start(bf16[96,2176]{1,0:T(8,128)(2,1)S(1)} %shard_map.148.refs_0_), channel_id=1, source_target_pairs={{4,0},{5,1},{8,4},{9,5},{12,8},{13,9},{14,12},{15,13},{10,14},{11,... | collective-permute-start | bytes 1253384 | tf_op jit(solution)/shard_map/ppermute | solution.py:341
  33.4 18.0 %collective-permute-start.6 = (bf16[96,2176]{1,0:T(8,128)(2,1)S(1)}, bf16[96,2176]{1,0:T(8,128)(2,1)}, u32[]{:S(2)}, u32[]{:S(2)}) collective-permute-start(bf16[96,2176]{1,0:T(8,128)(2,1)S(1)} %shard_map.148.refs_0_), channel_id=1, source_target_pairs={{0,4},{1,5},{4,8},{5,9},{8,12},{9,13},{12,14},{13,15},{14,10},{15,... | collective-permute-start | bytes 1253384 | tf_op jit(solution)/shard_map/ppermute | solution.py:341
  33.8 17.5 %collective-permute-start.8 = (bf16[96,2048]{1,0:T(8,128)(2,1)S(1)}, bf16[96,2048]{1,0:T(8,128)(2,1)}, u32[]{:S(2)}, u32[]{:S(2)}) collective-permute-start(bf16[96,2048]{1,0:T(8,128)(2,1)S(1)} %collective-permute-done.3.refs_3_), channel_id=1, source_target_pairs={{0,4},{1,5},{4,8},{5,9},{8,12},{9,13},{12,14},{13,15},{14,10},{15,... | collective-permute-start | bytes 1179656 | tf_op jit(solution)/shard_map/ppermute | solution.py:341
  34.4 17.0 %collective-permute-start.9 = (bf16[96,2048]{1,0:T(8,128)(2,1)S(1)}, bf16[96,2048]{1,0:T(8,128)(2,1)}, u32[]{:S(2)}, u32[]{:S(2)}) collective-permute-start(bf16[96,2048]{1,0:T(8,128)(2,1)S(1)} %collective-permute-done.4.refs_4_), channel_id=1, source_target_pairs={{4,0},{5,1},{8,4},{9,5},{12,8},{13,9},{14,12},{15,13},{10,14},{11,... | collective-permute-start | bytes 1179656 | tf_op jit(solution)/shard_map/ppermute | solution.py:341
  51.4 19.6 %collective-permute-start.15 = (bf16[2048,512]{1,0:T(8,128)(2,1)}, bf16[2048,512]{1,0:T(8,128)(2,1)}, u32[]{:S(2)}, u32[]{:S(2)}) collective-permute-start(bf16[2048,512]{1,0:T(8,128)(2,1)} %bitcast.8.refs_10_.refs_7_.refs_5_.refs_11_), channel_id=1, source_target_pairs={{0,1},{1,0},{2,3},{3,2},{4,5},{5,4},{6,7},{7,6},{8,9},{9,8},{10,11... | collective-permute-start | bytes 6291464 | tf_op jit(solution)/shard_map/ppermute | solution.py:442
  53.4 17.6 %copy-start.22 = (bf16[1,1,512,2048]{3,2,1,0:T(8,128)(2,1)S(1)}, bf16[1,1,512,2048]{3,2,1,0:T(8,128)(2,1)}, u32[]{:S(2)}) copy-start(bf16[1,1,512,2048]{3,2,1,0:T(8,128)(2,1)} %param.22) | copy-start | bytes 6291460
  53.4 7.8 %collective-permute-start.14 = (bf16[48,2048]{1,0:T(8,128)(2,1)S(1)}, bf16[48,2048]{1,0:T(8,128)(2,1)S(1)}, u32[]{:S(2)}, u32[]{:S(2)}) collective-permute-start(bf16[48,2048]{1,0:T(8,128)(2,1)S(1)} %slice.47), channel_id=1, source_target_pairs={{4,0},{5,1},{8,4},{9,5},{12,8},{13,9},{14,12},{15,13},{10,14},{11,... | collective-permute-start | bytes 589832 | tf_op jit(solution)/shard_map/ppermute | solution.py:341
  55.0 7.8 %collective-permute-start.13 = (bf16[48,2048]{1,0:T(8,128)(2,1)S(1)}, bf16[48,2048]{1,0:T(8,128)(2,1)S(1)}, u32[]{:S(2)}, u32[]{:S(2)}) collective-permute-start(bf16[48,2048]{1,0:T(8,128)(2,1)S(1)} %slice.46), channel_id=1, source_target_pairs={{0,4},{1,5},{4,8},{5,9},{8,12},{9,13},{12,14},{13,15},{14,10},{15,... | collective-permute-start | bytes 589832 | tf_op jit(solution)/shard_map/ppermute | solution.py:341
  55.5 15.5 %collective-permute-start.11 = (bf16[96,2176]{1,0:T(8,128)(2,1)}, bf16[96,2176]{1,0:T(8,128)(2,1)S(1)}, u32[]{:S(2)}, u32[]{:S(2)}) collective-permute-start(bf16[96,2176]{1,0:T(8,128)(2,1)} %collective-permute-done.6.refs_1_), channel_id=1, source_target_pairs={{0,4},{1,5},{4,8},{5,9},{8,12},{9,13},{12,14},{13,15},{14,10},{15,... | collective-permute-start | bytes 1253384 | tf_op jit(solution)/shard_map/ppermute | solution.py:341
  55.9 15.1 %collective-permute-start.12 = (bf16[96,2176]{1,0:T(8,128)(2,1)}, bf16[96,2176]{1,0:T(8,128)(2,1)S(1)}, u32[]{:S(2)}, u32[]{:S(2)}) collective-permute-start(bf16[96,2176]{1,0:T(8,128)(2,1)} %collective-permute-done.7.refs_2_), channel_id=1, source_target_pairs={{4,0},{5,1},{8,4},{9,5},{12,8},{13,9},{14,12},{15,13},{10,14},{11,... | collective-permute-start | bytes 1253384 | tf_op jit(solution)/shard_map/ppermute | solution.py:341
  58.4 28.8 %copy-start.5 = (bf16[96,2048]{1,0:T(8,128)(2,1)}, bf16[96,2048]{1,0:T(8,128)(2,1)S(1)}, u32[]{:S(2)}) copy-start(bf16[96,2048]{1,0:T(8,128)(2,1)S(1)} %get-tuple-element.282.refs_5_) | copy-start | bytes 1179652
  71.0 16.2 %copy-start.23 = (bf16[96,2176]{1,0:T(8,128)(2,1)}, bf16[96,2176]{1,0:T(8,128)(2,1)S(1)}, u32[]{:S(2)}) copy-start(bf16[96,2176]{1,0:T(8,128)(2,1)S(1)} %collective-permute-done.11.refs_3_) | copy-start | bytes 1253380
  71.0 16.2 %copy-start.24 = (bf16[96,2176]{1,0:T(8,128)(2,1)}, bf16[96,2176]{1,0:T(8,128)(2,1)S(1)}, u32[]{:S(2)}) copy-start(bf16[96,2176]{1,0:T(8,128)(2,1)S(1)} %collective-permute-done.12.refs_4_) | copy-start | bytes 1253380
  71.0 21.9 %collective-permute-start.20 = (bf16[512,2048]{1,0:T(8,128)(2,1)S(1)}, bf16[512,2048]{1,0:T(8,128)(2,1)}, u32[]{:S(2)}, u32[]{:S(2)}) collective-permute-start(bf16[512,2048]{1,0:T(8,128)(2,1)S(1)} %bitcast.68), channel_id=1, source_target_pairs={{0,1},{1,0},{2,3},{3,2},{4,5},{5,4},{6,7},{7,6},{8,9},{9,8},{10,11... | collective-permute-start | bytes 6291464 | tf_op jit(solution)/shard_map/ppermute | solution.py:442
  71.1 16.1 %collective-permute-start.19 = (bf16[96,2048]{1,0:T(8,128)(2,1)S(1)}, bf16[96,2048]{1,0:T(8,128)(2,1)S(1)}, u32[]{:S(2)}, u32[]{:S(2)}) collective-permute-start(bf16[96,2048]{1,0:T(8,128)(2,1)S(1)} %get-tuple-element.282.refs_5_), channel_id=1, source_target_pairs={{4,0},{5,1},{8,4},{9,5},{12,8},{13,9},{14,12},{15,13},{10,14},{11,... | collective-permute-start | bytes 1179656 | tf_op jit(solution)/shard_map/ppermute | solution.py:341
  72.7 14.5 %collective-permute-start.18 = (bf16[96,2048]{1,0:T(8,128)(2,1)S(1)}, bf16[96,2048]{1,0:T(8,128)(2,1)S(1)}, u32[]{:S(2)}, u32[]{:S(2)}) collective-permute-start(bf16[96,2048]{1,0:T(8,128)(2,1)S(1)} %get-tuple-element.282.refs_5_), channel_id=1, source_target_pairs={{0,4},{1,5},{4,8},{5,9},{8,12},{9,13},{12,14},{13,15},{14,10},{15,... | collective-permute-start | bytes 1179656 | tf_op jit(solution)/shard_map/ppermute | solution.py:341
  73.2 19.7 %collective-permute-start.16 = (bf16[96,2176]{1,0:T(8,128)(2,1)S(1)}, bf16[96,2176]{1,0:T(8,128)(2,1)S(1)}, u32[]{:S(2)}, u32[]{:S(2)}) collective-permute-start(bf16[96,2176]{1,0:T(8,128)(2,1)S(1)} %collective-permute-done.11.refs_3_), channel_id=1, source_target_pairs={{0,4},{1,5},{4,8},{5,9},{8,12},{9,13},{12,14},{13,15},{14,10},{15,... | collective-permute-start | bytes 1253384 | tf_op jit(solution)/shard_map/ppermute | solution.py:341
  73.6 19.2 %collective-permute-start.17 = (bf16[96,2176]{1,0:T(8,128)(2,1)S(1)}, bf16[96,2176]{1,0:T(8,128)(2,1)S(1)}, u32[]{:S(2)}, u32[]{:S(2)}) collective-permute-start(bf16[96,2176]{1,0:T(8,128)(2,1)S(1)} %collective-permute-done.12.refs_4_), channel_id=1, source_target_pairs={{4,0},{5,1},{8,4},{9,5},{12,8},{13,9},{14,12},{15,13},{10,14},{11,... | collective-permute-start | bytes 1253384 | tf_op jit(solution)/shard_map/ppermute | solution.py:341
  87.2 23.2 %copy-start.31 = (bf16[96,2048]{1,0:T(8,128)(2,1)}, bf16[96,2048]{1,0:T(8,128)(2,1)S(1)}, u32[]{:S(2)}) copy-start(bf16[96,2048]{1,0:T(8,128)(2,1)S(1)} %collective-permute-done.19.refs_7_) | copy-start | bytes 1179652
  87.2 23.1 %copy-start.32 = (bf16[96,2048]{1,0:T(8,128)(2,1)}, bf16[96,2048]{1,0:T(8,128)(2,1)S(1)}, u32[]{:S(2)}) copy-start(bf16[96,2048]{1,0:T(8,128)(2,1)S(1)} %collective-permute-done.18.refs_6_) | copy-start | bytes 1179652
  92.8 17.5 %copy-start.25 = (bf16[96,2176]{1,0:T(8,128)(2,1)}, bf16[96,2176]{1,0:T(8,128)(2,1)S(1)}, u32[]{:S(2)}) copy-start(bf16[96,2176]{1,0:T(8,128)(2,1)S(1)} %collective-permute-done.16.refs_0_) | copy-start | bytes 1253380
  92.9 17.5 %copy-start.26 = (bf16[96,2176]{1,0:T(8,128)(2,1)}, bf16[96,2176]{1,0:T(8,128)(2,1)S(1)}, u32[]{:S(2)}) copy-start(bf16[96,2176]{1,0:T(8,128)(2,1)S(1)} %collective-permute-done.17.refs_1_) | copy-start | bytes 1253380
  92.9 17.5 %collective-permute-start.22 = (bf16[96,2048]{1,0:T(8,128)(2,1)S(1)}, bf16[96,2048]{1,0:T(8,128)(2,1)S(1)}, u32[]{:S(2)}, u32[]{:S(2)}) collective-permute-start(bf16[96,2048]{1,0:T(8,128)(2,1)S(1)} %collective-permute-done.18.refs_6_), channel_id=1, source_target_pairs={{0,4},{1,5},{4,8},{5,9},{8,12},{9,13},{12,14},{13,15},{14,10},{15,... | collective-permute-start | bytes 1179656 | tf_op jit(solution)/shard_map/ppermute | solution.py:341
  93.4 17.0 %collective-permute-start.23 = (bf16[96,2048]{1,0:T(8,128)(2,1)S(1)}, bf16[96,2048]{1,0:T(8,128)(2,1)S(1)}, u32[]{:S(2)}, u32[]{:S(2)}) collective-permute-start(bf16[96,2048]{1,0:T(8,128)(2,1)S(1)} %collective-permute-done.19.refs_7_), channel_id=1, source_target_pairs={{4,0},{5,1},{8,4},{9,5},{12,8},{13,9},{14,12},{15,13},{10,14},{11,... | collective-permute-start | bytes 1179656 | tf_op jit(solution)/shard_map/ppermute | solution.py:341
  94.9 17.5 %collective-permute-start.21 = (bf16[96,2176]{1,0:T(8,128)(2,1)S(1)}, bf16[96,2176]{1,0:T(8,128)(2,1)S(1)}, u32[]{:S(2)}, u32[]{:S(2)}) collective-permute-start(bf16[96,2176]{1,0:T(8,128)(2,1)S(1)} %collective-permute-done.17.refs_1_), channel_id=1, source_target_pairs={{4,0},{5,1},{8,4},{9,5},{12,8},{13,9},{14,12},{15,13},{10,14},{11,... | collective-permute-start | bytes 1253384 | tf_op jit(solution)/shard_map/ppermute | solution.py:341
  112.4 14.0 %collective-permute-start.24 = (bf16[96,2048]{1,0:T(8,128)(2,1)S(1)}, bf16[96,2048]{1,0:T(8,128)(2,1)S(1)}, u32[]{:S(2)}, u32[]{:S(2)}) collective-permute-start(bf16[96,2048]{1,0:T(8,128)(2,1)S(1)} %collective-permute-done.22.refs_8_), channel_id=1, source_target_pairs={{0,4},{1,5},{4,8},{5,9},{8,12},{9,13},{12,14},{13,15},{14,10},{15,... | collective-permute-start | bytes 1179656 | tf_op jit(solution)/shard_map/ppermute | solution.py:341
  112.8 13.5 %collective-permute-start.25 = (bf16[96,2048]{1,0:T(8,128)(2,1)S(1)}, bf16[96,2048]{1,0:T(8,128)(2,1)S(1)}, u32[]{:S(2)}, u32[]{:S(2)}) collective-permute-start(bf16[96,2048]{1,0:T(8,128)(2,1)S(1)} %collective-permute-done.23.refs_9_), channel_id=1, source_target_pairs={{4,0},{5,1},{8,4},{9,5},{12,8},{13,9},{14,12},{15,13},{10,14},{11,... | collective-permute-start | bytes 1179656 | tf_op jit(solution)/shard_map/ppermute | solution.py:341
  126.4 16.2 %copy-start.34 = (bf16[96,2048]{1,0:T(8,128)(2,1)S(1)}, bf16[96,2048]{1,0:T(8,128)(2,1)}, u32[]{:S(2)}) copy-start(bf16[96,2048]{1,0:T(8,128)(2,1)} %get-tuple-element.321) | copy-start | bytes 1179652
  126.4 14.4 %collective-permute-start.27 = (bf16[96,2048]{1,0:T(8,128)(2,1)}, bf16[96,2048]{1,0:T(8,128)(2,1)S(1)}, u32[]{:S(2)}, u32[]{:S(2)}) collective-permute-start(bf16[96,2048]{1,0:T(8,128)(2,1)} %get-tuple-element.301), channel_id=1, source_target_pairs={{4,0},{5,1},{8,4},{9,5},{12,8},{13,9},{14,12},{15,13},{10,14},{11,... | collective-permute-start | bytes 1179656 | tf_op jit(solution)/shard_map/ppermute | solution.py:341
  128.0 12.8 %collective-permute-start.26 = (bf16[96,2048]{1,0:T(8,128)(2,1)S(1)}, bf16[96,2048]{1,0:T(8,128)(2,1)S(1)}, u32[]{:S(2)}, u32[]{:S(2)}) collective-permute-start(bf16[96,2048]{1,0:T(8,128)(2,1)S(1)} %collective-permute-done.24.refs_3_), channel_id=1, source_target_pairs={{0,4},{1,5},{4,8},{5,9},{8,12},{9,13},{12,14},{13,15},{14,10},{15,... | collective-permute-start | bytes 1179656 | tf_op jit(solution)/shard_map/ppermute | solution.py:341
  141.0 12.1 %collective-permute-start.29 = (bf16[96,2048]{1,0:T(8,128)(2,1)S(1)}, bf16[96,2048]{1,0:T(8,128)(2,1)S(1)}, u32[]{:S(2)}, u32[]{:S(2)}) collective-permute-start(bf16[96,2048]{1,0:T(8,128)(2,1)S(1)} %add_convert_fusion.8), channel_id=1, source_target_pairs={{4,0},{5,1},{8,4},{9,5},{12,8},{13,9},{14,12},{15,13},{10,14},{11,... | collective-permute-start | bytes 1179656 | tf_op jit(solution)/shard_map/ppermute | solution.py:341
  142.6 10.4 %collective-permute-start.28 = (bf16[96,2048]{1,0:T(8,128)(2,1)S(1)}, bf16[96,2048]{1,0:T(8,128)(2,1)S(1)}, u32[]{:S(2)}, u32[]{:S(2)}) collective-permute-start(bf16[96,2048]{1,0:T(8,128)(2,1)S(1)} %copy-done.34), channel_id=1, source_target_pairs={{0,4},{1,5},{4,8},{5,9},{8,12},{9,13},{12,14},{13,15},{14,10},{15,... | collective-permute-start | bytes 1179656 | tf_op jit(solution)/shard_map/ppermute | solution.py:341
  153.2 14.4 %collective-permute-start.31 = (bf16[96,2048]{1,0:T(8,128)(2,1)S(1)}, bf16[96,2048]{1,0:T(8,128)(2,1)S(1)}, u32[]{:S(2)}, u32[]{:S(2)}) collective-permute-start(bf16[96,2048]{1,0:T(8,128)(2,1)S(1)} %add_convert_fusion.6), channel_id=1, source_target_pairs={{4,0},{5,1},{8,4},{9,5},{12,8},{13,9},{14,12},{15,13},{10,14},{11,... | collective-permute-start | bytes 1179656 | tf_op jit(solution)/shard_map/ppermute | solution.py:341
  155.0 12.7 %collective-permute-start.30 = (bf16[96,2048]{1,0:T(8,128)(2,1)S(1)}, bf16[96,2048]{1,0:T(8,128)(2,1)S(1)}, u32[]{:S(2)}, u32[]{:S(2)}) collective-permute-start(bf16[96,2048]{1,0:T(8,128)(2,1)S(1)} %add_convert_fusion.7), channel_id=1, source_target_pairs={{0,4},{1,5},{4,8},{5,9},{8,12},{9,13},{12,14},{13,15},{14,10},{15,... | collective-permute-start | bytes 1179656 | tf_op jit(solution)/shard_map/ppermute | solution.py:341
  155.5 9.8 %collective-permute-start.33 = (bf16[48,2048]{1,0:T(8,128)(2,1)S(1)}, bf16[48,2048]{1,0:T(8,128)(2,1)S(1)}, u32[]{:S(2)}, u32[]{:S(2)}) collective-permute-start(bf16[48,2048]{1,0:T(8,128)(2,1)S(1)} %get-tuple-element.402), channel_id=1, source_target_pairs={{4,0},{5,1},{8,4},{9,5},{12,8},{13,9},{14,12},{15,13},{10,14},{11,... | collective-permute-start | bytes 589832 | tf_op jit(solution)/shard_map/ppermute | solution.py:341
  157.1 10.5 %collective-permute-start.32 = (bf16[48,2048]{1,0:T(8,128)(2,1)S(1)}, bf16[48,2048]{1,0:T(8,128)(2,1)S(1)}, u32[]{:S(2)}, u32[]{:S(2)}) collective-permute-start(bf16[48,2048]{1,0:T(8,128)(2,1)S(1)} %get-tuple-element.403), channel_id=1, source_target_pairs={{0,4},{1,5},{4,8},{5,9},{8,12},{9,13},{12,14},{13,15},{14,10},{15,... | collective-permute-start | bytes 589832 | tf_op jit(solution)/shard_map/ppermute | solution.py:341
  167.8 17.9 %copy-start.14 = (bf16[96,2048]{1,0:T(8,128)(2,1)S(1)}, bf16[96,2048]{1,0:T(8,128)(2,1)}, u32[]{:S(2)}) copy-start(bf16[96,2048]{1,0:T(8,128)(2,1)} %get-tuple-element.361) | copy-start | bytes 1179652
  168.0 18.5 %copy-start.12 = (bf16[96,2048]{1,0:T(8,128)(2,1)S(1)}, bf16[96,2048]{1,0:T(8,128)(2,1)}, u32[]{:S(2)}) copy-start(bf16[96,2048]{1,0:T(8,128)(2,1)} %get-tuple-element.359) | copy-start | bytes 1179652
  168.0 9.6 %collective-permute-start.35 = (bf16[96,2048]{1,0:T(8,128)(2,1)S(1)}, bf16[96,2048]{1,0:T(8,128)(2,1)S(1)}, u32[]{:S(2)}, u32[]{:S(2)}) collective-permute-start(bf16[96,2048]{1,0:T(8,128)(2,1)S(1)} %add_convert_fusion.4), channel_id=1, source_target_pairs={{4,0},{5,1},{8,4},{9,5},{12,8},{13,9},{14,12},{15,13},{10,14},{11,... | collective-permute-start | bytes 1179656 | tf_op jit(solution)/shard_map/ppermute | solution.py:341
  168.7 19.4 %copy-start.3 = (bf16[96,2048]{1,0:T(8,128)(2,1)S(1)}, bf16[96,2048]{1,0:T(8,128)(2,1)}, u32[]{:S(2)}) copy-start(bf16[96,2048]{1,0:T(8,128)(2,1)} %get-tuple-element.353) | copy-start | bytes 1179652
  168.7 10.3 %collective-permute-start.34 = (bf16[96,2048]{1,0:T(8,128)(2,1)S(1)}, bf16[96,2048]{1,0:T(8,128)(2,1)S(1)}, u32[]{:S(2)}, u32[]{:S(2)}) collective-permute-start(bf16[96,2048]{1,0:T(8,128)(2,1)S(1)} %add_convert_fusion.5), channel_id=1, source_target_pairs={{0,4},{1,5},{4,8},{5,9},{8,12},{9,13},{12,14},{13,15},{14,10},{15,... | collective-permute-start | bytes 1179656 | tf_op jit(solution)/shard_map/ppermute | solution.py:341
  170.2 13.1 %collective-permute-start.37 = (bf16[96,2048]{1,0:T(8,128)(2,1)S(1)}, bf16[96,2048]{1,0:T(8,128)(2,1)S(1)}, u32[]{:S(2)}, u32[]{:S(2)}) collective-permute-start(bf16[96,2048]{1,0:T(8,128)(2,1)S(1)} %pad_maximum_fusion.1), channel_id=1, source_target_pairs={{4,0},{5,1},{8,4},{9,5},{12,8},{13,9},{14,12},{15,13},{10,14},{11,... | collective-permute-start | bytes 1179656 | tf_op jit(solution)/shard_map/ppermute | solution.py:341
  170.9 14.9 %collective-permute-start.36 = (bf16[96,2048]{1,0:T(8,128)(2,1)S(1)}, bf16[96,2048]{1,0:T(8,128)(2,1)S(1)}, u32[]{:S(2)}, u32[]{:S(2)}) collective-permute-start(bf16[96,2048]{1,0:T(8,128)(2,1)S(1)} %pad_maximum_fusion), channel_id=1, source_target_pairs={{0,4},{1,5},{4,8},{5,9},{8,12},{9,13},{12,14},{13,15},{14,10},{15,... | collective-permute-start | bytes 1179656 | tf_op jit(solution)/shard_map/ppermute | solution.py:341
  185.9 11.5 %collective-permute-start.39 = (bf16[96,2048]{1,0:T(8,128)(2,1)S(1)}, bf16[96,2048]{1,0:T(8,128)(2,1)S(1)}, u32[]{:S(2)}, u32[]{:S(2)}) collective-permute-start(bf16[96,2048]{1,0:T(8,128)(2,1)S(1)} %add_convert_fusion.2), channel_id=1, source_target_pairs={{4,0},{5,1},{8,4},{9,5},{12,8},{13,9},{14,12},{15,13},{10,14},{11,... | collective-permute-start | bytes 1179656 | tf_op jit(solution)/shard_map/ppermute | solution.py:341
  186.5 11.8 %collective-permute-start.38 = (bf16[96,2048]{1,0:T(8,128)(2,1)S(1)}, bf16[96,2048]{1,0:T(8,128)(2,1)S(1)}, u32[]{:S(2)}, u32[]{:S(2)}) collective-permute-start(bf16[96,2048]{1,0:T(8,128)(2,1)S(1)} %add_convert_fusion.3), channel_id=1, source_target_pairs={{0,4},{1,5},{4,8},{5,9},{8,12},{9,13},{12,14},{13,15},{14,10},{15,... | collective-permute-start | bytes 1179656 | tf_op jit(solution)/shard_map/ppermute | solution.py:341
  188.5 17.9 %copy-start.19 = (bf16[96,2048]{1,0:T(8,128)(2,1)S(1)}, bf16[96,2048]{1,0:T(8,128)(2,1)}, u32[]{:S(2)}) copy-start(bf16[96,2048]{1,0:T(8,128)(2,1)} %get-tuple-element.364) | copy-start | bytes 1179652
  198.4 7.8 %collective-permute-start.41 = (bf16[96,2048]{1,0:T(8,128)(2,1)S(1)}, bf16[96,2048]{1,0:T(8,128)(2,1)S(1)}, u32[]{:S(2)}, u32[]{:S(2)}) collective-permute-start(bf16[96,2048]{1,0:T(8,128)(2,1)S(1)} %add_convert_fusion), channel_id=1, source_target_pairs={{4,0},{5,1},{8,4},{9,5},{12,8},{13,9},{14,12},{15,13},{10,14},{11,... | collective-permute-start | bytes 1179656 | tf_op jit(solution)/shard_map/ppermute | solution.py:341
  198.6 7.8 %collective-permute-start.40 = (bf16[96,2048]{1,0:T(8,128)(2,1)S(1)}, bf16[96,2048]{1,0:T(8,128)(2,1)S(1)}, u32[]{:S(2)}, u32[]{:S(2)}) collective-permute-start(bf16[96,2048]{1,0:T(8,128)(2,1)S(1)} %add_convert_fusion.1), channel_id=1, source_target_pairs={{0,4},{1,5},{4,8},{5,9},{8,12},{9,13},{12,14},{13,15},{14,10},{15,... | collective-permute-start | bytes 1179656 | tf_op jit(solution)/shard_map/ppermute | solution.py:341
  (19 other events, 227.8 us)

commit v6 on v5

--- a/solution.py
+++ b/solution.py
@@ -7,7 +7,7 @@
 from jax.sharding import PartitionSpec as P
 
 EPSILON = 1e-06
-VMEM_LIMIT = 56 * 1024 * 1024
+VMEM_LIMIT = 24 * 1024 * 1024
 NT = (((1,), (1,)), ((), ()))
 
 
@@ -50,7 +50,7 @@
     return pl.pallas_call(
         functools.partial(pack_kernel, experts),
         out_shape=jax.ShapeDtypeStruct((count, width + extra), jnp.bfloat16),
-        compiler_params=pltpu.CompilerParams(vmem_limit_bytes=VMEM_LIMIT // 4),
+        compiler_params=pltpu.CompilerParams(vmem_limit_bytes=VMEM_LIMIT),
         cost_estimate=pl.CostEstimate(flops=0, bytes_accessed=count * width * 8, transcendentals=0),
     )(rows, ids, gates)
 
@@ -92,24 +92,6 @@
         start += count
 
 
-def in_order(copies):
-    start_all(copies[:2])
-
-    def arrived(i):
-        copies[i].wait()
-        if i + 2 < len(copies):
-            copies[i + 2].start()
-
-    return arrived
-
-
-def matrix_copies(weights, targets, sems):
-    return [
-        pltpu.make_async_copy(weight, target, sems.at[i])
-        for i, (weight, target) in enumerate(zip(weights, targets))
-    ]
-
-
 def dot(first, second):
     return jnp.dot(first, second, preferred_element_type=jnp.float32)
 
@@ -122,54 +104,37 @@
     packed, rows = refs[:parts], refs[parts : 2 * parts]
     weights = refs[2 * parts : 2 * parts + 6]
     outs = refs[2 * parts + 6 : 3 * parts + 6]
-    (table, held, hidden, gate_w, up_w, down_w, table_sem, row_sem, weight_sem) = refs[
-        3 * parts + 6 :
-    ]
+    table, held, hidden, table_sem, row_sem = refs[3 * parts + 6 :]
     extra = table.shape[1]
-    inner = gate_w.shape[2]
-    first_copies = block_copies(rows, held, row_sem)
-    first_copies += block_copies(packed, table, table_sem, pl.ds(width, extra))
-    start_all(first_copies)
-    order = [(0, gate_w, 0), (1, up_w, 0), (3, gate_w, 1), (4, up_w, 1), (2, down_w, 0)]
-    order += [(5, down_w, 1)]
-    arrived = in_order(
-        matrix_copies(
-            [weights[i] for i, _, _ in order], [ref.at[e] for _, ref, e in order], weight_sem
-        )
-    )
-    wait_all(first_copies)
+    inner = weights[0].shape[1]
+    copies = block_copies(rows, held, row_sem)
+    copies += block_copies(packed, table, table_sem, pl.ds(width, extra))
+    start_all(copies)
+    wait_all(copies)
     for e in range(2):
         gate = gate_column(table[...].astype(jnp.float32), 0, experts, names_ref[e])
-        arrived(2 * e)
-        first = dot(held[...], gate_w[e])
-        arrived(2 * e + 1)
-        second = dot(held[...], up_w[e])
+        first = dot(held[...], weights[3 * e][...])
+        second = dot(held[...], weights[3 * e + 1][...])
         made = gate * (jax.nn.silu(first) * second)
         hidden[:, pl.ds(e * inner, inner)] = made.astype(jnp.bfloat16)
-    arrived(4)
-    arrived(5)
 
     @pl.loop(0, width // tile)
     def _(n):
         columns = pl.ds(pl.multiple_of(n * tile, tile), tile)
-        total = dot(hidden[:, :inner], down_w[0, :, columns])
-        total = total + dot(hidden[:, inner:], down_w[1, :, columns])
+        total = dot(hidden[:, :inner], weights[2][:, columns])
+        total = total + dot(hidden[:, inner:], weights[5][:, columns])
         write_tiles(total, outs, columns)
 
 
 def factor_kernel(parts, *refs):
     rows, weights, out = refs[:parts], refs[parts : parts + 4], refs[parts + 4]
-    held, gate_w, up_w, row_sem, weight_sem = refs[parts + 5 :]
-    first_copies = block_copies(rows, held, row_sem)
-    start_all(first_copies)
-    targets = [gate_w.at[0], up_w.at[0], gate_w.at[1], up_w.at[1]]
-    arrived = in_order(matrix_copies(weights, targets, weight_sem))
-    wait_all(first_copies)
+    held, row_sem = refs[parts + 5 :]
+    copies = block_copies(rows, held, row_sem)
+    start_all(copies)
+    wait_all(copies)
     for e in range(2):
-        arrived(2 * e)
-        first = dot(held[...], gate_w[e])
-        arrived(2 * e + 1)
-        second = dot(held[...], up_w[e])
+        first = dot(held[...], weights[2 * e][...])
+        second = dot(held[...], weights[2 * e + 1][...])
         sigmoid_part = jax.nn.sigmoid(first)
         out[2 * e] = (
             second * sigmoid_part * (1.0 + first * (1.0 - sigmoid_part))
@@ -181,45 +146,32 @@
     packed, factors = refs[:parts], refs[parts]
     weights = refs[parts + 1 : parts + 7]
     outs = refs[parts + 7 : 2 * parts + 7]
-    (cot, slot, grads, gate_w, up_w, down_w, cot_sem, factor_sem, weight_sem) = refs[
-        2 * parts + 7 :
-    ]
-    total_rows = slot.shape[0]
-    first_copies = block_copies(packed, cot, cot_sem)
-    start_all(first_copies)
-    order = [(2, down_w, 0), (5, down_w, 1), (0, gate_w, 0), (1, up_w, 0), (3, gate_w, 1)]
-    order += [(4, up_w, 1)]
-    arrived = in_order(
-        matrix_copies(
-            [weights[i] for i, _, _ in order], [ref.at[e] for _, ref, e in order], weight_sem
-        )
+    cot, slot, grads, cot_sem, factor_sem = refs[2 * parts + 7 :]
+    copies = block_copies(packed, cot, cot_sem)
+    factor_copy = pltpu.make_async_copy(
+        factors.at[:, pl.ds(start, slot.shape[0])], grads, factor_sem
     )
-    factor_copy = pltpu.make_async_copy(
-        factors.at[:, pl.ds(start, total_rows)], grads, factor_sem
-    )
+    start_all(copies)
     factor_copy.start()
-    wait_all(first_copies)
+    wait_all(copies)
     for e in range(2):
         table = cot[:, width:].astype(jnp.float32)
         gate = gate_column(table, 1, experts, names_ref[e])
         slot[...] = (gate * cot[:, :width].astype(jnp.float32)).astype(jnp.bfloat16)
-        arrived(e)
-        back = dot_nt(slot[...], down_w[e])
+        back = dot_nt(slot[...], weights[3 * e + 2][...])
         if e == 0:
             factor_copy.wait()
         for i in range(2):
             made = back * grads[2 * e + i].astype(jnp.float32)
             grads[2 * e + i] = made.astype(jnp.bfloat16)
-    for i in range(2, 6):
-        arrived(i)
 
     @pl.loop(0, width // tile)
     def _(n):
         columns = pl.ds(pl.multiple_of(n * tile, tile), tile)
         total = None
         for e in range(2):
-            for i, weight in enumerate((gate_w, up_w)):
-                term = dot_nt(grads[2 * e + i], weight[e, columns, :])
+            for i in range(2):
+                term = dot_nt(grads[2 * e + i], weights[3 * e + i][columns, :])
                 total = term if total is None else total + term
         write_tiles(total, outs, columns)
 
@@ -228,9 +180,11 @@
 TILE = 512
 
 
-def weight_scratch(width, inner, with_down=True):
-    shapes = [(2, width, inner), (2, width, inner), (2, inner, width)]
-    return [pltpu.VMEM(shape, jnp.bfloat16) for shape in shapes[: 3 if with_down else 2]]
+WHOLE = pl.BlockSpec(memory_space=pltpu.VMEM)
+
+
+def in_vmem(weights):
+    return [pltpu.with_memory_space_constraint(weight, pltpu.VMEM) for weight in weights]
 
 
 def cost(units, rows, width, inner, fixed):
@@ -252,17 +206,16 @@
     out = pl.pallas_call(
         functools.partial(forward_kernel, parts, experts, width, TILE),
         out_shape=[jax.ShapeDtypeStruct((count, width), jnp.bfloat16) for count in counts],
-        in_specs=[pl.BlockSpec(memory_space=pltpu.SMEM)] + [HBM] * (2 * parts + 6),
+        in_specs=[pl.BlockSpec(memory_space=pltpu.SMEM)] + [HBM] * (2 * parts) + [WHOLE] * 6,
         scratch_shapes=[
             pltpu.VMEM((total, full - width), jnp.bfloat16),
             pltpu.VMEM((total, width), jnp.bfloat16),
             pltpu.VMEM((total, 2 * inner), jnp.bfloat16),
         ]
-        + weight_scratch(width, inner)
-        + [pltpu.SemaphoreType.DMA((count,)) for count in (parts, parts, 6)],
+        + [pltpu.SemaphoreType.DMA((parts,)) for _ in range(2)],
         compiler_params=PARAMS,
         cost_estimate=cost(6, total, width, inner, 6e-6),
-    )(names, *packed, *rows, *weights)
+    )(names, *packed, *rows, *in_vmem(weights))
     return list(out)
 
 
@@ -273,13 +226,14 @@
     return pl.pallas_call(
         functools.partial(factor_kernel, parts),
         out_shape=jax.ShapeDtypeStruct((4, total, inner), jnp.bfloat16),
-        in_specs=[HBM] * (parts + 4),
-        scratch_shapes=[pltpu.VMEM((total, width), jnp.bfloat16)]
-        + weight_scratch(width, inner, False)
-        + [pltpu.SemaphoreType.DMA((count,)) for count in (parts, 4)],
+        in_specs=[HBM] * parts + [WHOLE] * 4,
+        scratch_shapes=[
+            pltpu.VMEM((total, width), jnp.bfloat16),
+            pltpu.SemaphoreType.DMA((parts,)),
+        ],
         compiler_params=PARAMS,
         cost_estimate=cost(4, total, width, inner, 5e-6),
-    )(*rows, weights[0], weights[1], weights[3], weights[4])
+    )(*rows, *in_vmem([weights[i] for i in (0, 1, 3, 4)]))
 
 
 def backward_call(names, packed, factors, start, weights, experts):
@@ -290,21 +244,17 @@
     out = pl.pallas_call(
         functools.partial(backward_kernel, parts, experts, width, TILE, start),
         out_shape=[jax.ShapeDtypeStruct((count, width), jnp.bfloat16) for count in counts],
-        in_specs=[pl.BlockSpec(memory_space=pltpu.SMEM)] + [HBM] * (parts + 7),
+        in_specs=[pl.BlockSpec(memory_space=pltpu.SMEM)] + [HBM] * (parts + 1) + [WHOLE] * 6,
         scratch_shapes=[
             pltpu.VMEM((total, full), jnp.bfloat16),
             pltpu.VMEM((total, width), jnp.bfloat16),
             pltpu.VMEM((4, total, inner), jnp.bfloat16),
-        ]
-        + weight_scratch(width, inner)
-        + [
             pltpu.SemaphoreType.DMA((parts,)),
             pltpu.SemaphoreType.DMA(()),
-            pltpu.SemaphoreType.DMA((6,)),
         ],
         compiler_params=PARAMS,
         cost_estimate=cost(6, total, width, inner, 6e-6),
-    )(names, *packed, factors, *weights)
+    )(names, *packed, factors, *in_vmem(weights))
     return list(out)
 
 
@@ -436,6 +386,7 @@
     ring.held["fall"] = {0: [fall_normal]}
     ring.gather("fall", 1)
     moved_cot = passed_along(leaving_cot, "pipe", 1)
+    moved_cot, leaving_rise = lax.optimization_barrier((moved_cot, leaving_rise))
     own = (w_gate[0, 0], w_up[0, 0], w_down[0, 0])
 
     def swapped(weight):
@@ -472,17 +423,17 @@
         own_gate, own_up, own_down = own
         other_gate = swapped(own_gate)
         heads = (head_rise, head_fall)
-        cot_in, leaving_rise, own_up, own_down, other_gate, heads, ring.names = ring.fence(
-            cot_in, leaving_rise, own_up, own_down, other_gate, heads, names
+        rise_in = entered(leaving_rise)
+        cot_in, rise_in, own_up, own_down, other_gate, heads, ring.names = ring.fence(
+            cot_in, rise_in, own_up, own_down, other_gate, heads, names
         )
         ring.gather("fall", 3)
         ring.gather("cot", 1)
-        rise_in = entered(leaving_rise)
-        rise_in, own_up, own_down = ring.fence(rise_in, own_up, own_down)
+        rise_normal = normed(rise_in.astype(jnp.float32), norm_row).astype(jnp.bfloat16)
+        rise_normal, own_up, own_down = ring.fence(rise_normal, own_up, own_down)
         ring.gather("fall", 4)
         ring.gather("cot", 2)
         other_up = swapped(own_up)
-        rise_normal = normed(rise_in.astype(jnp.float32), norm_row).astype(jnp.bfloat16)
         kept, exit_loss = exit_heads(rise_in, cot_in, *heads)
         rise_normal, kept, exit_loss, other_up, own_down = ring.fence(
             rise_normal, kept, exit_loss, other_up, own_down

time: 208 us -> 210 us (level)
  Pallas kernels: 61.6 us -> 53.4 us
  local copies, waits for them, and re-layouts: 5.07 us -> 8.67 us
  other arithmetic: 9.37 us -> 12.3 us
    ppermute x2, waiting for transfers between devices: 3.53 us -> 9.32 us  [passed_along(): return lax.ppermute(block, axis, route)]
    pallas_call x2, Pallas kernels: 26.7 us -> 21.2 us  [backward_call(): pl.pallas_call(functools.partial(backward_kernel, parts, experts, width,...]
    unnamed x84 -> x36, local copies, waits for them, and re-layouts: 1.79 us -> 7.24 us
    ppermute x37, waiting for transfers between devices: 78.5 us -> 74.3 us  [pass_on(): return lax.ppermute(block, 'ep', self.routes[way])]
    pallas_call x2, Pallas kernels: 22.3 us -> 19.6 us  [forward_call(): pl.pallas_call(functools.partial(forward_kernel, parts, experts, width, T...]
  transfers between devices with their start and end apart: 42 -> 42, of which waited for: 21 -> 18; matrix products, arithmetic and copies ran while one was open for 6% -> 7% of each run, Pallas kernels for 30% -> 26%
where the time goes in v6:
time: 210 us; the launch traced here: 209 us
  waiting for transfers between devices  83.6 us (40%)
  Pallas kernels  53.4 us (25%)
  starting transfers between devices  48.3 us (23%)
  other arithmetic  12.3 us (6%)
  local copies, waits for them, and re-layouts  8.67 us (4%)
  between operations  2.44 us (1%)
    ppermute x37, waiting for transfers between devices, pass_on(): return lax.ppermute(block, 'ep', self.routes[way])  74.3 us
    ppermute x37, starting transfers between devices, pass_on(): return lax.ppermute(block, 'ep', self.routes[way])  38.9 us
    pallas_call x2, Pallas kernels, backward_call(): pl.pallas_call(functools.partial(backward_kernel, parts, experts, width,...  21.2 us
    pallas_call x2, Pallas kernels, forward_call(): pl.pallas_call(functools.partial(forward_kernel, parts, experts, width, T...  19.6 us
    pallas_call x1, Pallas kernels, factor_call(): pl.pallas_call(functools.partial(factor_kernel, parts), out_shape=jax.Sha...  11.8 us
    ppermute x2, waiting for transfers between devices, passed_along(): return lax.ppermute(block, axis, route)  9.32 us
    ppermute x2, starting transfers between devices, passed_along(): return lax.ppermute(block, axis, route)  8.73 us
    unnamed x36, local copies, waits for them, and re-layouts  7.24 us
  transfers between devices with their start and end apart: 42, of which 18 were waited for; matrix products, arithmetic and copies ran while one was open for 7% of the time, Pallas kernels for 26%

profile of v6, /device:TPU:0, one launch (start us, length us, event | category | flops | bytes accessed | tf_op | source)
XLA Modules:
  0.0 208.8 jit_solution(6600425529695980914)
XLA Ops:
  1.1 1.2 fusion.16
  2.3 1.2 fusion.4.refs_0_
  3.5 4.4 %collective-permute-start = (bf16[96,2048]{1,0:T(8,128)(2,1)}, bf16[96,2048]{1,0:T(8,128)(2,1)S(1)}, u32[]{:S(2)}, u32[]{:S(2)}) collective-permute-start(bf16[96,2048]{1,0:T(8,128)(2,1)} %bitcast.69), channel_id=1, source_target_pairs={{0,16},{1,17},{2,18},{3,19},{4,20},{5,21},{6,22},{7,23},{8,24},{9,... | collective-permute-start | bytes 1179656 | tf_op jit(solution)/shard_map/ppermute | solution.py:17
  8.0 1.6 collective-permute-start.2
  10.1 7.2 %collective-permute-done = bf16[96,2048]{1,0:T(8,128)(2,1)S(1)} collective-permute-done((bf16[96,2048]{1,0:T(8,128)(2,1)}, bf16[96,2048]{1,0:T(8,128)(2,1)S(1)}, u32[]{:S(2)}, u32[]{:S(2)}) %collective-permute-start) | collective-permute-done | bytes 393248 | tf_op jit(solution)/shard_map/ppermute | solution.py:17
  17.3 4.3 %collective-permute-start.5 = (bf16[96,2048]{1,0:T(8,128)(2,1)}, bf16[96,2048]{1,0:T(8,128)(2,1)S(1)}, u32[]{:S(2)}, u32[]{:S(2)}) collective-permute-start(bf16[96,2048]{1,0:T(8,128)(2,1)} %bitcast.70), channel_id=1, source_target_pairs={{0,16},{1,17},{2,18},{3,19},{4,20},{5,21},{6,22},{7,23},{8,24},{9,... | collective-permute-start | bytes 1179656 | tf_op jit(solution)/shard_map/ppermute | solution.py:17
  21.6 0.8 fusion.22
  22.4 0.6 constant_dynamic-slice_fusion
  24.3 0.8 copy.16
  25.1 0.8 copy.17
  26.0 1.5 collective-permute-start.4
  28.0 2.1 %collective-permute-done.5 = bf16[96,2048]{1,0:T(8,128)(2,1)S(1)} collective-permute-done((bf16[96,2048]{1,0:T(8,128)(2,1)}, bf16[96,2048]{1,0:T(8,128)(2,1)S(1)}, u32[]{:S(2)}, u32[]{:S(2)}) %collective-permute-start.5) | collective-permute-done | bytes 393248 | tf_op jit(solution)/shard_map/ppermute | solution.py:17
  30.1 1.2 bitcast_select_fusion
  31.4 0.7 shard_map.148.refs_0_
  32.1 4.3 %collective-permute-done.4.refs_4_ = bf16[96,2048]{1,0:T(8,128)(2,1)S(1)} collective-permute-done((bf16[96,2048]{1,0:T(8,128)(2,1)S(1)}, bf16[96,2048]{1,0:T(8,128)(2,1)S(1)}, u32[]{:S(2)}, u32[]{:S(2)}) %collective-permute-start.4) | collective-permute-done | bytes 393248 | tf_op jit(solution)/shard_map/ppermute | solution.py:291
  36.4 1.2 collective-permute-done.3.refs_3_
  37.7 1.6 collective-permute-start.8
  40.4 1.5 collective-permute-start.10
  42.0 2.0 multiply_reduce_fusion
  43.9 13.2 %collective-permute-done.9.refs_5_ = bf16[96,2048]{1,0:T(8,128)(2,1)S(1)} collective-permute-done((bf16[96,2048]{1,0:T(8,128)(2,1)S(1)}, bf16[96,2048]{1,0:T(8,128)(2,1)S(1)}, u32[]{:S(2)}, u32[]{:S(2)}) %collective-permute-start.9) | collective-permute-done | bytes 393248 | tf_op jit(solution)/shard_map/ppermute | solution.py:291
  57.3 2.4 %fusion.13 = f32[96,2048]{1,0:T(8,128)} fusion(bf16[96,2048]{1,0:T(8,128)(2,1)S(1)} %get-tuple-element.214.rows_ref, bf16[1,96,2048]{2,1,0:T(8,128)(2,1)} %param.16, f32[96]{0:T(128)S(1)} %get-tuple-element.403, f32[2048]{0:T(1024)S(1)} %bitcast.67, f32[]{:T(128)} %bitcast.17, f32[96]{0:T(128)S(1)} %fusion.20, bf16[2,96,2048]{2,1,0:T(8,128)(2,1)} %param.17), kind=kLoop, calls=%fused_computation.24 | loop fusion | flops 2555904 | bytes 1975044 | tf_op jit(solution)/shard_map/add | solution.py:415
  60.2 1.6 collective-permute-start.12
  61.8 1.6 collective-permute-start.14
  63.9 0.6 maximum_bitcast_fusion
  64.5 11.7 %collective-permute-done.14.refs_8_ = bf16[48,2048]{1,0:T(8,128)(2,1)S(1)} collective-permute-done((bf16[48,2048]{1,0:T(8,128)(2,1)S(1)}, bf16[48,2048]{1,0:T(8,128)(2,1)S(1)}, u32[]{:S(2)}, u32[]{:S(2)}) %collective-permute-start.14) | collective-permute-done | bytes 196640 | tf_op jit(solution)/shard_map/ppermute | solution.py:291
  76.3 1.6 collective-permute-start.19
  78.4 0.7 collective-permute-start.16
  79.0 1.4 collective-permute-start.17
  80.4 1.6 copy-done
  82.0 1.0 copy-done.4
  83.0 1.0 copy-done.6
  84.0 1.0 copy-done.8
  85.0 1.0 copy-done.10
  86.0 11.8 %shard_map.149.refs_5_.refs_3_ = bf16[4,768,512]{2,1,0:T(8,128)(2,1)S(1)} custom-call(bf16[96,2048]{1,0:T(8,128)(2,1)S(1)} %fusion.4.refs_0_, bf16[96,2048]{1,0:T(8,128)(2,1)S(1)} %copy-done.6, bf16[96,2048]{1,0:T(8,128)(2,1)S(1)} %copy-done.4, bf16[96,2048]{1,0:T(8,128)(2,1)S(1)} %copy-done.10, bf16[96,2048]{1,0:T(8,128)(2,1)S(1)} %copy-done.8, ...), custom_call_target="tpu_custom_call" | custom-call | flops 11942451200 | bytes 12582912 | tf_op jit(solution)/shard_map/pallas_call | solution.py:226
  98.6 1.5 collective-permute-start.23
  100.1 1.6 collective-permute-start.21
  101.7 12.5 %shard_map.150 = (bf16[96,2048]{1,0:T(8,128)(2,1)S(1)}, bf16[96,2048]{1,0:T(8,128)(2,1)S(1)}, bf16[96,2048]{1,0:T(8,128)(2,1)S(1)}, bf16[96,2048]{1,0:T(8,128)(2,1)S(1)}, bf16[96,2048]{1,0:T(8,128)(2,1)S(1)}) custom-call(s32[2]{0:T(128)S(1)} %pad_add_fusion.names_ref, bf16[96,2176]{1,0:T(8,128)(2,1)S(1)} %shard_map.148.refs_0_, ...), custom_call_target="tpu_custom_call" | custom-call | flops 12639797248 | bytes 12582912 | tf_op jit(solution)/shard_map/pallas_call | solution.py:244
  114.1 3.4 %collective-permute-done.21.refs_2_ = bf16[96,2176]{1,0:T(8,128)(2,1)S(1)} collective-permute-done((bf16[96,2176]{1,0:T(8,128)(2,1)S(1)}, bf16[96,2176]{1,0:T(8,128)(2,1)S(1)}, u32[]{:S(2)}, u32[]{:S(2)}) %collective-permute-start.21) | collective-permute-done | bytes 417824 | tf_op jit(solution)/shard_map/ppermute | solution.py:291
  117.6 1.6 collective-permute-start.24
  119.6 8.8 %shard_map.151 = (bf16[96,2048]{1,0:T(8,128)(2,1)S(1)}, bf16[96,2048]{1,0:T(8,128)(2,1)S(1)}, bf16[96,2048]{1,0:T(8,128)(2,1)S(1)}) custom-call(s32[2]{0:T(128)S(1)} %pad_add_fusion.names_ref, bf16[96,2176]{1,0:T(8,128)(2,1)S(1)} %collective-permute-done.16.refs_0_, bf16[96,2176]{1,0:T(8,128)(2,1)S(1)} %collective-permute-done.17.refs_1_, ...), custom_call_target="tpu_custom_call" | custom-call | flops 10223878144 | bytes 12582912 | tf_op jit(solution)/shard_map/pallas_call | solution.py:244
  128.4 1.6 collective-permute-start.27
  130.5 11.6 %shard_map.152 = (bf16[96,2048]{1,0:T(8,128)(2,1)S(1)}, bf16[96,2048]{1,0:T(8,128)(2,1)S(1)}, bf16[96,2048]{1,0:T(8,128)(2,1)S(1)}, bf16[96,2048]{1,0:T(8,128)(2,1)S(1)}, bf16[96,2048]{1,0:T(8,128)(2,1)S(1)}) custom-call(s32[2]{0:T(128)S(1)} %pad_add_fusion.names_ref, bf16[96,2176]{1,0:T(8,128)(2,1)S(1)} %shard_map.148.refs_0_, ...), custom_call_target="tpu_custom_call" | custom-call | flops 12639797248 | bytes 12582912 | tf_op jit(solution)/shard_map/pallas_call | solution.py:206
  142.2 1.6 collective-permute-start.29
  144.3 8.0 %shard_map.153 = (bf16[96,2048]{1,0:T(8,128)(2,1)S(1)}, bf16[96,2048]{1,0:T(8,128)(2,1)S(1)}, bf16[96,2048]{1,0:T(8,128)(2,1)S(1)}) custom-call(s32[2]{0:T(128)S(1)} %pad_add_fusion.names_ref, bf16[96,2176]{1,0:T(8,128)(2,1)S(1)} %collective-permute-done.16.refs_0_, bf16[96,2176]{1,0:T(8,128)(2,1)S(1)} %collective-permute-done.17.refs_1_, ...), custom_call_target="tpu_custom_call" | custom-call | flops 10223878144 | bytes 12582912 | tf_op jit(solution)/shard_map/pallas_call | solution.py:206
  152.5 1.6 collective-permute-start.31
  154.1 0.6 collective-permute-start.30
  154.7 1.6 collective-permute-start.33
  156.8 7.7 %collective-permute-done.33 = bf16[48,2048]{1,0:T(8,128)(2,1)S(1)} collective-permute-done((bf16[48,2048]{1,0:T(8,128)(2,1)S(1)}, bf16[48,2048]{1,0:T(8,128)(2,1)S(1)}, u32[]{:S(2)}, u32[]{:S(2)}) %collective-permute-start.33) | collective-permute-done | bytes 196640 | tf_op jit(solution)/shard_map/ppermute | solution.py:291
  164.5 1.4 collective-permute-done.32
  166.2 1.6 collective-permute-start.35
  168.5 1.6 collective-permute-start.37
  170.6 6.2 %collective-permute-done.35 = bf16[96,2048]{1,0:T(8,128)(2,1)S(1)} collective-permute-done((bf16[96,2048]{1,0:T(8,128)(2,1)S(1)}, bf16[96,2048]{1,0:T(8,128)(2,1)S(1)}, u32[]{:S(2)}, u32[]{:S(2)}) %collective-permute-start.35) | collective-permute-done | bytes 393248 | tf_op jit(solution)/shard_map/ppermute | solution.py:291
  176.8 1.4 collective-permute-done.34
  178.2 4.5 %collective-permute-done.37 = bf16[96,2048]{1,0:T(8,128)(2,1)S(1)} collective-permute-done((bf16[96,2048]{1,0:T(8,128)(2,1)S(1)}, bf16[96,2048]{1,0:T(8,128)(2,1)S(1)}, u32[]{:S(2)}, u32[]{:S(2)}) %collective-permute-start.37) | collective-permute-done | bytes 393248 | tf_op jit(solution)/shard_map/ppermute | solution.py:291
  182.7 1.7 collective-permute-done.36
  184.5 1.8 collective-permute-start.39
  187.1 1.1 fusion.15
  188.3 7.2 %collective-permute-done.39 = bf16[96,2048]{1,0:T(8,128)(2,1)S(1)} collective-permute-done((bf16[96,2048]{1,0:T(8,128)(2,1)S(1)}, bf16[96,2048]{1,0:T(8,128)(2,1)S(1)}, u32[]{:S(2)}, u32[]{:S(2)}) %collective-permute-start.39) | collective-permute-done | bytes 393248 | tf_op jit(solution)/shard_map/ppermute | solution.py:291
  195.4 2.3 %collective-permute-done.38 = bf16[96,2048]{1,0:T(8,128)(2,1)S(1)} collective-permute-done((bf16[96,2048]{1,0:T(8,128)(2,1)S(1)}, bf16[96,2048]{1,0:T(8,128)(2,1)S(1)}, u32[]{:S(2)}, u32[]{:S(2)}) %collective-permute-start.38) | collective-permute-done | bytes 393248 | tf_op jit(solution)/shard_map/ppermute | solution.py:291
  197.9 1.4 collective-permute-start.41
  199.4 0.7 collective-permute-start.40
  200.1 5.6 %collective-permute-done.41 = bf16[96,2048]{1,0:T(8,128)(2,1)S(1)} collective-permute-done((bf16[96,2048]{1,0:T(8,128)(2,1)S(1)}, bf16[96,2048]{1,0:T(8,128)(2,1)S(1)}, u32[]{:S(2)}, u32[]{:S(2)}) %collective-permute-start.41) | collective-permute-done | bytes 393248 | tf_op jit(solution)/shard_map/ppermute | solution.py:291
  205.7 2.1 %collective-permute-done.40 = bf16[96,2048]{1,0:T(8,128)(2,1)S(1)} collective-permute-done((bf16[96,2048]{1,0:T(8,128)(2,1)S(1)}, bf16[96,2048]{1,0:T(8,128)(2,1)S(1)}, u32[]{:S(2)}, u32[]{:S(2)}) %collective-permute-start.40) | collective-permute-done | bytes 393248 | tf_op jit(solution)/shard_map/ppermute | solution.py:291
  207.8 1.0 fusion.19
  (99 shorter events, 10.0 us)
Async XLA Ops:
  0.6 37.0 %collective-permute-start.6 = (bf16[2048,512]{1,0:T(8,128)(2,1)}, bf16[2048,512]{1,0:T(8,128)(2,1)}, u32[]{:S(2)}, u32[]{:S(2)}) collective-permute-start(bf16[2048,512]{1,0:T(8,128)(2,1)} %bitcast.50), channel_id=1, source_target_pairs={{0,1},{1,0},{2,3},{3,2},{4,5},{5,4},{6,7},{7,6},{8,9},{9,8},{10,11... | collective-permute-start | bytes 6291464 | tf_op jit(solution)/shard_map/ppermute | solution.py:393
  3.5 38.5 %copy-start.15 = (f32[1,2048]{1,0:T(1,128)S(1)}, f32[1,2048]{1,0:T(1,128)}, u32[]{:S(2)}) copy-start(f32[1,2048]{1,0:T(1,128)} %param.18) | copy-start | bytes 24580
  3.5 38.4 %copy-start.16 = (f32[1,2048]{1,0:T(1,128)S(1)}, f32[1,2048]{1,0:T(1,128)}, u32[]{:S(2)}) copy-start(f32[1,2048]{1,0:T(1,128)} %param.19) | copy-start | bytes 24580
  3.5 13.7 %collective-permute-start = (bf16[96,2048]{1,0:T(8,128)(2,1)}, bf16[96,2048]{1,0:T(8,128)(2,1)S(1)}, u32[]{:S(2)}, u32[]{:S(2)}) collective-permute-start(bf16[96,2048]{1,0:T(8,128)(2,1)} %bitcast.69), channel_id=1, source_target_pairs={{0,16},{1,17},{2,18},{3,19},{4,20},{5,21},{6,22},{7,23},{8,24},{9,... | collective-permute-start | bytes 1179656 | tf_op jit(solution)/shard_map/ppermute | solution.py:17
  8.0 18.0 %collective-permute-start.2 = (bf16[96,2048]{1,0:T(8,128)(2,1)S(1)}, bf16[96,2048]{1,0:T(8,128)(2,1)S(1)}, u32[]{:S(2)}, u32[]{:S(2)}) collective-permute-start(bf16[96,2048]{1,0:T(8,128)(2,1)S(1)} %fusion.4.refs_0_), channel_id=1, source_target_pairs={{4,0},{5,1},{8,4},{9,5},{12,8},{13,9},{14,12},{15,13},{10,14},{11,... | collective-permute-start | bytes 1179656 | tf_op jit(solution)/shard_map/ppermute | solution.py:291
  9.5 17.9 %collective-permute-start.1 = (bf16[96,2048]{1,0:T(8,128)(2,1)S(1)}, bf16[96,2048]{1,0:T(8,128)(2,1)S(1)}, u32[]{:S(2)}, u32[]{:S(2)}) collective-permute-start(bf16[96,2048]{1,0:T(8,128)(2,1)S(1)} %fusion.4.refs_0_), channel_id=1, source_target_pairs={{0,4},{1,5},{4,8},{5,9},{8,12},{9,13},{12,14},{13,15},{14,10},{15,... | collective-permute-start | bytes 1179656 | tf_op jit(solution)/shard_map/ppermute | solution.py:291
  17.3 12.8 %collective-permute-start.5 = (bf16[96,2048]{1,0:T(8,128)(2,1)}, bf16[96,2048]{1,0:T(8,128)(2,1)S(1)}, u32[]{:S(2)}, u32[]{:S(2)}) collective-permute-start(bf16[96,2048]{1,0:T(8,128)(2,1)} %bitcast.70), channel_id=1, source_target_pairs={{0,16},{1,17},{2,18},{3,19},{4,20},{5,21},{6,22},{7,23},{8,24},{9,... | collective-permute-start | bytes 1179656 | tf_op jit(solution)/shard_map/ppermute | solution.py:17
  26.0 13.7 %copy-start.3 = (bf16[96,2048]{1,0:T(8,128)(2,1)}, bf16[96,2048]{1,0:T(8,128)(2,1)S(1)}, u32[]{:S(2)}) copy-start(bf16[96,2048]{1,0:T(8,128)(2,1)S(1)} %collective-permute-done.2.refs_2_) | copy-start | bytes 1179652
  26.0 10.5 %collective-permute-start.4 = (bf16[96,2048]{1,0:T(8,128)(2,1)S(1)}, bf16[96,2048]{1,0:T(8,128)(2,1)S(1)}, u32[]{:S(2)}, u32[]{:S(2)}) collective-permute-start(bf16[96,2048]{1,0:T(8,128)(2,1)S(1)} %collective-permute-done.2.refs_2_), channel_id=1, source_target_pairs={{4,0},{5,1},{8,4},{9,5},{12,8},{13,9},{14,12},{15,13},{10,14},{11,... | collective-permute-start | bytes 1179656 | tf_op jit(solution)/shard_map/ppermute | solution.py:291
  27.5 12.2 %copy-start.5 = (bf16[96,2048]{1,0:T(8,128)(2,1)}, bf16[96,2048]{1,0:T(8,128)(2,1)S(1)}, u32[]{:S(2)}) copy-start(bf16[96,2048]{1,0:T(8,128)(2,1)S(1)} %collective-permute-done.1.refs_1_) | copy-start | bytes 1179652
  27.5 10.2 %collective-permute-start.3 = (bf16[96,2048]{1,0:T(8,128)(2,1)S(1)}, bf16[96,2048]{1,0:T(8,128)(2,1)S(1)}, u32[]{:S(2)}, u32[]{:S(2)}) collective-permute-start(bf16[96,2048]{1,0:T(8,128)(2,1)S(1)} %collective-permute-done.1.refs_1_), channel_id=1, source_target_pairs={{0,4},{1,5},{4,8},{5,9},{8,12},{9,13},{12,14},{13,15},{14,10},{15,... | collective-permute-start | bytes 1179656 | tf_op jit(solution)/shard_map/ppermute | solution.py:291
  31.3 25.9 %copy-start.12 = (bf16[96,2048]{1,0:T(8,128)(2,1)}, bf16[96,2048]{1,0:T(8,128)(2,1)S(1)}, u32[]{:S(2)}) copy-start(bf16[96,2048]{1,0:T(8,128)(2,1)S(1)} %get-tuple-element.194) | copy-start | bytes 1179652
  36.4 20.8 %copy-start.7 = (bf16[96,2048]{1,0:T(8,128)(2,1)}, bf16[96,2048]{1,0:T(8,128)(2,1)S(1)}, u32[]{:S(2)}) copy-start(bf16[96,2048]{1,0:T(8,128)(2,1)S(1)} %collective-permute-done.4.refs_4_) | copy-start | bytes 1179652
  37.7 19.5 %copy-start.9 = (bf16[96,2048]{1,0:T(8,128)(2,1)}, bf16[96,2048]{1,0:T(8,128)(2,1)S(1)}, u32[]{:S(2)}) copy-start(bf16[96,2048]{1,0:T(8,128)(2,1)S(1)} %collective-permute-done.3.refs_3_) | copy-start | bytes 1179652
  37.7 19.5 %collective-permute-start.8 = (bf16[96,2176]{1,0:T(8,128)(2,1)S(1)}, bf16[96,2176]{1,0:T(8,128)(2,1)S(1)}, u32[]{:S(2)}, u32[]{:S(2)}) collective-permute-start(bf16[96,2176]{1,0:T(8,128)(2,1)S(1)} %shard_map.148.refs_0_), channel_id=1, source_target_pairs={{4,0},{5,1},{8,4},{9,5},{12,8},{13,9},{14,12},{15,13},{10,14},{11,... | collective-permute-start | bytes 1253384 | tf_op jit(solution)/shard_map/ppermute | solution.py:291
  39.3 17.9 %collective-permute-start.7 = (bf16[96,2176]{1,0:T(8,128)(2,1)S(1)}, bf16[96,2176]{1,0:T(8,128)(2,1)S(1)}, u32[]{:S(2)}, u32[]{:S(2)}) collective-permute-start(bf16[96,2176]{1,0:T(8,128)(2,1)S(1)} %shard_map.148.refs_0_), channel_id=1, source_target_pairs={{0,4},{1,5},{4,8},{5,9},{8,12},{9,13},{12,14},{13,15},{14,10},{15,... | collective-permute-start | bytes 1253384 | tf_op jit(solution)/shard_map/ppermute | solution.py:291
  39.9 17.3 %collective-permute-start.9 = (bf16[96,2048]{1,0:T(8,128)(2,1)S(1)}, bf16[96,2048]{1,0:T(8,128)(2,1)S(1)}, u32[]{:S(2)}, u32[]{:S(2)}) collective-permute-start(bf16[96,2048]{1,0:T(8,128)(2,1)S(1)} %collective-permute-done.3.refs_3_), channel_id=1, source_target_pairs={{0,4},{1,5},{4,8},{5,9},{8,12},{9,13},{12,14},{13,15},{14,10},{15,... | collective-permute-start | bytes 1179656 | tf_op jit(solution)/shard_map/ppermute | solution.py:291
  40.4 16.7 %collective-permute-start.10 = (bf16[96,2048]{1,0:T(8,128)(2,1)S(1)}, bf16[96,2048]{1,0:T(8,128)(2,1)S(1)}, u32[]{:S(2)}, u32[]{:S(2)}) collective-permute-start(bf16[96,2048]{1,0:T(8,128)(2,1)S(1)} %collective-permute-done.4.refs_4_), channel_id=1, source_target_pairs={{4,0},{5,1},{8,4},{9,5},{12,8},{13,9},{14,12},{15,13},{10,14},{11,... | collective-permute-start | bytes 1179656 | tf_op jit(solution)/shard_map/ppermute | solution.py:291
  57.2 19.0 %collective-permute-start.15 = (bf16[2048,512]{1,0:T(8,128)(2,1)}, bf16[2048,512]{1,0:T(8,128)(2,1)}, u32[]{:S(2)}, u32[]{:S(2)}) collective-permute-start(bf16[2048,512]{1,0:T(8,128)(2,1)} %bitcast.9.refs_10_.refs_7_.refs_5_.refs_11_), channel_id=1, source_target_pairs={{0,1},{1,0},{2,3},{3,2},{4,5},{5,4},{6,7},{7,6},{8,9},{9,8},{10,11... | collective-permute-start | bytes 6291464 | tf_op jit(solution)/shard_map/ppermute | solution.py:393
  59.8 16.4 %collective-permute-start.11 = (bf16[96,2176]{1,0:T(8,128)(2,1)S(1)}, bf16[96,2176]{1,0:T(8,128)(2,1)}, u32[]{:S(2)}, u32[]{:S(2)}) collective-permute-start(bf16[96,2176]{1,0:T(8,128)(2,1)S(1)} %collective-permute-done.7.refs_1_), channel_id=1, source_target_pairs={{0,4},{1,5},{4,8},{5,9},{8,12},{9,13},{12,14},{13,15},{14,10},{15,... | collective-permute-start | bytes 1253384 | tf_op jit(solution)/shard_map/ppermute | solution.py:291
  60.2 16.0 %collective-permute-start.12 = (bf16[96,2176]{1,0:T(8,128)(2,1)S(1)}, bf16[96,2176]{1,0:T(8,128)(2,1)}, u32[]{:S(2)}, u32[]{:S(2)}) collective-permute-start(bf16[96,2176]{1,0:T(8,128)(2,1)S(1)} %collective-permute-done.8.refs_2_), channel_id=1, source_target_pairs={{4,0},{5,1},{8,4},{9,5},{12,8},{13,9},{14,12},{15,13},{10,14},{11,... | collective-permute-start | bytes 1253384 | tf_op jit(solution)/shard_map/ppermute | solution.py:291
  61.8 14.3 %collective-permute-start.14 = (bf16[48,2048]{1,0:T(8,128)(2,1)S(1)}, bf16[48,2048]{1,0:T(8,128)(2,1)S(1)}, u32[]{:S(2)}, u32[]{:S(2)}) collective-permute-start(bf16[48,2048]{1,0:T(8,128)(2,1)S(1)} %slice.47), channel_id=1, source_target_pairs={{4,0},{5,1},{8,4},{9,5},{12,8},{13,9},{14,12},{15,13},{10,14},{11,... | collective-permute-start | bytes 589832 | tf_op jit(solution)/shard_map/ppermute | solution.py:291
  63.5 12.7 %collective-permute-start.13 = (bf16[48,2048]{1,0:T(8,128)(2,1)S(1)}, bf16[48,2048]{1,0:T(8,128)(2,1)S(1)}, u32[]{:S(2)}, u32[]{:S(2)}) collective-permute-start(bf16[48,2048]{1,0:T(8,128)(2,1)S(1)} %slice.46), channel_id=1, source_target_pairs={{0,4},{1,5},{4,8},{5,9},{8,12},{9,13},{12,14},{13,15},{14,10},{15,... | collective-permute-start | bytes 589832 | tf_op jit(solution)/shard_map/ppermute | solution.py:291
  76.2 21.9 %collective-permute-start.20 = (bf16[512,2048]{1,0:T(8,128)(2,1)}, bf16[512,2048]{1,0:T(8,128)(2,1)S(1)}, u32[]{:S(2)}, u32[]{:S(2)}) collective-permute-start(bf16[512,2048]{1,0:T(8,128)(2,1)} %bitcast.56), channel_id=1, source_target_pairs={{0,1},{1,0},{2,3},{3,2},{4,5},{5,4},{6,7},{7,6},{8,9},{9,8},{10,11... | collective-permute-start | bytes 6291464 | tf_op jit(solution)/shard_map/ppermute | solution.py:393
  76.3 21.5 %collective-permute-start.19 = (bf16[96,2048]{1,0:T(8,128)(2,1)S(1)}, bf16[96,2048]{1,0:T(8,128)(2,1)S(1)}, u32[]{:S(2)}, u32[]{:S(2)}) collective-permute-start(bf16[96,2048]{1,0:T(8,128)(2,1)S(1)} %get-tuple-element.286.refs_5_), channel_id=1, source_target_pairs={{4,0},{5,1},{8,4},{9,5},{12,8},{13,9},{14,12},{15,13},{10,14},{11,... | collective-permute-start | bytes 1179656 | tf_op jit(solution)/shard_map/ppermute | solution.py:291
  77.9 19.9 %collective-permute-start.18 = (bf16[96,2048]{1,0:T(8,128)(2,1)S(1)}, bf16[96,2048]{1,0:T(8,128)(2,1)S(1)}, u32[]{:S(2)}, u32[]{:S(2)}) collective-permute-start(bf16[96,2048]{1,0:T(8,128)(2,1)S(1)} %get-tuple-element.286.refs_5_), channel_id=1, source_target_pairs={{0,4},{1,5},{4,8},{5,9},{8,12},{9,13},{12,14},{13,15},{14,10},{15,... | collective-permute-start | bytes 1179656 | tf_op jit(solution)/shard_map/ppermute | solution.py:291
  78.4 19.7 %collective-permute-start.16 = (bf16[96,2176]{1,0:T(8,128)(2,1)}, bf16[96,2176]{1,0:T(8,128)(2,1)S(1)}, u32[]{:S(2)}, u32[]{:S(2)}) collective-permute-start(bf16[96,2176]{1,0:T(8,128)(2,1)} %collective-permute-done.11.refs_3_), channel_id=1, source_target_pairs={{0,4},{1,5},{4,8},{5,9},{8,12},{9,13},{12,14},{13,15},{14,10},{15,... | collective-permute-start | bytes 1253384 | tf_op jit(solution)/shard_map/ppermute | solution.py:291
  79.0 19.0 %collective-permute-start.17 = (bf16[96,2176]{1,0:T(8,128)(2,1)}, bf16[96,2176]{1,0:T(8,128)(2,1)S(1)}, u32[]{:S(2)}, u32[]{:S(2)}) collective-permute-start(bf16[96,2176]{1,0:T(8,128)(2,1)} %collective-permute-done.12.refs_4_), channel_id=1, source_target_pairs={{4,0},{5,1},{8,4},{9,5},{12,8},{13,9},{14,12},{15,13},{10,14},{11,... | collective-permute-start | bytes 1253384 | tf_op jit(solution)/shard_map/ppermute | solution.py:291
  80.4 1.6 copy-start
  82.0 1.0 copy-start.4
  83.0 1.0 copy-start.6
  84.0 1.0 copy-start.8
  85.0 1.0 copy-start.10
  86.0 15.7 %copy-start.1 = (bf16[1,1,2048,512]{3,2,1,0:T(8,128)(2,1)S(1)}, bf16[1,1,2048,512]{3,2,1,0:T(8,128)(2,1)}, u32[]{:S(2)}) copy-start(bf16[1,1,2048,512]{3,2,1,0:T(8,128)(2,1)} %param.20) | copy-start | bytes 6291460
  86.0 15.7 %copy-start.2 = (bf16[1,1,512,2048]{3,2,1,0:T(8,128)(2,1)S(1)}, bf16[1,1,512,2048]{3,2,1,0:T(8,128)(2,1)}, u32[]{:S(2)}) copy-start(bf16[1,1,512,2048]{3,2,1,0:T(8,128)(2,1)} %param.22) | copy-start | bytes 6291460
  98.0 16.1 %collective-permute-start.22 = (bf16[96,2048]{1,0:T(8,128)(2,1)S(1)}, bf16[96,2048]{1,0:T(8,128)(2,1)S(1)}, u32[]{:S(2)}, u32[]{:S(2)}) collective-permute-start(bf16[96,2048]{1,0:T(8,128)(2,1)S(1)} %collective-permute-done.18.refs_6_), channel_id=1, source_target_pairs={{0,4},{1,5},{4,8},{5,9},{8,12},{9,13},{12,14},{13,15},{14,10},{15,... | collective-permute-start | bytes 1179656 | tf_op jit(solution)/shard_map/ppermute | solution.py:291
  98.6 15.6 %collective-permute-start.23 = (bf16[96,2048]{1,0:T(8,128)(2,1)S(1)}, bf16[96,2048]{1,0:T(8,128)(2,1)S(1)}, u32[]{:S(2)}, u32[]{:S(2)}) collective-permute-start(bf16[96,2048]{1,0:T(8,128)(2,1)S(1)} %collective-permute-done.19.refs_7_), channel_id=1, source_target_pairs={{4,0},{5,1},{8,4},{9,5},{12,8},{13,9},{14,12},{15,13},{10,14},{11,... | collective-permute-start | bytes 1179656 | tf_op jit(solution)/shard_map/ppermute | solution.py:291
  100.1 17.5 %collective-permute-start.21 = (bf16[96,2176]{1,0:T(8,128)(2,1)S(1)}, bf16[96,2176]{1,0:T(8,128)(2,1)S(1)}, u32[]{:S(2)}, u32[]{:S(2)}) collective-permute-start(bf16[96,2176]{1,0:T(8,128)(2,1)S(1)} %collective-permute-done.17.refs_1_), channel_id=1, source_target_pairs={{4,0},{5,1},{8,4},{9,5},{12,8},{13,9},{14,12},{15,13},{10,14},{11,... | collective-permute-start | bytes 1253384 | tf_op jit(solution)/shard_map/ppermute | solution.py:291
  117.6 10.8 %collective-permute-start.24 = (bf16[96,2048]{1,0:T(8,128)(2,1)S(1)}, bf16[96,2048]{1,0:T(8,128)(2,1)S(1)}, u32[]{:S(2)}, u32[]{:S(2)}) collective-permute-start(bf16[96,2048]{1,0:T(8,128)(2,1)S(1)} %collective-permute-done.22.refs_8_), channel_id=1, source_target_pairs={{0,4},{1,5},{4,8},{5,9},{8,12},{9,13},{12,14},{13,15},{14,10},{15,... | collective-permute-start | bytes 1179656 | tf_op jit(solution)/shard_map/ppermute | solution.py:291
  119.2 9.2 %collective-permute-start.25 = (bf16[96,2048]{1,0:T(8,128)(2,1)S(1)}, bf16[96,2048]{1,0:T(8,128)(2,1)S(1)}, u32[]{:S(2)}, u32[]{:S(2)}) collective-permute-start(bf16[96,2048]{1,0:T(8,128)(2,1)S(1)} %collective-permute-done.23.refs_9_), channel_id=1, source_target_pairs={{4,0},{5,1},{8,4},{9,5},{12,8},{13,9},{14,12},{15,13},{10,14},{11,... | collective-permute-start | bytes 1179656 | tf_op jit(solution)/shard_map/ppermute | solution.py:291
  128.4 13.7 %collective-permute-start.27 = (bf16[96,2048]{1,0:T(8,128)(2,1)S(1)}, bf16[96,2048]{1,0:T(8,128)(2,1)S(1)}, u32[]{:S(2)}, u32[]{:S(2)}) collective-permute-start(bf16[96,2048]{1,0:T(8,128)(2,1)S(1)} %get-tuple-element.305), channel_id=1, source_target_pairs={{4,0},{5,1},{8,4},{9,5},{12,8},{13,9},{14,12},{15,13},{10,14},{11,... | collective-permute-start | bytes 1179656 | tf_op jit(solution)/shard_map/ppermute | solution.py:291
  130.0 12.1 %collective-permute-start.26 = (bf16[96,2048]{1,0:T(8,128)(2,1)S(1)}, bf16[96,2048]{1,0:T(8,128)(2,1)S(1)}, u32[]{:S(2)}, u32[]{:S(2)}) collective-permute-start(bf16[96,2048]{1,0:T(8,128)(2,1)S(1)} %collective-permute-done.24.refs_3_), channel_id=1, source_target_pairs={{0,4},{1,5},{4,8},{5,9},{8,12},{9,13},{12,14},{13,15},{14,10},{15,... | collective-permute-start | bytes 1179656 | tf_op jit(solution)/shard_map/ppermute | solution.py:291
  142.2 10.1 %collective-permute-start.29 = (bf16[96,2048]{1,0:T(8,128)(2,1)S(1)}, bf16[96,2048]{1,0:T(8,128)(2,1)S(1)}, u32[]{:S(2)}, u32[]{:S(2)}) collective-permute-start(bf16[96,2048]{1,0:T(8,128)(2,1)S(1)} %add_convert_fusion.8), channel_id=1, source_target_pairs={{4,0},{5,1},{8,4},{9,5},{12,8},{13,9},{14,12},{15,13},{10,14},{11,... | collective-permute-start | bytes 1179656 | tf_op jit(solution)/shard_map/ppermute | solution.py:291
  143.8 8.5 %collective-permute-start.28 = (bf16[96,2048]{1,0:T(8,128)(2,1)S(1)}, bf16[96,2048]{1,0:T(8,128)(2,1)S(1)}, u32[]{:S(2)}, u32[]{:S(2)}) collective-permute-start(bf16[96,2048]{1,0:T(8,128)(2,1)S(1)} %get-tuple-element.325), channel_id=1, source_target_pairs={{0,4},{1,5},{4,8},{5,9},{8,12},{9,13},{12,14},{13,15},{14,10},{15,... | collective-permute-start | bytes 1179656 | tf_op jit(solution)/shard_map/ppermute | solution.py:291
  152.5 13.5 %collective-permute-start.31 = (bf16[96,2048]{1,0:T(8,128)(2,1)S(1)}, bf16[96,2048]{1,0:T(8,128)(2,1)S(1)}, u32[]{:S(2)}, u32[]{:S(2)}) collective-permute-start(bf16[96,2048]{1,0:T(8,128)(2,1)S(1)} %add_convert_fusion.6), channel_id=1, source_target_pairs={{4,0},{5,1},{8,4},{9,5},{12,8},{13,9},{14,12},{15,13},{10,14},{11,... | collective-permute-start | bytes 1179656 | tf_op jit(solution)/shard_map/ppermute | solution.py:291
  154.1 11.8 %collective-permute-start.30 = (bf16[96,2048]{1,0:T(8,128)(2,1)S(1)}, bf16[96,2048]{1,0:T(8,128)(2,1)S(1)}, u32[]{:S(2)}, u32[]{:S(2)}) collective-permute-start(bf16[96,2048]{1,0:T(8,128)(2,1)S(1)} %add_convert_fusion.7), channel_id=1, source_target_pairs={{0,4},{1,5},{4,8},{5,9},{8,12},{9,13},{12,14},{13,15},{14,10},{15,... | collective-permute-start | bytes 1179656 | tf_op jit(solution)/shard_map/ppermute | solution.py:291
  154.7 9.8 %collective-permute-start.33 = (bf16[48,2048]{1,0:T(8,128)(2,1)S(1)}, bf16[48,2048]{1,0:T(8,128)(2,1)S(1)}, u32[]{:S(2)}, u32[]{:S(2)}) collective-permute-start(bf16[48,2048]{1,0:T(8,128)(2,1)S(1)} %get-tuple-element.408), channel_id=1, source_target_pairs={{4,0},{5,1},{8,4},{9,5},{12,8},{13,9},{14,12},{15,13},{10,14},{11,... | collective-permute-start | bytes 589832 | tf_op jit(solution)/shard_map/ppermute | solution.py:291
  156.3 9.6 %collective-permute-start.32 = (bf16[48,2048]{1,0:T(8,128)(2,1)S(1)}, bf16[48,2048]{1,0:T(8,128)(2,1)S(1)}, u32[]{:S(2)}, u32[]{:S(2)}) collective-permute-start(bf16[48,2048]{1,0:T(8,128)(2,1)S(1)} %get-tuple-element.409), channel_id=1, source_target_pairs={{0,4},{1,5},{4,8},{5,9},{8,12},{9,13},{12,14},{13,15},{14,10},{15,... | collective-permute-start | bytes 589832 | tf_op jit(solution)/shard_map/ppermute | solution.py:291
  166.2 10.6 %collective-permute-start.35 = (bf16[96,2048]{1,0:T(8,128)(2,1)S(1)}, bf16[96,2048]{1,0:T(8,128)(2,1)S(1)}, u32[]{:S(2)}, u32[]{:S(2)}) collective-permute-start(bf16[96,2048]{1,0:T(8,128)(2,1)S(1)} %add_convert_fusion.4), channel_id=1, source_target_pairs={{4,0},{5,1},{8,4},{9,5},{12,8},{13,9},{14,12},{15,13},{10,14},{11,... | collective-permute-start | bytes 1179656 | tf_op jit(solution)/shard_map/ppermute | solution.py:291
  167.9 18.9 %copy-start.11 = (bf16[1,96,2048]{2,1,0:T(8,128)(2,1)S(1)}, bf16[1,96,2048]{2,1,0:T(8,128)(2,1)}, u32[]{:S(2)}) copy-start(bf16[1,96,2048]{2,1,0:T(8,128)(2,1)} %param.16) | copy-start | bytes 1179652
  167.9 10.3 %collective-permute-start.34 = (bf16[96,2048]{1,0:T(8,128)(2,1)S(1)}, bf16[96,2048]{1,0:T(8,128)(2,1)S(1)}, u32[]{:S(2)}, u32[]{:S(2)}) collective-permute-start(bf16[96,2048]{1,0:T(8,128)(2,1)S(1)} %add_convert_fusion.5), channel_id=1, source_target_pairs={{0,4},{1,5},{4,8},{5,9},{8,12},{9,13},{12,14},{13,15},{14,10},{15,... | collective-permute-start | bytes 1179656 | tf_op jit(solution)/shard_map/ppermute | solution.py:291
  168.5 14.2 %collective-permute-start.37 = (bf16[96,2048]{1,0:T(8,128)(2,1)S(1)}, bf16[96,2048]{1,0:T(8,128)(2,1)S(1)}, u32[]{:S(2)}, u32[]{:S(2)}) collective-permute-start(bf16[96,2048]{1,0:T(8,128)(2,1)S(1)} %pad_maximum_fusion.1), channel_id=1, source_target_pairs={{4,0},{5,1},{8,4},{9,5},{12,8},{13,9},{14,12},{15,13},{10,14},{11,... | collective-permute-start | bytes 1179656 | tf_op jit(solution)/shard_map/ppermute | solution.py:291
  170.1 17.0 %copy-start.14 = (f32[96,2048]{1,0:T(8,128)S(1)}, f32[96,2048]{1,0:T(8,128)}, u32[]{:S(2)}) copy-start(f32[96,2048]{1,0:T(8,128)} %fusion.13) | copy-start | bytes 2359300
  170.1 14.3 %collective-permute-start.36 = (bf16[96,2048]{1,0:T(8,128)(2,1)S(1)}, bf16[96,2048]{1,0:T(8,128)(2,1)S(1)}, u32[]{:S(2)}, u32[]{:S(2)}) collective-permute-start(bf16[96,2048]{1,0:T(8,128)(2,1)S(1)} %pad_maximum_fusion), channel_id=1, source_target_pairs={{0,4},{1,5},{4,8},{5,9},{8,12},{9,13},{12,14},{13,15},{14,10},{15,... | collective-permute-start | bytes 1179656 | tf_op jit(solution)/shard_map/ppermute | solution.py:291
  184.5 10.9 %collective-permute-start.39 = (bf16[96,2048]{1,0:T(8,128)(2,1)S(1)}, bf16[96,2048]{1,0:T(8,128)(2,1)S(1)}, u32[]{:S(2)}, u32[]{:S(2)}) collective-permute-start(bf16[96,2048]{1,0:T(8,128)(2,1)S(1)} %add_convert_fusion.2), channel_id=1, source_target_pairs={{4,0},{5,1},{8,4},{9,5},{12,8},{13,9},{14,12},{15,13},{10,14},{11,... | collective-permute-start | bytes 1179656 | tf_op jit(solution)/shard_map/ppermute | solution.py:291
  186.4 11.4 %collective-permute-start.38 = (bf16[96,2048]{1,0:T(8,128)(2,1)S(1)}, bf16[96,2048]{1,0:T(8,128)(2,1)S(1)}, u32[]{:S(2)}, u32[]{:S(2)}) collective-permute-start(bf16[96,2048]{1,0:T(8,128)(2,1)S(1)} %add_convert_fusion.3), channel_id=1, source_target_pairs={{0,4},{1,5},{4,8},{5,9},{8,12},{9,13},{12,14},{13,15},{14,10},{15,... | collective-permute-start | bytes 1179656 | tf_op jit(solution)/shard_map/ppermute | solution.py:291
  187.1 20.7 %copy-start.13 = (bf16[96,2048]{1,0:T(8,128)(2,1)S(1)}, bf16[96,2048]{1,0:T(8,128)(2,1)}, u32[]{:S(2)}) copy-start(bf16[96,2048]{1,0:T(8,128)(2,1)} %copy-done.12) | copy-start | bytes 1179652
  197.9 7.8 %collective-permute-start.41 = (bf16[96,2048]{1,0:T(8,128)(2,1)S(1)}, bf16[96,2048]{1,0:T(8,128)(2,1)S(1)}, u32[]{:S(2)}, u32[]{:S(2)}) collective-permute-start(bf16[96,2048]{1,0:T(8,128)(2,1)S(1)} %add_convert_fusion), channel_id=1, source_target_pairs={{4,0},{5,1},{8,4},{9,5},{12,8},{13,9},{14,12},{15,13},{10,14},{11,... | collective-permute-start | bytes 1179656 | tf_op jit(solution)/shard_map/ppermute | solution.py:291
  199.4 8.4 %collective-permute-start.40 = (bf16[96,2048]{1,0:T(8,128)(2,1)S(1)}, bf16[96,2048]{1,0:T(8,128)(2,1)S(1)}, u32[]{:S(2)}, u32[]{:S(2)}) collective-permute-start(bf16[96,2048]{1,0:T(8,128)(2,1)S(1)} %add_convert_fusion.1), channel_id=1, source_target_pairs={{0,4},{1,5},{4,8},{5,9},{8,12},{9,13},{12,14},{13,15},{14,10},{15,... | collective-permute-start | bytes 1179656 | tf_op jit(solution)/shard_map/ppermute | solution.py:291

commit v7 on v6

--- a/solution.py
+++ b/solution.py
@@ -142,17 +142,23 @@
         out[2 * e + 1] = (first * sigmoid_part).astype(jnp.bfloat16)
 
 
-def backward_kernel(parts, experts, width, tile, start, names_ref, *refs):
-    packed, factors = refs[:parts], refs[parts]
-    weights = refs[parts + 1 : parts + 7]
-    outs = refs[parts + 7 : 2 * parts + 7]
-    cot, slot, grads, cot_sem, factor_sem = refs[2 * parts + 7 :]
+def backward_kernel(parts, experts, width, tile, pieces, names_ref, *refs):
+    packed, factors = refs[:parts], refs[parts : parts + len(pieces)]
+    weights = refs[parts + len(pieces) :][:6]
+    outs = refs[parts + len(pieces) + 6 :][:parts]
+    cot, slot, grads, cot_sem, factor_sem = refs[2 * parts + len(pieces) + 6 :]
     copies = block_copies(packed, cot, cot_sem)
-    factor_copy = pltpu.make_async_copy(
-        factors.at[:, pl.ds(start, slot.shape[0])], grads, factor_sem
-    )
-    start_all(copies)
-    factor_copy.start()
+    factor_copies, place = [], 0
+    for i, (start, count) in enumerate(pieces):
+        factor_copies.append(
+            pltpu.make_async_copy(
+                factors[i].at[:, pl.ds(start, count)],
+                grads.at[:, pl.ds(place, count)],
+                factor_sem.at[i],
+            )
+        )
+        place += count
+    start_all(copies + factor_copies)
     wait_all(copies)
     for e in range(2):
         table = cot[:, width:].astype(jnp.float32)
@@ -160,7 +166,7 @@
         slot[...] = (gate * cot[:, :width].astype(jnp.float32)).astype(jnp.bfloat16)
         back = dot_nt(slot[...], weights[3 * e + 2][...])
         if e == 0:
-            factor_copy.wait()
+            wait_all(factor_copies)
         for i in range(2):
             made = back * grads[2 * e + i].astype(jnp.float32)
             grads[2 * e + i] = made.astype(jnp.bfloat16)
@@ -185,6 +191,36 @@
 
 def in_vmem(weights):
     return [pltpu.with_memory_space_constraint(weight, pltpu.VMEM) for weight in weights]
+
+
+def in_hbm(blocks):
+    return [pltpu.with_memory_space_constraint(block, pltpu.HBM) for block in blocks]
+
+
+def fetch_kernel(count, *refs):
+    sems = refs[2 * count]
+    copies = [
+        pltpu.make_async_copy(refs[i], refs[count + i], sems.at[i]) for i in range(count)
+    ]
+    start_all(copies)
+    wait_all(copies)
+
+
+def fetched(weights):
+    count = len(weights)
+    return tuple(
+        pl.pallas_call(
+            functools.partial(fetch_kernel, count),
+            out_shape=[pltpu.VMEM(weight.shape, weight.dtype) for weight in weights],
+            in_specs=[HBM] * count,
+            out_specs=[WHOLE] * count,
+            scratch_shapes=[pltpu.SemaphoreType.DMA((count,))],
+            compiler_params=PARAMS,
+            cost_estimate=pl.CostEstimate(
+                flops=0, bytes_accessed=8 * 2**20, transcendentals=0
+            ),
+        )(*weights)
+    )
 
 
 def cost(units, rows, width, inner, fixed):
@@ -233,28 +269,28 @@
         ],
         compiler_params=PARAMS,
         cost_estimate=cost(4, total, width, inner, 5e-6),
-    )(*rows, *in_vmem([weights[i] for i in (0, 1, 3, 4)]))
-
-
-def backward_call(names, packed, factors, start, weights, experts):
+    )(*in_hbm(rows), *in_vmem([weights[i] for i in (0, 1, 3, 4)]))
+
+
+def backward_call(names, packed, factors, pieces, weights, experts):
     parts = len(packed)
     counts = [block.shape[0] for block in packed]
     total, full = sum(counts), packed[0].shape[1]
     width, inner = weights[0].shape
     out = pl.pallas_call(
-        functools.partial(backward_kernel, parts, experts, width, TILE, start),
+        functools.partial(backward_kernel, parts, experts, width, TILE, pieces),
         out_shape=[jax.ShapeDtypeStruct((count, width), jnp.bfloat16) for count in counts],
-        in_specs=[pl.BlockSpec(memory_space=pltpu.SMEM)] + [HBM] * (parts + 1) + [WHOLE] * 6,
+        in_specs=[pl.BlockSpec(memory_space=pltpu.SMEM)] + [HBM] * (parts + len(pieces)) + [WHOLE] * 6,
         scratch_shapes=[
             pltpu.VMEM((total, full), jnp.bfloat16),
             pltpu.VMEM((total, width), jnp.bfloat16),
             pltpu.VMEM((4, total, inner), jnp.bfloat16),
             pltpu.SemaphoreType.DMA((parts,)),
-            pltpu.SemaphoreType.DMA(()),
+            pltpu.SemaphoreType.DMA((len(pieces),)),
         ],
         compiler_params=PARAMS,
         cost_estimate=cost(6, total, width, inner, 6e-6),
-    )(names, *packed, factors, *in_vmem(weights))
+    )(names, *packed, *factors, *in_vmem(weights))
     return list(out)
 
 
@@ -303,19 +339,26 @@
 
     def prepare(self, distances):
         blocks = [block for d in distances for block in self.held["fall"][d]]
-        factors, start = factor_call(blocks, self.weights), 0
+        key, start = f"factors{distances[0]}", 0
+        self.held[key] = {0: [factor_call(blocks, self.weights)]}
         for d in distances:
-            self.held[f"factors{d}"] = {0: [factors]}
-            self.starts[d] = start
-            start += sum(block.shape[0] for block in self.held["fall"][d])
+            count = sum(block.shape[0] for block in self.held["fall"][d])
+            self.starts[d] = (key, start, count)
+            start += count
 
     def work(self, kind, distances):
         packed = [block for d in distances for block in self.held["cot"][d]]
         if kind == "backward":
-            factors = self.held[f"factors{distances[0]}"][0][0]
-            start = self.starts[distances[0]]
+            runs = []
+            for key, start, count in [self.starts[d] for d in distances]:
+                if runs and runs[-1][0] == key and sum(runs[-1][1:]) == start:
+                    runs[-1][2] += count
+                else:
+                    runs.append([key, start, count])
+            factors = [self.held[key][0][0] for key, _, _ in runs]
+            pieces = tuple((start, count) for _, start, count in runs)
             outs = backward_call(
-                self.names, packed, factors, start, self.weights, self.sources
+                self.names, packed, factors, pieces, self.weights, self.sources
             )
         else:
             blocks = [block for d in distances for block in self.held["rise"][d]]
@@ -386,7 +429,6 @@
     ring.held["fall"] = {0: [fall_normal]}
     ring.gather("fall", 1)
     moved_cot = passed_along(leaving_cot, "pipe", 1)
-    moved_cot, leaving_rise = lax.optimization_barrier((moved_cot, leaving_rise))
     own = (w_gate[0, 0], w_up[0, 0], w_down[0, 0])
 
     def swapped(weight):
@@ -395,8 +437,7 @@
     at_start = section_index == 0
     cot_in = jnp.where(at_start, entering[1], moved_cot)
 
-    def entered(leaving_rise):
-        moved_rise = passed_along(leaving_rise, "pipe", 1)
+    def entered(moved_rise):
         return jnp.where(at_start, entering[0], moved_rise)
 
     ring.held["cot"] = {0: [packed_rows(cot_in, route_ids[:, 0], route_gates[:, 0], sources)]}
@@ -421,41 +462,45 @@
     if planned:
         ring.gather("fall", 2)
         own_gate, own_up, own_down = own
-        other_gate = swapped(own_gate)
+        other_gate, other_up = swapped(own_gate), swapped(own_up)
         heads = (head_rise, head_fall)
-        rise_in = entered(leaving_rise)
-        cot_in, rise_in, own_up, own_down, other_gate, heads, ring.names = ring.fence(
-            cot_in, rise_in, own_up, own_down, other_gate, heads, names
+        cot_in, leaving_rise, own, other_gate, other_up, heads, ring.names = ring.fence(
+            cot_in, leaving_rise, own, other_gate, other_up, heads, names
         )
         ring.gather("fall", 3)
         ring.gather("cot", 1)
-        rise_normal = normed(rise_in.astype(jnp.float32), norm_row).astype(jnp.bfloat16)
-        rise_normal, own_up, own_down = ring.fence(rise_normal, own_up, own_down)
+        moved_rise = passed_along(leaving_rise, "pipe", 1)
+        own_down = own[2]
+        own = fetched(own)
+        moved_rise, own, own_down = ring.fence(moved_rise, own, own_down)
         ring.gather("fall", 4)
         ring.gather("cot", 2)
-        other_up = swapped(own_up)
+        other_down = swapped(own_down)
+        rise_in = entered(moved_rise)
+        rise_normal = normed(rise_in.astype(jnp.float32), norm_row).astype(jnp.bfloat16)
         kept, exit_loss = exit_heads(rise_in, cot_in, *heads)
-        rise_normal, kept, exit_loss, other_up, own_down = ring.fence(
-            rise_normal, kept, exit_loss, other_up, own_down
+        ring.weights = own + (other_gate, other_up, None)
+        ring.prepare([0, 1, 2, 3])
+        rise_normal, kept, exit_loss, other_down = ring.fence(
+            rise_normal, kept, exit_loss, other_down
         )
+        ring.weights = own + (other_gate, other_up, other_down)
         ring.held["rise"] = {0: [rise_normal]}
         ring.gather("cot", 3)
         ring.gather("rise", 1)
-        other_down = swapped(own_down)
-        ring.weights = own + (other_gate, other_up, other_down)
-        ring.prepare([0, 1, 2, 3, 4])
-        (other_down,) = ring.fence(other_down)
-        ring.weights = own + (other_gate, other_up, other_down)
-        ring.gather("cot", 4, 1)
+        ring.work("backward", [0, 1, 2])
+        ring.fence()
+        ring.gather("cot", 4)
         ring.gather("rise", 2)
-        ring.work("backward", [0, 1, 2])
+        ring.prepare([4])
+        ring.work("forward", [0, 1])
         ring.fence()
         ring.gather("rise", 3)
         ring.work("backward", [3, 4])
         ring.fence()
-        ring.gather("rise", 4, 0)
-        ring.scatter("backward", 1, 1)
-        ring.work("forward", [0, 1, 2])
+        ring.gather("rise", 4)
+        ring.scatter("backward", 1)
+        ring.work("forward", [2])
         ring.fence()
         ring.scatter("backward", 2)
         ring.work("forward", [3, 4])
@@ -471,7 +516,7 @@
         (fall_total,) = ring.fence(fall_total)
         ring.scatter("forward", 4)
     else:
-        rise_in = entered(leaving_rise)
+        rise_in = entered(passed_along(leaving_rise, "pipe", 1))
         ring.weights = own + tuple(swapped(own))
         kept, exit_loss = exit_heads(rise_in, cot_in, head_rise, head_fall)
         rise_normal = normed(rise_in.astype(jnp.float32), norm_row).astype(jnp.bfloat16)

time: 210 us -> 191 us (0.910)
  waiting for transfers between devices: 83.6 us -> 61.2 us
  Pallas kernels: 53.4 us -> 59.1 us
  starting transfers between devices: 48.3 us -> 52 us
  other arithmetic: 12.3 us -> 8.92 us
    ppermute x37 -> x40, waiting for transfers between devices: 74.3 us -> 60.5 us  [pass_on(): return lax.ppermute(block, 'ep', self.routes[way])]
    ppermute x2, waiting for transfers between devices: 9.32 us -> 0.71 us  [passed_along(): return lax.ppermute(block, axis, route)]
    unnamed x36 -> x22, local copies, waits for them, and re-layouts: 7.24 us -> 3.24 us
    ppermute x37 -> x40, starting transfers between devices: 38.9 us -> 42.8 us  [pass_on(): return lax.ppermute(block, 'ep', self.routes[way])]
    pallas_call x1 -> x2, Pallas kernels: 11.8 us -> 14.8 us  [factor_call(): pl.pallas_call(functools.partial(factor_kernel, parts), out_shape=jax.Sha...]
    pallas_call x2 -> x3, Pallas kernels: 19.6 us -> 21.9 us  [forward_call(): pl.pallas_call(functools.partial(forward_kernel, parts, experts, width, T...]
  transfers between devices with their start and end apart: 42 -> 45, of which waited for: 18 -> 15; matrix products, arithmetic and copies ran while one was open for 7% -> 5% of each run, Pallas kernels for 26% -> 31%
where the time goes in v7:
time: 191 us; the launch traced here: 190 us
  waiting for transfers between devices  61.2 us (32%)
  Pallas kernels  59.1 us (31%)
  starting transfers between devices  52 us (27%)
  other arithmetic  8.92 us (5%)
  local copies, waits for them, and re-layouts  6.68 us (3%)
  between operations  2.58 us (1%)
    ppermute x40, waiting for transfers between devices, pass_on(): return lax.ppermute(block, 'ep', self.routes[way])  60.5 us
    ppermute x40, starting transfers between devices, pass_on(): return lax.ppermute(block, 'ep', self.routes[way])  42.8 us
    pallas_call x3, Pallas kernels, forward_call(): pl.pallas_call(functools.partial(forward_kernel, parts, experts, width, T...  21.9 us
    pallas_call x2, Pallas kernels, backward_call(): pl.pallas_call(functools.partial(backward_kernel, parts, experts, width,...  19.7 us
    pallas_call x2, Pallas kernels, factor_call(): pl.pallas_call(functools.partial(factor_kernel, parts), out_shape=jax.Sha...  14.8 us
    ppermute x2, starting transfers between devices, passed_along(): return lax.ppermute(block, axis, route)  8.66 us
  transfers between devices with their start and end apart: 45, of which 15 were waited for; matrix products, arithmetic and copies ran while one was open for 5% of the time, Pallas kernels for 31%

profile of v7, /device:TPU:0, one launch (start us, length us, event | category | flops | bytes accessed | tf_op | source)
XLA Modules:
  0.0 190.5 jit_solution(15735695185386208418)
XLA Ops:
  0.6 0.5 collective-permute-start.5
  1.2 1.2 fusion.16
  2.5 1.2 fusion.4.refs_0_
  3.6 3.0 %collective-permute-start.2 = (bf16[96,2048]{1,0:T(8,128)(2,1)S(1)}, bf16[96,2048]{1,0:T(8,128)(2,1)}, u32[]{:S(2)}, u32[]{:S(2)}) collective-permute-start(bf16[96,2048]{1,0:T(8,128)(2,1)S(1)} %fusion.4.refs_0_), channel_id=1, source_target_pairs={{4,0},{5,1},{8,4},{9,5},{12,8},{13,9},{14,12},{15,13},{10,14},{11,... | collective-permute-start | bytes 1179656 | tf_op jit(solution)/shard_map/ppermute | solution.py:327
  6.8 4.5 %collective-permute-start = (bf16[96,2048]{1,0:T(8,128)(2,1)}, bf16[96,2048]{1,0:T(8,128)(2,1)}, u32[]{:S(2)}, u32[]{:S(2)}) collective-permute-start(bf16[96,2048]{1,0:T(8,128)(2,1)} %bitcast.63), channel_id=1, source_target_pairs={{0,16},{1,17},{2,18},{3,19},{4,20},{5,21},{6,22},{7,23},{8,24},{9,... | collective-permute-start | bytes 1179656 | tf_op jit(solution)/shard_map/ppermute | solution.py:17
  11.3 0.8 fusion.21
  12.1 0.7 constant_dynamic-slice_fusion
  14.1 0.8 copy.16
  14.9 0.8 copy.17
  16.1 1.7 collective-permute-start.4
  18.2 0.7 collective-permute-done
  18.9 1.0 bitcast_select_fusion.rows_ref
  19.9 0.7 shard_map.148.refs_0_
  20.7 6.3 %collective-permute-done.4.refs_4_ = bf16[96,2048]{1,0:T(8,128)(2,1)} collective-permute-done((bf16[96,2048]{1,0:T(8,128)(2,1)}, bf16[96,2048]{1,0:T(8,128)(2,1)}, u32[]{:S(2)}, u32[]{:S(2)}) %collective-permute-start.4) | collective-permute-done | bytes 393248 | tf_op jit(solution)/shard_map/ppermute | solution.py:327
  27.0 1.1 collective-permute-done.3.refs_3_
  28.1 1.6 collective-permute-start.8
  30.1 4.1 %collective-permute-start.11 = (bf16[96,2048]{1,0:T(8,128)(2,1)}, bf16[96,2048]{1,0:T(8,128)(2,1)}, u32[]{:S(2)}, u32[]{:S(2)}) collective-permute-start(bf16[96,2048]{1,0:T(8,128)(2,1)} %bitcast.6), channel_id=1, source_target_pairs={{0,16},{1,17},{2,18},{3,19},{4,20},{5,21},{6,22},{7,23},{8,24},{9,... | collective-permute-start | bytes 1179656 | tf_op jit(solution)/shard_map/ppermute | solution.py:17
  34.2 0.5 collective-permute-start.9
  34.7 1.5 collective-permute-start.10
  36.3 1.6 copy-done.1
  37.9 1.9 shard_map.149
  39.8 7.6 %collective-permute-done.9.refs_5_ = bf16[96,2048]{1,0:T(8,128)(2,1)} collective-permute-done((bf16[96,2048]{1,0:T(8,128)(2,1)}, bf16[96,2048]{1,0:T(8,128)(2,1)}, u32[]{:S(2)}, u32[]{:S(2)}) %collective-permute-start.9) | collective-permute-done | bytes 393248 | tf_op jit(solution)/shard_map/ppermute | solution.py:327
  47.7 1.0 slice.64
  48.7 0.9 slice.65
  49.6 1.6 collective-permute-start.15
  51.7 0.7 multiply_reduce_fusion
  52.9 1.6 collective-permute-start.13
  54.9 10.1 %shard_map.150.refs_5_.refs_4_ = bf16[4,672,512]{2,1,0:T(8,128)(2,1)S(1)} custom-call(bf16[96,2048]{1,0:T(8,128)(2,1)} %copy-done.5, bf16[96,2048]{1,0:T(8,128)(2,1)} %collective-permute-done.1.refs_1_, bf16[96,2048]{1,0:T(8,128)(2,1)} %collective-permute-done.2.refs_2_, bf16[96,2048]{1,0:T(8,128)(2,1)} %collective-permute-done.3.refs_3_, ...), custom_call_target="tpu_custom_call" | custom-call | flops 11137144832 | bytes 12582912 | tf_op jit(solution)/shard_map/pallas_call | solution.py:262
  65.0 0.6 maximum_bitcast_fusion
  65.6 1.6 collective-permute-start.20
  68.1 1.6 collective-permute-start.18
  69.7 11.3 %shard_map.151 = (bf16[96,2048]{1,0:T(8,128)(2,1)S(1)}, bf16[96,2048]{1,0:T(8,128)(2,1)S(1)}, bf16[96,2048]{1,0:T(8,128)(2,1)S(1)}, bf16[96,2048]{1,0:T(8,128)(2,1)S(1)}, bf16[96,2048]{1,0:T(8,128)(2,1)S(1)}) custom-call(s32[2]{0:T(128)S(1)} %pad_add_fusion.names_ref, bf16[96,2176]{1,0:T(8,128)(2,1)S(1)} %shard_map.148.refs_0_, ...), custom_call_target="tpu_custom_call" | custom-call | flops 12639797248 | bytes 12582912 | tf_op jit(solution)/shard_map/pallas_call | solution.py:280
  81.0 6.4 %collective-permute-done.17.refs_0_ = bf16[96,2176]{1,0:T(8,128)(2,1)S(1)} collective-permute-done((bf16[96,2176]{1,0:T(8,128)(2,1)S(1)}, bf16[96,2176]{1,0:T(8,128)(2,1)S(1)}, u32[]{:S(2)}, u32[]{:S(2)}) %collective-permute-start.17) | collective-permute-done | bytes 417824 | tf_op jit(solution)/shard_map/ppermute | solution.py:327
  87.5 1.6 collective-permute-start.22
  90.0 1.6 collective-permute-start.24
  91.6 8.1 %shard_map.153 = (bf16[96,2048]{1,0:T(8,128)(2,1)S(1)}, bf16[96,2048]{1,0:T(8,128)(2,1)S(1)}, bf16[96,2048]{1,0:T(8,128)(2,1)S(1)}) custom-call(s32[2]{0:T(128)S(1)} %pad_add_fusion.names_ref, bf16[96,2176]{1,0:T(8,128)(2,1)S(1)} %shard_map.148.refs_0_, bf16[96,2176]{1,0:T(8,128)(2,1)} %collective-permute-done.7.refs_1_, ...), custom_call_target="tpu_custom_call" | custom-call | flops 10223878144 | bytes 12582912 | tf_op jit(solution)/shard_map/pallas_call | solution.py:242
  99.7 4.7 %shard_map.152.refs_5_ = bf16[4,96,512]{2,1,0:T(8,128)(2,1)S(1)} custom-call(bf16[48,2048]{1,0:T(8,128)(2,1)} %copy-done.9, bf16[48,2048]{1,0:T(8,128)(2,1)} %copy-done.8, bf16[2048,512]{1,0:T(8,128)(2,1)S(1)} %get-tuple-element.223.refs_7_.refs_6_.refs_2_.refs_4_.refs_8_, bf16[2048,512]{1,0:T(8,128)(2,1)S(1)} %get-tuple-element.224.refs_8_.refs_7_.refs_3_.refs_5_.refs_9_, ...), custom_call_target="tpu_custom_call" | custom-call | flops 6305306624 | bytes 12582912 | tf_op jit(solution)/shard_map/pallas_call | solution.py:262
  105.0 1.6 collective-permute-start.26
  106.6 8.5 %shard_map.154 = (bf16[96,2048]{1,0:T(8,128)(2,1)S(1)}, bf16[96,2048]{1,0:T(8,128)(2,1)S(1)}, bf16[48,2048]{1,0:T(8,128)(2,1)S(1)}, bf16[48,2048]{1,0:T(8,128)(2,1)S(1)}) custom-call(s32[2]{0:T(128)S(1)} %pad_add_fusion.names_ref, bf16[96,2176]{1,0:T(8,128)(2,1)S(1)} %collective-permute-done.17.refs_0_, ...), custom_call_target="tpu_custom_call" | custom-call | flops 10223878144 | bytes 12582912 | tf_op jit(solution)/shard_map/pallas_call | solution.py:280
  115.1 1.6 collective-permute-start.28
  117.6 1.6 collective-permute-start.30
  119.2 6.0 %shard_map.155 = (bf16[96,2048]{1,0:T(8,128)(2,1)S(1)}, bf16[96,2048]{1,0:T(8,128)(2,1)S(1)}) custom-call(s32[2]{0:T(128)S(1)} %pad_add_fusion.names_ref, bf16[96,2176]{1,0:T(8,128)(2,1)S(1)} %collective-permute-done.12.refs_3_.refs_0_, bf16[96,2176]{1,0:T(8,128)(2,1)S(1)} %collective-permute-done.13.refs_4_.refs_1_, ...), custom_call_target="tpu_custom_call" | custom-call | flops 9015918592 | bytes 12582912 | tf_op jit(solution)/shard_map/pallas_call | solution.py:242
  125.5 1.6 collective-permute-start.32
  127.2 0.7 collective-permute-start.31
  127.9 7.7 %shard_map.156 = (bf16[96,2048]{1,0:T(8,128)(2,1)S(1)}, bf16[96,2048]{1,0:T(8,128)(2,1)S(1)}, bf16[48,2048]{1,0:T(8,128)(2,1)S(1)}, bf16[48,2048]{1,0:T(8,128)(2,1)S(1)}) custom-call(s32[2]{0:T(128)S(1)} %pad_add_fusion.names_ref, bf16[96,2176]{1,0:T(8,128)(2,1)S(1)} %collective-permute-done.17.refs_0_, ...), custom_call_target="tpu_custom_call" | custom-call | flops 10223878144 | bytes 12582912 | tf_op jit(solution)/shard_map/pallas_call | solution.py:242
  135.7 1.6 collective-permute-start.34
  138.4 1.6 collective-permute-start.36
  140.0 10.2 %collective-permute-done.35 = bf16[48,2048]{1,0:T(8,128)(2,1)S(1)} collective-permute-done((bf16[48,2048]{1,0:T(8,128)(2,1)S(1)}, bf16[48,2048]{1,0:T(8,128)(2,1)S(1)}, u32[]{:S(2)}, u32[]{:S(2)}) %collective-permute-start.35) | collective-permute-done | bytes 196640 | tf_op jit(solution)/shard_map/ppermute | solution.py:327
  150.4 0.6 collective-permute-start.38
  151.1 1.5 collective-permute-start.37
  152.7 0.6 collective-permute-start.40
  153.3 1.5 collective-permute-start.39
  154.9 4.9 %collective-permute-done.38 = bf16[96,2048]{1,0:T(8,128)(2,1)S(1)} collective-permute-done((bf16[96,2048]{1,0:T(8,128)(2,1)S(1)}, bf16[96,2048]{1,0:T(8,128)(2,1)S(1)}, u32[]{:S(2)}, u32[]{:S(2)}) %collective-permute-start.38) | collective-permute-done | bytes 393248 | tf_op jit(solution)/shard_map/ppermute | solution.py:327
  159.7 1.4 collective-permute-done.37
  161.2 4.7 %collective-permute-done.40 = bf16[96,2048]{1,0:T(8,128)(2,1)S(1)} collective-permute-done((bf16[96,2048]{1,0:T(8,128)(2,1)S(1)}, bf16[96,2048]{1,0:T(8,128)(2,1)S(1)}, u32[]{:S(2)}, u32[]{:S(2)}) %collective-permute-start.40) | collective-permute-done | bytes 393248 | tf_op jit(solution)/shard_map/ppermute | solution.py:327
  165.9 2.4 %collective-permute-done.39 = bf16[96,2048]{1,0:T(8,128)(2,1)S(1)} collective-permute-done((bf16[96,2048]{1,0:T(8,128)(2,1)S(1)}, bf16[96,2048]{1,0:T(8,128)(2,1)S(1)}, u32[]{:S(2)}, u32[]{:S(2)}) %collective-permute-start.39) | collective-permute-done | bytes 393248 | tf_op jit(solution)/shard_map/ppermute | solution.py:327
  168.4 0.9 collective-permute-start.42
  169.3 1.3 collective-permute-start.41
  171.0 1.1 fusion.15
  172.1 8.2 %collective-permute-done.42 = bf16[96,2048]{1,0:T(8,128)(2,1)S(1)} collective-permute-done((bf16[96,2048]{1,0:T(8,128)(2,1)S(1)}, bf16[96,2048]{1,0:T(8,128)(2,1)S(1)}, u32[]{:S(2)}, u32[]{:S(2)}) %collective-permute-start.42) | collective-permute-done | bytes 393248 | tf_op jit(solution)/shard_map/ppermute | solution.py:327
  180.3 0.9 collective-permute-done.41
  181.7 1.8 collective-permute-start.43
  183.5 5.6 %collective-permute-done.44 = bf16[96,2048]{1,0:T(8,128)(2,1)S(1)} collective-permute-done((bf16[96,2048]{1,0:T(8,128)(2,1)S(1)}, bf16[96,2048]{1,0:T(8,128)(2,1)S(1)}, u32[]{:S(2)}, u32[]{:S(2)}) %collective-permute-start.44) | collective-permute-done | bytes 393248 | tf_op jit(solution)/shard_map/ppermute | solution.py:327
  189.5 1.0 fusion.19
  (102 shorter events, 9.7 us)
Async XLA Ops:
  0.6 35.6 %copy-start = (bf16[1,1,2048,512]{3,2,1,0:T(8,128)(2,1)S(1)}, bf16[1,1,2048,512]{3,2,1,0:T(8,128)(2,1)}, u32[]{:S(2)}) copy-start(bf16[1,1,2048,512]{3,2,1,0:T(8,128)(2,1)} %param.20) | copy-start | bytes 6291460
  0.6 27.4 %collective-permute-start.5 = (bf16[2048,512]{1,0:T(8,128)(2,1)}, bf16[2048,512]{1,0:T(8,128)(2,1)}, u32[]{:S(2)}, u32[]{:S(2)}) collective-permute-start(bf16[2048,512]{1,0:T(8,128)(2,1)} %bitcast.49), channel_id=1, source_target_pairs={{0,1},{1,0},{2,3},{3,2},{4,5},{5,4},{6,7},{7,6},{8,9},{9,8},{10,11... | collective-permute-start | bytes 6291464 | tf_op jit(solution)/shard_map/ppermute | solution.py:435
  1.2 26.9 %collective-permute-start.6 = (bf16[2048,512]{1,0:T(8,128)(2,1)}, bf16[2048,512]{1,0:T(8,128)(2,1)}, u32[]{:S(2)}, u32[]{:S(2)}) collective-permute-start(bf16[2048,512]{1,0:T(8,128)(2,1)} %bitcast.51), channel_id=1, source_target_pairs={{0,1},{1,0},{2,3},{3,2},{4,5},{5,4},{6,7},{7,6},{8,9},{9,8},{10,11... | collective-permute-start | bytes 6291464 | tf_op jit(solution)/shard_map/ppermute | solution.py:435
  3.6 16.3 %copy-start.5 = (bf16[96,2048]{1,0:T(8,128)(2,1)}, bf16[96,2048]{1,0:T(8,128)(2,1)S(1)}, u32[]{:S(2)}) copy-start(bf16[96,2048]{1,0:T(8,128)(2,1)S(1)} %fusion.4.refs_0_) | copy-start | bytes 1179652
  3.6 12.5 %collective-permute-start.2 = (bf16[96,2048]{1,0:T(8,128)(2,1)S(1)}, bf16[96,2048]{1,0:T(8,128)(2,1)}, u32[]{:S(2)}, u32[]{:S(2)}) collective-permute-start(bf16[96,2048]{1,0:T(8,128)(2,1)S(1)} %fusion.4.refs_0_), channel_id=1, source_target_pairs={{4,0},{5,1},{8,4},{9,5},{12,8},{13,9},{14,12},{15,13},{10,14},{11,... | collective-permute-start | bytes 1179656 | tf_op jit(solution)/shard_map/ppermute | solution.py:327
  6.7 11.2 %collective-permute-start.1 = (bf16[96,2048]{1,0:T(8,128)(2,1)S(1)}, bf16[96,2048]{1,0:T(8,128)(2,1)}, u32[]{:S(2)}, u32[]{:S(2)}) collective-permute-start(bf16[96,2048]{1,0:T(8,128)(2,1)S(1)} %fusion.4.refs_0_), channel_id=1, source_target_pairs={{0,4},{1,5},{4,8},{5,9},{8,12},{9,13},{12,14},{13,15},{14,10},{15,... | collective-permute-start | bytes 1179656 | tf_op jit(solution)/shard_map/ppermute | solution.py:327
  6.8 12.1 %collective-permute-start = (bf16[96,2048]{1,0:T(8,128)(2,1)}, bf16[96,2048]{1,0:T(8,128)(2,1)}, u32[]{:S(2)}, u32[]{:S(2)}) collective-permute-start(bf16[96,2048]{1,0:T(8,128)(2,1)} %bitcast.63), channel_id=1, source_target_pairs={{0,16},{1,17},{2,18},{3,19},{4,20},{5,21},{6,22},{7,23},{8,24},{9,... | collective-permute-start | bytes 1179656 | tf_op jit(solution)/shard_map/ppermute | solution.py:17
  16.1 10.8 %collective-permute-start.4 = (bf16[96,2048]{1,0:T(8,128)(2,1)}, bf16[96,2048]{1,0:T(8,128)(2,1)}, u32[]{:S(2)}, u32[]{:S(2)}) collective-permute-start(bf16[96,2048]{1,0:T(8,128)(2,1)} %collective-permute-done.2.refs_2_), channel_id=1, source_target_pairs={{4,0},{5,1},{8,4},{9,5},{12,8},{13,9},{14,12},{15,13},{10,14},{11,... | collective-permute-start | bytes 1179656 | tf_op jit(solution)/shard_map/ppermute | solution.py:327
  17.8 10.2 %collective-permute-start.3 = (bf16[96,2048]{1,0:T(8,128)(2,1)}, bf16[96,2048]{1,0:T(8,128)(2,1)}, u32[]{:S(2)}, u32[]{:S(2)}) collective-permute-start(bf16[96,2048]{1,0:T(8,128)(2,1)} %collective-permute-done.1.refs_1_), channel_id=1, source_target_pairs={{0,4},{1,5},{4,8},{5,9},{8,12},{9,13},{12,14},{13,15},{14,10},{15,... | collective-permute-start | bytes 1179656 | tf_op jit(solution)/shard_map/ppermute | solution.py:327
  28.1 19.4 %collective-permute-start.8 = (bf16[96,2176]{1,0:T(8,128)(2,1)S(1)}, bf16[96,2176]{1,0:T(8,128)(2,1)S(1)}, u32[]{:S(2)}, u32[]{:S(2)}) collective-permute-start(bf16[96,2176]{1,0:T(8,128)(2,1)S(1)} %shard_map.148.refs_0_), channel_id=1, source_target_pairs={{4,0},{5,1},{8,4},{9,5},{12,8},{13,9},{14,12},{15,13},{10,14},{11,... | collective-permute-start | bytes 1253384 | tf_op jit(solution)/shard_map/ppermute | solution.py:327
  29.6 17.8 %collective-permute-start.7 = (bf16[96,2176]{1,0:T(8,128)(2,1)S(1)}, bf16[96,2176]{1,0:T(8,128)(2,1)}, u32[]{:S(2)}, u32[]{:S(2)}) collective-permute-start(bf16[96,2176]{1,0:T(8,128)(2,1)S(1)} %shard_map.148.refs_0_), channel_id=1, source_target_pairs={{0,4},{1,5},{4,8},{5,9},{8,12},{9,13},{12,14},{13,15},{14,10},{15,... | collective-permute-start | bytes 1253384 | tf_op jit(solution)/shard_map/ppermute | solution.py:327
  30.1 9.7 %collective-permute-start.11 = (bf16[96,2048]{1,0:T(8,128)(2,1)}, bf16[96,2048]{1,0:T(8,128)(2,1)}, u32[]{:S(2)}, u32[]{:S(2)}) collective-permute-start(bf16[96,2048]{1,0:T(8,128)(2,1)} %bitcast.6), channel_id=1, source_target_pairs={{0,16},{1,17},{2,18},{3,19},{4,20},{5,21},{6,22},{7,23},{8,24},{9,... | collective-permute-start | bytes 1179656 | tf_op jit(solution)/shard_map/ppermute | solution.py:17
  34.2 13.2 %collective-permute-start.9 = (bf16[96,2048]{1,0:T(8,128)(2,1)}, bf16[96,2048]{1,0:T(8,128)(2,1)}, u32[]{:S(2)}, u32[]{:S(2)}) collective-permute-start(bf16[96,2048]{1,0:T(8,128)(2,1)} %collective-permute-done.3.refs_3_), channel_id=1, source_target_pairs={{0,4},{1,5},{4,8},{5,9},{8,12},{9,13},{12,14},{13,15},{14,10},{15,... | collective-permute-start | bytes 1179656 | tf_op jit(solution)/shard_map/ppermute | solution.py:327
  34.7 12.7 %collective-permute-start.10 = (bf16[96,2048]{1,0:T(8,128)(2,1)}, bf16[96,2048]{1,0:T(8,128)(2,1)}, u32[]{:S(2)}, u32[]{:S(2)}) collective-permute-start(bf16[96,2048]{1,0:T(8,128)(2,1)} %collective-permute-done.4.refs_4_), channel_id=1, source_target_pairs={{4,0},{5,1},{8,4},{9,5},{12,8},{13,9},{14,12},{15,13},{10,14},{11,... | collective-permute-start | bytes 1179656 | tf_op jit(solution)/shard_map/ppermute | solution.py:327
  36.3 1.6 copy-start.1
  37.9 9.6 %copy-start.4 = (bf16[2,96,2048]{2,1,0:T(8,128)(2,1)S(1)}, bf16[2,96,2048]{2,1,0:T(8,128)(2,1)}, u32[]{:S(2)}) copy-start(bf16[2,96,2048]{2,1,0:T(8,128)(2,1)} %param.13) | copy-start | bytes 2359300
  37.9 13.8 %copy-start.6 = (f32[1,2048]{1,0:T(1,128)S(1)}, f32[1,2048]{1,0:T(1,128)}, u32[]{:S(2)}) copy-start(f32[1,2048]{1,0:T(1,128)} %param.18) | copy-start | bytes 24580
  37.9 13.8 %copy-start.7 = (f32[1,2048]{1,0:T(1,128)S(1)}, f32[1,2048]{1,0:T(1,128)}, u32[]{:S(2)}) copy-start(f32[1,2048]{1,0:T(1,128)} %param.19) | copy-start | bytes 24580
  39.8 11.9 %copy-start.2 = (bf16[1,96,2048]{2,1,0:T(8,128)(2,1)S(1)}, bf16[1,96,2048]{2,1,0:T(8,128)(2,1)}, u32[]{:S(2)}) copy-start(bf16[1,96,2048]{2,1,0:T(8,128)(2,1)} %param.16) | copy-start | bytes 1179652
  39.8 11.9 %copy-start.3 = (bf16[2,96,2048]{2,1,0:T(8,128)(2,1)S(1)}, bf16[2,96,2048]{2,1,0:T(8,128)(2,1)}, u32[]{:S(2)}) copy-start(bf16[2,96,2048]{2,1,0:T(8,128)(2,1)} %param.17) | copy-start | bytes 2359300
  49.6 15.9 %collective-permute-start.15 = (bf16[48,2048]{1,0:T(8,128)(2,1)S(1)}, bf16[48,2048]{1,0:T(8,128)(2,1)S(1)}, u32[]{:S(2)}, u32[]{:S(2)}) collective-permute-start(bf16[48,2048]{1,0:T(8,128)(2,1)S(1)} %slice.65), channel_id=1, source_target_pairs={{4,0},{5,1},{8,4},{9,5},{12,8},{13,9},{14,12},{15,13},{10,14},{11,... | collective-permute-start | bytes 589832 | tf_op jit(solution)/shard_map/ppermute | solution.py:327
  51.2 14.3 %collective-permute-start.14 = (bf16[48,2048]{1,0:T(8,128)(2,1)S(1)}, bf16[48,2048]{1,0:T(8,128)(2,1)S(1)}, u32[]{:S(2)}, u32[]{:S(2)}) collective-permute-start(bf16[48,2048]{1,0:T(8,128)(2,1)S(1)} %slice.64), channel_id=1, source_target_pairs={{0,4},{1,5},{4,8},{5,9},{8,12},{9,13},{12,14},{13,15},{14,10},{15,... | collective-permute-start | bytes 589832 | tf_op jit(solution)/shard_map/ppermute | solution.py:327
  52.4 13.2 %collective-permute-start.12 = (bf16[96,2176]{1,0:T(8,128)(2,1)}, bf16[96,2176]{1,0:T(8,128)(2,1)S(1)}, u32[]{:S(2)}, u32[]{:S(2)}) collective-permute-start(bf16[96,2176]{1,0:T(8,128)(2,1)} %collective-permute-done.7.refs_1_), channel_id=1, source_target_pairs={{0,4},{1,5},{4,8},{5,9},{8,12},{9,13},{12,14},{13,15},{14,10},{15,... | collective-permute-start | bytes 1253384 | tf_op jit(solution)/shard_map/ppermute | solution.py:327
  52.9 12.7 %collective-permute-start.13 = (bf16[96,2176]{1,0:T(8,128)(2,1)S(1)}, bf16[96,2176]{1,0:T(8,128)(2,1)S(1)}, u32[]{:S(2)}, u32[]{:S(2)}) collective-permute-start(bf16[96,2176]{1,0:T(8,128)(2,1)S(1)} %collective-permute-done.8.refs_2_), channel_id=1, source_target_pairs={{4,0},{5,1},{8,4},{9,5},{12,8},{13,9},{14,12},{15,13},{10,14},{11,... | collective-permute-start | bytes 1253384 | tf_op jit(solution)/shard_map/ppermute | solution.py:327
  54.5 11.1 %collective-permute-start.16 = (bf16[512,2048]{1,0:T(8,128)(2,1)}, bf16[512,2048]{1,0:T(8,128)(2,1)S(1)}, u32[]{:S(2)}, u32[]{:S(2)}) collective-permute-start(bf16[512,2048]{1,0:T(8,128)(2,1)} %bitcast.11.refs_2_), channel_id=1, source_target_pairs={{0,1},{1,0},{2,3},{3,2},{4,5},{5,4},{6,7},{7,6},{8,9},{9,8},{10,11... | collective-permute-start | bytes 6291464 | tf_op jit(solution)/shard_map/ppermute | solution.py:435
  65.5 15.5 %copy-start.8 = (bf16[48,2048]{1,0:T(8,128)(2,1)}, bf16[48,2048]{1,0:T(8,128)(2,1)S(1)}, u32[]{:S(2)}) copy-start(bf16[48,2048]{1,0:T(8,128)(2,1)S(1)} %collective-permute-done.15.refs_1_) | copy-start | bytes 589828
  65.6 15.5 %copy-start.9 = (bf16[48,2048]{1,0:T(8,128)(2,1)}, bf16[48,2048]{1,0:T(8,128)(2,1)S(1)}, u32[]{:S(2)}) copy-start(bf16[48,2048]{1,0:T(8,128)(2,1)S(1)} %collective-permute-done.14.refs_0_) | copy-start | bytes 589828
  65.6 15.4 %collective-permute-start.20 = (bf16[96,2048]{1,0:T(8,128)(2,1)S(1)}, bf16[96,2048]{1,0:T(8,128)(2,1)S(1)}, u32[]{:S(2)}, u32[]{:S(2)}) collective-permute-start(bf16[96,2048]{1,0:T(8,128)(2,1)S(1)} %get-tuple-element.258.refs_3_), channel_id=1, source_target_pairs={{4,0},{5,1},{8,4},{9,5},{12,8},{13,9},{14,12},{15,13},{10,14},{11,... | collective-permute-start | bytes 1179656 | tf_op jit(solution)/shard_map/ppermute | solution.py:327
  67.2 13.8 %collective-permute-start.19 = (bf16[96,2048]{1,0:T(8,128)(2,1)S(1)}, bf16[96,2048]{1,0:T(8,128)(2,1)S(1)}, u32[]{:S(2)}, u32[]{:S(2)}) collective-permute-start(bf16[96,2048]{1,0:T(8,128)(2,1)S(1)} %get-tuple-element.258.refs_3_), channel_id=1, source_target_pairs={{0,4},{1,5},{4,8},{5,9},{8,12},{9,13},{12,14},{13,15},{14,10},{15,... | collective-permute-start | bytes 1179656 | tf_op jit(solution)/shard_map/ppermute | solution.py:327
  67.7 19.8 %collective-permute-start.17 = (bf16[96,2176]{1,0:T(8,128)(2,1)S(1)}, bf16[96,2176]{1,0:T(8,128)(2,1)S(1)}, u32[]{:S(2)}, u32[]{:S(2)}) collective-permute-start(bf16[96,2176]{1,0:T(8,128)(2,1)S(1)} %collective-permute-done.12.refs_3_.refs_0_), channel_id=1, source_target_pairs={{0,4},{1,5},{4,8},{5,9},{8,12},{9,13},{12,14},{13,15},{14,10},{15,... | collective-permute-start | bytes 1253384 | tf_op jit(solution)/shard_map/ppermute | solution.py:327
  68.1 19.3 %collective-permute-start.18 = (bf16[96,2176]{1,0:T(8,128)(2,1)S(1)}, bf16[96,2176]{1,0:T(8,128)(2,1)S(1)}, u32[]{:S(2)}, u32[]{:S(2)}) collective-permute-start(bf16[96,2176]{1,0:T(8,128)(2,1)S(1)} %collective-permute-done.13.refs_4_.refs_1_), channel_id=1, source_target_pairs={{4,0},{5,1},{8,4},{9,5},{12,8},{13,9},{14,12},{15,13},{10,14},{11,... | collective-permute-start | bytes 1253384 | tf_op jit(solution)/shard_map/ppermute | solution.py:327
  87.5 17.0 %collective-permute-start.22 = (bf16[48,2176]{1,0:T(8,128)(2,1)S(1)}, bf16[48,2176]{1,0:T(8,128)(2,1)S(1)}, u32[]{:S(2)}, u32[]{:S(2)}) collective-permute-start(bf16[48,2176]{1,0:T(8,128)(2,1)S(1)} %slice.69), channel_id=1, source_target_pairs={{4,0},{5,1},{8,4},{9,5},{12,8},{13,9},{14,12},{15,13},{10,14},{11,... | collective-permute-start | bytes 626696 | tf_op jit(solution)/shard_map/ppermute | solution.py:327
  89.1 15.4 %collective-permute-start.21 = (bf16[48,2176]{1,0:T(8,128)(2,1)S(1)}, bf16[48,2176]{1,0:T(8,128)(2,1)S(1)}, u32[]{:S(2)}, u32[]{:S(2)}) collective-permute-start(bf16[48,2176]{1,0:T(8,128)(2,1)S(1)} %slice.68), channel_id=1, source_target_pairs={{0,4},{1,5},{4,8},{5,9},{8,12},{9,13},{12,14},{13,15},{14,10},{15,... | collective-permute-start | bytes 626696 | tf_op jit(solution)/shard_map/ppermute | solution.py:327
  89.6 14.9 %collective-permute-start.23 = (bf16[96,2048]{1,0:T(8,128)(2,1)S(1)}, bf16[96,2048]{1,0:T(8,128)(2,1)S(1)}, u32[]{:S(2)}, u32[]{:S(2)}) collective-permute-start(bf16[96,2048]{1,0:T(8,128)(2,1)S(1)} %collective-permute-done.19.refs_4_), channel_id=1, source_target_pairs={{0,4},{1,5},{4,8},{5,9},{8,12},{9,13},{12,14},{13,15},{14,10},{15,... | collective-permute-start | bytes 1179656 | tf_op jit(solution)/shard_map/ppermute | solution.py:327
  90.0 14.5 %collective-permute-start.24 = (bf16[96,2048]{1,0:T(8,128)(2,1)S(1)}, bf16[96,2048]{1,0:T(8,128)(2,1)S(1)}, u32[]{:S(2)}, u32[]{:S(2)}) collective-permute-start(bf16[96,2048]{1,0:T(8,128)(2,1)S(1)} %collective-permute-done.20.refs_5_), channel_id=1, source_target_pairs={{4,0},{5,1},{8,4},{9,5},{12,8},{13,9},{14,12},{15,13},{10,14},{11,... | collective-permute-start | bytes 1179656 | tf_op jit(solution)/shard_map/ppermute | solution.py:327
  104.5 10.5 %collective-permute-start.25 = (bf16[96,2048]{1,0:T(8,128)(2,1)S(1)}, bf16[96,2048]{1,0:T(8,128)(2,1)S(1)}, u32[]{:S(2)}, u32[]{:S(2)}) collective-permute-start(bf16[96,2048]{1,0:T(8,128)(2,1)S(1)} %collective-permute-done.23.refs_2_), channel_id=1, source_target_pairs={{0,4},{1,5},{4,8},{5,9},{8,12},{9,13},{12,14},{13,15},{14,10},{15,... | collective-permute-start | bytes 1179656 | tf_op jit(solution)/shard_map/ppermute | solution.py:327
  105.0 10.1 %collective-permute-start.26 = (bf16[96,2048]{1,0:T(8,128)(2,1)S(1)}, bf16[96,2048]{1,0:T(8,128)(2,1)S(1)}, u32[]{:S(2)}, u32[]{:S(2)}) collective-permute-start(bf16[96,2048]{1,0:T(8,128)(2,1)S(1)} %collective-permute-done.24.refs_3_), channel_id=1, source_target_pairs={{4,0},{5,1},{8,4},{9,5},{12,8},{13,9},{14,12},{15,13},{10,14},{11,... | collective-permute-start | bytes 1179656 | tf_op jit(solution)/shard_map/ppermute | solution.py:327
  115.1 10.2 %collective-permute-start.28 = (bf16[48,2048]{1,0:T(8,128)(2,1)S(1)}, bf16[48,2048]{1,0:T(8,128)(2,1)S(1)}, u32[]{:S(2)}, u32[]{:S(2)}) collective-permute-start(bf16[48,2048]{1,0:T(8,128)(2,1)S(1)} %slice.71), channel_id=1, source_target_pairs={{4,0},{5,1},{8,4},{9,5},{12,8},{13,9},{14,12},{15,13},{10,14},{11,... | collective-permute-start | bytes 589832 | tf_op jit(solution)/shard_map/ppermute | solution.py:327
  116.7 8.5 %collective-permute-start.27 = (bf16[48,2048]{1,0:T(8,128)(2,1)S(1)}, bf16[48,2048]{1,0:T(8,128)(2,1)S(1)}, u32[]{:S(2)}, u32[]{:S(2)}) collective-permute-start(bf16[48,2048]{1,0:T(8,128)(2,1)S(1)} %slice.70), channel_id=1, source_target_pairs={{0,4},{1,5},{4,8},{5,9},{8,12},{9,13},{12,14},{13,15},{14,10},{15,... | collective-permute-start | bytes 589832 | tf_op jit(solution)/shard_map/ppermute | solution.py:327
  117.2 8.1 %collective-permute-start.29 = (bf16[48,2048]{1,0:T(8,128)(2,1)S(1)}, bf16[48,2048]{1,0:T(8,128)(2,1)S(1)}, u32[]{:S(2)}, u32[]{:S(2)}) collective-permute-start(bf16[48,2048]{1,0:T(8,128)(2,1)S(1)} %get-tuple-element.313), channel_id=1, source_target_pairs={{0,4},{1,5},{4,8},{5,9},{8,12},{9,13},{12,14},{13,15},{14,10},{15,... | collective-permute-start | bytes 589832 | tf_op jit(solution)/shard_map/ppermute | solution.py:327
  117.6 7.7 %collective-permute-start.30 = (bf16[48,2048]{1,0:T(8,128)(2,1)S(1)}, bf16[48,2048]{1,0:T(8,128)(2,1)S(1)}, u32[]{:S(2)}, u32[]{:S(2)}) collective-permute-start(bf16[48,2048]{1,0:T(8,128)(2,1)S(1)} %get-tuple-element.314), channel_id=1, source_target_pairs={{4,0},{5,1},{8,4},{9,5},{12,8},{13,9},{14,12},{15,13},{10,14},{11,... | collective-permute-start | bytes 589832 | tf_op jit(solution)/shard_map/ppermute | solution.py:327
  125.5 10.1 %collective-permute-start.32 = (bf16[96,2048]{1,0:T(8,128)(2,1)S(1)}, bf16[96,2048]{1,0:T(8,128)(2,1)S(1)}, u32[]{:S(2)}, u32[]{:S(2)}) collective-permute-start(bf16[96,2048]{1,0:T(8,128)(2,1)S(1)} %pad_maximum_fusion.1), channel_id=1, source_target_pairs={{4,0},{5,1},{8,4},{9,5},{12,8},{13,9},{14,12},{15,13},{10,14},{11,... | collective-permute-start | bytes 1179656 | tf_op jit(solution)/shard_map/ppermute | solution.py:327
  127.2 8.5 %collective-permute-start.31 = (bf16[96,2048]{1,0:T(8,128)(2,1)S(1)}, bf16[96,2048]{1,0:T(8,128)(2,1)S(1)}, u32[]{:S(2)}, u32[]{:S(2)}) collective-permute-start(bf16[96,2048]{1,0:T(8,128)(2,1)S(1)} %pad_maximum_fusion), channel_id=1, source_target_pairs={{0,4},{1,5},{4,8},{5,9},{8,12},{9,13},{12,14},{13,15},{14,10},{15,... | collective-permute-start | bytes 1179656 | tf_op jit(solution)/shard_map/ppermute | solution.py:327
  135.7 14.4 %collective-permute-start.34 = (bf16[96,2048]{1,0:T(8,128)(2,1)S(1)}, bf16[96,2048]{1,0:T(8,128)(2,1)S(1)}, u32[]{:S(2)}, u32[]{:S(2)}) collective-permute-start(bf16[96,2048]{1,0:T(8,128)(2,1)S(1)} %add_convert_fusion.6), channel_id=1, source_target_pairs={{4,0},{5,1},{8,4},{9,5},{12,8},{13,9},{14,12},{15,13},{10,14},{11,... | collective-permute-start | bytes 1179656 | tf_op jit(solution)/shard_map/ppermute | solution.py:327
  137.5 12.7 %collective-permute-start.33 = (bf16[96,2048]{1,0:T(8,128)(2,1)S(1)}, bf16[96,2048]{1,0:T(8,128)(2,1)S(1)}, u32[]{:S(2)}, u32[]{:S(2)}) collective-permute-start(bf16[96,2048]{1,0:T(8,128)(2,1)S(1)} %add_convert_fusion.7), channel_id=1, source_target_pairs={{0,4},{1,5},{4,8},{5,9},{8,12},{9,13},{12,14},{13,15},{14,10},{15,... | collective-permute-start | bytes 1179656 | tf_op jit(solution)/shard_map/ppermute | solution.py:327
  138.0 12.2 %collective-permute-start.35 = (bf16[48,2048]{1,0:T(8,128)(2,1)S(1)}, bf16[48,2048]{1,0:T(8,128)(2,1)S(1)}, u32[]{:S(2)}, u32[]{:S(2)}) collective-permute-start(bf16[48,2048]{1,0:T(8,128)(2,1)S(1)} %get-tuple-element.355), channel_id=1, source_target_pairs={{0,4},{1,5},{4,8},{5,9},{8,12},{9,13},{12,14},{13,15},{14,10},{15,... | collective-permute-start | bytes 589832 | tf_op jit(solution)/shard_map/ppermute | solution.py:327
  138.4 11.7 %collective-permute-start.36 = (bf16[48,2048]{1,0:T(8,128)(2,1)S(1)}, bf16[48,2048]{1,0:T(8,128)(2,1)S(1)}, u32[]{:S(2)}, u32[]{:S(2)}) collective-permute-start(bf16[48,2048]{1,0:T(8,128)(2,1)S(1)} %get-tuple-element.356), channel_id=1, source_target_pairs={{4,0},{5,1},{8,4},{9,5},{12,8},{13,9},{14,12},{15,13},{10,14},{11,... | collective-permute-start | bytes 589832 | tf_op jit(solution)/shard_map/ppermute | solution.py:327
  150.4 9.3 %collective-permute-start.38 = (bf16[96,2048]{1,0:T(8,128)(2,1)S(1)}, bf16[96,2048]{1,0:T(8,128)(2,1)S(1)}, u32[]{:S(2)}, u32[]{:S(2)}) collective-permute-start(bf16[96,2048]{1,0:T(8,128)(2,1)S(1)} %add_convert_fusion.4), channel_id=1, source_target_pairs={{4,0},{5,1},{8,4},{9,5},{12,8},{13,9},{14,12},{15,13},{10,14},{11,... | collective-permute-start | bytes 1179656 | tf_op jit(solution)/shard_map/ppermute | solution.py:327
  151.1 10.0 %collective-permute-start.37 = (bf16[96,2048]{1,0:T(8,128)(2,1)S(1)}, bf16[96,2048]{1,0:T(8,128)(2,1)S(1)}, u32[]{:S(2)}, u32[]{:S(2)}) collective-permute-start(bf16[96,2048]{1,0:T(8,128)(2,1)S(1)} %add_convert_fusion.5), channel_id=1, source_target_pairs={{0,4},{1,5},{4,8},{5,9},{8,12},{9,13},{12,14},{13,15},{14,10},{15,... | collective-permute-start | bytes 1179656 | tf_op jit(solution)/shard_map/ppermute | solution.py:327
  152.7 13.2 %collective-permute-start.40 = (bf16[96,2048]{1,0:T(8,128)(2,1)S(1)}, bf16[96,2048]{1,0:T(8,128)(2,1)S(1)}, u32[]{:S(2)}, u32[]{:S(2)}) collective-permute-start(bf16[96,2048]{1,0:T(8,128)(2,1)S(1)} %pad_maximum_fusion.3), channel_id=1, source_target_pairs={{4,0},{5,1},{8,4},{9,5},{12,8},{13,9},{14,12},{15,13},{10,14},{11,... | collective-permute-start | bytes 1179656 | tf_op jit(solution)/shard_map/ppermute | solution.py:327
  153.3 14.9 %collective-permute-start.39 = (bf16[96,2048]{1,0:T(8,128)(2,1)S(1)}, bf16[96,2048]{1,0:T(8,128)(2,1)S(1)}, u32[]{:S(2)}, u32[]{:S(2)}) collective-permute-start(bf16[96,2048]{1,0:T(8,128)(2,1)S(1)} %pad_maximum_fusion.2), channel_id=1, source_target_pairs={{0,4},{1,5},{4,8},{5,9},{8,12},{9,13},{12,14},{13,15},{14,10},{15,... | collective-permute-start | bytes 1179656 | tf_op jit(solution)/shard_map/ppermute | solution.py:327
  168.4 11.9 %collective-permute-start.42 = (bf16[96,2048]{1,0:T(8,128)(2,1)S(1)}, bf16[96,2048]{1,0:T(8,128)(2,1)S(1)}, u32[]{:S(2)}, u32[]{:S(2)}) collective-permute-start(bf16[96,2048]{1,0:T(8,128)(2,1)S(1)} %add_convert_fusion.2), channel_id=1, source_target_pairs={{4,0},{5,1},{8,4},{9,5},{12,8},{13,9},{14,12},{15,13},{10,14},{11,... | collective-permute-start | bytes 1179656 | tf_op jit(solution)/shard_map/ppermute | solution.py:327
  169.3 11.8 %collective-permute-start.41 = (bf16[96,2048]{1,0:T(8,128)(2,1)S(1)}, bf16[96,2048]{1,0:T(8,128)(2,1)S(1)}, u32[]{:S(2)}, u32[]{:S(2)}) collective-permute-start(bf16[96,2048]{1,0:T(8,128)(2,1)S(1)} %add_convert_fusion.3), channel_id=1, source_target_pairs={{0,4},{1,5},{4,8},{5,9},{8,12},{9,13},{12,14},{13,15},{14,10},{15,... | collective-permute-start | bytes 1179656 | tf_op jit(solution)/shard_map/ppermute | solution.py:327
  181.2 7.8 %collective-permute-start.44 = (bf16[96,2048]{1,0:T(8,128)(2,1)S(1)}, bf16[96,2048]{1,0:T(8,128)(2,1)S(1)}, u32[]{:S(2)}, u32[]{:S(2)}) collective-permute-start(bf16[96,2048]{1,0:T(8,128)(2,1)S(1)} %add_convert_fusion), channel_id=1, source_target_pairs={{4,0},{5,1},{8,4},{9,5},{12,8},{13,9},{14,12},{15,13},{10,14},{11,... | collective-permute-start | bytes 1179656 | tf_op jit(solution)/shard_map/ppermute | solution.py:327
  181.7 7.8 %collective-permute-start.43 = (bf16[96,2048]{1,0:T(8,128)(2,1)S(1)}, bf16[96,2048]{1,0:T(8,128)(2,1)S(1)}, u32[]{:S(2)}, u32[]{:S(2)}) collective-permute-start(bf16[96,2048]{1,0:T(8,128)(2,1)S(1)} %add_convert_fusion.1), channel_id=1, source_target_pairs={{0,4},{1,5},{4,8},{5,9},{8,12},{9,13},{12,14},{13,15},{14,10},{15,... | collective-permute-start | bytes 1179656 | tf_op jit(solution)/shard_map/ppermute | solution.py:327

commit v8 on v7

--- a/solution.py
+++ b/solution.py
@@ -26,6 +26,20 @@
 def norm_pullback(values, gain_row, upstream):
     _, pullback = jax.vjp(lambda argument: normed(argument, gain_row), values)
     return pullback(upstream)[0]
+
+
+def norm_kernel(rows_ref, gain_ref, out_ref):
+    out_ref[...] = normed(rows_ref[...].astype(jnp.float32), gain_ref[...]).astype(jnp.bfloat16)
+
+
+def normed_rows(rows, gain_row):
+    count, width = rows.shape
+    return pl.pallas_call(
+        norm_kernel,
+        out_shape=jax.ShapeDtypeStruct((count, width), jnp.bfloat16),
+        compiler_params=pltpu.CompilerParams(vmem_limit_bytes=VMEM_LIMIT),
+        cost_estimate=pl.CostEstimate(flops=0, bytes_accessed=count * width * 4, transcendentals=0),
+    )(rows, gain_row)
 
 
 def pack_kernel(experts, rows_ref, ids_ref, gates_ref, out_ref):
@@ -219,7 +233,7 @@
             cost_estimate=pl.CostEstimate(
                 flops=0, bytes_accessed=8 * 2**20, transcendentals=0
             ),
-        )(*weights)
+        )(*in_hbm(weights))
     )
 
 
@@ -422,7 +436,7 @@
     planned = far == 4
 
     fall_wide = falling_saved[0].astype(jnp.float32)
-    fall_normal = normed(fall_wide, norm_row).astype(jnp.bfloat16)
+    fall_normal = normed_rows(falling_saved[0], norm_gain)
     fall_normal, leaving_cot, leaving_rise = lax.optimization_barrier(
         (fall_normal, falling_cot[0], rising_prev[0])
     )
@@ -463,24 +477,25 @@
         ring.gather("fall", 2)
         own_gate, own_up, own_down = own
         other_gate, other_up = swapped(own_gate), swapped(own_up)
+        packed, leaving_rise = lax.optimization_barrier((ring.held["cot"][0][0], leaving_rise))
+        ring.held["cot"][0] = [packed]
+        moved_rise = passed_along(leaving_rise, "pipe", 1)
+        own = fetched(own)
         heads = (head_rise, head_fall)
-        cot_in, leaving_rise, own, other_gate, other_up, heads, ring.names = ring.fence(
-            cot_in, leaving_rise, own, other_gate, other_up, heads, names
+        cot_in, own, own_down, other_gate, other_up, heads, ring.names = ring.fence(
+            cot_in, own, own_down, other_gate, other_up, heads, names
         )
         ring.gather("fall", 3)
         ring.gather("cot", 1)
-        moved_rise = passed_along(leaving_rise, "pipe", 1)
-        own_down = own[2]
-        own = fetched(own)
-        moved_rise, own, own_down = ring.fence(moved_rise, own, own_down)
+        ring.weights = own + (other_gate, other_up, None)
+        ring.prepare([0, 1, 2])
+        moved_rise, own_down = ring.fence(moved_rise, own_down)
         ring.gather("fall", 4)
         ring.gather("cot", 2)
         other_down = swapped(own_down)
         rise_in = entered(moved_rise)
         rise_normal = normed(rise_in.astype(jnp.float32), norm_row).astype(jnp.bfloat16)
         kept, exit_loss = exit_heads(rise_in, cot_in, *heads)
-        ring.weights = own + (other_gate, other_up, None)
-        ring.prepare([0, 1, 2, 3])
         rise_normal, kept, exit_loss, other_down = ring.fence(
             rise_normal, kept, exit_loss, other_down
         )
@@ -489,10 +504,10 @@
         ring.gather("cot", 3)
         ring.gather("rise", 1)
         ring.work("backward", [0, 1, 2])
+        ring.prepare([3, 4])
         ring.fence()
         ring.gather("cot", 4)
         ring.gather("rise", 2)
-        ring.prepare([4])
         ring.work("forward", [0, 1])
         ring.fence()
         ring.gather("rise", 3)

time: 191 us -> 199 us (1.042)
  local copies, waits for them, and re-layouts: 6.68 us -> 16.9 us
  starting transfers between devices: 52 us -> 48.2 us
  Pallas kernels: 59.1 us -> 62.8 us
  other arithmetic: 8.92 us -> 6.83 us
    unnamed x22 -> x62, local copies, waits for them, and re-layouts: 3.24 us -> 13.5 us
    ppermute x2, starting transfers between devices: 8.66 us -> 5.11 us  [passed_along(): return lax.ppermute(block, axis, route)]
  transfers between devices with their start and end apart: 45 -> 45, of which waited for: 15 -> 17; matrix products, arithmetic and copies ran while one was open for 5% -> 5% of each run, Pallas kernels for 31% -> 32%
where the time goes in v8:
time: 199 us; the launch traced here: 198 us
  Pallas kernels  62.8 us (32%)
  waiting for transfers between devices  60.9 us (31%)
  starting transfers between devices  48.2 us (24%)
  local copies, waits for them, and re-layouts  16.9 us (8%)
  other arithmetic  6.83 us (3%)
  between operations  2.61 us (1%)
    ppermute x40, waiting for transfers between devices, pass_on(): return lax.ppermute(block, 'ep', self.routes[way])  60.9 us
    ppermute x40, starting transfers between devices, pass_on(): return lax.ppermute(block, 'ep', self.routes[way])  42.5 us
    pallas_call x3, Pallas kernels, forward_call(): pl.pallas_call(functools.partial(forward_kernel, parts, experts, width, T...  23 us
    pallas_call x2, Pallas kernels, backward_call(): pl.pallas_call(functools.partial(backward_kernel, parts, experts, width,...  21.3 us
    pallas_call x2, Pallas kernels, factor_call(): pl.pallas_call(functools.partial(factor_kernel, parts), out_shape=jax.Sha...  14.5 us
    unnamed x62, local copies, waits for them, and re-layouts  13.5 us
    ppermute x2, starting transfers between devices, passed_along(): return lax.ppermute(block, axis, route)  5.11 us
  transfers between devices with their start and end apart: 45, of which 17 were waited for; matrix products, arithmetic and copies ran while one was open for 5% of the time, Pallas kernels for 32%

profile of v8, /device:TPU:0, one launch (start us, length us, event | category | flops | bytes accessed | tf_op | source)
XLA Modules:
  0.0 198.2 jit_solution(5971012683243988745)
XLA Ops:
  1.2 1.0 copy-done
  2.2 0.7 copy-done.3
  3.1 3.0 %collective-permute-start.2 = (bf16[96,2048]{1,0:T(8,128)(2,1)S(1)}, bf16[96,2048]{1,0:T(8,128)(2,1)}, u32[]{:S(2)}, u32[]{:S(2)}) collective-permute-start(bf16[96,2048]{1,0:T(8,128)(2,1)S(1)} %shard_map.148.refs_0_), channel_id=1, source_target_pairs={{4,0},{5,1},{8,4},{9,5},{12,8},{13,9},{14,12},{15,13},{10,14},{11,... | collective-permute-start | bytes 1179656 | tf_op jit(solution)/shard_map/ppermute | solution.py:341
  6.2 3.8 %collective-permute-start = (bf16[96,2048]{1,0:T(8,128)(2,1)}, bf16[96,2048]{1,0:T(8,128)(2,1)S(1)}, u32[]{:S(2)}, u32[]{:S(2)}) collective-permute-start(bf16[96,2048]{1,0:T(8,128)(2,1)} %bitcast.61), channel_id=1, source_target_pairs={{0,16},{1,17},{2,18},{3,19},{4,20},{5,21},{6,22},{7,23},{8,24},{9,... | collective-permute-start | bytes 1179656 | tf_op jit(solution)/shard_map/ppermute | solution.py:17
  10.1 0.8 fusion.19
  12.7 0.8 copy.16
  13.5 0.8 copy.17
  14.3 3.0 %shard_map.150 = (bf16[2048,512]{1,0:T(8,128)(2,1)S(1)}, bf16[2048,512]{1,0:T(8,128)(2,1)S(1)}, bf16[512,2048]{1,0:T(8,128)(2,1)S(1)}) custom-call(bf16[2048,512]{1,0:T(8,128)(2,1)} %bitcast.54, bf16[2048,512]{1,0:T(8,128)(2,1)} %bitcast.56, bf16[512,2048]{1,0:T(8,128)(2,1)} %bitcast.9.refs_2_), custom_call_target="tpu_custom_call" | custom-call | bytes 8388608 | tf_op jit(solution)/shard_map/pallas_call | solution.py:226
  17.4 1.4 copy-done.5
  18.7 1.4 copy-done.8
  20.1 1.4 copy-done.11
  21.8 1.6 collective-permute-start.4
  23.9 0.7 shard_map.149.refs_0_
  24.7 1.3 collective-permute-start.11
  26.0 6.3 %collective-permute-done.4.refs_4_ = bf16[96,2048]{1,0:T(8,128)(2,1)S(1)} collective-permute-done((bf16[96,2048]{1,0:T(8,128)(2,1)}, bf16[96,2048]{1,0:T(8,128)(2,1)S(1)}, u32[]{:S(2)}, u32[]{:S(2)}) %collective-permute-start.4) | collective-permute-done | bytes 393248 | tf_op jit(solution)/shard_map/ppermute | solution.py:341
  32.3 1.2 collective-permute-done.3.refs_3_
  33.6 1.6 collective-permute-start.8
  36.1 1.5 collective-permute-start.10
  37.7 1.6 copy-done.9
  39.3 8.3 %shard_map.151.refs_5_ = bf16[4,480,512]{2,1,0:T(8,128)(2,1)S(1)} custom-call(bf16[96,2048]{1,0:T(8,128)(2,1)} %copy-done.2, bf16[96,2048]{1,0:T(8,128)(2,1)} %collective-permute-done.1.refs_1_, bf16[96,2048]{1,0:T(8,128)(2,1)} %collective-permute-done.2.refs_2_, bf16[96,2048]{1,0:T(8,128)(2,1)} %copy-done.27, bf16[96,2048]{1,0:T(8,128)(2,1)} %copy-done.26, ...), custom_call_target="tpu_custom_call" | custom-call | flops 9526532096 | bytes 12582912 | tf_op jit(solution)/shard_map/pallas_call | solution.py:276
  47.6 1.2 copy-done.17
  48.9 4.0 %collective-permute-done.9.refs_0_ = bf16[96,2048]{1,0:T(8,128)(2,1)S(1)} collective-permute-done((bf16[96,2048]{1,0:T(8,128)(2,1)S(1)}, bf16[96,2048]{1,0:T(8,128)(2,1)S(1)}, u32[]{:S(2)}, u32[]{:S(2)}) %collective-permute-start.9) | collective-permute-done | bytes 393248 | tf_op jit(solution)/shard_map/ppermute | solution.py:341
  52.9 0.8 copy-done.13
  54.5 1.0 slice.64
  55.5 0.9 slice.65
  56.5 1.6 collective-permute-start.15
  59.0 1.6 collective-permute-start.13
  60.6 1.4 fusion.6
  62.0 0.6 multiply_reduce_fusion
  64.3 1.6 collective-permute-done.14.refs_2_
  65.9 7.4 %collective-permute-done.12.refs_3_.refs_0_ = bf16[96,2176]{1,0:T(8,128)(2,1)S(1)} collective-permute-done((bf16[96,2176]{1,0:T(8,128)(2,1)}, bf16[96,2176]{1,0:T(8,128)(2,1)S(1)}, u32[]{:S(2)}, u32[]{:S(2)}) %collective-permute-start.12) | collective-permute-done | bytes 417824 | tf_op jit(solution)/shard_map/ppermute | solution.py:341
  73.4 1.6 collective-permute-start.20
  75.8 1.6 collective-permute-start.18
  77.4 1.5 copy-done.18
  79.0 12.1 %shard_map.153 = (bf16[96,2048]{1,0:T(8,128)(2,1)S(1)}, bf16[96,2048]{1,0:T(8,128)(2,1)S(1)}, bf16[96,2048]{1,0:T(8,128)(2,1)S(1)}, bf16[96,2048]{1,0:T(8,128)(2,1)S(1)}, bf16[96,2048]{1,0:T(8,128)(2,1)S(1)}) custom-call(s32[2]{0:T(128)S(1)} %pad_add_fusion.names_ref, bf16[96,2176]{1,0:T(8,128)(2,1)S(1)} %shard_map.149.refs_0_, ...), custom_call_target="tpu_custom_call" | custom-call | flops 12639797248 | bytes 12582912 | tf_op jit(solution)/shard_map/pallas_call | solution.py:294
  91.1 6.2 %shard_map.152.refs_4_ = bf16[4,288,512]{2,1,0:T(8,128)(2,1)S(1)} custom-call(bf16[96,2048]{1,0:T(8,128)(2,1)} %copy-done.22, bf16[96,2048]{1,0:T(8,128)(2,1)} %copy-done.23, bf16[48,2048]{1,0:T(8,128)(2,1)} %copy-done.29, bf16[48,2048]{1,0:T(8,128)(2,1)} %copy-done.28, bf16[2048,512]{1,0:T(8,128)(2,1)S(1)} %copy-done.7, bf16[2048,512]{1,0:T(8,128)(2,1)S(1)} %copy-done.10, ...), custom_call_target="tpu_custom_call" | custom-call | flops 7915919360 | bytes 12582912 | tf_op jit(solution)/shard_map/pallas_call | solution.py:276
  97.4 1.6 collective-permute-start.22
  99.9 1.6 collective-permute-start.24
  101.5 8.0 %shard_map.154 = (bf16[96,2048]{1,0:T(8,128)(2,1)S(1)}, bf16[96,2048]{1,0:T(8,128)(2,1)S(1)}, bf16[96,2048]{1,0:T(8,128)(2,1)S(1)}) custom-call(s32[2]{0:T(128)S(1)} %pad_add_fusion.names_ref, bf16[96,2176]{1,0:T(8,128)(2,1)S(1)} %shard_map.149.refs_0_, bf16[96,2176]{1,0:T(8,128)(2,1)S(1)} %copy-done.16, bf16[96,2176]{1,0:T(8,128)(2,1)S(1)} %copy-done.14, ...), custom_call_target="tpu_custom_call" | custom-call | flops 10223878144 | bytes 12582912 | tf_op jit(solution)/shard_map/pallas_call | solution.py:256
  109.5 3.2 %collective-permute-done.23.refs_2_ = bf16[96,2048]{1,0:T(8,128)(2,1)S(1)} collective-permute-done((bf16[96,2048]{1,0:T(8,128)(2,1)S(1)}, bf16[96,2048]{1,0:T(8,128)(2,1)S(1)}, u32[]{:S(2)}, u32[]{:S(2)}) %collective-permute-start.23) | collective-permute-done | bytes 393248 | tf_op jit(solution)/shard_map/ppermute | solution.py:341
  113.2 1.6 collective-permute-start.26
  114.8 9.2 %shard_map.155 = (bf16[96,2048]{1,0:T(8,128)(2,1)S(1)}, bf16[96,2048]{1,0:T(8,128)(2,1)S(1)}, bf16[48,2048]{1,0:T(8,128)(2,1)S(1)}, bf16[48,2048]{1,0:T(8,128)(2,1)S(1)}) custom-call(s32[2]{0:T(128)S(1)} %pad_add_fusion.names_ref, bf16[96,2176]{1,0:T(8,128)(2,1)S(1)} %collective-permute-done.17.refs_0_, ...), custom_call_target="tpu_custom_call" | custom-call | flops 10223878144 | bytes 12582912 | tf_op jit(solution)/shard_map/pallas_call | solution.py:294
  124.7 1.5 collective-permute-start.27
  126.6 1.6 collective-permute-start.30
  128.2 6.7 %shard_map.156 = (bf16[96,2048]{1,0:T(8,128)(2,1)S(1)}, bf16[96,2048]{1,0:T(8,128)(2,1)S(1)}) custom-call(s32[2]{0:T(128)S(1)} %pad_add_fusion.names_ref, bf16[96,2176]{1,0:T(8,128)(2,1)S(1)} %collective-permute-done.12.refs_3_.refs_0_, bf16[96,2176]{1,0:T(8,128)(2,1)S(1)} %collective-permute-done.13.refs_4_.refs_1_, ...), custom_call_target="tpu_custom_call" | custom-call | flops 9015918592 | bytes 12582912 | tf_op jit(solution)/shard_map/pallas_call | solution.py:256
  135.1 1.0 collective-permute-start.32
  136.1 1.1 collective-permute-start.31
  137.2 8.4 %shard_map.157 = (bf16[96,2048]{1,0:T(8,128)(2,1)S(1)}, bf16[96,2048]{1,0:T(8,128)(2,1)S(1)}, bf16[48,2048]{1,0:T(8,128)(2,1)S(1)}, bf16[48,2048]{1,0:T(8,128)(2,1)S(1)}) custom-call(s32[2]{0:T(128)S(1)} %pad_add_fusion.names_ref, bf16[96,2176]{1,0:T(8,128)(2,1)S(1)} %collective-permute-done.17.refs_0_, ...), custom_call_target="tpu_custom_call" | custom-call | flops 10223878144 | bytes 12582912 | tf_op jit(solution)/shard_map/pallas_call | solution.py:256
  146.9 1.5 collective-permute-start.33
  148.4 0.7 collective-permute-start.35
  149.1 1.3 collective-permute-start.36
  150.4 9.6 %collective-permute-done.35 = bf16[48,2048]{1,0:T(8,128)(2,1)S(1)} collective-permute-done((bf16[48,2048]{1,0:T(8,128)(2,1)S(1)}, bf16[48,2048]{1,0:T(8,128)(2,1)S(1)}, u32[]{:S(2)}, u32[]{:S(2)}) %collective-permute-start.35) | collective-permute-done | bytes 196640 | tf_op jit(solution)/shard_map/ppermute | solution.py:341
  160.8 1.8 collective-permute-start.37
  163.0 1.8 collective-permute-start.39
  164.7 4.0 %collective-permute-done.38 = bf16[96,2048]{1,0:T(8,128)(2,1)S(1)} collective-permute-done((bf16[96,2048]{1,0:T(8,128)(2,1)S(1)}, bf16[96,2048]{1,0:T(8,128)(2,1)S(1)}, u32[]{:S(2)}, u32[]{:S(2)}) %collective-permute-start.38) | collective-permute-done | bytes 393248 | tf_op jit(solution)/shard_map/ppermute | solution.py:341
  168.7 1.0 collective-permute-done.37
  169.8 7.2 %collective-permute-done.40 = bf16[96,2048]{1,0:T(8,128)(2,1)S(1)} collective-permute-done((bf16[96,2048]{1,0:T(8,128)(2,1)S(1)}, bf16[96,2048]{1,0:T(8,128)(2,1)S(1)}, u32[]{:S(2)}, u32[]{:S(2)}) %collective-permute-start.40) | collective-permute-done | bytes 393248 | tf_op jit(solution)/shard_map/ppermute | solution.py:341
  177.0 0.9 collective-permute-done.39
  178.1 2.1 %collective-permute-start.41 = (bf16[96,2048]{1,0:T(8,128)(2,1)S(1)}, bf16[96,2048]{1,0:T(8,128)(2,1)S(1)}, u32[]{:S(2)}, u32[]{:S(2)}) collective-permute-start(bf16[96,2048]{1,0:T(8,128)(2,1)S(1)} %add_convert_fusion.3), channel_id=1, source_target_pairs={{0,4},{1,5},{4,8},{5,9},{8,12},{9,13},{12,14},{13,15},{14,10},{15,... | collective-permute-start | bytes 1179656 | tf_op jit(solution)/shard_map/ppermute | solution.py:341
  180.6 1.1 fusion.11
  181.7 7.1 %collective-permute-done.42 = bf16[96,2048]{1,0:T(8,128)(2,1)S(1)} collective-permute-done((bf16[96,2048]{1,0:T(8,128)(2,1)S(1)}, bf16[96,2048]{1,0:T(8,128)(2,1)S(1)}, u32[]{:S(2)}, u32[]{:S(2)}) %collective-permute-start.42) | collective-permute-done | bytes 393248 | tf_op jit(solution)/shard_map/ppermute | solution.py:341
  189.4 2.0 collective-permute-start.43
  191.3 5.6 %collective-permute-done.44 = bf16[96,2048]{1,0:T(8,128)(2,1)S(1)} collective-permute-done((bf16[96,2048]{1,0:T(8,128)(2,1)S(1)}, bf16[96,2048]{1,0:T(8,128)(2,1)S(1)}, u32[]{:S(2)}, u32[]{:S(2)}) %collective-permute-start.44) | collective-permute-done | bytes 393248 | tf_op jit(solution)/shard_map/ppermute | solution.py:341
  197.2 1.0 fusion.17
  (142 shorter events, 14.0 us)
Async XLA Ops:
  0.6 32.9 %collective-permute-start.5 = (bf16[2048,512]{1,0:T(8,128)(2,1)}, bf16[2048,512]{1,0:T(8,128)(2,1)}, u32[]{:S(2)}, u32[]{:S(2)}) collective-permute-start(bf16[2048,512]{1,0:T(8,128)(2,1)} %bitcast.53), channel_id=1, source_target_pairs={{0,1},{1,0},{2,3},{3,2},{4,5},{5,4},{6,7},{7,6},{8,9},{9,8},{10,11... | collective-permute-start | bytes 6291464 | tf_op jit(solution)/shard_map/ppermute | solution.py:449
  1.1 32.4 %collective-permute-start.6 = (bf16[2048,512]{1,0:T(8,128)(2,1)}, bf16[2048,512]{1,0:T(8,128)(2,1)}, u32[]{:S(2)}, u32[]{:S(2)}) collective-permute-start(bf16[2048,512]{1,0:T(8,128)(2,1)} %bitcast.55), channel_id=1, source_target_pairs={{0,1},{1,0},{2,3},{3,2},{4,5},{5,4},{6,7},{7,6},{8,9},{9,8},{10,11... | collective-permute-start | bytes 6291464 | tf_op jit(solution)/shard_map/ppermute | solution.py:449
  3.1 14.2 %copy-start.2 = (bf16[96,2048]{1,0:T(8,128)(2,1)}, bf16[96,2048]{1,0:T(8,128)(2,1)S(1)}, u32[]{:S(2)}) copy-start(bf16[96,2048]{1,0:T(8,128)(2,1)S(1)} %shard_map.148.refs_0_) | copy-start | bytes 1179652
  3.1 18.6 %collective-permute-start.2 = (bf16[96,2048]{1,0:T(8,128)(2,1)S(1)}, bf16[96,2048]{1,0:T(8,128)(2,1)}, u32[]{:S(2)}, u32[]{:S(2)}) collective-permute-start(bf16[96,2048]{1,0:T(8,128)(2,1)S(1)} %shard_map.148.refs_0_), channel_id=1, source_target_pairs={{4,0},{5,1},{8,4},{9,5},{12,8},{13,9},{14,12},{15,13},{10,14},{11,... | collective-permute-start | bytes 1179656 | tf_op jit(solution)/shard_map/ppermute | solution.py:341
  6.1 17.2 %collective-permute-start.1 = (bf16[96,2048]{1,0:T(8,128)(2,1)S(1)}, bf16[96,2048]{1,0:T(8,128)(2,1)}, u32[]{:S(2)}, u32[]{:S(2)}) collective-permute-start(bf16[96,2048]{1,0:T(8,128)(2,1)S(1)} %shard_map.148.refs_0_), channel_id=1, source_target_pairs={{0,4},{1,5},{4,8},{5,9},{8,12},{9,13},{12,14},{13,15},{14,10},{15,... | collective-permute-start | bytes 1179656 | tf_op jit(solution)/shard_map/ppermute | solution.py:341
  6.2 17.6 %collective-permute-start = (bf16[96,2048]{1,0:T(8,128)(2,1)}, bf16[96,2048]{1,0:T(8,128)(2,1)S(1)}, u32[]{:S(2)}, u32[]{:S(2)}) collective-permute-start(bf16[96,2048]{1,0:T(8,128)(2,1)} %bitcast.61), channel_id=1, source_target_pairs={{0,16},{1,17},{2,18},{3,19},{4,20},{5,21},{6,22},{7,23},{8,24},{9,... | collective-permute-start | bytes 1179656 | tf_op jit(solution)/shard_map/ppermute | solution.py:17
  14.3 7.3 %copy-start.1 = (bf16[1,96,2048]{2,1,0:T(8,128)(2,1)S(1)}, bf16[1,96,2048]{2,1,0:T(8,128)(2,1)}, u32[]{:S(2)}) copy-start(bf16[1,96,2048]{2,1,0:T(8,128)(2,1)} %param.16) | copy-start | bytes 1179652
  14.3 9.5 %copy-start.20 = (bf16[2,96,2048]{2,1,0:T(8,128)(2,1)S(1)}, bf16[2,96,2048]{2,1,0:T(8,128)(2,1)}, u32[]{:S(2)}) copy-start(bf16[2,96,2048]{2,1,0:T(8,128)(2,1)} %param.13) | copy-start | bytes 2359300
  21.5 3.1 %copy-start.25 = (bf16[1,96,2048]{2,1,0:T(8,128)(2,1)S(1)}, bf16[1,96,2048]{2,1,0:T(8,128)(2,1)}, u32[]{:S(2)}) copy-start(bf16[1,96,2048]{2,1,0:T(8,128)(2,1)} %param.14) | copy-start | bytes 1179652
  21.5 16.2 %copy-start.6 = (bf16[2048,512]{1,0:T(8,128)(2,1)S(1)}, bf16[2048,512]{1,0:T(8,128)(2,1)}, u32[]{:S(2)}) copy-start(bf16[2048,512]{1,0:T(8,128)(2,1)} %copy-done.5) | copy-start | bytes 6291460
  21.8 10.5 %collective-permute-start.4 = (bf16[96,2048]{1,0:T(8,128)(2,1)}, bf16[96,2048]{1,0:T(8,128)(2,1)S(1)}, u32[]{:S(2)}, u32[]{:S(2)}) collective-permute-start(bf16[96,2048]{1,0:T(8,128)(2,1)} %collective-permute-done.2.refs_2_), channel_id=1, source_target_pairs={{4,0},{5,1},{8,4},{9,5},{12,8},{13,9},{14,12},{15,13},{10,14},{11,... | collective-permute-start | bytes 1179656 | tf_op jit(solution)/shard_map/ppermute | solution.py:341
  23.3 10.2 %collective-permute-start.3 = (bf16[96,2048]{1,0:T(8,128)(2,1)}, bf16[96,2048]{1,0:T(8,128)(2,1)S(1)}, u32[]{:S(2)}, u32[]{:S(2)}) collective-permute-start(bf16[96,2048]{1,0:T(8,128)(2,1)} %collective-permute-done.1.refs_1_), channel_id=1, source_target_pairs={{0,4},{1,5},{4,8},{5,9},{8,12},{9,13},{12,14},{13,15},{14,10},{15,... | collective-permute-start | bytes 1179656 | tf_op jit(solution)/shard_map/ppermute | solution.py:341
  24.7 24.2 %collective-permute-start.11 = (bf16[96,2048]{1,0:T(8,128)(2,1)S(1)}, bf16[96,2048]{1,0:T(8,128)(2,1)S(1)}, u32[]{:S(2)}, u32[]{:S(2)}) collective-permute-start(bf16[96,2048]{1,0:T(8,128)(2,1)S(1)} %bitcast.62), channel_id=1, source_target_pairs={{0,16},{1,17},{2,18},{3,19},{4,20},{5,21},{6,22},{7,23},{8,24},{9,... | collective-permute-start | bytes 1179656 | tf_op jit(solution)/shard_map/ppermute | solution.py:17
  32.3 5.4 %copy-start.26 = (bf16[96,2048]{1,0:T(8,128)(2,1)}, bf16[96,2048]{1,0:T(8,128)(2,1)S(1)}, u32[]{:S(2)}) copy-start(bf16[96,2048]{1,0:T(8,128)(2,1)S(1)} %collective-permute-done.4.refs_4_) | copy-start | bytes 1179652
  33.5 4.1 %copy-start.27 = (bf16[96,2048]{1,0:T(8,128)(2,1)}, bf16[96,2048]{1,0:T(8,128)(2,1)S(1)}, u32[]{:S(2)}) copy-start(bf16[96,2048]{1,0:T(8,128)(2,1)S(1)} %collective-permute-done.3.refs_3_) | copy-start | bytes 1179652
  33.5 28.5 %copy-start.4 = (f32[1,2048]{1,0:T(1,128)S(1)}, f32[1,2048]{1,0:T(1,128)}, u32[]{:S(2)}) copy-start(f32[1,2048]{1,0:T(1,128)} %gain_ref.1) | copy-start | bytes 24580
  33.6 19.4 %collective-permute-start.8 = (bf16[96,2176]{1,0:T(8,128)(2,1)S(1)}, bf16[96,2176]{1,0:T(8,128)(2,1)S(1)}, u32[]{:S(2)}, u32[]{:S(2)}) collective-permute-start(bf16[96,2176]{1,0:T(8,128)(2,1)S(1)} %shard_map.149.refs_0_), channel_id=1, source_target_pairs={{4,0},{5,1},{8,4},{9,5},{12,8},{13,9},{14,12},{15,13},{10,14},{11,... | collective-permute-start | bytes 1253384 | tf_op jit(solution)/shard_map/ppermute | solution.py:341
  35.2 17.8 %collective-permute-start.7 = (bf16[96,2176]{1,0:T(8,128)(2,1)S(1)}, bf16[96,2176]{1,0:T(8,128)(2,1)S(1)}, u32[]{:S(2)}, u32[]{:S(2)}) collective-permute-start(bf16[96,2176]{1,0:T(8,128)(2,1)S(1)} %shard_map.149.refs_0_), channel_id=1, source_target_pairs={{0,4},{1,5},{4,8},{5,9},{8,12},{9,13},{12,14},{13,15},{14,10},{15,... | collective-permute-start | bytes 1253384 | tf_op jit(solution)/shard_map/ppermute | solution.py:341
  35.6 17.3 %collective-permute-start.9 = (bf16[96,2048]{1,0:T(8,128)(2,1)S(1)}, bf16[96,2048]{1,0:T(8,128)(2,1)S(1)}, u32[]{:S(2)}, u32[]{:S(2)}) collective-permute-start(bf16[96,2048]{1,0:T(8,128)(2,1)S(1)} %collective-permute-done.3.refs_3_), channel_id=1, source_target_pairs={{0,4},{1,5},{4,8},{5,9},{8,12},{9,13},{12,14},{13,15},{14,10},{15,... | collective-permute-start | bytes 1179656 | tf_op jit(solution)/shard_map/ppermute | solution.py:341
  36.1 16.8 %collective-permute-start.10 = (bf16[96,2048]{1,0:T(8,128)(2,1)S(1)}, bf16[96,2048]{1,0:T(8,128)(2,1)S(1)}, u32[]{:S(2)}, u32[]{:S(2)}) collective-permute-start(bf16[96,2048]{1,0:T(8,128)(2,1)S(1)} %collective-permute-done.4.refs_4_), channel_id=1, source_target_pairs={{4,0},{5,1},{8,4},{9,5},{12,8},{13,9},{14,12},{15,13},{10,14},{11,... | collective-permute-start | bytes 1179656 | tf_op jit(solution)/shard_map/ppermute | solution.py:341
  37.7 1.6 copy-start.9
  39.3 22.8 %copy-start.24 = (f32[1,2048]{1,0:T(1,128)S(1)}, f32[1,2048]{1,0:T(1,128)}, u32[]{:S(2)}) copy-start(f32[1,2048]{1,0:T(1,128)} %param.19) | copy-start | bytes 24580
  39.3 38.2 %copy-start.12 = (bf16[512,2048]{1,0:T(8,128)(2,1)S(1)}, bf16[512,2048]{1,0:T(8,128)(2,1)}, u32[]{:S(2)}) copy-start(bf16[512,2048]{1,0:T(8,128)(2,1)} %copy-done.11) | copy-start | bytes 6291460
  48.9 4.9 %copy-start.21 = (bf16[96,2048]{1,0:T(8,128)(2,1)}, bf16[96,2048]{1,0:T(8,128)(2,1)S(1)}, u32[]{:S(2)}) copy-start(bf16[96,2048]{1,0:T(8,128)(2,1)S(1)} %collective-permute-done.11) | copy-start | bytes 1179652
  53.7 19.6 %collective-permute-start.16 = (bf16[512,2048]{1,0:T(8,128)(2,1)}, bf16[512,2048]{1,0:T(8,128)(2,1)}, u32[]{:S(2)}, u32[]{:S(2)}) collective-permute-start(bf16[512,2048]{1,0:T(8,128)(2,1)} %bitcast.9.refs_2_), channel_id=1, source_target_pairs={{0,1},{1,0},{2,3},{3,2},{4,5},{5,4},{6,7},{7,6},{8,9},{9,8},{10,11... | collective-permute-start | bytes 6291464 | tf_op jit(solution)/shard_map/ppermute | solution.py:449
  54.5 7.5 %copy-start.19 = (bf16[2,96,2048]{2,1,0:T(8,128)(2,1)S(1)}, bf16[2,96,2048]{2,1,0:T(8,128)(2,1)}, u32[]{:S(2)}) copy-start(bf16[2,96,2048]{2,1,0:T(8,128)(2,1)} %param.17) | copy-start | bytes 2359300
  56.5 7.9 %collective-permute-start.15 = (bf16[48,2048]{1,0:T(8,128)(2,1)S(1)}, bf16[48,2048]{1,0:T(8,128)(2,1)S(1)}, u32[]{:S(2)}, u32[]{:S(2)}) collective-permute-start(bf16[48,2048]{1,0:T(8,128)(2,1)S(1)} %slice.65), channel_id=1, source_target_pairs={{4,0},{5,1},{8,4},{9,5},{12,8},{13,9},{14,12},{15,13},{10,14},{11,... | collective-permute-start | bytes 589832 | tf_op jit(solution)/shard_map/ppermute | solution.py:341
  58.1 7.8 %collective-permute-start.14 = (bf16[48,2048]{1,0:T(8,128)(2,1)S(1)}, bf16[48,2048]{1,0:T(8,128)(2,1)S(1)}, u32[]{:S(2)}, u32[]{:S(2)}) collective-permute-start(bf16[48,2048]{1,0:T(8,128)(2,1)S(1)} %slice.64), channel_id=1, source_target_pairs={{0,4},{1,5},{4,8},{5,9},{8,12},{9,13},{12,14},{13,15},{14,10},{15,... | collective-permute-start | bytes 589832 | tf_op jit(solution)/shard_map/ppermute | solution.py:341
  58.5 14.8 %collective-permute-start.12 = (bf16[96,2176]{1,0:T(8,128)(2,1)}, bf16[96,2176]{1,0:T(8,128)(2,1)S(1)}, u32[]{:S(2)}, u32[]{:S(2)}) collective-permute-start(bf16[96,2176]{1,0:T(8,128)(2,1)} %copy-done.15), channel_id=1, source_target_pairs={{0,4},{1,5},{4,8},{5,9},{8,12},{9,13},{12,14},{13,15},{14,10},{15,... | collective-permute-start | bytes 1253384 | tf_op jit(solution)/shard_map/ppermute | solution.py:341
  59.0 14.4 %collective-permute-start.13 = (bf16[96,2176]{1,0:T(8,128)(2,1)}, bf16[96,2176]{1,0:T(8,128)(2,1)S(1)}, u32[]{:S(2)}, u32[]{:S(2)}) collective-permute-start(bf16[96,2176]{1,0:T(8,128)(2,1)} %copy-done.13), channel_id=1, source_target_pairs={{4,0},{5,1},{8,4},{9,5},{12,8},{13,9},{14,12},{15,13},{10,14},{11,... | collective-permute-start | bytes 1253384 | tf_op jit(solution)/shard_map/ppermute | solution.py:341
  60.6 16.8 %copy-start.10 = (bf16[2048,512]{1,0:T(8,128)(2,1)S(1)}, bf16[2048,512]{1,0:T(8,128)(2,1)}, u32[]{:S(2)}) copy-start(bf16[2048,512]{1,0:T(8,128)(2,1)} %copy-done.8) | copy-start | bytes 6291460
  62.0 15.5 %copy-start.7 = (bf16[2048,512]{1,0:T(8,128)(2,1)S(1)}, bf16[2048,512]{1,0:T(8,128)(2,1)}, u32[]{:S(2)}) copy-start(bf16[2048,512]{1,0:T(8,128)(2,1)} %copy-done.5) | copy-start | bytes 6291460
  62.0 15.4 %copy-start.14 = (bf16[96,2176]{1,0:T(8,128)(2,1)S(1)}, bf16[96,2176]{1,0:T(8,128)(2,1)}, u32[]{:S(2)}) copy-start(bf16[96,2176]{1,0:T(8,128)(2,1)} %copy-done.13) | copy-start | bytes 1253380
  62.0 15.4 %copy-start.16 = (bf16[96,2176]{1,0:T(8,128)(2,1)S(1)}, bf16[96,2176]{1,0:T(8,128)(2,1)}, u32[]{:S(2)}) copy-start(bf16[96,2176]{1,0:T(8,128)(2,1)} %copy-done.15) | copy-start | bytes 1253380
  64.3 26.7 %copy-start.28 = (bf16[48,2048]{1,0:T(8,128)(2,1)}, bf16[48,2048]{1,0:T(8,128)(2,1)S(1)}, u32[]{:S(2)}) copy-start(bf16[48,2048]{1,0:T(8,128)(2,1)S(1)} %collective-permute-done.15.refs_3_) | copy-start | bytes 589828
  65.9 25.1 %copy-start.29 = (bf16[48,2048]{1,0:T(8,128)(2,1)}, bf16[48,2048]{1,0:T(8,128)(2,1)S(1)}, u32[]{:S(2)}) copy-start(bf16[48,2048]{1,0:T(8,128)(2,1)S(1)} %collective-permute-done.14.refs_2_) | copy-start | bytes 589828
  73.4 23.9 %collective-permute-start.20 = (bf16[96,2048]{1,0:T(8,128)(2,1)S(1)}, bf16[96,2048]{1,0:T(8,128)(2,1)S(1)}, u32[]{:S(2)}, u32[]{:S(2)}) collective-permute-start(bf16[96,2048]{1,0:T(8,128)(2,1)S(1)} %get-tuple-element.247.refs_3_), channel_id=1, source_target_pairs={{4,0},{5,1},{8,4},{9,5},{12,8},{13,9},{14,12},{15,13},{10,14},{11,... | collective-permute-start | bytes 1179656 | tf_op jit(solution)/shard_map/ppermute | solution.py:341
  74.9 22.3 %collective-permute-start.19 = (bf16[96,2048]{1,0:T(8,128)(2,1)S(1)}, bf16[96,2048]{1,0:T(8,128)(2,1)S(1)}, u32[]{:S(2)}, u32[]{:S(2)}) collective-permute-start(bf16[96,2048]{1,0:T(8,128)(2,1)S(1)} %get-tuple-element.247.refs_3_), channel_id=1, source_target_pairs={{0,4},{1,5},{4,8},{5,9},{8,12},{9,13},{12,14},{13,15},{14,10},{15,... | collective-permute-start | bytes 1179656 | tf_op jit(solution)/shard_map/ppermute | solution.py:341
  75.4 21.9 %collective-permute-start.17 = (bf16[96,2176]{1,0:T(8,128)(2,1)S(1)}, bf16[96,2176]{1,0:T(8,128)(2,1)S(1)}, u32[]{:S(2)}, u32[]{:S(2)}) collective-permute-start(bf16[96,2176]{1,0:T(8,128)(2,1)S(1)} %collective-permute-done.12.refs_3_.refs_0_), channel_id=1, source_target_pairs={{0,4},{1,5},{4,8},{5,9},{8,12},{9,13},{12,14},{13,15},{14,10},{15,... | collective-permute-start | bytes 1253384 | tf_op jit(solution)/shard_map/ppermute | solution.py:341
  75.8 21.5 %collective-permute-start.18 = (bf16[96,2176]{1,0:T(8,128)(2,1)S(1)}, bf16[96,2176]{1,0:T(8,128)(2,1)S(1)}, u32[]{:S(2)}, u32[]{:S(2)}) collective-permute-start(bf16[96,2176]{1,0:T(8,128)(2,1)S(1)} %collective-permute-done.13.refs_4_.refs_1_), channel_id=1, source_target_pairs={{4,0},{5,1},{8,4},{9,5},{12,8},{13,9},{14,12},{15,13},{10,14},{11,... | collective-permute-start | bytes 1253384 | tf_op jit(solution)/shard_map/ppermute | solution.py:341
  97.4 12.1 %collective-permute-start.22 = (bf16[48,2176]{1,0:T(8,128)(2,1)S(1)}, bf16[48,2176]{1,0:T(8,128)(2,1)S(1)}, u32[]{:S(2)}, u32[]{:S(2)}) collective-permute-start(bf16[48,2176]{1,0:T(8,128)(2,1)S(1)} %slice.69), channel_id=1, source_target_pairs={{4,0},{5,1},{8,4},{9,5},{12,8},{13,9},{14,12},{15,13},{10,14},{11,... | collective-permute-start | bytes 626696 | tf_op jit(solution)/shard_map/ppermute | solution.py:341
  99.0 10.5 %collective-permute-start.21 = (bf16[48,2176]{1,0:T(8,128)(2,1)S(1)}, bf16[48,2176]{1,0:T(8,128)(2,1)S(1)}, u32[]{:S(2)}, u32[]{:S(2)}) collective-permute-start(bf16[48,2176]{1,0:T(8,128)(2,1)S(1)} %slice.68), channel_id=1, source_target_pairs={{0,4},{1,5},{4,8},{5,9},{8,12},{9,13},{12,14},{13,15},{14,10},{15,... | collective-permute-start | bytes 626696 | tf_op jit(solution)/shard_map/ppermute | solution.py:341
  99.4 13.3 %collective-permute-start.23 = (bf16[96,2048]{1,0:T(8,128)(2,1)S(1)}, bf16[96,2048]{1,0:T(8,128)(2,1)S(1)}, u32[]{:S(2)}, u32[]{:S(2)}) collective-permute-start(bf16[96,2048]{1,0:T(8,128)(2,1)S(1)} %collective-permute-done.19.refs_4_), channel_id=1, source_target_pairs={{0,4},{1,5},{4,8},{5,9},{8,12},{9,13},{12,14},{13,15},{14,10},{15,... | collective-permute-start | bytes 1179656 | tf_op jit(solution)/shard_map/ppermute | solution.py:341
  99.9 12.9 %collective-permute-start.24 = (bf16[96,2048]{1,0:T(8,128)(2,1)S(1)}, bf16[96,2048]{1,0:T(8,128)(2,1)S(1)}, u32[]{:S(2)}, u32[]{:S(2)}) collective-permute-start(bf16[96,2048]{1,0:T(8,128)(2,1)S(1)} %collective-permute-done.20.refs_5_), channel_id=1, source_target_pairs={{4,0},{5,1},{8,4},{9,5},{12,8},{13,9},{14,12},{15,13},{10,14},{11,... | collective-permute-start | bytes 1179656 | tf_op jit(solution)/shard_map/ppermute | solution.py:341
  112.7 11.3 %collective-permute-start.25 = (bf16[96,2048]{1,0:T(8,128)(2,1)S(1)}, bf16[96,2048]{1,0:T(8,128)(2,1)S(1)}, u32[]{:S(2)}, u32[]{:S(2)}) collective-permute-start(bf16[96,2048]{1,0:T(8,128)(2,1)S(1)} %collective-permute-done.23.refs_2_), channel_id=1, source_target_pairs={{0,4},{1,5},{4,8},{5,9},{8,12},{9,13},{12,14},{13,15},{14,10},{15,... | collective-permute-start | bytes 1179656 | tf_op jit(solution)/shard_map/ppermute | solution.py:341
  113.2 10.8 %collective-permute-start.26 = (bf16[96,2048]{1,0:T(8,128)(2,1)S(1)}, bf16[96,2048]{1,0:T(8,128)(2,1)S(1)}, u32[]{:S(2)}, u32[]{:S(2)}) collective-permute-start(bf16[96,2048]{1,0:T(8,128)(2,1)S(1)} %collective-permute-done.24.refs_3_), channel_id=1, source_target_pairs={{4,0},{5,1},{8,4},{9,5},{12,8},{13,9},{14,12},{15,13},{10,14},{11,... | collective-permute-start | bytes 1179656 | tf_op jit(solution)/shard_map/ppermute | solution.py:341
  124.1 10.8 %collective-permute-start.28 = (bf16[48,2048]{1,0:T(8,128)(2,1)S(1)}, bf16[48,2048]{1,0:T(8,128)(2,1)S(1)}, u32[]{:S(2)}, u32[]{:S(2)}) collective-permute-start(bf16[48,2048]{1,0:T(8,128)(2,1)S(1)} %slice.71), channel_id=1, source_target_pairs={{4,0},{5,1},{8,4},{9,5},{12,8},{13,9},{14,12},{15,13},{10,14},{11,... | collective-permute-start | bytes 589832 | tf_op jit(solution)/shard_map/ppermute | solution.py:341
  124.7 10.2 %collective-permute-start.27 = (bf16[48,2048]{1,0:T(8,128)(2,1)S(1)}, bf16[48,2048]{1,0:T(8,128)(2,1)S(1)}, u32[]{:S(2)}, u32[]{:S(2)}) collective-permute-start(bf16[48,2048]{1,0:T(8,128)(2,1)S(1)} %slice.70), channel_id=1, source_target_pairs={{0,4},{1,5},{4,8},{5,9},{8,12},{9,13},{12,14},{13,15},{14,10},{15,... | collective-permute-start | bytes 589832 | tf_op jit(solution)/shard_map/ppermute | solution.py:341
  126.1 8.7 %collective-permute-start.29 = (bf16[48,2048]{1,0:T(8,128)(2,1)S(1)}, bf16[48,2048]{1,0:T(8,128)(2,1)S(1)}, u32[]{:S(2)}, u32[]{:S(2)}) collective-permute-start(bf16[48,2048]{1,0:T(8,128)(2,1)S(1)} %get-tuple-element.301), channel_id=1, source_target_pairs={{0,4},{1,5},{4,8},{5,9},{8,12},{9,13},{12,14},{13,15},{14,10},{15,... | collective-permute-start | bytes 589832 | tf_op jit(solution)/shard_map/ppermute | solution.py:341
  126.6 8.3 %collective-permute-start.30 = (bf16[48,2048]{1,0:T(8,128)(2,1)S(1)}, bf16[48,2048]{1,0:T(8,128)(2,1)S(1)}, u32[]{:S(2)}, u32[]{:S(2)}) collective-permute-start(bf16[48,2048]{1,0:T(8,128)(2,1)S(1)} %get-tuple-element.302), channel_id=1, source_target_pairs={{4,0},{5,1},{8,4},{9,5},{12,8},{13,9},{14,12},{15,13},{10,14},{11,... | collective-permute-start | bytes 589832 | tf_op jit(solution)/shard_map/ppermute | solution.py:341
  135.1 10.5 %collective-permute-start.32 = (bf16[96,2048]{1,0:T(8,128)(2,1)S(1)}, bf16[96,2048]{1,0:T(8,128)(2,1)S(1)}, u32[]{:S(2)}, u32[]{:S(2)}) collective-permute-start(bf16[96,2048]{1,0:T(8,128)(2,1)S(1)} %pad_maximum_fusion.1), channel_id=1, source_target_pairs={{4,0},{5,1},{8,4},{9,5},{12,8},{13,9},{14,12},{15,13},{10,14},{11,... | collective-permute-start | bytes 1179656 | tf_op jit(solution)/shard_map/ppermute | solution.py:341
  136.1 9.9 %collective-permute-start.31 = (bf16[96,2048]{1,0:T(8,128)(2,1)S(1)}, bf16[96,2048]{1,0:T(8,128)(2,1)S(1)}, u32[]{:S(2)}, u32[]{:S(2)}) collective-permute-start(bf16[96,2048]{1,0:T(8,128)(2,1)S(1)} %pad_maximum_fusion), channel_id=1, source_target_pairs={{0,4},{1,5},{4,8},{5,9},{8,12},{9,13},{12,14},{13,15},{14,10},{15,... | collective-permute-start | bytes 1179656 | tf_op jit(solution)/shard_map/ppermute | solution.py:341
  146.2 13.9 %collective-permute-start.34 = (bf16[96,2048]{1,0:T(8,128)(2,1)S(1)}, bf16[96,2048]{1,0:T(8,128)(2,1)S(1)}, u32[]{:S(2)}, u32[]{:S(2)}) collective-permute-start(bf16[96,2048]{1,0:T(8,128)(2,1)S(1)} %add_convert_fusion.6), channel_id=1, source_target_pairs={{4,0},{5,1},{8,4},{9,5},{12,8},{13,9},{14,12},{15,13},{10,14},{11,... | collective-permute-start | bytes 1179656 | tf_op jit(solution)/shard_map/ppermute | solution.py:341
  146.9 13.2 %collective-permute-start.33 = (bf16[96,2048]{1,0:T(8,128)(2,1)S(1)}, bf16[96,2048]{1,0:T(8,128)(2,1)S(1)}, u32[]{:S(2)}, u32[]{:S(2)}) collective-permute-start(bf16[96,2048]{1,0:T(8,128)(2,1)S(1)} %add_convert_fusion.7), channel_id=1, source_target_pairs={{0,4},{1,5},{4,8},{5,9},{8,12},{9,13},{12,14},{13,15},{14,10},{15,... | collective-permute-start | bytes 1179656 | tf_op jit(solution)/shard_map/ppermute | solution.py:341
  148.4 11.6 %collective-permute-start.35 = (bf16[48,2048]{1,0:T(8,128)(2,1)S(1)}, bf16[48,2048]{1,0:T(8,128)(2,1)S(1)}, u32[]{:S(2)}, u32[]{:S(2)}) collective-permute-start(bf16[48,2048]{1,0:T(8,128)(2,1)S(1)} %get-tuple-element.343), channel_id=1, source_target_pairs={{0,4},{1,5},{4,8},{5,9},{8,12},{9,13},{12,14},{13,15},{14,10},{15,... | collective-permute-start | bytes 589832 | tf_op jit(solution)/shard_map/ppermute | solution.py:341
  149.1 10.9 %collective-permute-start.36 = (bf16[48,2048]{1,0:T(8,128)(2,1)S(1)}, bf16[48,2048]{1,0:T(8,128)(2,1)S(1)}, u32[]{:S(2)}, u32[]{:S(2)}) collective-permute-start(bf16[48,2048]{1,0:T(8,128)(2,1)S(1)} %get-tuple-element.344), channel_id=1, source_target_pairs={{4,0},{5,1},{8,4},{9,5},{12,8},{13,9},{14,12},{15,13},{10,14},{11,... | collective-permute-start | bytes 589832 | tf_op jit(solution)/shard_map/ppermute | solution.py:341
  160.3 8.4 %collective-permute-start.38 = (bf16[96,2048]{1,0:T(8,128)(2,1)S(1)}, bf16[96,2048]{1,0:T(8,128)(2,1)S(1)}, u32[]{:S(2)}, u32[]{:S(2)}) collective-permute-start(bf16[96,2048]{1,0:T(8,128)(2,1)S(1)} %add_convert_fusion.4), channel_id=1, source_target_pairs={{4,0},{5,1},{8,4},{9,5},{12,8},{13,9},{14,12},{15,13},{10,14},{11,... | collective-permute-start | bytes 1179656 | tf_op jit(solution)/shard_map/ppermute | solution.py:341
  160.8 9.0 %collective-permute-start.37 = (bf16[96,2048]{1,0:T(8,128)(2,1)S(1)}, bf16[96,2048]{1,0:T(8,128)(2,1)S(1)}, u32[]{:S(2)}, u32[]{:S(2)}) collective-permute-start(bf16[96,2048]{1,0:T(8,128)(2,1)S(1)} %add_convert_fusion.5), channel_id=1, source_target_pairs={{0,4},{1,5},{4,8},{5,9},{8,12},{9,13},{12,14},{13,15},{14,10},{15,... | collective-permute-start | bytes 1179656 | tf_op jit(solution)/shard_map/ppermute | solution.py:341
  162.6 14.4 %collective-permute-start.40 = (bf16[96,2048]{1,0:T(8,128)(2,1)S(1)}, bf16[96,2048]{1,0:T(8,128)(2,1)S(1)}, u32[]{:S(2)}, u32[]{:S(2)}) collective-permute-start(bf16[96,2048]{1,0:T(8,128)(2,1)S(1)} %pad_maximum_fusion.3), channel_id=1, source_target_pairs={{4,0},{5,1},{8,4},{9,5},{12,8},{13,9},{14,12},{15,13},{10,14},{11,... | collective-permute-start | bytes 1179656 | tf_op jit(solution)/shard_map/ppermute | solution.py:341
  163.0 14.9 %collective-permute-start.39 = (bf16[96,2048]{1,0:T(8,128)(2,1)S(1)}, bf16[96,2048]{1,0:T(8,128)(2,1)S(1)}, u32[]{:S(2)}, u32[]{:S(2)}) collective-permute-start(bf16[96,2048]{1,0:T(8,128)(2,1)S(1)} %pad_maximum_fusion.2), channel_id=1, source_target_pairs={{0,4},{1,5},{4,8},{5,9},{8,12},{9,13},{12,14},{13,15},{14,10},{15,... | collective-permute-start | bytes 1179656 | tf_op jit(solution)/shard_map/ppermute | solution.py:341
  178.0 10.8 %collective-permute-start.42 = (bf16[96,2048]{1,0:T(8,128)(2,1)S(1)}, bf16[96,2048]{1,0:T(8,128)(2,1)S(1)}, u32[]{:S(2)}, u32[]{:S(2)}) collective-permute-start(bf16[96,2048]{1,0:T(8,128)(2,1)S(1)} %add_convert_fusion.2), channel_id=1, source_target_pairs={{4,0},{5,1},{8,4},{9,5},{12,8},{13,9},{14,12},{15,13},{10,14},{11,... | collective-permute-start | bytes 1179656 | tf_op jit(solution)/shard_map/ppermute | solution.py:341
  178.1 10.8 %collective-permute-start.41 = (bf16[96,2048]{1,0:T(8,128)(2,1)S(1)}, bf16[96,2048]{1,0:T(8,128)(2,1)S(1)}, u32[]{:S(2)}, u32[]{:S(2)}) collective-permute-start(bf16[96,2048]{1,0:T(8,128)(2,1)S(1)} %add_convert_fusion.3), channel_id=1, source_target_pairs={{0,4},{1,5},{4,8},{5,9},{8,12},{9,13},{12,14},{13,15},{14,10},{15,... | collective-permute-start | bytes 1179656 | tf_op jit(solution)/shard_map/ppermute | solution.py:341
  189.1 7.8 %collective-permute-start.44 = (bf16[96,2048]{1,0:T(8,128)(2,1)S(1)}, bf16[96,2048]{1,0:T(8,128)(2,1)S(1)}, u32[]{:S(2)}, u32[]{:S(2)}) collective-permute-start(bf16[96,2048]{1,0:T(8,128)(2,1)S(1)} %add_convert_fusion), channel_id=1, source_target_pairs={{4,0},{5,1},{8,4},{9,5},{12,8},{13,9},{14,12},{15,13},{10,14},{11,... | collective-permute-start | bytes 1179656 | tf_op jit(solution)/shard_map/ppermute | solution.py:341
  189.4 7.8 %collective-permute-start.43 = (bf16[96,2048]{1,0:T(8,128)(2,1)S(1)}, bf16[96,2048]{1,0:T(8,128)(2,1)S(1)}, u32[]{:S(2)}, u32[]{:S(2)}) collective-permute-start(bf16[96,2048]{1,0:T(8,128)(2,1)S(1)} %add_convert_fusion.1), channel_id=1, source_target_pairs={{0,4},{1,5},{4,8},{5,9},{8,12},{9,13},{12,14},{13,15},{14,10},{15,... | collective-permute-start | bytes 1179656 | tf_op jit(solution)/shard_map/ppermute | solution.py:341
  (11 other events, 12.1 us)

commit v9 on v8

--- a/solution.py
+++ b/solution.py
@@ -7,7 +7,7 @@
 from jax.sharding import PartitionSpec as P
 
 EPSILON = 1e-06
-VMEM_LIMIT = 24 * 1024 * 1024
+VMEM_LIMIT = 16 * 1024 * 1024
 NT = (((1,), (1,)), ((), ()))
 
 
@@ -480,18 +480,18 @@
         packed, leaving_rise = lax.optimization_barrier((ring.held["cot"][0][0], leaving_rise))
         ring.held["cot"][0] = [packed]
         moved_rise = passed_along(leaving_rise, "pipe", 1)
-        own = fetched(own)
         heads = (head_rise, head_fall)
         cot_in, own, own_down, other_gate, other_up, heads, ring.names = ring.fence(
             cot_in, own, own_down, other_gate, other_up, heads, names
         )
         ring.gather("fall", 3)
         ring.gather("cot", 1)
-        ring.weights = own + (other_gate, other_up, None)
-        ring.prepare([0, 1, 2])
-        moved_rise, own_down = ring.fence(moved_rise, own_down)
+        own = fetched(own)
+        moved_rise, own, own_down = ring.fence(moved_rise, own, own_down)
         ring.gather("fall", 4)
         ring.gather("cot", 2)
+        ring.weights = own + (other_gate, other_up, None)
+        ring.prepare([0, 1, 2, 3])
         other_down = swapped(own_down)
         rise_in = entered(moved_rise)
         rise_normal = normed(rise_in.astype(jnp.float32), norm_row).astype(jnp.bfloat16)
@@ -504,7 +504,7 @@
         ring.gather("cot", 3)
         ring.gather("rise", 1)
         ring.work("backward", [0, 1, 2])
-        ring.prepare([3, 4])
+        ring.prepare([4])
         ring.fence()
         ring.gather("cot", 4)
         ring.gather("rise", 2)

time: 199 us -> 188 us (0.945)
  local copies, waits for them, and re-layouts: 16.9 us -> 5.79 us
  Pallas kernels: 62.8 us -> 59.9 us
  starting transfers between devices: 48.2 us -> 50.6 us
    unnamed x62 -> x30, local copies, waits for them, and re-layouts: 13.5 us -> 3.36 us
    ppermute x2, starting transfers between devices: 5.11 us -> 7.2 us  [passed_along(): return lax.ppermute(block, axis, route)]
  transfers between devices with their start and end apart: 45 -> 45, of which waited for: 17 -> 17; matrix products, arithmetic and copies ran while one was open for 5% -> 4% of each run, Pallas kernels for 32% -> 32%
where the time goes in v9:
time: 188 us; the launch traced here: 187 us
  waiting for transfers between devices  61.5 us (33%)
  Pallas kernels  59.9 us (32%)
  starting transfers between devices  50.6 us (27%)
  other arithmetic  6.73 us (4%)
  local copies, waits for them, and re-layouts  5.79 us (3%)
  between operations  2.47 us (1%)
    ppermute x40, waiting for transfers between devices, pass_on(): return lax.ppermute(block, 'ep', self.routes[way])  59.8 us
    ppermute x40, starting transfers between devices, pass_on(): return lax.ppermute(block, 'ep', self.routes[way])  42.8 us
    pallas_call x3, Pallas kernels, forward_call(): pl.pallas_call(functools.partial(forward_kernel, parts, experts, width, T...  21.3 us
    pallas_call x2, Pallas kernels, backward_call(): pl.pallas_call(functools.partial(backward_kernel, parts, experts, width,...  19.8 us
    pallas_call x2, Pallas kernels, factor_call(): pl.pallas_call(functools.partial(factor_kernel, parts), out_shape=jax.Sha...  14.9 us
    ppermute x2, starting transfers between devices, passed_along(): return lax.ppermute(block, axis, route)  7.2 us
  transfers between devices with their start and end apart: 45, of which 17 were waited for; matrix products, arithmetic and copies ran while one was open for 4% of the time, Pallas kernels for 32%

profile of v9, /device:TPU:0, one launch (start us, length us, event | category | flops | bytes accessed | tf_op | source)
XLA Modules:
  0.0 187.0 jit_solution(17758755481025590775)
XLA Ops:
  1.2 1.0 copy-done
  2.2 0.7 copy-done.3
  3.1 3.0 %collective-permute-start.2 = (bf16[96,2048]{1,0:T(8,128)(2,1)S(1)}, bf16[96,2048]{1,0:T(8,128)(2,1)S(1)}, u32[]{:S(2)}, u32[]{:S(2)}) collective-permute-start(bf16[96,2048]{1,0:T(8,128)(2,1)S(1)} %shard_map.148.refs_0_), channel_id=1, source_target_pairs={{4,0},{5,1},{8,4},{9,5},{12,8},{13,9},{14,12},{15,13},{10,14},{11,... | collective-permute-start | bytes 1179656 | tf_op jit(solution)/shard_map/ppermute | solution.py:341
  6.2 3.8 %collective-permute-start = (bf16[96,2048]{1,0:T(8,128)(2,1)}, bf16[96,2048]{1,0:T(8,128)(2,1)S(1)}, u32[]{:S(2)}, u32[]{:S(2)}) collective-permute-start(bf16[96,2048]{1,0:T(8,128)(2,1)} %bitcast.63), channel_id=1, source_target_pairs={{0,16},{1,17},{2,18},{3,19},{4,20},{5,21},{6,22},{7,23},{8,24},{9,... | collective-permute-start | bytes 1179656 | tf_op jit(solution)/shard_map/ppermute | solution.py:17
  10.1 0.8 fusion.19
  10.8 0.6 constant_dynamic-slice_fusion
  12.6 0.8 copy.16
  13.4 0.8 copy.17
  14.3 1.2 collective-permute-done.2.refs_2_
  15.5 1.7 collective-permute-start.4
  17.6 0.8 collective-permute-done
  18.4 1.0 bitcast_select_fusion.rows_ref
  19.4 0.7 shard_map.149.refs_0_
  20.2 6.1 %collective-permute-done.4.refs_4_ = bf16[96,2048]{1,0:T(8,128)(2,1)} collective-permute-done((bf16[96,2048]{1,0:T(8,128)(2,1)S(1)}, bf16[96,2048]{1,0:T(8,128)(2,1)}, u32[]{:S(2)}, u32[]{:S(2)}) %collective-permute-start.4) | collective-permute-done | bytes 393248 | tf_op jit(solution)/shard_map/ppermute | solution.py:341
  26.2 1.1 collective-permute-done.3.refs_3_
  27.3 1.6 collective-permute-start.8
  29.4 3.4 %collective-permute-start.11 = (bf16[96,2048]{1,0:T(8,128)(2,1)}, bf16[96,2048]{1,0:T(8,128)(2,1)S(1)}, u32[]{:S(2)}, u32[]{:S(2)}) collective-permute-start(bf16[96,2048]{1,0:T(8,128)(2,1)} %bitcast.4), channel_id=1, source_target_pairs={{0,16},{1,17},{2,18},{3,19},{4,20},{5,21},{6,22},{7,23},{8,24},{9,... | collective-permute-start | bytes 1179656 | tf_op jit(solution)/shard_map/ppermute | solution.py:17
  33.4 1.5 collective-permute-start.10
  35.1 3.0 %shard_map.150 = (bf16[2048,512]{1,0:T(8,128)(2,1)S(1)}, bf16[2048,512]{1,0:T(8,128)(2,1)S(1)}, bf16[512,2048]{1,0:T(8,128)(2,1)S(1)}) custom-call(bf16[2048,512]{1,0:T(8,128)(2,1)} %bitcast.54, bf16[2048,512]{1,0:T(8,128)(2,1)} %bitcast.56, bf16[512,2048]{1,0:T(8,128)(2,1)} %bitcast.57), custom_call_target="tpu_custom_call" | custom-call | bytes 8388608 | tf_op jit(solution)/shard_map/pallas_call | solution.py:226
  38.2 1.0 collective-permute-done.11
  39.1 7.6 %collective-permute-done.9.refs_5_ = bf16[96,2048]{1,0:T(8,128)(2,1)S(1)} collective-permute-done((bf16[96,2048]{1,0:T(8,128)(2,1)}, bf16[96,2048]{1,0:T(8,128)(2,1)S(1)}, u32[]{:S(2)}, u32[]{:S(2)}) %collective-permute-start.9) | collective-permute-done | bytes 393248 | tf_op jit(solution)/shard_map/ppermute | solution.py:341
  47.0 0.9 slice.65
  47.9 1.6 collective-permute-start.15
  50.0 0.6 multiply_reduce_fusion
  51.2 1.6 collective-permute-start.13
  53.2 10.1 %shard_map.151.refs_5_.refs_4_ = bf16[4,672,512]{2,1,0:T(8,128)(2,1)S(1)} custom-call(bf16[96,2048]{1,0:T(8,128)(2,1)} %copy-done.2, bf16[96,2048]{1,0:T(8,128)(2,1)} %copy-done.11, bf16[96,2048]{1,0:T(8,128)(2,1)} %copy-done.10, bf16[96,2048]{1,0:T(8,128)(2,1)} %collective-permute-done.3.refs_3_, bf16[96,2048]{1,0:T(8,128)(2,1)} %collective-permute-done.4.refs_4_, ...), custom_call_target="tpu_custom_call" | custom-call | flops 11137144832 | bytes 12582912 | tf_op jit(solution)/shard_map/pallas_call | solution.py:276
  63.4 0.6 maximum_bitcast_fusion
  64.0 1.6 collective-permute-start.20
  66.5 1.6 collective-permute-start.18
  68.1 11.3 %shard_map.153 = (bf16[96,2048]{1,0:T(8,128)(2,1)S(1)}, bf16[96,2048]{1,0:T(8,128)(2,1)S(1)}, bf16[96,2048]{1,0:T(8,128)(2,1)S(1)}, bf16[96,2048]{1,0:T(8,128)(2,1)S(1)}, bf16[96,2048]{1,0:T(8,128)(2,1)S(1)}) custom-call(s32[2]{0:T(128)S(1)} %pad_add_fusion.names_ref, bf16[96,2176]{1,0:T(8,128)(2,1)S(1)} %shard_map.149.refs_0_, ...), custom_call_target="tpu_custom_call" | custom-call | flops 12639797248 | bytes 12582912 | tf_op jit(solution)/shard_map/pallas_call | solution.py:294
  79.4 4.8 %shard_map.152.refs_5_ = bf16[4,96,512]{2,1,0:T(8,128)(2,1)S(1)} custom-call(bf16[48,2048]{1,0:T(8,128)(2,1)} %copy-done.13, bf16[48,2048]{1,0:T(8,128)(2,1)} %copy-done.12, bf16[2048,512]{1,0:T(8,128)(2,1)S(1)} %get-tuple-element.226.refs_7_.refs_2_.refs_6_.refs_4_.refs_8_, bf16[2048,512]{1,0:T(8,128)(2,1)S(1)} %get-tuple-element.227.refs_8_.refs_3_.refs_7_.refs_5_.refs_9_, ...), custom_call_target="tpu_custom_call" | custom-call | flops 6305306624 | bytes 12582912 | tf_op jit(solution)/shard_map/pallas_call | solution.py:276
  84.2 1.6 collective-permute-done.17.refs_0_
  85.9 1.6 collective-permute-start.22
  88.4 1.6 collective-permute-start.24
  90.0 7.4 %shard_map.154 = (bf16[96,2048]{1,0:T(8,128)(2,1)S(1)}, bf16[96,2048]{1,0:T(8,128)(2,1)S(1)}, bf16[96,2048]{1,0:T(8,128)(2,1)S(1)}) custom-call(s32[2]{0:T(128)S(1)} %pad_add_fusion.names_ref, bf16[96,2176]{1,0:T(8,128)(2,1)S(1)} %shard_map.149.refs_0_, bf16[96,2176]{1,0:T(8,128)(2,1)S(1)} %collective-permute-done.7.refs_1_, ...), custom_call_target="tpu_custom_call" | custom-call | flops 10223878144 | bytes 12582912 | tf_op jit(solution)/shard_map/pallas_call | solution.py:256
  97.4 4.6 %collective-permute-done.23.refs_2_ = bf16[96,2048]{1,0:T(8,128)(2,1)S(1)} collective-permute-done((bf16[96,2048]{1,0:T(8,128)(2,1)S(1)}, bf16[96,2048]{1,0:T(8,128)(2,1)S(1)}, u32[]{:S(2)}, u32[]{:S(2)}) %collective-permute-start.23) | collective-permute-done | bytes 393248 | tf_op jit(solution)/shard_map/ppermute | solution.py:341
  102.6 1.5 collective-permute-start.26
  104.1 8.5 %shard_map.155 = (bf16[96,2048]{1,0:T(8,128)(2,1)S(1)}, bf16[96,2048]{1,0:T(8,128)(2,1)S(1)}, bf16[48,2048]{1,0:T(8,128)(2,1)S(1)}, bf16[48,2048]{1,0:T(8,128)(2,1)S(1)}) custom-call(s32[2]{0:T(128)S(1)} %pad_add_fusion.names_ref, bf16[96,2176]{1,0:T(8,128)(2,1)S(1)} %collective-permute-done.17.refs_0_, ...), custom_call_target="tpu_custom_call" | custom-call | flops 10223878144 | bytes 12582912 | tf_op jit(solution)/shard_map/pallas_call | solution.py:294
  112.7 0.7 collective-permute-start.28
  113.3 1.4 collective-permute-start.27
  115.2 1.5 collective-permute-start.30
  116.8 6.1 %shard_map.156 = (bf16[96,2048]{1,0:T(8,128)(2,1)S(1)}, bf16[96,2048]{1,0:T(8,128)(2,1)S(1)}) custom-call(s32[2]{0:T(128)S(1)} %pad_add_fusion.names_ref, bf16[96,2176]{1,0:T(8,128)(2,1)S(1)} %collective-permute-done.12.refs_3_.refs_0_, bf16[96,2176]{1,0:T(8,128)(2,1)S(1)} %collective-permute-done.13.refs_4_.refs_1_, ...), custom_call_target="tpu_custom_call" | custom-call | flops 9015918592 | bytes 12582912 | tf_op jit(solution)/shard_map/pallas_call | solution.py:256
  123.1 0.7 collective-permute-start.32
  123.8 1.7 collective-permute-start.31
  125.5 7.8 %shard_map.157 = (bf16[96,2048]{1,0:T(8,128)(2,1)S(1)}, bf16[96,2048]{1,0:T(8,128)(2,1)S(1)}, bf16[48,2048]{1,0:T(8,128)(2,1)S(1)}, bf16[48,2048]{1,0:T(8,128)(2,1)S(1)}) custom-call(s32[2]{0:T(128)S(1)} %pad_add_fusion.names_ref, bf16[96,2176]{1,0:T(8,128)(2,1)S(1)} %collective-permute-done.17.refs_0_, ...), custom_call_target="tpu_custom_call" | custom-call | flops 10223878144 | bytes 12582912 | tf_op jit(solution)/shard_map/pallas_call | solution.py:256
  133.4 0.7 collective-permute-start.34
  134.2 1.4 collective-permute-start.33
  136.1 1.5 collective-permute-start.36
  137.6 9.2 %collective-permute-done.35 = bf16[48,2048]{1,0:T(8,128)(2,1)S(1)} collective-permute-done((bf16[48,2048]{1,0:T(8,128)(2,1)S(1)}, bf16[48,2048]{1,0:T(8,128)(2,1)S(1)}, u32[]{:S(2)}, u32[]{:S(2)}) %collective-permute-start.35) | collective-permute-done | bytes 196640 | tf_op jit(solution)/shard_map/ppermute | solution.py:341
  147.1 0.6 collective-permute-start.38
  147.8 1.5 collective-permute-start.37
  149.4 0.6 collective-permute-start.40
  150.0 1.5 collective-permute-start.39
  151.6 5.7 %collective-permute-done.38 = bf16[96,2048]{1,0:T(8,128)(2,1)S(1)} collective-permute-done((bf16[96,2048]{1,0:T(8,128)(2,1)S(1)}, bf16[96,2048]{1,0:T(8,128)(2,1)S(1)}, u32[]{:S(2)}, u32[]{:S(2)}) %collective-permute-start.38) | collective-permute-done | bytes 393248 | tf_op jit(solution)/shard_map/ppermute | solution.py:341
  157.2 0.6 collective-permute-done.37
  157.8 6.4 %collective-permute-done.40 = bf16[96,2048]{1,0:T(8,128)(2,1)S(1)} collective-permute-done((bf16[96,2048]{1,0:T(8,128)(2,1)S(1)}, bf16[96,2048]{1,0:T(8,128)(2,1)S(1)}, u32[]{:S(2)}, u32[]{:S(2)}) %collective-permute-start.40) | collective-permute-done | bytes 393248 | tf_op jit(solution)/shard_map/ppermute | solution.py:341
  164.2 0.9 collective-permute-done.39
  165.5 1.9 %collective-permute-start.41 = (bf16[96,2048]{1,0:T(8,128)(2,1)S(1)}, bf16[96,2048]{1,0:T(8,128)(2,1)S(1)}, u32[]{:S(2)}, u32[]{:S(2)}) collective-permute-start(bf16[96,2048]{1,0:T(8,128)(2,1)S(1)} %add_convert_fusion.3), channel_id=1, source_target_pairs={{0,4},{1,5},{4,8},{5,9},{8,12},{9,13},{12,14},{13,15},{14,10},{15,... | collective-permute-start | bytes 1179656 | tf_op jit(solution)/shard_map/ppermute | solution.py:341
  167.8 1.1 fusion.11
  169.0 8.3 %collective-permute-done.42 = bf16[96,2048]{1,0:T(8,128)(2,1)S(1)} collective-permute-done((bf16[96,2048]{1,0:T(8,128)(2,1)S(1)}, bf16[96,2048]{1,0:T(8,128)(2,1)S(1)}, u32[]{:S(2)}, u32[]{:S(2)}) %collective-permute-start.42) | collective-permute-done | bytes 393248 | tf_op jit(solution)/shard_map/ppermute | solution.py:341
  178.2 1.6 collective-permute-start.43
  179.8 5.6 %collective-permute-done.44 = bf16[96,2048]{1,0:T(8,128)(2,1)S(1)} collective-permute-done((bf16[96,2048]{1,0:T(8,128)(2,1)S(1)}, bf16[96,2048]{1,0:T(8,128)(2,1)S(1)}, u32[]{:S(2)}, u32[]{:S(2)}) %collective-permute-start.44) | collective-permute-done | bytes 393248 | tf_op jit(solution)/shard_map/ppermute | solution.py:341
  185.4 0.7 collective-permute-done.43
  186.0 1.0 fusion.17
  (110 shorter events, 10.0 us)
Async XLA Ops:
  0.6 26.7 %collective-permute-start.5 = (bf16[2048,512]{1,0:T(8,128)(2,1)}, bf16[2048,512]{1,0:T(8,128)(2,1)}, u32[]{:S(2)}, u32[]{:S(2)}) collective-permute-start(bf16[2048,512]{1,0:T(8,128)(2,1)} %bitcast.53), channel_id=1, source_target_pairs={{0,1},{1,0},{2,3},{3,2},{4,5},{5,4},{6,7},{7,6},{8,9},{9,8},{10,11... | collective-permute-start | bytes 6291464 | tf_op jit(solution)/shard_map/ppermute | solution.py:449
  1.1 26.2 %collective-permute-start.6 = (bf16[2048,512]{1,0:T(8,128)(2,1)}, bf16[2048,512]{1,0:T(8,128)(2,1)}, u32[]{:S(2)}, u32[]{:S(2)}) collective-permute-start(bf16[2048,512]{1,0:T(8,128)(2,1)} %bitcast.55), channel_id=1, source_target_pairs={{0,1},{1,0},{2,3},{3,2},{4,5},{5,4},{6,7},{7,6},{8,9},{9,8},{10,11... | collective-permute-start | bytes 6291464 | tf_op jit(solution)/shard_map/ppermute | solution.py:449
  1.2 1.0 copy-start
  2.2 0.7 copy-start.3
  2.9 32.0 %copy-start.1 = (bf16[1,96,2048]{2,1,0:T(8,128)(2,1)S(1)}, bf16[1,96,2048]{2,1,0:T(8,128)(2,1)}, u32[]{:S(2)}) copy-start(bf16[1,96,2048]{2,1,0:T(8,128)(2,1)} %param.16) | copy-start | bytes 1179652
  3.1 35.0 %copy-start.2 = (bf16[96,2048]{1,0:T(8,128)(2,1)}, bf16[96,2048]{1,0:T(8,128)(2,1)S(1)}, u32[]{:S(2)}) copy-start(bf16[96,2048]{1,0:T(8,128)(2,1)S(1)} %shard_map.148.refs_0_) | copy-start | bytes 1179652
  3.1 12.4 %collective-permute-start.2 = (bf16[96,2048]{1,0:T(8,128)(2,1)S(1)}, bf16[96,2048]{1,0:T(8,128)(2,1)S(1)}, u32[]{:S(2)}, u32[]{:S(2)}) collective-permute-start(bf16[96,2048]{1,0:T(8,128)(2,1)S(1)} %shard_map.148.refs_0_), channel_id=1, source_target_pairs={{4,0},{5,1},{8,4},{9,5},{12,8},{13,9},{14,12},{15,13},{10,14},{11,... | collective-permute-start | bytes 1179656 | tf_op jit(solution)/shard_map/ppermute | solution.py:341
  6.1 11.1 %collective-permute-start.1 = (bf16[96,2048]{1,0:T(8,128)(2,1)S(1)}, bf16[96,2048]{1,0:T(8,128)(2,1)S(1)}, u32[]{:S(2)}, u32[]{:S(2)}) collective-permute-start(bf16[96,2048]{1,0:T(8,128)(2,1)S(1)} %shard_map.148.refs_0_), channel_id=1, source_target_pairs={{0,4},{1,5},{4,8},{5,9},{8,12},{9,13},{12,14},{13,15},{14,10},{15,... | collective-permute-start | bytes 1179656 | tf_op jit(solution)/shard_map/ppermute | solution.py:341
  6.2 12.1 %collective-permute-start = (bf16[96,2048]{1,0:T(8,128)(2,1)}, bf16[96,2048]{1,0:T(8,128)(2,1)S(1)}, u32[]{:S(2)}, u32[]{:S(2)}) collective-permute-start(bf16[96,2048]{1,0:T(8,128)(2,1)} %bitcast.63), channel_id=1, source_target_pairs={{0,16},{1,17},{2,18},{3,19},{4,20},{5,21},{6,22},{7,23},{8,24},{9,... | collective-permute-start | bytes 1179656 | tf_op jit(solution)/shard_map/ppermute | solution.py:17
  15.5 11.8 %copy-start.10 = (bf16[96,2048]{1,0:T(8,128)(2,1)}, bf16[96,2048]{1,0:T(8,128)(2,1)S(1)}, u32[]{:S(2)}) copy-start(bf16[96,2048]{1,0:T(8,128)(2,1)S(1)} %collective-permute-done.2.refs_2_) | copy-start | bytes 1179652
  15.5 10.7 %collective-permute-start.4 = (bf16[96,2048]{1,0:T(8,128)(2,1)S(1)}, bf16[96,2048]{1,0:T(8,128)(2,1)}, u32[]{:S(2)}, u32[]{:S(2)}) collective-permute-start(bf16[96,2048]{1,0:T(8,128)(2,1)S(1)} %collective-permute-done.2.refs_2_), channel_id=1, source_target_pairs={{4,0},{5,1},{8,4},{9,5},{12,8},{13,9},{14,12},{15,13},{10,14},{11,... | collective-permute-start | bytes 1179656 | tf_op jit(solution)/shard_map/ppermute | solution.py:341
  17.2 11.7 %copy-start.11 = (bf16[96,2048]{1,0:T(8,128)(2,1)}, bf16[96,2048]{1,0:T(8,128)(2,1)S(1)}, u32[]{:S(2)}) copy-start(bf16[96,2048]{1,0:T(8,128)(2,1)S(1)} %collective-permute-done.1.refs_1_) | copy-start | bytes 1179652
  17.2 10.1 %collective-permute-start.3 = (bf16[96,2048]{1,0:T(8,128)(2,1)S(1)}, bf16[96,2048]{1,0:T(8,128)(2,1)}, u32[]{:S(2)}, u32[]{:S(2)}) collective-permute-start(bf16[96,2048]{1,0:T(8,128)(2,1)S(1)} %collective-permute-done.1.refs_1_), channel_id=1, source_target_pairs={{0,4},{1,5},{4,8},{5,9},{8,12},{9,13},{12,14},{13,15},{14,10},{15,... | collective-permute-start | bytes 1179656 | tf_op jit(solution)/shard_map/ppermute | solution.py:341
  27.3 19.4 %collective-permute-start.8 = (bf16[96,2176]{1,0:T(8,128)(2,1)S(1)}, bf16[96,2176]{1,0:T(8,128)(2,1)S(1)}, u32[]{:S(2)}, u32[]{:S(2)}) collective-permute-start(bf16[96,2176]{1,0:T(8,128)(2,1)S(1)} %shard_map.149.refs_0_), channel_id=1, source_target_pairs={{4,0},{5,1},{8,4},{9,5},{12,8},{13,9},{14,12},{15,13},{10,14},{11,... | collective-permute-start | bytes 1253384 | tf_op jit(solution)/shard_map/ppermute | solution.py:341
  29.0 17.7 %collective-permute-start.7 = (bf16[96,2176]{1,0:T(8,128)(2,1)S(1)}, bf16[96,2176]{1,0:T(8,128)(2,1)S(1)}, u32[]{:S(2)}, u32[]{:S(2)}) collective-permute-start(bf16[96,2176]{1,0:T(8,128)(2,1)S(1)} %shard_map.149.refs_0_), channel_id=1, source_target_pairs={{0,4},{1,5},{4,8},{5,9},{8,12},{9,13},{12,14},{13,15},{14,10},{15,... | collective-permute-start | bytes 1253384 | tf_op jit(solution)/shard_map/ppermute | solution.py:341
  29.4 9.7 %collective-permute-start.11 = (bf16[96,2048]{1,0:T(8,128)(2,1)}, bf16[96,2048]{1,0:T(8,128)(2,1)S(1)}, u32[]{:S(2)}, u32[]{:S(2)}) collective-permute-start(bf16[96,2048]{1,0:T(8,128)(2,1)} %bitcast.4), channel_id=1, source_target_pairs={{0,16},{1,17},{2,18},{3,19},{4,20},{5,21},{6,22},{7,23},{8,24},{9,... | collective-permute-start | bytes 1179656 | tf_op jit(solution)/shard_map/ppermute | solution.py:17
  32.8 13.9 %collective-permute-start.9 = (bf16[96,2048]{1,0:T(8,128)(2,1)}, bf16[96,2048]{1,0:T(8,128)(2,1)S(1)}, u32[]{:S(2)}, u32[]{:S(2)}) collective-permute-start(bf16[96,2048]{1,0:T(8,128)(2,1)} %collective-permute-done.3.refs_3_), channel_id=1, source_target_pairs={{0,4},{1,5},{4,8},{5,9},{8,12},{9,13},{12,14},{13,15},{14,10},{15,... | collective-permute-start | bytes 1179656 | tf_op jit(solution)/shard_map/ppermute | solution.py:341
  33.4 13.3 %collective-permute-start.10 = (bf16[96,2048]{1,0:T(8,128)(2,1)}, bf16[96,2048]{1,0:T(8,128)(2,1)}, u32[]{:S(2)}, u32[]{:S(2)}) collective-permute-start(bf16[96,2048]{1,0:T(8,128)(2,1)} %collective-permute-done.4.refs_4_), channel_id=1, source_target_pairs={{4,0},{5,1},{8,4},{9,5},{12,8},{13,9},{14,12},{15,13},{10,14},{11,... | collective-permute-start | bytes 1179656 | tf_op jit(solution)/shard_map/ppermute | solution.py:341
  35.1 11.6 %copy-start.7 = (bf16[2,96,2048]{2,1,0:T(8,128)(2,1)S(1)}, bf16[2,96,2048]{2,1,0:T(8,128)(2,1)}, u32[]{:S(2)}) copy-start(bf16[2,96,2048]{2,1,0:T(8,128)(2,1)} %param.13) | copy-start | bytes 2359300
  35.1 14.9 %copy-start.4 = (f32[1,2048]{1,0:T(1,128)S(1)}, f32[1,2048]{1,0:T(1,128)}, u32[]{:S(2)}) copy-start(f32[1,2048]{1,0:T(1,128)} %gain_ref.1) | copy-start | bytes 24580
  35.1 14.9 %copy-start.6 = (bf16[2,96,2048]{2,1,0:T(8,128)(2,1)S(1)}, bf16[2,96,2048]{2,1,0:T(8,128)(2,1)}, u32[]{:S(2)}) copy-start(bf16[2,96,2048]{2,1,0:T(8,128)(2,1)} %param.17) | copy-start | bytes 2359300
  35.1 14.9 %copy-start.9 = (f32[1,2048]{1,0:T(1,128)S(1)}, f32[1,2048]{1,0:T(1,128)}, u32[]{:S(2)}) copy-start(f32[1,2048]{1,0:T(1,128)} %param.19) | copy-start | bytes 24580
  38.2 14.6 %copy-start.5 = (bf16[1,1,512,2048]{3,2,1,0:T(8,128)(2,1)S(1)}, bf16[1,1,512,2048]{3,2,1,0:T(8,128)(2,1)}, u32[]{:S(2)}) copy-start(bf16[1,1,512,2048]{3,2,1,0:T(8,128)(2,1)} %param.22) | copy-start | bytes 6291460
  46.7 6.5 %copy-start.8 = (bf16[96,2048]{1,0:T(8,128)(2,1)}, bf16[96,2048]{1,0:T(8,128)(2,1)S(1)}, u32[]{:S(2)}) copy-start(bf16[96,2048]{1,0:T(8,128)(2,1)S(1)} %collective-permute-done.9.refs_5_) | copy-start | bytes 1179652
  47.9 16.0 %collective-permute-start.15 = (bf16[48,2048]{1,0:T(8,128)(2,1)S(1)}, bf16[48,2048]{1,0:T(8,128)(2,1)S(1)}, u32[]{:S(2)}, u32[]{:S(2)}) collective-permute-start(bf16[48,2048]{1,0:T(8,128)(2,1)S(1)} %slice.65), channel_id=1, source_target_pairs={{4,0},{5,1},{8,4},{9,5},{12,8},{13,9},{14,12},{15,13},{10,14},{11,... | collective-permute-start | bytes 589832 | tf_op jit(solution)/shard_map/ppermute | solution.py:341
  49.6 14.4 %collective-permute-start.14 = (bf16[48,2048]{1,0:T(8,128)(2,1)S(1)}, bf16[48,2048]{1,0:T(8,128)(2,1)S(1)}, u32[]{:S(2)}, u32[]{:S(2)}) collective-permute-start(bf16[48,2048]{1,0:T(8,128)(2,1)S(1)} %slice.64), channel_id=1, source_target_pairs={{0,4},{1,5},{4,8},{5,9},{8,12},{9,13},{12,14},{13,15},{14,10},{15,... | collective-permute-start | bytes 589832 | tf_op jit(solution)/shard_map/ppermute | solution.py:341
  50.7 13.3 %collective-permute-start.12 = (bf16[96,2176]{1,0:T(8,128)(2,1)S(1)}, bf16[96,2176]{1,0:T(8,128)(2,1)S(1)}, u32[]{:S(2)}, u32[]{:S(2)}) collective-permute-start(bf16[96,2176]{1,0:T(8,128)(2,1)S(1)} %collective-permute-done.7.refs_1_), channel_id=1, source_target_pairs={{0,4},{1,5},{4,8},{5,9},{8,12},{9,13},{12,14},{13,15},{14,10},{15,... | collective-permute-start | bytes 1253384 | tf_op jit(solution)/shard_map/ppermute | solution.py:341
  51.2 12.8 %collective-permute-start.13 = (bf16[96,2176]{1,0:T(8,128)(2,1)S(1)}, bf16[96,2176]{1,0:T(8,128)(2,1)S(1)}, u32[]{:S(2)}, u32[]{:S(2)}) collective-permute-start(bf16[96,2176]{1,0:T(8,128)(2,1)S(1)} %collective-permute-done.8.refs_2_), channel_id=1, source_target_pairs={{4,0},{5,1},{8,4},{9,5},{12,8},{13,9},{14,12},{15,13},{10,14},{11,... | collective-permute-start | bytes 1253384 | tf_op jit(solution)/shard_map/ppermute | solution.py:341
  52.8 11.2 %collective-permute-start.16 = (bf16[512,2048]{1,0:T(8,128)(2,1)S(1)}, bf16[512,2048]{1,0:T(8,128)(2,1)S(1)}, u32[]{:S(2)}, u32[]{:S(2)}) collective-permute-start(bf16[512,2048]{1,0:T(8,128)(2,1)S(1)} %bitcast.58), channel_id=1, source_target_pairs={{0,1},{1,0},{2,3},{3,2},{4,5},{5,4},{6,7},{7,6},{8,9},{9,8},{10,11... | collective-permute-start | bytes 6291464 | tf_op jit(solution)/shard_map/ppermute | solution.py:449
  63.9 15.5 %copy-start.12 = (bf16[48,2048]{1,0:T(8,128)(2,1)}, bf16[48,2048]{1,0:T(8,128)(2,1)S(1)}, u32[]{:S(2)}) copy-start(bf16[48,2048]{1,0:T(8,128)(2,1)S(1)} %collective-permute-done.15.refs_1_) | copy-start | bytes 589828
  63.9 15.5 %copy-start.13 = (bf16[48,2048]{1,0:T(8,128)(2,1)}, bf16[48,2048]{1,0:T(8,128)(2,1)S(1)}, u32[]{:S(2)}) copy-start(bf16[48,2048]{1,0:T(8,128)(2,1)S(1)} %collective-permute-done.14.refs_0_) | copy-start | bytes 589828
  64.0 20.2 %collective-permute-start.20 = (bf16[96,2048]{1,0:T(8,128)(2,1)S(1)}, bf16[96,2048]{1,0:T(8,128)(2,1)S(1)}, u32[]{:S(2)}, u32[]{:S(2)}) collective-permute-start(bf16[96,2048]{1,0:T(8,128)(2,1)S(1)} %get-tuple-element.260.refs_3_), channel_id=1, source_target_pairs={{4,0},{5,1},{8,4},{9,5},{12,8},{13,9},{14,12},{15,13},{10,14},{11,... | collective-permute-start | bytes 1179656 | tf_op jit(solution)/shard_map/ppermute | solution.py:341
  65.6 18.6 %collective-permute-start.19 = (bf16[96,2048]{1,0:T(8,128)(2,1)S(1)}, bf16[96,2048]{1,0:T(8,128)(2,1)S(1)}, u32[]{:S(2)}, u32[]{:S(2)}) collective-permute-start(bf16[96,2048]{1,0:T(8,128)(2,1)S(1)} %get-tuple-element.260.refs_3_), channel_id=1, source_target_pairs={{0,4},{1,5},{4,8},{5,9},{8,12},{9,13},{12,14},{13,15},{14,10},{15,... | collective-permute-start | bytes 1179656 | tf_op jit(solution)/shard_map/ppermute | solution.py:341
  66.1 19.8 %collective-permute-start.17 = (bf16[96,2176]{1,0:T(8,128)(2,1)S(1)}, bf16[96,2176]{1,0:T(8,128)(2,1)S(1)}, u32[]{:S(2)}, u32[]{:S(2)}) collective-permute-start(bf16[96,2176]{1,0:T(8,128)(2,1)S(1)} %collective-permute-done.12.refs_3_.refs_0_), channel_id=1, source_target_pairs={{0,4},{1,5},{4,8},{5,9},{8,12},{9,13},{12,14},{13,15},{14,10},{15,... | collective-permute-start | bytes 1253384 | tf_op jit(solution)/shard_map/ppermute | solution.py:341
  66.5 19.3 %collective-permute-start.18 = (bf16[96,2176]{1,0:T(8,128)(2,1)S(1)}, bf16[96,2176]{1,0:T(8,128)(2,1)S(1)}, u32[]{:S(2)}, u32[]{:S(2)}) collective-permute-start(bf16[96,2176]{1,0:T(8,128)(2,1)S(1)} %collective-permute-done.13.refs_4_.refs_1_), channel_id=1, source_target_pairs={{4,0},{5,1},{8,4},{9,5},{12,8},{13,9},{14,12},{15,13},{10,14},{11,... | collective-permute-start | bytes 1253384 | tf_op jit(solution)/shard_map/ppermute | solution.py:341
  85.9 11.6 %collective-permute-start.22 = (bf16[48,2176]{1,0:T(8,128)(2,1)S(1)}, bf16[48,2176]{1,0:T(8,128)(2,1)S(1)}, u32[]{:S(2)}, u32[]{:S(2)}) collective-permute-start(bf16[48,2176]{1,0:T(8,128)(2,1)S(1)} %slice.69), channel_id=1, source_target_pairs={{4,0},{5,1},{8,4},{9,5},{12,8},{13,9},{14,12},{15,13},{10,14},{11,... | collective-permute-start | bytes 626696 | tf_op jit(solution)/shard_map/ppermute | solution.py:341
  87.5 9.9 %collective-permute-start.21 = (bf16[48,2176]{1,0:T(8,128)(2,1)S(1)}, bf16[48,2176]{1,0:T(8,128)(2,1)S(1)}, u32[]{:S(2)}, u32[]{:S(2)}) collective-permute-start(bf16[48,2176]{1,0:T(8,128)(2,1)S(1)} %slice.68), channel_id=1, source_target_pairs={{0,4},{1,5},{4,8},{5,9},{8,12},{9,13},{12,14},{13,15},{14,10},{15,... | collective-permute-start | bytes 626696 | tf_op jit(solution)/shard_map/ppermute | solution.py:341
  87.9 14.1 %collective-permute-start.23 = (bf16[96,2048]{1,0:T(8,128)(2,1)S(1)}, bf16[96,2048]{1,0:T(8,128)(2,1)S(1)}, u32[]{:S(2)}, u32[]{:S(2)}) collective-permute-start(bf16[96,2048]{1,0:T(8,128)(2,1)S(1)} %collective-permute-done.19.refs_4_), channel_id=1, source_target_pairs={{0,4},{1,5},{4,8},{5,9},{8,12},{9,13},{12,14},{13,15},{14,10},{15,... | collective-permute-start | bytes 1179656 | tf_op jit(solution)/shard_map/ppermute | solution.py:341
  88.4 13.7 %collective-permute-start.24 = (bf16[96,2048]{1,0:T(8,128)(2,1)S(1)}, bf16[96,2048]{1,0:T(8,128)(2,1)S(1)}, u32[]{:S(2)}, u32[]{:S(2)}) collective-permute-start(bf16[96,2048]{1,0:T(8,128)(2,1)S(1)} %collective-permute-done.20.refs_5_), channel_id=1, source_target_pairs={{4,0},{5,1},{8,4},{9,5},{12,8},{13,9},{14,12},{15,13},{10,14},{11,... | collective-permute-start | bytes 1179656 | tf_op jit(solution)/shard_map/ppermute | solution.py:341
  102.1 10.5 %collective-permute-start.25 = (bf16[96,2048]{1,0:T(8,128)(2,1)S(1)}, bf16[96,2048]{1,0:T(8,128)(2,1)S(1)}, u32[]{:S(2)}, u32[]{:S(2)}) collective-permute-start(bf16[96,2048]{1,0:T(8,128)(2,1)S(1)} %collective-permute-done.23.refs_2_), channel_id=1, source_target_pairs={{0,4},{1,5},{4,8},{5,9},{8,12},{9,13},{12,14},{13,15},{14,10},{15,... | collective-permute-start | bytes 1179656 | tf_op jit(solution)/shard_map/ppermute | solution.py:341
  102.6 10.0 %collective-permute-start.26 = (bf16[96,2048]{1,0:T(8,128)(2,1)S(1)}, bf16[96,2048]{1,0:T(8,128)(2,1)S(1)}, u32[]{:S(2)}, u32[]{:S(2)}) collective-permute-start(bf16[96,2048]{1,0:T(8,128)(2,1)S(1)} %collective-permute-done.24.refs_3_), channel_id=1, source_target_pairs={{4,0},{5,1},{8,4},{9,5},{12,8},{13,9},{14,12},{15,13},{10,14},{11,... | collective-permute-start | bytes 1179656 | tf_op jit(solution)/shard_map/ppermute | solution.py:341
  112.7 10.2 %collective-permute-start.28 = (bf16[48,2048]{1,0:T(8,128)(2,1)S(1)}, bf16[48,2048]{1,0:T(8,128)(2,1)S(1)}, u32[]{:S(2)}, u32[]{:S(2)}) collective-permute-start(bf16[48,2048]{1,0:T(8,128)(2,1)S(1)} %slice.71), channel_id=1, source_target_pairs={{4,0},{5,1},{8,4},{9,5},{12,8},{13,9},{14,12},{15,13},{10,14},{11,... | collective-permute-start | bytes 589832 | tf_op jit(solution)/shard_map/ppermute | solution.py:341
  113.3 9.5 %collective-permute-start.27 = (bf16[48,2048]{1,0:T(8,128)(2,1)S(1)}, bf16[48,2048]{1,0:T(8,128)(2,1)S(1)}, u32[]{:S(2)}, u32[]{:S(2)}) collective-permute-start(bf16[48,2048]{1,0:T(8,128)(2,1)S(1)} %slice.70), channel_id=1, source_target_pairs={{0,4},{1,5},{4,8},{5,9},{8,12},{9,13},{12,14},{13,15},{14,10},{15,... | collective-permute-start | bytes 589832 | tf_op jit(solution)/shard_map/ppermute | solution.py:341
  114.7 8.1 %collective-permute-start.29 = (bf16[48,2048]{1,0:T(8,128)(2,1)S(1)}, bf16[48,2048]{1,0:T(8,128)(2,1)S(1)}, u32[]{:S(2)}, u32[]{:S(2)}) collective-permute-start(bf16[48,2048]{1,0:T(8,128)(2,1)S(1)} %get-tuple-element.315), channel_id=1, source_target_pairs={{0,4},{1,5},{4,8},{5,9},{8,12},{9,13},{12,14},{13,15},{14,10},{15,... | collective-permute-start | bytes 589832 | tf_op jit(solution)/shard_map/ppermute | solution.py:341
  115.2 7.6 %collective-permute-start.30 = (bf16[48,2048]{1,0:T(8,128)(2,1)S(1)}, bf16[48,2048]{1,0:T(8,128)(2,1)S(1)}, u32[]{:S(2)}, u32[]{:S(2)}) collective-permute-start(bf16[48,2048]{1,0:T(8,128)(2,1)S(1)} %get-tuple-element.316), channel_id=1, source_target_pairs={{4,0},{5,1},{8,4},{9,5},{12,8},{13,9},{14,12},{15,13},{10,14},{11,... | collective-permute-start | bytes 589832 | tf_op jit(solution)/shard_map/ppermute | solution.py:341
  123.1 10.2 %collective-permute-start.32 = (bf16[96,2048]{1,0:T(8,128)(2,1)S(1)}, bf16[96,2048]{1,0:T(8,128)(2,1)S(1)}, u32[]{:S(2)}, u32[]{:S(2)}) collective-permute-start(bf16[96,2048]{1,0:T(8,128)(2,1)S(1)} %pad_maximum_fusion.1), channel_id=1, source_target_pairs={{4,0},{5,1},{8,4},{9,5},{12,8},{13,9},{14,12},{15,13},{10,14},{11,... | collective-permute-start | bytes 1179656 | tf_op jit(solution)/shard_map/ppermute | solution.py:341
  123.8 9.5 %collective-permute-start.31 = (bf16[96,2048]{1,0:T(8,128)(2,1)S(1)}, bf16[96,2048]{1,0:T(8,128)(2,1)S(1)}, u32[]{:S(2)}, u32[]{:S(2)}) collective-permute-start(bf16[96,2048]{1,0:T(8,128)(2,1)S(1)} %pad_maximum_fusion), channel_id=1, source_target_pairs={{0,4},{1,5},{4,8},{5,9},{8,12},{9,13},{12,14},{13,15},{14,10},{15,... | collective-permute-start | bytes 1179656 | tf_op jit(solution)/shard_map/ppermute | solution.py:341
  133.4 13.5 %collective-permute-start.34 = (bf16[96,2048]{1,0:T(8,128)(2,1)S(1)}, bf16[96,2048]{1,0:T(8,128)(2,1)S(1)}, u32[]{:S(2)}, u32[]{:S(2)}) collective-permute-start(bf16[96,2048]{1,0:T(8,128)(2,1)S(1)} %add_convert_fusion.6), channel_id=1, source_target_pairs={{4,0},{5,1},{8,4},{9,5},{12,8},{13,9},{14,12},{15,13},{10,14},{11,... | collective-permute-start | bytes 1179656 | tf_op jit(solution)/shard_map/ppermute | solution.py:341
  134.2 12.7 %collective-permute-start.33 = (bf16[96,2048]{1,0:T(8,128)(2,1)S(1)}, bf16[96,2048]{1,0:T(8,128)(2,1)S(1)}, u32[]{:S(2)}, u32[]{:S(2)}) collective-permute-start(bf16[96,2048]{1,0:T(8,128)(2,1)S(1)} %add_convert_fusion.7), channel_id=1, source_target_pairs={{0,4},{1,5},{4,8},{5,9},{8,12},{9,13},{12,14},{13,15},{14,10},{15,... | collective-permute-start | bytes 1179656 | tf_op jit(solution)/shard_map/ppermute | solution.py:341
  135.6 11.2 %collective-permute-start.35 = (bf16[48,2048]{1,0:T(8,128)(2,1)S(1)}, bf16[48,2048]{1,0:T(8,128)(2,1)S(1)}, u32[]{:S(2)}, u32[]{:S(2)}) collective-permute-start(bf16[48,2048]{1,0:T(8,128)(2,1)S(1)} %get-tuple-element.357), channel_id=1, source_target_pairs={{0,4},{1,5},{4,8},{5,9},{8,12},{9,13},{12,14},{13,15},{14,10},{15,... | collective-permute-start | bytes 589832 | tf_op jit(solution)/shard_map/ppermute | solution.py:341
  136.1 10.8 %collective-permute-start.36 = (bf16[48,2048]{1,0:T(8,128)(2,1)S(1)}, bf16[48,2048]{1,0:T(8,128)(2,1)S(1)}, u32[]{:S(2)}, u32[]{:S(2)}) collective-permute-start(bf16[48,2048]{1,0:T(8,128)(2,1)S(1)} %get-tuple-element.358), channel_id=1, source_target_pairs={{4,0},{5,1},{8,4},{9,5},{12,8},{13,9},{14,12},{15,13},{10,14},{11,... | collective-permute-start | bytes 589832 | tf_op jit(solution)/shard_map/ppermute | solution.py:341
  147.1 10.1 %collective-permute-start.38 = (bf16[96,2048]{1,0:T(8,128)(2,1)S(1)}, bf16[96,2048]{1,0:T(8,128)(2,1)S(1)}, u32[]{:S(2)}, u32[]{:S(2)}) collective-permute-start(bf16[96,2048]{1,0:T(8,128)(2,1)S(1)} %add_convert_fusion.4), channel_id=1, source_target_pairs={{4,0},{5,1},{8,4},{9,5},{12,8},{13,9},{14,12},{15,13},{10,14},{11,... | collective-permute-start | bytes 1179656 | tf_op jit(solution)/shard_map/ppermute | solution.py:341
  147.8 10.0 %collective-permute-start.37 = (bf16[96,2048]{1,0:T(8,128)(2,1)S(1)}, bf16[96,2048]{1,0:T(8,128)(2,1)S(1)}, u32[]{:S(2)}, u32[]{:S(2)}) collective-permute-start(bf16[96,2048]{1,0:T(8,128)(2,1)S(1)} %add_convert_fusion.5), channel_id=1, source_target_pairs={{0,4},{1,5},{4,8},{5,9},{8,12},{9,13},{12,14},{13,15},{14,10},{15,... | collective-permute-start | bytes 1179656 | tf_op jit(solution)/shard_map/ppermute | solution.py:341
  149.4 14.8 %collective-permute-start.40 = (bf16[96,2048]{1,0:T(8,128)(2,1)S(1)}, bf16[96,2048]{1,0:T(8,128)(2,1)S(1)}, u32[]{:S(2)}, u32[]{:S(2)}) collective-permute-start(bf16[96,2048]{1,0:T(8,128)(2,1)S(1)} %pad_maximum_fusion.3), channel_id=1, source_target_pairs={{4,0},{5,1},{8,4},{9,5},{12,8},{13,9},{14,12},{15,13},{10,14},{11,... | collective-permute-start | bytes 1179656 | tf_op jit(solution)/shard_map/ppermute | solution.py:341
  150.0 15.1 %collective-permute-start.39 = (bf16[96,2048]{1,0:T(8,128)(2,1)S(1)}, bf16[96,2048]{1,0:T(8,128)(2,1)S(1)}, u32[]{:S(2)}, u32[]{:S(2)}) collective-permute-start(bf16[96,2048]{1,0:T(8,128)(2,1)S(1)} %pad_maximum_fusion.2), channel_id=1, source_target_pairs={{0,4},{1,5},{4,8},{5,9},{8,12},{9,13},{12,14},{13,15},{14,10},{15,... | collective-permute-start | bytes 1179656 | tf_op jit(solution)/shard_map/ppermute | solution.py:341
  165.3 12.0 %collective-permute-start.42 = (bf16[96,2048]{1,0:T(8,128)(2,1)S(1)}, bf16[96,2048]{1,0:T(8,128)(2,1)S(1)}, u32[]{:S(2)}, u32[]{:S(2)}) collective-permute-start(bf16[96,2048]{1,0:T(8,128)(2,1)S(1)} %add_convert_fusion.2), channel_id=1, source_target_pairs={{4,0},{5,1},{8,4},{9,5},{12,8},{13,9},{14,12},{15,13},{10,14},{11,... | collective-permute-start | bytes 1179656 | tf_op jit(solution)/shard_map/ppermute | solution.py:341
  165.5 11.9 %collective-permute-start.41 = (bf16[96,2048]{1,0:T(8,128)(2,1)S(1)}, bf16[96,2048]{1,0:T(8,128)(2,1)S(1)}, u32[]{:S(2)}, u32[]{:S(2)}) collective-permute-start(bf16[96,2048]{1,0:T(8,128)(2,1)S(1)} %add_convert_fusion.3), channel_id=1, source_target_pairs={{0,4},{1,5},{4,8},{5,9},{8,12},{9,13},{12,14},{13,15},{14,10},{15,... | collective-permute-start | bytes 1179656 | tf_op jit(solution)/shard_map/ppermute | solution.py:341
  177.5 7.8 %collective-permute-start.44 = (bf16[96,2048]{1,0:T(8,128)(2,1)S(1)}, bf16[96,2048]{1,0:T(8,128)(2,1)S(1)}, u32[]{:S(2)}, u32[]{:S(2)}) collective-permute-start(bf16[96,2048]{1,0:T(8,128)(2,1)S(1)} %add_convert_fusion), channel_id=1, source_target_pairs={{4,0},{5,1},{8,4},{9,5},{12,8},{13,9},{14,12},{15,13},{10,14},{11,... | collective-permute-start | bytes 1179656 | tf_op jit(solution)/shard_map/ppermute | solution.py:341
  178.2 7.8 %collective-permute-start.43 = (bf16[96,2048]{1,0:T(8,128)(2,1)S(1)}, bf16[96,2048]{1,0:T(8,128)(2,1)S(1)}, u32[]{:S(2)}, u32[]{:S(2)}) collective-permute-start(bf16[96,2048]{1,0:T(8,128)(2,1)S(1)} %add_convert_fusion.1), channel_id=1, source_target_pairs={{0,4},{1,5},{4,8},{5,9},{8,12},{9,13},{12,14},{13,15},{14,10},{15,... | collective-permute-start | bytes 1179656 | tf_op jit(solution)/shard_map/ppermute | solution.py:341

commit v10 on v9

--- a/solution.py
+++ b/solution.py
@@ -39,7 +39,7 @@
         out_shape=jax.ShapeDtypeStruct((count, width), jnp.bfloat16),
         compiler_params=pltpu.CompilerParams(vmem_limit_bytes=VMEM_LIMIT),
         cost_estimate=pl.CostEstimate(flops=0, bytes_accessed=count * width * 4, transcendentals=0),
-    )(rows, gain_row)
+    )(*in_hbm([rows, gain_row]))
 
 
 def pack_kernel(experts, rows_ref, ids_ref, gates_ref, out_ref):
@@ -160,30 +160,24 @@
     packed, factors = refs[:parts], refs[parts : parts + len(pieces)]
     weights = refs[parts + len(pieces) :][:6]
     outs = refs[parts + len(pieces) + 6 :][:parts]
-    cot, slot, grads, cot_sem, factor_sem = refs[2 * parts + len(pieces) + 6 :]
-    copies = block_copies(packed, cot, cot_sem)
-    factor_copies, place = [], 0
-    for i, (start, count) in enumerate(pieces):
-        factor_copies.append(
-            pltpu.make_async_copy(
-                factors[i].at[:, pl.ds(start, count)],
-                grads.at[:, pl.ds(place, count)],
-                factor_sem.at[i],
-            )
-        )
-        place += count
-    start_all(copies + factor_copies)
-    wait_all(copies)
+    slot, grads = refs[2 * parts + len(pieces) + 6 :]
     for e in range(2):
-        table = cot[:, width:].astype(jnp.float32)
-        gate = gate_column(table, 1, experts, names_ref[e])
-        slot[...] = (gate * cot[:, :width].astype(jnp.float32)).astype(jnp.bfloat16)
+        row = 0
+        for block in packed:
+            count = block.shape[0]
+            table = block[:, width:].astype(jnp.float32)
+            gate = gate_column(table, 1, experts, names_ref[e])
+            made = gate * block[:, :width].astype(jnp.float32)
+            slot[row : row + count] = made.astype(jnp.bfloat16)
+            row += count
         back = dot_nt(slot[...], weights[3 * e + 2][...])
-        if e == 0:
-            wait_all(factor_copies)
-        for i in range(2):
-            made = back * grads[2 * e + i].astype(jnp.float32)
-            grads[2 * e + i] = made.astype(jnp.bfloat16)
+        row = 0
+        for factor, (start, count) in zip(factors, pieces):
+            part = back[row : row + count]
+            for i in range(2):
+                made = part * factor[2 * e + i, start : start + count].astype(jnp.float32)
+                grads[2 * e + i, row : row + count] = made.astype(jnp.bfloat16)
+            row += count
 
     @pl.loop(0, width // tile)
     def _(n):
@@ -289,22 +283,19 @@
 def backward_call(names, packed, factors, pieces, weights, experts):
     parts = len(packed)
     counts = [block.shape[0] for block in packed]
-    total, full = sum(counts), packed[0].shape[1]
+    total = sum(counts)
     width, inner = weights[0].shape
     out = pl.pallas_call(
         functools.partial(backward_kernel, parts, experts, width, TILE, pieces),
         out_shape=[jax.ShapeDtypeStruct((count, width), jnp.bfloat16) for count in counts],
-        in_specs=[pl.BlockSpec(memory_space=pltpu.SMEM)] + [HBM] * (parts + len(pieces)) + [WHOLE] * 6,
+        in_specs=[pl.BlockSpec(memory_space=pltpu.SMEM)] + [WHOLE] * (parts + len(pieces) + 6),
         scratch_shapes=[
-            pltpu.VMEM((total, full), jnp.bfloat16),
             pltpu.VMEM((total, width), jnp.bfloat16),
             pltpu.VMEM((4, total, inner), jnp.bfloat16),
-            pltpu.SemaphoreType.DMA((parts,)),
-            pltpu.SemaphoreType.DMA((len(pieces),)),
         ],
         compiler_params=PARAMS,
         cost_estimate=cost(6, total, width, inner, 6e-6),
-    )(names, *packed, *factors, *in_vmem(weights))
+    )(names, *in_vmem(packed), *in_vmem(factors), *in_vmem(weights))
     return list(out)
 
 
@@ -474,20 +465,20 @@
         return kept + norm_pullback(fall_wide, norm_row, ring.total("backward"))
 
     if planned:
+        first_hop, leaving_rise = lax.optimization_barrier((ring.held["fall"][1], leaving_rise))
+        ring.held["fall"][1] = first_hop
         ring.gather("fall", 2)
+        moved_rise = passed_along(leaving_rise, "pipe", 1)
         own_gate, own_up, own_down = own
         other_gate, other_up = swapped(own_gate), swapped(own_up)
-        packed, leaving_rise = lax.optimization_barrier((ring.held["cot"][0][0], leaving_rise))
-        ring.held["cot"][0] = [packed]
-        moved_rise = passed_along(leaving_rise, "pipe", 1)
         heads = (head_rise, head_fall)
-        cot_in, own, own_down, other_gate, other_up, heads, ring.names = ring.fence(
-            cot_in, own, own_down, other_gate, other_up, heads, names
+        cot_in, moved_rise, own, own_down, other_gate, other_up, heads, ring.names = ring.fence(
+            cot_in, moved_rise, own, own_down, other_gate, other_up, heads, names
         )
         ring.gather("fall", 3)
         ring.gather("cot", 1)
         own = fetched(own)
-        moved_rise, own, own_down = ring.fence(moved_rise, own, own_down)
+        moved_rise, cot_in, own, own_down = ring.fence(moved_rise, cot_in, own, own_down)
         ring.gather("fall", 4)
         ring.gather("cot", 2)
         ring.weights = own + (other_gate, other_up, None)

time: 188 us -> 191 us (1.016)
  waiting for transfers between devices: 61.5 us -> 71 us
  Pallas kernels: 59.9 us -> 54.2 us
    ppermute x40, waiting for transfers between devices: 59.8 us -> 67.1 us  [pass_on(): return lax.ppermute(block, 'ep', self.routes[way])]
    pallas_call x2, Pallas kernels: 19.8 us -> 15.5 us  [backward_call(): pl.pallas_call(functools.partial(backward_kernel, parts, experts, width,...]
    ppermute x2, waiting for transfers between devices: 1.76 us -> 3.84 us  [passed_along(): return lax.ppermute(block, axis, route)]
  transfers between devices with their start and end apart: 45 -> 45, of which waited for: 17 -> 21; matrix products, arithmetic and copies ran while one was open for 4% -> 4% of each run, Pallas kernels for 32% -> 29%
where the time goes in v10:
time: 191 us; the launch traced here: 190 us
  waiting for transfers between devices  71 us (37%)
  Pallas kernels  54.2 us (28%)
  starting transfers between devices  50.6 us (26%)
  other arithmetic  6.76 us (4%)
  local copies, waits for them, and re-layouts  5.05 us (3%)
  between operations  2.52 us (1%)
    ppermute x40, waiting for transfers between devices, pass_on(): return lax.ppermute(block, 'ep', self.routes[way])  67.1 us
    ppermute x40, starting transfers between devices, pass_on(): return lax.ppermute(block, 'ep', self.routes[way])  42.8 us
    pallas_call x3, Pallas kernels, forward_call(): pl.pallas_call(functools.partial(forward_kernel, parts, experts, width, T...  20.1 us
    pallas_call x2, Pallas kernels, backward_call(): pl.pallas_call(functools.partial(backward_kernel, parts, experts, width,...  15.5 us
    pallas_call x2, Pallas kernels, factor_call(): pl.pallas_call(functools.partial(factor_kernel, parts), out_shape=jax.Sha...  13.6 us
    ppermute x2, starting transfers between devices, passed_along(): return lax.ppermute(block, axis, route)  7.2 us
    ppermute x2, waiting for transfers between devices, passed_along(): return lax.ppermute(block, axis, route)  3.84 us
  transfers between devices with their start and end apart: 45, of which 21 were waited for; matrix products, arithmetic and copies ran while one was open for 4% of the time, Pallas kernels for 29%

profile of v10, /device:TPU:0, one launch (start us, length us, event | category | flops | bytes accessed | tf_op | source)
XLA Modules:
  0.0 190.1 jit_solution(443286252631934493)
XLA Ops:
  1.2 1.2 shard_map.148.refs_0_
  2.4 3.0 %collective-permute-start.2 = (bf16[96,2048]{1,0:T(8,128)(2,1)S(1)}, bf16[96,2048]{1,0:T(8,128)(2,1)}, u32[]{:S(2)}, u32[]{:S(2)}) collective-permute-start(bf16[96,2048]{1,0:T(8,128)(2,1)S(1)} %shard_map.148.refs_0_), channel_id=1, source_target_pairs={{4,0},{5,1},{8,4},{9,5},{12,8},{13,9},{14,12},{15,13},{10,14},{11,... | collective-permute-start | bytes 1179656 | tf_op jit(solution)/shard_map/ppermute | solution.py:332
  5.5 3.8 %collective-permute-start = (bf16[96,2048]{1,0:T(8,128)(2,1)}, bf16[96,2048]{1,0:T(8,128)(2,1)S(1)}, u32[]{:S(2)}, u32[]{:S(2)}) collective-permute-start(bf16[96,2048]{1,0:T(8,128)(2,1)} %bitcast.63), channel_id=1, source_target_pairs={{0,16},{1,17},{2,18},{3,19},{4,20},{5,21},{6,22},{7,23},{8,24},{9,... | collective-permute-start | bytes 1179656 | tf_op jit(solution)/shard_map/ppermute | solution.py:17
  9.4 0.8 fusion.19
  12.0 0.8 copy.16
  12.8 0.8 copy.17
  13.7 1.2 collective-permute-done.2.refs_2_
  14.9 1.4 collective-permute-done.1.refs_1_
  16.4 3.4 %collective-permute-start.5 = (bf16[96,2048]{1,0:T(8,128)(2,1)}, bf16[96,2048]{1,0:T(8,128)(2,1)S(1)}, u32[]{:S(2)}, u32[]{:S(2)}) collective-permute-start(bf16[96,2048]{1,0:T(8,128)(2,1)} %bitcast.64), channel_id=1, source_target_pairs={{0,16},{1,17},{2,18},{3,19},{4,20},{5,21},{6,22},{7,23},{8,24},{9,... | collective-permute-start | bytes 1179656 | tf_op jit(solution)/shard_map/ppermute | solution.py:17
  20.3 1.5 collective-permute-start.4
  21.9 1.1 bitcast_select_fusion.rows_ref
  22.9 0.7 shard_map.149.refs_0_
  23.7 3.8 %collective-permute-done.5 = bf16[96,2048]{1,0:T(8,128)(2,1)S(1)} collective-permute-done((bf16[96,2048]{1,0:T(8,128)(2,1)}, bf16[96,2048]{1,0:T(8,128)(2,1)S(1)}, u32[]{:S(2)}, u32[]{:S(2)}) %collective-permute-start.5) | collective-permute-done | bytes 393248 | tf_op jit(solution)/shard_map/ppermute | solution.py:17
  27.5 2.3 %collective-permute-done.3.refs_3_ = bf16[96,2048]{1,0:T(8,128)(2,1)} collective-permute-done((bf16[96,2048]{1,0:T(8,128)(2,1)}, bf16[96,2048]{1,0:T(8,128)(2,1)}, u32[]{:S(2)}, u32[]{:S(2)}) %collective-permute-start.3) | collective-permute-done | bytes 393248 | tf_op jit(solution)/shard_map/ppermute | solution.py:332
  30.2 1.4 collective-permute-start.9
  31.6 0.7 collective-permute-start.8
  32.2 1.6 collective-permute-start.10
  34.5 3.0 %shard_map.150 = (bf16[2048,512]{1,0:T(8,128)(2,1)S(1)}, bf16[2048,512]{1,0:T(8,128)(2,1)S(1)}, bf16[512,2048]{1,0:T(8,128)(2,1)S(1)}) custom-call(bf16[2048,512]{1,0:T(8,128)(2,1)} %bitcast.51, bf16[2048,512]{1,0:T(8,128)(2,1)} %bitcast.53, bf16[512,2048]{1,0:T(8,128)(2,1)} %bitcast.54), custom_call_target="tpu_custom_call" | custom-call | bytes 8388608 | tf_op jit(solution)/shard_map/pallas_call | solution.py:220
  37.6 11.4 %collective-permute-done.10.refs_5_ = bf16[96,2048]{1,0:T(8,128)(2,1)} collective-permute-done((bf16[96,2048]{1,0:T(8,128)(2,1)}, bf16[96,2048]{1,0:T(8,128)(2,1)}, u32[]{:S(2)}, u32[]{:S(2)}) %collective-permute-start.10) | collective-permute-done | bytes 393248 | tf_op jit(solution)/shard_map/ppermute | solution.py:332
  49.2 0.9 slice.64
  50.2 0.9 slice.65
  51.1 1.6 collective-permute-start.15
  53.2 0.6 multiply_reduce_fusion
  53.9 0.7 collective-permute-start.12
  54.6 1.4 collective-permute-start.13
  56.4 9.5 %shard_map.151.refs_5_.refs_4_ = bf16[4,672,512]{2,1,0:T(8,128)(2,1)S(1)} custom-call(bf16[96,2048]{1,0:T(8,128)(2,1)} %copy-done, bf16[96,2048]{1,0:T(8,128)(2,1)} %collective-permute-done.1.refs_1_, bf16[96,2048]{1,0:T(8,128)(2,1)} %collective-permute-done.2.refs_2_, bf16[96,2048]{1,0:T(8,128)(2,1)} %collective-permute-done.3.refs_3_, ...), custom_call_target="tpu_custom_call" | custom-call | flops 11137144832 | bytes 12582912 | tf_op jit(solution)/shard_map/pallas_call | solution.py:270
  66.5 1.6 collective-permute-start.20
  69.3 1.4 collective-permute-start.18
  70.6 9.1 %shard_map.153 = (bf16[96,2048]{1,0:T(8,128)(2,1)S(1)}, bf16[96,2048]{1,0:T(8,128)(2,1)S(1)}, bf16[96,2048]{1,0:T(8,128)(2,1)S(1)}, bf16[96,2048]{1,0:T(8,128)(2,1)S(1)}, bf16[96,2048]{1,0:T(8,128)(2,1)S(1)}) custom-call(s32[2]{0:T(128)S(1)} %pad_add_fusion.names_ref, bf16[96,2176]{1,0:T(8,128)(2,1)S(1)} %shard_map.149.refs_0_, ...), custom_call_target="tpu_custom_call" | custom-call | flops 12639797248 | bytes 12582912 | tf_op jit(solution)/shard_map/pallas_call | solution.py:288
  79.8 4.1 %shard_map.152.refs_5_ = bf16[4,96,512]{2,1,0:T(8,128)(2,1)S(1)} custom-call(bf16[48,2048]{1,0:T(8,128)(2,1)} %copy-done.11, bf16[48,2048]{1,0:T(8,128)(2,1)} %copy-done.10, bf16[2048,512]{1,0:T(8,128)(2,1)S(1)} %get-tuple-element.232.refs_7_.refs_2_.refs_6_.refs_4_.refs_8_, bf16[2048,512]{1,0:T(8,128)(2,1)S(1)} %get-tuple-element.233.refs_8_.refs_3_.refs_7_.refs_5_.refs_9_, ...), custom_call_target="tpu_custom_call" | custom-call | flops 6305306624 | bytes 12582912 | tf_op jit(solution)/shard_map/pallas_call | solution.py:270
  84.0 4.4 %collective-permute-done.17.refs_0_ = bf16[96,2176]{1,0:T(8,128)(2,1)S(1)} collective-permute-done((bf16[96,2176]{1,0:T(8,128)(2,1)S(1)}, bf16[96,2176]{1,0:T(8,128)(2,1)S(1)}, u32[]{:S(2)}, u32[]{:S(2)}) %collective-permute-start.17) | collective-permute-done | bytes 417824 | tf_op jit(solution)/shard_map/ppermute | solution.py:332
  88.4 1.6 collective-permute-start.22
  90.9 1.6 collective-permute-start.24
  92.5 7.6 %shard_map.154 = (bf16[96,2048]{1,0:T(8,128)(2,1)S(1)}, bf16[96,2048]{1,0:T(8,128)(2,1)S(1)}, bf16[96,2048]{1,0:T(8,128)(2,1)S(1)}) custom-call(s32[2]{0:T(128)S(1)} %pad_add_fusion.names_ref, bf16[96,2176]{1,0:T(8,128)(2,1)S(1)} %shard_map.149.refs_0_, bf16[96,2176]{1,0:T(8,128)(2,1)} %collective-permute-done.8.refs_1_, ...), custom_call_target="tpu_custom_call" | custom-call | flops 10223878144 | bytes 12582912 | tf_op jit(solution)/shard_map/pallas_call | solution.py:250
  100.1 4.6 %collective-permute-done.23.refs_2_ = bf16[96,2048]{1,0:T(8,128)(2,1)S(1)} collective-permute-done((bf16[96,2048]{1,0:T(8,128)(2,1)S(1)}, bf16[96,2048]{1,0:T(8,128)(2,1)S(1)}, u32[]{:S(2)}, u32[]{:S(2)}) %collective-permute-start.23) | collective-permute-done | bytes 393248 | tf_op jit(solution)/shard_map/ppermute | solution.py:332
  105.1 1.6 collective-permute-start.26
  106.7 6.4 %shard_map.155 = (bf16[96,2048]{1,0:T(8,128)(2,1)S(1)}, bf16[96,2048]{1,0:T(8,128)(2,1)S(1)}, bf16[48,2048]{1,0:T(8,128)(2,1)S(1)}, bf16[48,2048]{1,0:T(8,128)(2,1)S(1)}) custom-call(s32[2]{0:T(128)S(1)} %pad_add_fusion.names_ref, bf16[96,2176]{1,0:T(8,128)(2,1)S(1)} %collective-permute-done.17.refs_0_, ...), custom_call_target="tpu_custom_call" | custom-call | flops 10223878144 | bytes 12582912 | tf_op jit(solution)/shard_map/pallas_call | solution.py:288
  113.1 0.8 collective-permute-done.25.refs_4_
  114.1 1.9 collective-permute-start.28
  116.2 0.7 collective-permute-start.29
  116.9 1.3 collective-permute-start.30
  118.2 5.4 %shard_map.156 = (bf16[96,2048]{1,0:T(8,128)(2,1)S(1)}, bf16[96,2048]{1,0:T(8,128)(2,1)S(1)}) custom-call(s32[2]{0:T(128)S(1)} %pad_add_fusion.names_ref, bf16[96,2176]{1,0:T(8,128)(2,1)S(1)} %collective-permute-done.12.refs_3_.refs_0_, bf16[96,2176]{1,0:T(8,128)(2,1)S(1)} %collective-permute-done.13.refs_4_.refs_1_, ...), custom_call_target="tpu_custom_call" | custom-call | flops 9015918592 | bytes 12582912 | tf_op jit(solution)/shard_map/pallas_call | solution.py:250
  124.0 1.8 collective-permute-start.32
  126.3 7.2 %shard_map.157 = (bf16[96,2048]{1,0:T(8,128)(2,1)S(1)}, bf16[96,2048]{1,0:T(8,128)(2,1)S(1)}, bf16[48,2048]{1,0:T(8,128)(2,1)S(1)}, bf16[48,2048]{1,0:T(8,128)(2,1)S(1)}) custom-call(s32[2]{0:T(128)S(1)} %pad_add_fusion.names_ref, bf16[96,2176]{1,0:T(8,128)(2,1)S(1)} %collective-permute-done.17.refs_0_, ...), custom_call_target="tpu_custom_call" | custom-call | flops 10223878144 | bytes 12582912 | tf_op jit(solution)/shard_map/pallas_call | solution.py:250
  133.5 1.1 collective-permute-done.31
  134.7 1.5 collective-permute-start.34
  136.3 0.7 collective-permute-start.33
  137.0 2.0 %collective-permute-start.36 = (bf16[48,2048]{1,0:T(8,128)(2,1)S(1)}, bf16[48,2048]{1,0:T(8,128)(2,1)S(1)}, u32[]{:S(2)}, u32[]{:S(2)}) collective-permute-start(bf16[48,2048]{1,0:T(8,128)(2,1)S(1)} %get-tuple-element.364), channel_id=1, source_target_pairs={{4,0},{5,1},{8,4},{9,5},{12,8},{13,9},{14,12},{15,13},{10,14},{11,... | collective-permute-start | bytes 589832 | tf_op jit(solution)/shard_map/ppermute | solution.py:332
  139.0 9.4 %collective-permute-done.35 = bf16[48,2048]{1,0:T(8,128)(2,1)S(1)} collective-permute-done((bf16[48,2048]{1,0:T(8,128)(2,1)S(1)}, bf16[48,2048]{1,0:T(8,128)(2,1)S(1)}, u32[]{:S(2)}, u32[]{:S(2)}) %collective-permute-start.35) | collective-permute-done | bytes 196640 | tf_op jit(solution)/shard_map/ppermute | solution.py:332
  148.7 1.6 collective-permute-start.38
  150.9 1.6 collective-permute-start.40
  153.1 4.2 %collective-permute-done.38 = bf16[96,2048]{1,0:T(8,128)(2,1)S(1)} collective-permute-done((bf16[96,2048]{1,0:T(8,128)(2,1)S(1)}, bf16[96,2048]{1,0:T(8,128)(2,1)S(1)}, u32[]{:S(2)}, u32[]{:S(2)}) %collective-permute-start.38) | collective-permute-done | bytes 393248 | tf_op jit(solution)/shard_map/ppermute | solution.py:332
  157.3 1.8 collective-permute-done.37
  159.1 5.2 %collective-permute-done.40 = bf16[96,2048]{1,0:T(8,128)(2,1)S(1)} collective-permute-done((bf16[96,2048]{1,0:T(8,128)(2,1)S(1)}, bf16[96,2048]{1,0:T(8,128)(2,1)S(1)}, u32[]{:S(2)}, u32[]{:S(2)}) %collective-permute-start.40) | collective-permute-done | bytes 393248 | tf_op jit(solution)/shard_map/ppermute | solution.py:332
  164.4 1.6 collective-permute-done.39
  166.1 1.9 %collective-permute-start.42 = (bf16[96,2048]{1,0:T(8,128)(2,1)S(1)}, bf16[96,2048]{1,0:T(8,128)(2,1)S(1)}, u32[]{:S(2)}, u32[]{:S(2)}) collective-permute-start(bf16[96,2048]{1,0:T(8,128)(2,1)S(1)} %add_convert_fusion.2), channel_id=1, source_target_pairs={{4,0},{5,1},{8,4},{9,5},{12,8},{13,9},{14,12},{15,13},{10,14},{11,... | collective-permute-start | bytes 1179656 | tf_op jit(solution)/shard_map/ppermute | solution.py:332
  168.7 1.1 fusion.11
  169.8 8.0 %collective-permute-done.42 = bf16[96,2048]{1,0:T(8,128)(2,1)S(1)} collective-permute-done((bf16[96,2048]{1,0:T(8,128)(2,1)S(1)}, bf16[96,2048]{1,0:T(8,128)(2,1)S(1)}, u32[]{:S(2)}, u32[]{:S(2)}) %collective-permute-start.42) | collective-permute-done | bytes 393248 | tf_op jit(solution)/shard_map/ppermute | solution.py:332
  177.8 2.1 %collective-permute-done.41 = bf16[96,2048]{1,0:T(8,128)(2,1)S(1)} collective-permute-done((bf16[96,2048]{1,0:T(8,128)(2,1)S(1)}, bf16[96,2048]{1,0:T(8,128)(2,1)S(1)}, u32[]{:S(2)}, u32[]{:S(2)}) %collective-permute-start.41) | collective-permute-done | bytes 393248 | tf_op jit(solution)/shard_map/ppermute | solution.py:332
  180.0 1.2 collective-permute-start.44
  181.3 0.9 collective-permute-start.43
  182.2 5.6 %collective-permute-done.44 = bf16[96,2048]{1,0:T(8,128)(2,1)S(1)} collective-permute-done((bf16[96,2048]{1,0:T(8,128)(2,1)S(1)}, bf16[96,2048]{1,0:T(8,128)(2,1)S(1)}, u32[]{:S(2)}, u32[]{:S(2)}) %collective-permute-start.44) | collective-permute-done | bytes 393248 | tf_op jit(solution)/shard_map/ppermute | solution.py:332
  187.8 1.3 collective-permute-done.43
  189.1 1.0 fusion.17
  (106 shorter events, 11.1 us)
Async XLA Ops:
  0.6 29.6 %collective-permute-start.6 = (bf16[2048,512]{1,0:T(8,128)(2,1)}, bf16[2048,512]{1,0:T(8,128)(2,1)S(1)}, u32[]{:S(2)}, u32[]{:S(2)}) collective-permute-start(bf16[2048,512]{1,0:T(8,128)(2,1)} %bitcast.50), channel_id=1, source_target_pairs={{0,1},{1,0},{2,3},{3,2},{4,5},{5,4},{6,7},{7,6},{8,9},{9,8},{10,11... | collective-permute-start | bytes 6291464 | tf_op jit(solution)/shard_map/ppermute | solution.py:440
  1.1 29.0 %collective-permute-start.7 = (bf16[2048,512]{1,0:T(8,128)(2,1)}, bf16[2048,512]{1,0:T(8,128)(2,1)}, u32[]{:S(2)}, u32[]{:S(2)}) collective-permute-start(bf16[2048,512]{1,0:T(8,128)(2,1)} %bitcast.52), channel_id=1, source_target_pairs={{0,1},{1,0},{2,3},{3,2},{4,5},{5,4},{6,7},{7,6},{8,9},{9,8},{10,11... | collective-permute-start | bytes 6291464 | tf_op jit(solution)/shard_map/ppermute | solution.py:440
  2.4 35.1 %copy-start = (bf16[96,2048]{1,0:T(8,128)(2,1)}, bf16[96,2048]{1,0:T(8,128)(2,1)S(1)}, u32[]{:S(2)}) copy-start(bf16[96,2048]{1,0:T(8,128)(2,1)S(1)} %shard_map.148.refs_0_) | copy-start | bytes 1179652
  2.4 12.5 %collective-permute-start.2 = (bf16[96,2048]{1,0:T(8,128)(2,1)S(1)}, bf16[96,2048]{1,0:T(8,128)(2,1)}, u32[]{:S(2)}, u32[]{:S(2)}) collective-permute-start(bf16[96,2048]{1,0:T(8,128)(2,1)S(1)} %shard_map.148.refs_0_), channel_id=1, source_target_pairs={{4,0},{5,1},{8,4},{9,5},{12,8},{13,9},{14,12},{15,13},{10,14},{11,... | collective-permute-start | bytes 1179656 | tf_op jit(solution)/shard_map/ppermute | solution.py:332
  5.4 10.9 %collective-permute-start.1 = (bf16[96,2048]{1,0:T(8,128)(2,1)S(1)}, bf16[96,2048]{1,0:T(8,128)(2,1)}, u32[]{:S(2)}, u32[]{:S(2)}) collective-permute-start(bf16[96,2048]{1,0:T(8,128)(2,1)S(1)} %shard_map.148.refs_0_), channel_id=1, source_target_pairs={{0,4},{1,5},{4,8},{5,9},{8,12},{9,13},{12,14},{13,15},{14,10},{15,... | collective-permute-start | bytes 1179656 | tf_op jit(solution)/shard_map/ppermute | solution.py:332
  5.5 14.8 %collective-permute-start = (bf16[96,2048]{1,0:T(8,128)(2,1)}, bf16[96,2048]{1,0:T(8,128)(2,1)S(1)}, u32[]{:S(2)}, u32[]{:S(2)}) collective-permute-start(bf16[96,2048]{1,0:T(8,128)(2,1)} %bitcast.63), channel_id=1, source_target_pairs={{0,16},{1,17},{2,18},{3,19},{4,20},{5,21},{6,22},{7,23},{8,24},{9,... | collective-permute-start | bytes 1179656 | tf_op jit(solution)/shard_map/ppermute | solution.py:17
  13.7 20.6 %copy-start.1 = (bf16[1,96,2048]{2,1,0:T(8,128)(2,1)S(1)}, bf16[1,96,2048]{2,1,0:T(8,128)(2,1)}, u32[]{:S(2)}) copy-start(bf16[1,96,2048]{2,1,0:T(8,128)(2,1)} %param.16) | copy-start | bytes 1179652
  16.4 11.1 %collective-permute-start.5 = (bf16[96,2048]{1,0:T(8,128)(2,1)}, bf16[96,2048]{1,0:T(8,128)(2,1)S(1)}, u32[]{:S(2)}, u32[]{:S(2)}) collective-permute-start(bf16[96,2048]{1,0:T(8,128)(2,1)} %bitcast.64), channel_id=1, source_target_pairs={{0,16},{1,17},{2,18},{3,19},{4,20},{5,21},{6,22},{7,23},{8,24},{9,... | collective-permute-start | bytes 1179656 | tf_op jit(solution)/shard_map/ppermute | solution.py:17
  19.8 10.0 %collective-permute-start.3 = (bf16[96,2048]{1,0:T(8,128)(2,1)}, bf16[96,2048]{1,0:T(8,128)(2,1)}, u32[]{:S(2)}, u32[]{:S(2)}) collective-permute-start(bf16[96,2048]{1,0:T(8,128)(2,1)} %collective-permute-done.1.refs_1_), channel_id=1, source_target_pairs={{0,4},{1,5},{4,8},{5,9},{8,12},{9,13},{12,14},{13,15},{14,10},{15,... | collective-permute-start | bytes 1179656 | tf_op jit(solution)/shard_map/ppermute | solution.py:332
  20.3 9.8 %collective-permute-start.4 = (bf16[96,2048]{1,0:T(8,128)(2,1)}, bf16[96,2048]{1,0:T(8,128)(2,1)}, u32[]{:S(2)}, u32[]{:S(2)}) collective-permute-start(bf16[96,2048]{1,0:T(8,128)(2,1)} %collective-permute-done.2.refs_2_), channel_id=1, source_target_pairs={{4,0},{5,1},{8,4},{9,5},{12,8},{13,9},{14,12},{15,13},{10,14},{11,... | collective-permute-start | bytes 1179656 | tf_op jit(solution)/shard_map/ppermute | solution.py:332
  27.5 6.9 %copy-start.6 = (bf16[96,2048]{1,0:T(8,128)(2,1)}, bf16[96,2048]{1,0:T(8,128)(2,1)S(1)}, u32[]{:S(2)}) copy-start(bf16[96,2048]{1,0:T(8,128)(2,1)S(1)} %collective-permute-done.5) | copy-start | bytes 1179652
  30.2 18.8 %collective-permute-start.9 = (bf16[96,2176]{1,0:T(8,128)(2,1)S(1)}, bf16[96,2176]{1,0:T(8,128)(2,1)}, u32[]{:S(2)}, u32[]{:S(2)}) collective-permute-start(bf16[96,2176]{1,0:T(8,128)(2,1)S(1)} %shard_map.149.refs_0_), channel_id=1, source_target_pairs={{4,0},{5,1},{8,4},{9,5},{12,8},{13,9},{14,12},{15,13},{10,14},{11,... | collective-permute-start | bytes 1253384 | tf_op jit(solution)/shard_map/ppermute | solution.py:332
  31.6 17.4 %collective-permute-start.8 = (bf16[96,2176]{1,0:T(8,128)(2,1)S(1)}, bf16[96,2176]{1,0:T(8,128)(2,1)}, u32[]{:S(2)}, u32[]{:S(2)}) collective-permute-start(bf16[96,2176]{1,0:T(8,128)(2,1)S(1)} %shard_map.149.refs_0_), channel_id=1, source_target_pairs={{0,4},{1,5},{4,8},{5,9},{8,12},{9,13},{12,14},{13,15},{14,10},{15,... | collective-permute-start | bytes 1253384 | tf_op jit(solution)/shard_map/ppermute | solution.py:332
  32.2 16.7 %collective-permute-start.10 = (bf16[96,2048]{1,0:T(8,128)(2,1)}, bf16[96,2048]{1,0:T(8,128)(2,1)}, u32[]{:S(2)}, u32[]{:S(2)}) collective-permute-start(bf16[96,2048]{1,0:T(8,128)(2,1)} %collective-permute-done.3.refs_3_), channel_id=1, source_target_pairs={{0,4},{1,5},{4,8},{5,9},{8,12},{9,13},{12,14},{13,15},{14,10},{15,... | collective-permute-start | bytes 1179656 | tf_op jit(solution)/shard_map/ppermute | solution.py:332
  33.8 15.2 %collective-permute-start.11 = (bf16[96,2048]{1,0:T(8,128)(2,1)}, bf16[96,2048]{1,0:T(8,128)(2,1)}, u32[]{:S(2)}, u32[]{:S(2)}) collective-permute-start(bf16[96,2048]{1,0:T(8,128)(2,1)} %collective-permute-done.4.refs_4_), channel_id=1, source_target_pairs={{4,0},{5,1},{8,4},{9,5},{12,8},{13,9},{14,12},{15,13},{10,14},{11,... | collective-permute-start | bytes 1179656 | tf_op jit(solution)/shard_map/ppermute | solution.py:332
  34.4 14.5 %copy-start.5 = (bf16[2,96,2048]{2,1,0:T(8,128)(2,1)S(1)}, bf16[2,96,2048]{2,1,0:T(8,128)(2,1)}, u32[]{:S(2)}) copy-start(bf16[2,96,2048]{2,1,0:T(8,128)(2,1)} %param.13) | copy-start | bytes 2359300
  34.4 14.5 %copy-start.7 = (bf16[96,2048]{1,0:T(8,128)(2,1)S(1)}, bf16[96,2048]{1,0:T(8,128)(2,1)}, u32[]{:S(2)}) copy-start(bf16[96,2048]{1,0:T(8,128)(2,1)} %copy-done.6) | copy-start | bytes 1179652
  34.5 18.8 %copy-start.4 = (bf16[2,96,2048]{2,1,0:T(8,128)(2,1)S(1)}, bf16[2,96,2048]{2,1,0:T(8,128)(2,1)}, u32[]{:S(2)}) copy-start(bf16[2,96,2048]{2,1,0:T(8,128)(2,1)} %param.17) | copy-start | bytes 2359300
  34.5 18.7 %copy-start.8 = (f32[1,2048]{1,0:T(1,128)S(1)}, f32[1,2048]{1,0:T(1,128)}, u32[]{:S(2)}) copy-start(f32[1,2048]{1,0:T(1,128)} %gain_ref.1) | copy-start | bytes 24580
  34.5 18.7 %copy-start.9 = (f32[1,2048]{1,0:T(1,128)S(1)}, f32[1,2048]{1,0:T(1,128)}, u32[]{:S(2)}) copy-start(f32[1,2048]{1,0:T(1,128)} %param.19) | copy-start | bytes 24580
  37.5 15.7 %copy-start.2 = (bf16[1,96,2048]{2,1,0:T(8,128)(2,1)S(1)}, bf16[1,96,2048]{2,1,0:T(8,128)(2,1)}, u32[]{:S(2)}) copy-start(bf16[1,96,2048]{2,1,0:T(8,128)(2,1)} %param.16) | copy-start | bytes 1179652
  37.5 18.4 %copy-start.3 = (bf16[1,1,512,2048]{3,2,1,0:T(8,128)(2,1)S(1)}, bf16[1,1,512,2048]{3,2,1,0:T(8,128)(2,1)}, u32[]{:S(2)}) copy-start(bf16[1,1,512,2048]{3,2,1,0:T(8,128)(2,1)} %param.22) | copy-start | bytes 6291460
  51.1 15.3 %collective-permute-start.15 = (bf16[48,2048]{1,0:T(8,128)(2,1)S(1)}, bf16[48,2048]{1,0:T(8,128)(2,1)S(1)}, u32[]{:S(2)}, u32[]{:S(2)}) collective-permute-start(bf16[48,2048]{1,0:T(8,128)(2,1)S(1)} %slice.65), channel_id=1, source_target_pairs={{4,0},{5,1},{8,4},{9,5},{12,8},{13,9},{14,12},{15,13},{10,14},{11,... | collective-permute-start | bytes 589832 | tf_op jit(solution)/shard_map/ppermute | solution.py:332
  52.8 13.7 %collective-permute-start.14 = (bf16[48,2048]{1,0:T(8,128)(2,1)S(1)}, bf16[48,2048]{1,0:T(8,128)(2,1)S(1)}, u32[]{:S(2)}, u32[]{:S(2)}) collective-permute-start(bf16[48,2048]{1,0:T(8,128)(2,1)S(1)} %slice.64), channel_id=1, source_target_pairs={{0,4},{1,5},{4,8},{5,9},{8,12},{9,13},{12,14},{13,15},{14,10},{15,... | collective-permute-start | bytes 589832 | tf_op jit(solution)/shard_map/ppermute | solution.py:332
  53.9 12.6 %collective-permute-start.12 = (bf16[96,2176]{1,0:T(8,128)(2,1)}, bf16[96,2176]{1,0:T(8,128)(2,1)S(1)}, u32[]{:S(2)}, u32[]{:S(2)}) collective-permute-start(bf16[96,2176]{1,0:T(8,128)(2,1)} %collective-permute-done.8.refs_1_), channel_id=1, source_target_pairs={{0,4},{1,5},{4,8},{5,9},{8,12},{9,13},{12,14},{13,15},{14,10},{15,... | collective-permute-start | bytes 1253384 | tf_op jit(solution)/shard_map/ppermute | solution.py:332
  54.6 11.9 %collective-permute-start.13 = (bf16[96,2176]{1,0:T(8,128)(2,1)}, bf16[96,2176]{1,0:T(8,128)(2,1)S(1)}, u32[]{:S(2)}, u32[]{:S(2)}) collective-permute-start(bf16[96,2176]{1,0:T(8,128)(2,1)} %collective-permute-done.9.refs_2_), channel_id=1, source_target_pairs={{4,0},{5,1},{8,4},{9,5},{12,8},{13,9},{14,12},{15,13},{10,14},{11,... | collective-permute-start | bytes 1253384 | tf_op jit(solution)/shard_map/ppermute | solution.py:332
  56.0 10.6 %collective-permute-start.16 = (bf16[512,2048]{1,0:T(8,128)(2,1)S(1)}, bf16[512,2048]{1,0:T(8,128)(2,1)S(1)}, u32[]{:S(2)}, u32[]{:S(2)}) collective-permute-start(bf16[512,2048]{1,0:T(8,128)(2,1)S(1)} %bitcast.55), channel_id=1, source_target_pairs={{0,1},{1,0},{2,3},{3,2},{4,5},{5,4},{6,7},{7,6},{8,9},{9,8},{10,11... | collective-permute-start | bytes 6291464 | tf_op jit(solution)/shard_map/ppermute | solution.py:440
  66.5 13.3 %copy-start.10 = (bf16[48,2048]{1,0:T(8,128)(2,1)}, bf16[48,2048]{1,0:T(8,128)(2,1)S(1)}, u32[]{:S(2)}) copy-start(bf16[48,2048]{1,0:T(8,128)(2,1)S(1)} %collective-permute-done.15.refs_1_) | copy-start | bytes 589828
  66.5 13.3 %copy-start.11 = (bf16[48,2048]{1,0:T(8,128)(2,1)}, bf16[48,2048]{1,0:T(8,128)(2,1)S(1)}, u32[]{:S(2)}) copy-start(bf16[48,2048]{1,0:T(8,128)(2,1)S(1)} %collective-permute-done.14.refs_0_) | copy-start | bytes 589828
  66.5 17.4 %collective-permute-start.20 = (bf16[96,2048]{1,0:T(8,128)(2,1)S(1)}, bf16[96,2048]{1,0:T(8,128)(2,1)S(1)}, u32[]{:S(2)}, u32[]{:S(2)}) collective-permute-start(bf16[96,2048]{1,0:T(8,128)(2,1)S(1)} %get-tuple-element.266.refs_3_), channel_id=1, source_target_pairs={{4,0},{5,1},{8,4},{9,5},{12,8},{13,9},{14,12},{15,13},{10,14},{11,... | collective-permute-start | bytes 1179656 | tf_op jit(solution)/shard_map/ppermute | solution.py:332
  68.2 15.8 %collective-permute-start.19 = (bf16[96,2048]{1,0:T(8,128)(2,1)S(1)}, bf16[96,2048]{1,0:T(8,128)(2,1)S(1)}, u32[]{:S(2)}, u32[]{:S(2)}) collective-permute-start(bf16[96,2048]{1,0:T(8,128)(2,1)S(1)} %get-tuple-element.266.refs_3_), channel_id=1, source_target_pairs={{0,4},{1,5},{4,8},{5,9},{8,12},{9,13},{12,14},{13,15},{14,10},{15,... | collective-permute-start | bytes 1179656 | tf_op jit(solution)/shard_map/ppermute | solution.py:332
  68.6 19.8 %collective-permute-start.17 = (bf16[96,2176]{1,0:T(8,128)(2,1)S(1)}, bf16[96,2176]{1,0:T(8,128)(2,1)S(1)}, u32[]{:S(2)}, u32[]{:S(2)}) collective-permute-start(bf16[96,2176]{1,0:T(8,128)(2,1)S(1)} %collective-permute-done.12.refs_3_.refs_0_), channel_id=1, source_target_pairs={{0,4},{1,5},{4,8},{5,9},{8,12},{9,13},{12,14},{13,15},{14,10},{15,... | collective-permute-start | bytes 1253384 | tf_op jit(solution)/shard_map/ppermute | solution.py:332
  69.3 19.1 %collective-permute-start.18 = (bf16[96,2176]{1,0:T(8,128)(2,1)S(1)}, bf16[96,2176]{1,0:T(8,128)(2,1)S(1)}, u32[]{:S(2)}, u32[]{:S(2)}) collective-permute-start(bf16[96,2176]{1,0:T(8,128)(2,1)S(1)} %collective-permute-done.13.refs_4_.refs_1_), channel_id=1, source_target_pairs={{4,0},{5,1},{8,4},{9,5},{12,8},{13,9},{14,12},{15,13},{10,14},{11,... | collective-permute-start | bytes 1253384 | tf_op jit(solution)/shard_map/ppermute | solution.py:332
  88.4 11.7 %collective-permute-start.22 = (bf16[48,2176]{1,0:T(8,128)(2,1)S(1)}, bf16[48,2176]{1,0:T(8,128)(2,1)S(1)}, u32[]{:S(2)}, u32[]{:S(2)}) collective-permute-start(bf16[48,2176]{1,0:T(8,128)(2,1)S(1)} %slice.69), channel_id=1, source_target_pairs={{4,0},{5,1},{8,4},{9,5},{12,8},{13,9},{14,12},{15,13},{10,14},{11,... | collective-permute-start | bytes 626696 | tf_op jit(solution)/shard_map/ppermute | solution.py:332
  90.0 10.0 %collective-permute-start.21 = (bf16[48,2176]{1,0:T(8,128)(2,1)S(1)}, bf16[48,2176]{1,0:T(8,128)(2,1)S(1)}, u32[]{:S(2)}, u32[]{:S(2)}) collective-permute-start(bf16[48,2176]{1,0:T(8,128)(2,1)S(1)} %slice.68), channel_id=1, source_target_pairs={{0,4},{1,5},{4,8},{5,9},{8,12},{9,13},{12,14},{13,15},{14,10},{15,... | collective-permute-start | bytes 626696 | tf_op jit(solution)/shard_map/ppermute | solution.py:332
  90.5 14.2 %collective-permute-start.23 = (bf16[96,2048]{1,0:T(8,128)(2,1)S(1)}, bf16[96,2048]{1,0:T(8,128)(2,1)S(1)}, u32[]{:S(2)}, u32[]{:S(2)}) collective-permute-start(bf16[96,2048]{1,0:T(8,128)(2,1)S(1)} %collective-permute-done.19.refs_4_), channel_id=1, source_target_pairs={{0,4},{1,5},{4,8},{5,9},{8,12},{9,13},{12,14},{13,15},{14,10},{15,... | collective-permute-start | bytes 1179656 | tf_op jit(solution)/shard_map/ppermute | solution.py:332
  90.9 13.7 %collective-permute-start.24 = (bf16[96,2048]{1,0:T(8,128)(2,1)S(1)}, bf16[96,2048]{1,0:T(8,128)(2,1)S(1)}, u32[]{:S(2)}, u32[]{:S(2)}) collective-permute-start(bf16[96,2048]{1,0:T(8,128)(2,1)S(1)} %collective-permute-done.20.refs_5_), channel_id=1, source_target_pairs={{4,0},{5,1},{8,4},{9,5},{12,8},{13,9},{14,12},{15,13},{10,14},{11,... | collective-permute-start | bytes 1179656 | tf_op jit(solution)/shard_map/ppermute | solution.py:332
  104.7 9.2 %collective-permute-start.25 = (bf16[96,2048]{1,0:T(8,128)(2,1)S(1)}, bf16[96,2048]{1,0:T(8,128)(2,1)S(1)}, u32[]{:S(2)}, u32[]{:S(2)}) collective-permute-start(bf16[96,2048]{1,0:T(8,128)(2,1)S(1)} %collective-permute-done.23.refs_2_), channel_id=1, source_target_pairs={{0,4},{1,5},{4,8},{5,9},{8,12},{9,13},{12,14},{13,15},{14,10},{15,... | collective-permute-start | bytes 1179656 | tf_op jit(solution)/shard_map/ppermute | solution.py:332
  105.1 9.0 %collective-permute-start.26 = (bf16[96,2048]{1,0:T(8,128)(2,1)S(1)}, bf16[96,2048]{1,0:T(8,128)(2,1)S(1)}, u32[]{:S(2)}, u32[]{:S(2)}) collective-permute-start(bf16[96,2048]{1,0:T(8,128)(2,1)S(1)} %collective-permute-done.24.refs_3_), channel_id=1, source_target_pairs={{4,0},{5,1},{8,4},{9,5},{12,8},{13,9},{14,12},{15,13},{10,14},{11,... | collective-permute-start | bytes 1179656 | tf_op jit(solution)/shard_map/ppermute | solution.py:332
  114.1 9.6 %collective-permute-start.28 = (bf16[48,2048]{1,0:T(8,128)(2,1)S(1)}, bf16[48,2048]{1,0:T(8,128)(2,1)S(1)}, u32[]{:S(2)}, u32[]{:S(2)}) collective-permute-start(bf16[48,2048]{1,0:T(8,128)(2,1)S(1)} %slice.71), channel_id=1, source_target_pairs={{4,0},{5,1},{8,4},{9,5},{12,8},{13,9},{14,12},{15,13},{10,14},{11,... | collective-permute-start | bytes 589832 | tf_op jit(solution)/shard_map/ppermute | solution.py:332
  116.0 7.7 %collective-permute-start.27 = (bf16[48,2048]{1,0:T(8,128)(2,1)S(1)}, bf16[48,2048]{1,0:T(8,128)(2,1)S(1)}, u32[]{:S(2)}, u32[]{:S(2)}) collective-permute-start(bf16[48,2048]{1,0:T(8,128)(2,1)S(1)} %slice.70), channel_id=1, source_target_pairs={{0,4},{1,5},{4,8},{5,9},{8,12},{9,13},{12,14},{13,15},{14,10},{15,... | collective-permute-start | bytes 589832 | tf_op jit(solution)/shard_map/ppermute | solution.py:332
  116.2 7.6 %collective-permute-start.29 = (bf16[48,2048]{1,0:T(8,128)(2,1)S(1)}, bf16[48,2048]{1,0:T(8,128)(2,1)S(1)}, u32[]{:S(2)}, u32[]{:S(2)}) collective-permute-start(bf16[48,2048]{1,0:T(8,128)(2,1)S(1)} %get-tuple-element.321), channel_id=1, source_target_pairs={{0,4},{1,5},{4,8},{5,9},{8,12},{9,13},{12,14},{13,15},{14,10},{15,... | collective-permute-start | bytes 589832 | tf_op jit(solution)/shard_map/ppermute | solution.py:332
  116.9 6.9 %collective-permute-start.30 = (bf16[48,2048]{1,0:T(8,128)(2,1)S(1)}, bf16[48,2048]{1,0:T(8,128)(2,1)S(1)}, u32[]{:S(2)}, u32[]{:S(2)}) collective-permute-start(bf16[48,2048]{1,0:T(8,128)(2,1)S(1)} %get-tuple-element.322), channel_id=1, source_target_pairs={{4,0},{5,1},{8,4},{9,5},{12,8},{13,9},{14,12},{15,13},{10,14},{11,... | collective-permute-start | bytes 589832 | tf_op jit(solution)/shard_map/ppermute | solution.py:332
  124.0 9.5 %collective-permute-start.32 = (bf16[96,2048]{1,0:T(8,128)(2,1)S(1)}, bf16[96,2048]{1,0:T(8,128)(2,1)S(1)}, u32[]{:S(2)}, u32[]{:S(2)}) collective-permute-start(bf16[96,2048]{1,0:T(8,128)(2,1)S(1)} %pad_maximum_fusion.1), channel_id=1, source_target_pairs={{4,0},{5,1},{8,4},{9,5},{12,8},{13,9},{14,12},{15,13},{10,14},{11,... | collective-permute-start | bytes 1179656 | tf_op jit(solution)/shard_map/ppermute | solution.py:332
  125.8 8.8 %collective-permute-start.31 = (bf16[96,2048]{1,0:T(8,128)(2,1)S(1)}, bf16[96,2048]{1,0:T(8,128)(2,1)S(1)}, u32[]{:S(2)}, u32[]{:S(2)}) collective-permute-start(bf16[96,2048]{1,0:T(8,128)(2,1)S(1)} %pad_maximum_fusion), channel_id=1, source_target_pairs={{0,4},{1,5},{4,8},{5,9},{8,12},{9,13},{12,14},{13,15},{14,10},{15,... | collective-permute-start | bytes 1179656 | tf_op jit(solution)/shard_map/ppermute | solution.py:332
  134.7 13.7 %collective-permute-start.34 = (bf16[96,2048]{1,0:T(8,128)(2,1)S(1)}, bf16[96,2048]{1,0:T(8,128)(2,1)S(1)}, u32[]{:S(2)}, u32[]{:S(2)}) collective-permute-start(bf16[96,2048]{1,0:T(8,128)(2,1)S(1)} %add_convert_fusion.6), channel_id=1, source_target_pairs={{4,0},{5,1},{8,4},{9,5},{12,8},{13,9},{14,12},{15,13},{10,14},{11,... | collective-permute-start | bytes 1179656 | tf_op jit(solution)/shard_map/ppermute | solution.py:332
  136.3 12.1 %collective-permute-start.33 = (bf16[96,2048]{1,0:T(8,128)(2,1)S(1)}, bf16[96,2048]{1,0:T(8,128)(2,1)S(1)}, u32[]{:S(2)}, u32[]{:S(2)}) collective-permute-start(bf16[96,2048]{1,0:T(8,128)(2,1)S(1)} %add_convert_fusion.7), channel_id=1, source_target_pairs={{0,4},{1,5},{4,8},{5,9},{8,12},{9,13},{12,14},{13,15},{14,10},{15,... | collective-permute-start | bytes 1179656 | tf_op jit(solution)/shard_map/ppermute | solution.py:332
  137.0 11.4 %collective-permute-start.35 = (bf16[48,2048]{1,0:T(8,128)(2,1)S(1)}, bf16[48,2048]{1,0:T(8,128)(2,1)S(1)}, u32[]{:S(2)}, u32[]{:S(2)}) collective-permute-start(bf16[48,2048]{1,0:T(8,128)(2,1)S(1)} %get-tuple-element.363), channel_id=1, source_target_pairs={{0,4},{1,5},{4,8},{5,9},{8,12},{9,13},{12,14},{13,15},{14,10},{15,... | collective-permute-start | bytes 589832 | tf_op jit(solution)/shard_map/ppermute | solution.py:332
  137.0 11.4 %collective-permute-start.36 = (bf16[48,2048]{1,0:T(8,128)(2,1)S(1)}, bf16[48,2048]{1,0:T(8,128)(2,1)S(1)}, u32[]{:S(2)}, u32[]{:S(2)}) collective-permute-start(bf16[48,2048]{1,0:T(8,128)(2,1)S(1)} %get-tuple-element.364), channel_id=1, source_target_pairs={{4,0},{5,1},{8,4},{9,5},{12,8},{13,9},{14,12},{15,13},{10,14},{11,... | collective-permute-start | bytes 589832 | tf_op jit(solution)/shard_map/ppermute | solution.py:332
  148.7 8.6 %collective-permute-start.38 = (bf16[96,2048]{1,0:T(8,128)(2,1)S(1)}, bf16[96,2048]{1,0:T(8,128)(2,1)S(1)}, u32[]{:S(2)}, u32[]{:S(2)}) collective-permute-start(bf16[96,2048]{1,0:T(8,128)(2,1)S(1)} %add_convert_fusion.4), channel_id=1, source_target_pairs={{4,0},{5,1},{8,4},{9,5},{12,8},{13,9},{14,12},{15,13},{10,14},{11,... | collective-permute-start | bytes 1179656 | tf_op jit(solution)/shard_map/ppermute | solution.py:332
  150.4 8.7 %collective-permute-start.37 = (bf16[96,2048]{1,0:T(8,128)(2,1)S(1)}, bf16[96,2048]{1,0:T(8,128)(2,1)S(1)}, u32[]{:S(2)}, u32[]{:S(2)}) collective-permute-start(bf16[96,2048]{1,0:T(8,128)(2,1)S(1)} %add_convert_fusion.5), channel_id=1, source_target_pairs={{0,4},{1,5},{4,8},{5,9},{8,12},{9,13},{12,14},{13,15},{14,10},{15,... | collective-permute-start | bytes 1179656 | tf_op jit(solution)/shard_map/ppermute | solution.py:332
  150.9 13.4 %collective-permute-start.40 = (bf16[96,2048]{1,0:T(8,128)(2,1)S(1)}, bf16[96,2048]{1,0:T(8,128)(2,1)S(1)}, u32[]{:S(2)}, u32[]{:S(2)}) collective-permute-start(bf16[96,2048]{1,0:T(8,128)(2,1)S(1)} %pad_maximum_fusion.3), channel_id=1, source_target_pairs={{4,0},{5,1},{8,4},{9,5},{12,8},{13,9},{14,12},{15,13},{10,14},{11,... | collective-permute-start | bytes 1179656 | tf_op jit(solution)/shard_map/ppermute | solution.py:332
  152.6 13.4 %collective-permute-start.39 = (bf16[96,2048]{1,0:T(8,128)(2,1)S(1)}, bf16[96,2048]{1,0:T(8,128)(2,1)S(1)}, u32[]{:S(2)}, u32[]{:S(2)}) collective-permute-start(bf16[96,2048]{1,0:T(8,128)(2,1)S(1)} %pad_maximum_fusion.2), channel_id=1, source_target_pairs={{0,4},{1,5},{4,8},{5,9},{8,12},{9,13},{12,14},{13,15},{14,10},{15,... | collective-permute-start | bytes 1179656 | tf_op jit(solution)/shard_map/ppermute | solution.py:332
  166.1 11.7 %collective-permute-start.42 = (bf16[96,2048]{1,0:T(8,128)(2,1)S(1)}, bf16[96,2048]{1,0:T(8,128)(2,1)S(1)}, u32[]{:S(2)}, u32[]{:S(2)}) collective-permute-start(bf16[96,2048]{1,0:T(8,128)(2,1)S(1)} %add_convert_fusion.2), channel_id=1, source_target_pairs={{4,0},{5,1},{8,4},{9,5},{12,8},{13,9},{14,12},{15,13},{10,14},{11,... | collective-permute-start | bytes 1179656 | tf_op jit(solution)/shard_map/ppermute | solution.py:332
  168.1 11.8 %collective-permute-start.41 = (bf16[96,2048]{1,0:T(8,128)(2,1)S(1)}, bf16[96,2048]{1,0:T(8,128)(2,1)S(1)}, u32[]{:S(2)}, u32[]{:S(2)}) collective-permute-start(bf16[96,2048]{1,0:T(8,128)(2,1)S(1)} %add_convert_fusion.3), channel_id=1, source_target_pairs={{0,4},{1,5},{4,8},{5,9},{8,12},{9,13},{12,14},{13,15},{14,10},{15,... | collective-permute-start | bytes 1179656 | tf_op jit(solution)/shard_map/ppermute | solution.py:332
  180.0 7.8 %collective-permute-start.44 = (bf16[96,2048]{1,0:T(8,128)(2,1)S(1)}, bf16[96,2048]{1,0:T(8,128)(2,1)S(1)}, u32[]{:S(2)}, u32[]{:S(2)}) collective-permute-start(bf16[96,2048]{1,0:T(8,128)(2,1)S(1)} %add_convert_fusion), channel_id=1, source_target_pairs={{4,0},{5,1},{8,4},{9,5},{12,8},{13,9},{14,12},{15,13},{10,14},{11,... | collective-permute-start | bytes 1179656 | tf_op jit(solution)/shard_map/ppermute | solution.py:332
  181.3 7.8 %collective-permute-start.43 = (bf16[96,2048]{1,0:T(8,128)(2,1)S(1)}, bf16[96,2048]{1,0:T(8,128)(2,1)S(1)}, u32[]{:S(2)}, u32[]{:S(2)}) collective-permute-start(bf16[96,2048]{1,0:T(8,128)(2,1)S(1)} %add_convert_fusion.1), channel_id=1, source_target_pairs={{0,4},{1,5},{4,8},{5,9},{8,12},{9,13},{12,14},{13,15},{14,10},{15,... | collective-permute-start | bytes 1179656 | tf_op jit(solution)/shard_map/ppermute | solution.py:332

commit v11 on v10

--- a/solution.py
+++ b/solution.py
@@ -465,20 +465,20 @@
         return kept + norm_pullback(fall_wide, norm_row, ring.total("backward"))
 
     if planned:
-        first_hop, leaving_rise = lax.optimization_barrier((ring.held["fall"][1], leaving_rise))
-        ring.held["fall"][1] = first_hop
         ring.gather("fall", 2)
-        moved_rise = passed_along(leaving_rise, "pipe", 1)
         own_gate, own_up, own_down = own
         other_gate, other_up = swapped(own_gate), swapped(own_up)
+        packed, leaving_rise = lax.optimization_barrier((ring.held["cot"][0][0], leaving_rise))
+        ring.held["cot"][0] = [packed]
+        moved_rise = passed_along(leaving_rise, "pipe", 1)
         heads = (head_rise, head_fall)
-        cot_in, moved_rise, own, own_down, other_gate, other_up, heads, ring.names = ring.fence(
-            cot_in, moved_rise, own, own_down, other_gate, other_up, heads, names
+        cot_in, own, own_down, other_gate, other_up, heads, ring.names = ring.fence(
+            cot_in, own, own_down, other_gate, other_up, heads, names
         )
         ring.gather("fall", 3)
         ring.gather("cot", 1)
         own = fetched(own)
-        moved_rise, cot_in, own, own_down = ring.fence(moved_rise, cot_in, own, own_down)
+        moved_rise, own, own_down = ring.fence(moved_rise, own, own_down)
         ring.gather("fall", 4)
         ring.gather("cot", 2)
         ring.weights = own + (other_gate, other_up, None)

time: 191 us -> 187 us (0.979)
  waiting for transfers between devices: 71 us -> 66.9 us
    ppermute x2, waiting for transfers between devices: 3.84 us -> 0.97 us  [passed_along(): return lax.ppermute(block, axis, route)]
where the time goes in v11:
time: 187 us
  waiting for transfers between devices  66.9 us (36%)
  Pallas kernels  54.2 us (29%)
  starting transfers between devices  51.3 us (27%)
  other arithmetic  6.77 us (4%)
  local copies, waits for them, and re-layouts  5.03 us (3%)
  between operations  2.43 us (1%)
    ppermute x40, waiting for transfers between devices, pass_on(): return lax.ppermute(block, 'ep', self.routes[way])  65.9 us
    ppermute x40, starting transfers between devices, pass_on(): return lax.ppermute(block, 'ep', self.routes[way])  42.8 us
    pallas_call x3, Pallas kernels, forward_call(): pl.pallas_call(functools.partial(forward_kernel, parts, experts, width, T...  20.1 us
    pallas_call x2, Pallas kernels, backward_call(): pl.pallas_call(functools.partial(backward_kernel, parts, experts, width,...  15.5 us
    pallas_call x2, Pallas kernels, factor_call(): pl.pallas_call(functools.partial(factor_kernel, parts), out_shape=jax.Sha...  13.6 us
    ppermute x2, starting transfers between devices, passed_along(): return lax.ppermute(block, axis, route)  7.94 us
  transfers between devices with their start and end apart: 45, of which 21 were waited for; matrix products, arithmetic and copies ran while one was open for 4% of the time, Pallas kernels for 29%

profile of v11, /device:TPU:0, one launch (start us, length us, event | category | flops | bytes accessed | tf_op | source)
XLA Modules:
  0.0 186.6 jit_solution(6699174041581942868)
XLA Ops:
  1.2 1.2 shard_map.148.refs_0_
  2.4 3.0 %collective-permute-start.2 = (bf16[96,2048]{1,0:T(8,128)(2,1)S(1)}, bf16[96,2048]{1,0:T(8,128)(2,1)}, u32[]{:S(2)}, u32[]{:S(2)}) collective-permute-start(bf16[96,2048]{1,0:T(8,128)(2,1)S(1)} %shard_map.148.refs_0_), channel_id=1, source_target_pairs={{4,0},{5,1},{8,4},{9,5},{12,8},{13,9},{14,12},{15,13},{10,14},{11,... | collective-permute-start | bytes 1179656 | tf_op jit(solution)/shard_map/ppermute | solution.py:332
  5.5 3.8 %collective-permute-start = (bf16[96,2048]{1,0:T(8,128)(2,1)}, bf16[96,2048]{1,0:T(8,128)(2,1)S(1)}, u32[]{:S(2)}, u32[]{:S(2)}) collective-permute-start(bf16[96,2048]{1,0:T(8,128)(2,1)} %bitcast.63), channel_id=1, source_target_pairs={{0,16},{1,17},{2,18},{3,19},{4,20},{5,21},{6,22},{7,23},{8,24},{9,... | collective-permute-start | bytes 1179656 | tf_op jit(solution)/shard_map/ppermute | solution.py:17
  9.4 0.8 fusion.19
  10.1 0.6 constant_dynamic-slice_fusion
  11.9 0.8 copy.16
  12.7 0.8 copy.17
  13.7 1.3 collective-permute-done.2.refs_2_
  14.9 1.7 collective-permute-start.4
  17.0 0.7 collective-permute-done
  17.7 1.1 bitcast_select_fusion.rows_ref
  18.7 0.7 shard_map.149.refs_0_
  19.5 6.3 %collective-permute-done.4.refs_4_ = bf16[96,2048]{1,0:T(8,128)(2,1)} collective-permute-done((bf16[96,2048]{1,0:T(8,128)(2,1)}, bf16[96,2048]{1,0:T(8,128)(2,1)}, u32[]{:S(2)}, u32[]{:S(2)}) %collective-permute-start.4) | collective-permute-done | bytes 393248 | tf_op jit(solution)/shard_map/ppermute | solution.py:332
  25.8 1.1 collective-permute-done.3.refs_3_
  26.9 1.6 collective-permute-start.8
  29.0 4.1 %collective-permute-start.11 = (bf16[96,2048]{1,0:T(8,128)(2,1)}, bf16[96,2048]{1,0:T(8,128)(2,1)}, u32[]{:S(2)}, u32[]{:S(2)}) collective-permute-start(bf16[96,2048]{1,0:T(8,128)(2,1)} %bitcast.4), channel_id=1, source_target_pairs={{0,16},{1,17},{2,18},{3,19},{4,20},{5,21},{6,22},{7,23},{8,24},{9,... | collective-permute-start | bytes 1179656 | tf_op jit(solution)/shard_map/ppermute | solution.py:17
  33.6 1.5 collective-permute-start.10
  35.4 3.0 %shard_map.150 = (bf16[2048,512]{1,0:T(8,128)(2,1)S(1)}, bf16[2048,512]{1,0:T(8,128)(2,1)S(1)}, bf16[512,2048]{1,0:T(8,128)(2,1)S(1)}) custom-call(bf16[2048,512]{1,0:T(8,128)(2,1)} %bitcast.51, bf16[2048,512]{1,0:T(8,128)(2,1)} %bitcast.53, bf16[512,2048]{1,0:T(8,128)(2,1)} %bitcast.54), custom_call_target="tpu_custom_call" | custom-call | bytes 8388608 | tf_op jit(solution)/shard_map/pallas_call | solution.py:220
  38.7 7.7 %collective-permute-done.9.refs_5_ = bf16[96,2048]{1,0:T(8,128)(2,1)} collective-permute-done((bf16[96,2048]{1,0:T(8,128)(2,1)}, bf16[96,2048]{1,0:T(8,128)(2,1)}, u32[]{:S(2)}, u32[]{:S(2)}) %collective-permute-start.9) | collective-permute-done | bytes 393248 | tf_op jit(solution)/shard_map/ppermute | solution.py:332
  46.6 1.0 slice.64
  47.6 0.9 slice.65
  48.5 1.6 collective-permute-start.15
  50.6 0.6 multiply_reduce_fusion
  51.8 1.6 collective-permute-start.13
  53.8 9.5 %shard_map.151.refs_5_.refs_4_ = bf16[4,672,512]{2,1,0:T(8,128)(2,1)S(1)} custom-call(bf16[96,2048]{1,0:T(8,128)(2,1)} %copy-done, bf16[96,2048]{1,0:T(8,128)(2,1)} %collective-permute-done.1.refs_1_, bf16[96,2048]{1,0:T(8,128)(2,1)} %collective-permute-done.2.refs_2_, bf16[96,2048]{1,0:T(8,128)(2,1)} %collective-permute-done.3.refs_3_, ...), custom_call_target="tpu_custom_call" | custom-call | flops 11137144832 | bytes 12582912 | tf_op jit(solution)/shard_map/pallas_call | solution.py:270
  63.3 0.6 maximum_bitcast_fusion
  63.9 1.6 collective-permute-start.20
  66.5 1.6 collective-permute-start.18
  68.1 9.1 %shard_map.153 = (bf16[96,2048]{1,0:T(8,128)(2,1)S(1)}, bf16[96,2048]{1,0:T(8,128)(2,1)S(1)}, bf16[96,2048]{1,0:T(8,128)(2,1)S(1)}, bf16[96,2048]{1,0:T(8,128)(2,1)S(1)}, bf16[96,2048]{1,0:T(8,128)(2,1)S(1)}) custom-call(s32[2]{0:T(128)S(1)} %pad_add_fusion.names_ref, bf16[96,2176]{1,0:T(8,128)(2,1)S(1)} %shard_map.149.refs_0_, ...), custom_call_target="tpu_custom_call" | custom-call | flops 12639797248 | bytes 12582912 | tf_op jit(solution)/shard_map/pallas_call | solution.py:288
  77.2 4.1 %shard_map.152.refs_5_ = bf16[4,96,512]{2,1,0:T(8,128)(2,1)S(1)} custom-call(bf16[48,2048]{1,0:T(8,128)(2,1)} %copy-done.9, bf16[48,2048]{1,0:T(8,128)(2,1)} %copy-done.8, bf16[2048,512]{1,0:T(8,128)(2,1)S(1)} %get-tuple-element.226.refs_7_.refs_2_.refs_6_.refs_4_.refs_8_, bf16[2048,512]{1,0:T(8,128)(2,1)S(1)} %get-tuple-element.227.refs_8_.refs_3_.refs_7_.refs_5_.refs_9_, ...), custom_call_target="tpu_custom_call" | custom-call | flops 6305306624 | bytes 12582912 | tf_op jit(solution)/shard_map/pallas_call | solution.py:270
  81.4 4.4 %collective-permute-done.17.refs_0_ = bf16[96,2176]{1,0:T(8,128)(2,1)S(1)} collective-permute-done((bf16[96,2176]{1,0:T(8,128)(2,1)S(1)}, bf16[96,2176]{1,0:T(8,128)(2,1)S(1)}, u32[]{:S(2)}, u32[]{:S(2)}) %collective-permute-start.17) | collective-permute-done | bytes 417824 | tf_op jit(solution)/shard_map/ppermute | solution.py:332
  85.8 1.6 collective-permute-start.22
  88.3 1.6 collective-permute-start.24
  89.9 7.5 %shard_map.154 = (bf16[96,2048]{1,0:T(8,128)(2,1)S(1)}, bf16[96,2048]{1,0:T(8,128)(2,1)S(1)}, bf16[96,2048]{1,0:T(8,128)(2,1)S(1)}) custom-call(s32[2]{0:T(128)S(1)} %pad_add_fusion.names_ref, bf16[96,2176]{1,0:T(8,128)(2,1)S(1)} %shard_map.149.refs_0_, bf16[96,2176]{1,0:T(8,128)(2,1)} %collective-permute-done.7.refs_1_, ...), custom_call_target="tpu_custom_call" | custom-call | flops 10223878144 | bytes 12582912 | tf_op jit(solution)/shard_map/pallas_call | solution.py:250
  97.5 4.6 %collective-permute-done.23.refs_2_ = bf16[96,2048]{1,0:T(8,128)(2,1)S(1)} collective-permute-done((bf16[96,2048]{1,0:T(8,128)(2,1)S(1)}, bf16[96,2048]{1,0:T(8,128)(2,1)S(1)}, u32[]{:S(2)}, u32[]{:S(2)}) %collective-permute-start.23) | collective-permute-done | bytes 393248 | tf_op jit(solution)/shard_map/ppermute | solution.py:332
  102.5 1.6 collective-permute-start.26
  104.1 6.4 %shard_map.155 = (bf16[96,2048]{1,0:T(8,128)(2,1)S(1)}, bf16[96,2048]{1,0:T(8,128)(2,1)S(1)}, bf16[48,2048]{1,0:T(8,128)(2,1)S(1)}, bf16[48,2048]{1,0:T(8,128)(2,1)S(1)}) custom-call(s32[2]{0:T(128)S(1)} %pad_add_fusion.names_ref, bf16[96,2176]{1,0:T(8,128)(2,1)S(1)} %collective-permute-done.17.refs_0_, ...), custom_call_target="tpu_custom_call" | custom-call | flops 10223878144 | bytes 12582912 | tf_op jit(solution)/shard_map/pallas_call | solution.py:288
  110.5 0.8 collective-permute-done.25.refs_4_
  111.5 1.9 %collective-permute-start.28 = (bf16[48,2048]{1,0:T(8,128)(2,1)S(1)}, bf16[48,2048]{1,0:T(8,128)(2,1)S(1)}, u32[]{:S(2)}, u32[]{:S(2)}) collective-permute-start(bf16[48,2048]{1,0:T(8,128)(2,1)S(1)} %slice.71), channel_id=1, source_target_pairs={{4,0},{5,1},{8,4},{9,5},{12,8},{13,9},{14,12},{15,13},{10,14},{11,... | collective-permute-start | bytes 589832 | tf_op jit(solution)/shard_map/ppermute | solution.py:332
  113.5 0.6 collective-permute-start.29
  114.1 1.4 collective-permute-start.30
  115.6 5.4 %shard_map.156 = (bf16[96,2048]{1,0:T(8,128)(2,1)S(1)}, bf16[96,2048]{1,0:T(8,128)(2,1)S(1)}) custom-call(s32[2]{0:T(128)S(1)} %pad_add_fusion.names_ref, bf16[96,2176]{1,0:T(8,128)(2,1)S(1)} %collective-permute-done.12.refs_3_.refs_0_, bf16[96,2176]{1,0:T(8,128)(2,1)S(1)} %collective-permute-done.13.refs_4_.refs_1_, ...), custom_call_target="tpu_custom_call" | custom-call | flops 9015918592 | bytes 12582912 | tf_op jit(solution)/shard_map/pallas_call | solution.py:250
  121.4 1.8 collective-permute-start.32
  123.7 7.2 %shard_map.157 = (bf16[96,2048]{1,0:T(8,128)(2,1)S(1)}, bf16[96,2048]{1,0:T(8,128)(2,1)S(1)}, bf16[48,2048]{1,0:T(8,128)(2,1)S(1)}, bf16[48,2048]{1,0:T(8,128)(2,1)S(1)}) custom-call(s32[2]{0:T(128)S(1)} %pad_add_fusion.names_ref, bf16[96,2176]{1,0:T(8,128)(2,1)S(1)} %collective-permute-done.17.refs_0_, ...), custom_call_target="tpu_custom_call" | custom-call | flops 10223878144 | bytes 12582912 | tf_op jit(solution)/shard_map/pallas_call | solution.py:250
  130.9 1.1 collective-permute-done.31
  132.1 2.0 %collective-permute-start.34 = (bf16[96,2048]{1,0:T(8,128)(2,1)S(1)}, bf16[96,2048]{1,0:T(8,128)(2,1)S(1)}, u32[]{:S(2)}, u32[]{:S(2)}) collective-permute-start(bf16[96,2048]{1,0:T(8,128)(2,1)S(1)} %add_convert_fusion.6), channel_id=1, source_target_pairs={{4,0},{5,1},{8,4},{9,5},{12,8},{13,9},{14,12},{15,13},{10,14},{11,... | collective-permute-start | bytes 1179656 | tf_op jit(solution)/shard_map/ppermute | solution.py:332
  134.4 2.0 %collective-permute-start.36 = (bf16[48,2048]{1,0:T(8,128)(2,1)S(1)}, bf16[48,2048]{1,0:T(8,128)(2,1)S(1)}, u32[]{:S(2)}, u32[]{:S(2)}) collective-permute-start(bf16[48,2048]{1,0:T(8,128)(2,1)S(1)} %get-tuple-element.358), channel_id=1, source_target_pairs={{4,0},{5,1},{8,4},{9,5},{12,8},{13,9},{14,12},{15,13},{10,14},{11,... | collective-permute-start | bytes 589832 | tf_op jit(solution)/shard_map/ppermute | solution.py:332
  136.4 9.3 %collective-permute-done.35 = bf16[48,2048]{1,0:T(8,128)(2,1)S(1)} collective-permute-done((bf16[48,2048]{1,0:T(8,128)(2,1)S(1)}, bf16[48,2048]{1,0:T(8,128)(2,1)S(1)}, u32[]{:S(2)}, u32[]{:S(2)}) %collective-permute-start.35) | collective-permute-done | bytes 196640 | tf_op jit(solution)/shard_map/ppermute | solution.py:332
  146.0 1.5 collective-permute-start.38
  147.5 0.7 collective-permute-start.37
  148.2 1.5 collective-permute-start.40
  149.7 0.7 collective-permute-start.39
  150.4 4.3 %collective-permute-done.38 = bf16[96,2048]{1,0:T(8,128)(2,1)S(1)} collective-permute-done((bf16[96,2048]{1,0:T(8,128)(2,1)S(1)}, bf16[96,2048]{1,0:T(8,128)(2,1)S(1)}, u32[]{:S(2)}, u32[]{:S(2)}) %collective-permute-start.38) | collective-permute-done | bytes 393248 | tf_op jit(solution)/shard_map/ppermute | solution.py:332
  154.7 2.1 %collective-permute-done.37 = bf16[96,2048]{1,0:T(8,128)(2,1)S(1)} collective-permute-done((bf16[96,2048]{1,0:T(8,128)(2,1)S(1)}, bf16[96,2048]{1,0:T(8,128)(2,1)S(1)}, u32[]{:S(2)}, u32[]{:S(2)}) %collective-permute-start.37) | collective-permute-done | bytes 393248 | tf_op jit(solution)/shard_map/ppermute | solution.py:332
  156.8 4.2 %collective-permute-done.40 = bf16[96,2048]{1,0:T(8,128)(2,1)S(1)} collective-permute-done((bf16[96,2048]{1,0:T(8,128)(2,1)S(1)}, bf16[96,2048]{1,0:T(8,128)(2,1)S(1)}, u32[]{:S(2)}, u32[]{:S(2)}) %collective-permute-start.40) | collective-permute-done | bytes 393248 | tf_op jit(solution)/shard_map/ppermute | solution.py:332
  161.0 2.6 %collective-permute-done.39 = bf16[96,2048]{1,0:T(8,128)(2,1)S(1)} collective-permute-done((bf16[96,2048]{1,0:T(8,128)(2,1)S(1)}, bf16[96,2048]{1,0:T(8,128)(2,1)S(1)}, u32[]{:S(2)}, u32[]{:S(2)}) %collective-permute-start.39) | collective-permute-done | bytes 393248 | tf_op jit(solution)/shard_map/ppermute | solution.py:332
  163.8 1.6 collective-permute-start.42
  166.4 1.1 fusion.11
  167.5 8.0 %collective-permute-done.42 = bf16[96,2048]{1,0:T(8,128)(2,1)S(1)} collective-permute-done((bf16[96,2048]{1,0:T(8,128)(2,1)S(1)}, bf16[96,2048]{1,0:T(8,128)(2,1)S(1)}, u32[]{:S(2)}, u32[]{:S(2)}) %collective-permute-start.42) | collective-permute-done | bytes 393248 | tf_op jit(solution)/shard_map/ppermute | solution.py:332
  175.5 1.6 collective-permute-done.41
  177.8 1.6 collective-permute-start.43
  179.4 5.6 %collective-permute-done.44 = bf16[96,2048]{1,0:T(8,128)(2,1)S(1)} collective-permute-done((bf16[96,2048]{1,0:T(8,128)(2,1)S(1)}, bf16[96,2048]{1,0:T(8,128)(2,1)S(1)}, u32[]{:S(2)}, u32[]{:S(2)}) %collective-permute-start.44) | collective-permute-done | bytes 393248 | tf_op jit(solution)/shard_map/ppermute | solution.py:332
  185.0 0.6 collective-permute-done.43
  185.6 1.0 fusion.17
  (102 shorter events, 10.2 us)
Async XLA Ops:
  0.6 26.3 %collective-permute-start.5 = (bf16[2048,512]{1,0:T(8,128)(2,1)}, bf16[2048,512]{1,0:T(8,128)(2,1)S(1)}, u32[]{:S(2)}, u32[]{:S(2)}) collective-permute-start(bf16[2048,512]{1,0:T(8,128)(2,1)} %bitcast.50), channel_id=1, source_target_pairs={{0,1},{1,0},{2,3},{3,2},{4,5},{5,4},{6,7},{7,6},{8,9},{9,8},{10,11... | collective-permute-start | bytes 6291464 | tf_op jit(solution)/shard_map/ppermute | solution.py:440
  1.1 25.8 %collective-permute-start.6 = (bf16[2048,512]{1,0:T(8,128)(2,1)}, bf16[2048,512]{1,0:T(8,128)(2,1)}, u32[]{:S(2)}, u32[]{:S(2)}) collective-permute-start(bf16[2048,512]{1,0:T(8,128)(2,1)} %bitcast.52), channel_id=1, source_target_pairs={{0,1},{1,0},{2,3},{3,2},{4,5},{5,4},{6,7},{7,6},{8,9},{9,8},{10,11... | collective-permute-start | bytes 6291464 | tf_op jit(solution)/shard_map/ppermute | solution.py:440
  2.4 36.0 %copy-start = (bf16[96,2048]{1,0:T(8,128)(2,1)}, bf16[96,2048]{1,0:T(8,128)(2,1)S(1)}, u32[]{:S(2)}) copy-start(bf16[96,2048]{1,0:T(8,128)(2,1)S(1)} %shard_map.148.refs_0_) | copy-start | bytes 1179652
  2.4 12.5 %collective-permute-start.2 = (bf16[96,2048]{1,0:T(8,128)(2,1)S(1)}, bf16[96,2048]{1,0:T(8,128)(2,1)}, u32[]{:S(2)}, u32[]{:S(2)}) collective-permute-start(bf16[96,2048]{1,0:T(8,128)(2,1)S(1)} %shard_map.148.refs_0_), channel_id=1, source_target_pairs={{4,0},{5,1},{8,4},{9,5},{12,8},{13,9},{14,12},{15,13},{10,14},{11,... | collective-permute-start | bytes 1179656 | tf_op jit(solution)/shard_map/ppermute | solution.py:332
  5.4 11.2 %collective-permute-start.1 = (bf16[96,2048]{1,0:T(8,128)(2,1)S(1)}, bf16[96,2048]{1,0:T(8,128)(2,1)}, u32[]{:S(2)}, u32[]{:S(2)}) collective-permute-start(bf16[96,2048]{1,0:T(8,128)(2,1)S(1)} %shard_map.148.refs_0_), channel_id=1, source_target_pairs={{0,4},{1,5},{4,8},{5,9},{8,12},{9,13},{12,14},{13,15},{14,10},{15,... | collective-permute-start | bytes 1179656 | tf_op jit(solution)/shard_map/ppermute | solution.py:332
  5.5 12.1 %collective-permute-start = (bf16[96,2048]{1,0:T(8,128)(2,1)}, bf16[96,2048]{1,0:T(8,128)(2,1)S(1)}, u32[]{:S(2)}, u32[]{:S(2)}) collective-permute-start(bf16[96,2048]{1,0:T(8,128)(2,1)} %bitcast.63), channel_id=1, source_target_pairs={{0,16},{1,17},{2,18},{3,19},{4,20},{5,21},{6,22},{7,23},{8,24},{9,... | collective-permute-start | bytes 1179656 | tf_op jit(solution)/shard_map/ppermute | solution.py:17
  13.6 21.6 %copy-start.1 = (bf16[1,96,2048]{2,1,0:T(8,128)(2,1)S(1)}, bf16[1,96,2048]{2,1,0:T(8,128)(2,1)}, u32[]{:S(2)}) copy-start(bf16[1,96,2048]{2,1,0:T(8,128)(2,1)} %param.16) | copy-start | bytes 1179652
  14.9 10.9 %collective-permute-start.4 = (bf16[96,2048]{1,0:T(8,128)(2,1)}, bf16[96,2048]{1,0:T(8,128)(2,1)}, u32[]{:S(2)}, u32[]{:S(2)}) collective-permute-start(bf16[96,2048]{1,0:T(8,128)(2,1)} %collective-permute-done.2.refs_2_), channel_id=1, source_target_pairs={{4,0},{5,1},{8,4},{9,5},{12,8},{13,9},{14,12},{15,13},{10,14},{11,... | collective-permute-start | bytes 1179656 | tf_op jit(solution)/shard_map/ppermute | solution.py:332
  16.6 10.3 %collective-permute-start.3 = (bf16[96,2048]{1,0:T(8,128)(2,1)}, bf16[96,2048]{1,0:T(8,128)(2,1)}, u32[]{:S(2)}, u32[]{:S(2)}) collective-permute-start(bf16[96,2048]{1,0:T(8,128)(2,1)} %collective-permute-done.1.refs_1_), channel_id=1, source_target_pairs={{0,4},{1,5},{4,8},{5,9},{8,12},{9,13},{12,14},{13,15},{14,10},{15,... | collective-permute-start | bytes 1179656 | tf_op jit(solution)/shard_map/ppermute | solution.py:332
  26.9 19.4 %collective-permute-start.8 = (bf16[96,2176]{1,0:T(8,128)(2,1)S(1)}, bf16[96,2176]{1,0:T(8,128)(2,1)}, u32[]{:S(2)}, u32[]{:S(2)}) collective-permute-start(bf16[96,2176]{1,0:T(8,128)(2,1)S(1)} %shard_map.149.refs_0_), channel_id=1, source_target_pairs={{4,0},{5,1},{8,4},{9,5},{12,8},{13,9},{14,12},{15,13},{10,14},{11,... | collective-permute-start | bytes 1253384 | tf_op jit(solution)/shard_map/ppermute | solution.py:332
  28.5 17.8 %collective-permute-start.7 = (bf16[96,2176]{1,0:T(8,128)(2,1)S(1)}, bf16[96,2176]{1,0:T(8,128)(2,1)}, u32[]{:S(2)}, u32[]{:S(2)}) collective-permute-start(bf16[96,2176]{1,0:T(8,128)(2,1)S(1)} %shard_map.149.refs_0_), channel_id=1, source_target_pairs={{0,4},{1,5},{4,8},{5,9},{8,12},{9,13},{12,14},{13,15},{14,10},{15,... | collective-permute-start | bytes 1253384 | tf_op jit(solution)/shard_map/ppermute | solution.py:332
  29.0 9.7 %collective-permute-start.11 = (bf16[96,2048]{1,0:T(8,128)(2,1)}, bf16[96,2048]{1,0:T(8,128)(2,1)}, u32[]{:S(2)}, u32[]{:S(2)}) collective-permute-start(bf16[96,2048]{1,0:T(8,128)(2,1)} %bitcast.4), channel_id=1, source_target_pairs={{0,16},{1,17},{2,18},{3,19},{4,20},{5,21},{6,22},{7,23},{8,24},{9,... | collective-permute-start | bytes 1179656 | tf_op jit(solution)/shard_map/ppermute | solution.py:17
  33.1 13.2 %collective-permute-start.9 = (bf16[96,2048]{1,0:T(8,128)(2,1)}, bf16[96,2048]{1,0:T(8,128)(2,1)}, u32[]{:S(2)}, u32[]{:S(2)}) collective-permute-start(bf16[96,2048]{1,0:T(8,128)(2,1)} %collective-permute-done.3.refs_3_), channel_id=1, source_target_pairs={{0,4},{1,5},{4,8},{5,9},{8,12},{9,13},{12,14},{13,15},{14,10},{15,... | collective-permute-start | bytes 1179656 | tf_op jit(solution)/shard_map/ppermute | solution.py:332
  33.6 12.7 %collective-permute-start.10 = (bf16[96,2048]{1,0:T(8,128)(2,1)}, bf16[96,2048]{1,0:T(8,128)(2,1)}, u32[]{:S(2)}, u32[]{:S(2)}) collective-permute-start(bf16[96,2048]{1,0:T(8,128)(2,1)} %collective-permute-done.4.refs_4_), channel_id=1, source_target_pairs={{4,0},{5,1},{8,4},{9,5},{12,8},{13,9},{14,12},{15,13},{10,14},{11,... | collective-permute-start | bytes 1179656 | tf_op jit(solution)/shard_map/ppermute | solution.py:332
  35.3 11.0 %copy-start.5 = (bf16[2,96,2048]{2,1,0:T(8,128)(2,1)S(1)}, bf16[2,96,2048]{2,1,0:T(8,128)(2,1)}, u32[]{:S(2)}) copy-start(bf16[2,96,2048]{2,1,0:T(8,128)(2,1)} %param.13) | copy-start | bytes 2359300
  35.3 15.3 %copy-start.4 = (bf16[2,96,2048]{2,1,0:T(8,128)(2,1)S(1)}, bf16[2,96,2048]{2,1,0:T(8,128)(2,1)}, u32[]{:S(2)}) copy-start(bf16[2,96,2048]{2,1,0:T(8,128)(2,1)} %param.17) | copy-start | bytes 2359300
  35.3 15.3 %copy-start.6 = (f32[1,2048]{1,0:T(1,128)S(1)}, f32[1,2048]{1,0:T(1,128)}, u32[]{:S(2)}) copy-start(f32[1,2048]{1,0:T(1,128)} %gain_ref.1) | copy-start | bytes 24580
  35.4 15.3 %copy-start.7 = (f32[1,2048]{1,0:T(1,128)S(1)}, f32[1,2048]{1,0:T(1,128)}, u32[]{:S(2)}) copy-start(f32[1,2048]{1,0:T(1,128)} %param.19) | copy-start | bytes 24580
  38.4 12.2 %copy-start.2 = (bf16[1,96,2048]{2,1,0:T(8,128)(2,1)S(1)}, bf16[1,96,2048]{2,1,0:T(8,128)(2,1)}, u32[]{:S(2)}) copy-start(bf16[1,96,2048]{2,1,0:T(8,128)(2,1)} %param.16) | copy-start | bytes 1179652
  38.4 15.0 %copy-start.3 = (bf16[1,1,512,2048]{3,2,1,0:T(8,128)(2,1)S(1)}, bf16[1,1,512,2048]{3,2,1,0:T(8,128)(2,1)}, u32[]{:S(2)}) copy-start(bf16[1,1,512,2048]{3,2,1,0:T(8,128)(2,1)} %param.22) | copy-start | bytes 6291460
  48.5 15.3 %collective-permute-start.15 = (bf16[48,2048]{1,0:T(8,128)(2,1)S(1)}, bf16[48,2048]{1,0:T(8,128)(2,1)S(1)}, u32[]{:S(2)}, u32[]{:S(2)}) collective-permute-start(bf16[48,2048]{1,0:T(8,128)(2,1)S(1)} %slice.65), channel_id=1, source_target_pairs={{4,0},{5,1},{8,4},{9,5},{12,8},{13,9},{14,12},{15,13},{10,14},{11,... | collective-permute-start | bytes 589832 | tf_op jit(solution)/shard_map/ppermute | solution.py:332
  50.2 13.7 %collective-permute-start.14 = (bf16[48,2048]{1,0:T(8,128)(2,1)S(1)}, bf16[48,2048]{1,0:T(8,128)(2,1)S(1)}, u32[]{:S(2)}, u32[]{:S(2)}) collective-permute-start(bf16[48,2048]{1,0:T(8,128)(2,1)S(1)} %slice.64), channel_id=1, source_target_pairs={{0,4},{1,5},{4,8},{5,9},{8,12},{9,13},{12,14},{13,15},{14,10},{15,... | collective-permute-start | bytes 589832 | tf_op jit(solution)/shard_map/ppermute | solution.py:332
  51.3 12.6 %collective-permute-start.12 = (bf16[96,2176]{1,0:T(8,128)(2,1)}, bf16[96,2176]{1,0:T(8,128)(2,1)S(1)}, u32[]{:S(2)}, u32[]{:S(2)}) collective-permute-start(bf16[96,2176]{1,0:T(8,128)(2,1)} %collective-permute-done.7.refs_1_), channel_id=1, source_target_pairs={{0,4},{1,5},{4,8},{5,9},{8,12},{9,13},{12,14},{13,15},{14,10},{15,... | collective-permute-start | bytes 1253384 | tf_op jit(solution)/shard_map/ppermute | solution.py:332
  51.8 12.1 %collective-permute-start.13 = (bf16[96,2176]{1,0:T(8,128)(2,1)}, bf16[96,2176]{1,0:T(8,128)(2,1)S(1)}, u32[]{:S(2)}, u32[]{:S(2)}) collective-permute-start(bf16[96,2176]{1,0:T(8,128)(2,1)} %collective-permute-done.8.refs_2_), channel_id=1, source_target_pairs={{4,0},{5,1},{8,4},{9,5},{12,8},{13,9},{14,12},{15,13},{10,14},{11,... | collective-permute-start | bytes 1253384 | tf_op jit(solution)/shard_map/ppermute | solution.py:332
  53.4 10.6 %collective-permute-start.16 = (bf16[512,2048]{1,0:T(8,128)(2,1)S(1)}, bf16[512,2048]{1,0:T(8,128)(2,1)S(1)}, u32[]{:S(2)}, u32[]{:S(2)}) collective-permute-start(bf16[512,2048]{1,0:T(8,128)(2,1)S(1)} %bitcast.55), channel_id=1, source_target_pairs={{0,1},{1,0},{2,3},{3,2},{4,5},{5,4},{6,7},{7,6},{8,9},{9,8},{10,11... | collective-permute-start | bytes 6291464 | tf_op jit(solution)/shard_map/ppermute | solution.py:440
  63.9 13.3 %copy-start.8 = (bf16[48,2048]{1,0:T(8,128)(2,1)}, bf16[48,2048]{1,0:T(8,128)(2,1)S(1)}, u32[]{:S(2)}) copy-start(bf16[48,2048]{1,0:T(8,128)(2,1)S(1)} %collective-permute-done.15.refs_1_) | copy-start | bytes 589828
  63.9 13.3 %copy-start.9 = (bf16[48,2048]{1,0:T(8,128)(2,1)}, bf16[48,2048]{1,0:T(8,128)(2,1)S(1)}, u32[]{:S(2)}) copy-start(bf16[48,2048]{1,0:T(8,128)(2,1)S(1)} %collective-permute-done.14.refs_0_) | copy-start | bytes 589828
  63.9 17.4 %collective-permute-start.20 = (bf16[96,2048]{1,0:T(8,128)(2,1)S(1)}, bf16[96,2048]{1,0:T(8,128)(2,1)S(1)}, u32[]{:S(2)}, u32[]{:S(2)}) collective-permute-start(bf16[96,2048]{1,0:T(8,128)(2,1)S(1)} %get-tuple-element.260.refs_3_), channel_id=1, source_target_pairs={{4,0},{5,1},{8,4},{9,5},{12,8},{13,9},{14,12},{15,13},{10,14},{11,... | collective-permute-start | bytes 1179656 | tf_op jit(solution)/shard_map/ppermute | solution.py:332
  65.6 15.8 %collective-permute-start.19 = (bf16[96,2048]{1,0:T(8,128)(2,1)S(1)}, bf16[96,2048]{1,0:T(8,128)(2,1)S(1)}, u32[]{:S(2)}, u32[]{:S(2)}) collective-permute-start(bf16[96,2048]{1,0:T(8,128)(2,1)S(1)} %get-tuple-element.260.refs_3_), channel_id=1, source_target_pairs={{0,4},{1,5},{4,8},{5,9},{8,12},{9,13},{12,14},{13,15},{14,10},{15,... | collective-permute-start | bytes 1179656 | tf_op jit(solution)/shard_map/ppermute | solution.py:332
  66.0 19.7 %collective-permute-start.17 = (bf16[96,2176]{1,0:T(8,128)(2,1)S(1)}, bf16[96,2176]{1,0:T(8,128)(2,1)S(1)}, u32[]{:S(2)}, u32[]{:S(2)}) collective-permute-start(bf16[96,2176]{1,0:T(8,128)(2,1)S(1)} %collective-permute-done.12.refs_3_.refs_0_), channel_id=1, source_target_pairs={{0,4},{1,5},{4,8},{5,9},{8,12},{9,13},{12,14},{13,15},{14,10},{15,... | collective-permute-start | bytes 1253384 | tf_op jit(solution)/shard_map/ppermute | solution.py:332
  66.5 19.3 %collective-permute-start.18 = (bf16[96,2176]{1,0:T(8,128)(2,1)S(1)}, bf16[96,2176]{1,0:T(8,128)(2,1)S(1)}, u32[]{:S(2)}, u32[]{:S(2)}) collective-permute-start(bf16[96,2176]{1,0:T(8,128)(2,1)S(1)} %collective-permute-done.13.refs_4_.refs_1_), channel_id=1, source_target_pairs={{4,0},{5,1},{8,4},{9,5},{12,8},{13,9},{14,12},{15,13},{10,14},{11,... | collective-permute-start | bytes 1253384 | tf_op jit(solution)/shard_map/ppermute | solution.py:332
  85.8 11.7 %collective-permute-start.22 = (bf16[48,2176]{1,0:T(8,128)(2,1)S(1)}, bf16[48,2176]{1,0:T(8,128)(2,1)S(1)}, u32[]{:S(2)}, u32[]{:S(2)}) collective-permute-start(bf16[48,2176]{1,0:T(8,128)(2,1)S(1)} %slice.69), channel_id=1, source_target_pairs={{4,0},{5,1},{8,4},{9,5},{12,8},{13,9},{14,12},{15,13},{10,14},{11,... | collective-permute-start | bytes 626696 | tf_op jit(solution)/shard_map/ppermute | solution.py:332
  87.4 10.0 %collective-permute-start.21 = (bf16[48,2176]{1,0:T(8,128)(2,1)S(1)}, bf16[48,2176]{1,0:T(8,128)(2,1)S(1)}, u32[]{:S(2)}, u32[]{:S(2)}) collective-permute-start(bf16[48,2176]{1,0:T(8,128)(2,1)S(1)} %slice.68), channel_id=1, source_target_pairs={{0,4},{1,5},{4,8},{5,9},{8,12},{9,13},{12,14},{13,15},{14,10},{15,... | collective-permute-start | bytes 626696 | tf_op jit(solution)/shard_map/ppermute | solution.py:332
  87.9 14.2 %collective-permute-start.23 = (bf16[96,2048]{1,0:T(8,128)(2,1)S(1)}, bf16[96,2048]{1,0:T(8,128)(2,1)S(1)}, u32[]{:S(2)}, u32[]{:S(2)}) collective-permute-start(bf16[96,2048]{1,0:T(8,128)(2,1)S(1)} %collective-permute-done.19.refs_4_), channel_id=1, source_target_pairs={{0,4},{1,5},{4,8},{5,9},{8,12},{9,13},{12,14},{13,15},{14,10},{15,... | collective-permute-start | bytes 1179656 | tf_op jit(solution)/shard_map/ppermute | solution.py:332
  88.3 13.7 %collective-permute-start.24 = (bf16[96,2048]{1,0:T(8,128)(2,1)S(1)}, bf16[96,2048]{1,0:T(8,128)(2,1)S(1)}, u32[]{:S(2)}, u32[]{:S(2)}) collective-permute-start(bf16[96,2048]{1,0:T(8,128)(2,1)S(1)} %collective-permute-done.20.refs_5_), channel_id=1, source_target_pairs={{4,0},{5,1},{8,4},{9,5},{12,8},{13,9},{14,12},{15,13},{10,14},{11,... | collective-permute-start | bytes 1179656 | tf_op jit(solution)/shard_map/ppermute | solution.py:332
  102.1 9.2 %collective-permute-start.25 = (bf16[96,2048]{1,0:T(8,128)(2,1)S(1)}, bf16[96,2048]{1,0:T(8,128)(2,1)S(1)}, u32[]{:S(2)}, u32[]{:S(2)}) collective-permute-start(bf16[96,2048]{1,0:T(8,128)(2,1)S(1)} %collective-permute-done.23.refs_2_), channel_id=1, source_target_pairs={{0,4},{1,5},{4,8},{5,9},{8,12},{9,13},{12,14},{13,15},{14,10},{15,... | collective-permute-start | bytes 1179656 | tf_op jit(solution)/shard_map/ppermute | solution.py:332
  102.5 8.9 %collective-permute-start.26 = (bf16[96,2048]{1,0:T(8,128)(2,1)S(1)}, bf16[96,2048]{1,0:T(8,128)(2,1)S(1)}, u32[]{:S(2)}, u32[]{:S(2)}) collective-permute-start(bf16[96,2048]{1,0:T(8,128)(2,1)S(1)} %collective-permute-done.24.refs_3_), channel_id=1, source_target_pairs={{4,0},{5,1},{8,4},{9,5},{12,8},{13,9},{14,12},{15,13},{10,14},{11,... | collective-permute-start | bytes 1179656 | tf_op jit(solution)/shard_map/ppermute | solution.py:332
  111.5 9.6 %collective-permute-start.28 = (bf16[48,2048]{1,0:T(8,128)(2,1)S(1)}, bf16[48,2048]{1,0:T(8,128)(2,1)S(1)}, u32[]{:S(2)}, u32[]{:S(2)}) collective-permute-start(bf16[48,2048]{1,0:T(8,128)(2,1)S(1)} %slice.71), channel_id=1, source_target_pairs={{4,0},{5,1},{8,4},{9,5},{12,8},{13,9},{14,12},{15,13},{10,14},{11,... | collective-permute-start | bytes 589832 | tf_op jit(solution)/shard_map/ppermute | solution.py:332
  113.4 7.6 %collective-permute-start.27 = (bf16[48,2048]{1,0:T(8,128)(2,1)S(1)}, bf16[48,2048]{1,0:T(8,128)(2,1)S(1)}, u32[]{:S(2)}, u32[]{:S(2)}) collective-permute-start(bf16[48,2048]{1,0:T(8,128)(2,1)S(1)} %slice.70), channel_id=1, source_target_pairs={{0,4},{1,5},{4,8},{5,9},{8,12},{9,13},{12,14},{13,15},{14,10},{15,... | collective-permute-start | bytes 589832 | tf_op jit(solution)/shard_map/ppermute | solution.py:332
  113.5 7.6 %collective-permute-start.29 = (bf16[48,2048]{1,0:T(8,128)(2,1)S(1)}, bf16[48,2048]{1,0:T(8,128)(2,1)S(1)}, u32[]{:S(2)}, u32[]{:S(2)}) collective-permute-start(bf16[48,2048]{1,0:T(8,128)(2,1)S(1)} %get-tuple-element.315), channel_id=1, source_target_pairs={{0,4},{1,5},{4,8},{5,9},{8,12},{9,13},{12,14},{13,15},{14,10},{15,... | collective-permute-start | bytes 589832 | tf_op jit(solution)/shard_map/ppermute | solution.py:332
  114.1 7.0 %collective-permute-start.30 = (bf16[48,2048]{1,0:T(8,128)(2,1)S(1)}, bf16[48,2048]{1,0:T(8,128)(2,1)S(1)}, u32[]{:S(2)}, u32[]{:S(2)}) collective-permute-start(bf16[48,2048]{1,0:T(8,128)(2,1)S(1)} %get-tuple-element.316), channel_id=1, source_target_pairs={{4,0},{5,1},{8,4},{9,5},{12,8},{13,9},{14,12},{15,13},{10,14},{11,... | collective-permute-start | bytes 589832 | tf_op jit(solution)/shard_map/ppermute | solution.py:332
  121.4 9.5 %collective-permute-start.32 = (bf16[96,2048]{1,0:T(8,128)(2,1)S(1)}, bf16[96,2048]{1,0:T(8,128)(2,1)S(1)}, u32[]{:S(2)}, u32[]{:S(2)}) collective-permute-start(bf16[96,2048]{1,0:T(8,128)(2,1)S(1)} %pad_maximum_fusion.1), channel_id=1, source_target_pairs={{4,0},{5,1},{8,4},{9,5},{12,8},{13,9},{14,12},{15,13},{10,14},{11,... | collective-permute-start | bytes 1179656 | tf_op jit(solution)/shard_map/ppermute | solution.py:332
  123.2 8.8 %collective-permute-start.31 = (bf16[96,2048]{1,0:T(8,128)(2,1)S(1)}, bf16[96,2048]{1,0:T(8,128)(2,1)S(1)}, u32[]{:S(2)}, u32[]{:S(2)}) collective-permute-start(bf16[96,2048]{1,0:T(8,128)(2,1)S(1)} %pad_maximum_fusion), channel_id=1, source_target_pairs={{0,4},{1,5},{4,8},{5,9},{8,12},{9,13},{12,14},{13,15},{14,10},{15,... | collective-permute-start | bytes 1179656 | tf_op jit(solution)/shard_map/ppermute | solution.py:332
  132.1 13.6 %collective-permute-start.34 = (bf16[96,2048]{1,0:T(8,128)(2,1)S(1)}, bf16[96,2048]{1,0:T(8,128)(2,1)S(1)}, u32[]{:S(2)}, u32[]{:S(2)}) collective-permute-start(bf16[96,2048]{1,0:T(8,128)(2,1)S(1)} %add_convert_fusion.6), channel_id=1, source_target_pairs={{4,0},{5,1},{8,4},{9,5},{12,8},{13,9},{14,12},{15,13},{10,14},{11,... | collective-permute-start | bytes 1179656 | tf_op jit(solution)/shard_map/ppermute | solution.py:332
  134.2 11.5 %collective-permute-start.33 = (bf16[96,2048]{1,0:T(8,128)(2,1)S(1)}, bf16[96,2048]{1,0:T(8,128)(2,1)S(1)}, u32[]{:S(2)}, u32[]{:S(2)}) collective-permute-start(bf16[96,2048]{1,0:T(8,128)(2,1)S(1)} %add_convert_fusion.7), channel_id=1, source_target_pairs={{0,4},{1,5},{4,8},{5,9},{8,12},{9,13},{12,14},{13,15},{14,10},{15,... | collective-permute-start | bytes 1179656 | tf_op jit(solution)/shard_map/ppermute | solution.py:332
  134.4 11.3 %collective-permute-start.35 = (bf16[48,2048]{1,0:T(8,128)(2,1)S(1)}, bf16[48,2048]{1,0:T(8,128)(2,1)S(1)}, u32[]{:S(2)}, u32[]{:S(2)}) collective-permute-start(bf16[48,2048]{1,0:T(8,128)(2,1)S(1)} %get-tuple-element.357), channel_id=1, source_target_pairs={{0,4},{1,5},{4,8},{5,9},{8,12},{9,13},{12,14},{13,15},{14,10},{15,... | collective-permute-start | bytes 589832 | tf_op jit(solution)/shard_map/ppermute | solution.py:332
  134.4 11.3 %collective-permute-start.36 = (bf16[48,2048]{1,0:T(8,128)(2,1)S(1)}, bf16[48,2048]{1,0:T(8,128)(2,1)S(1)}, u32[]{:S(2)}, u32[]{:S(2)}) collective-permute-start(bf16[48,2048]{1,0:T(8,128)(2,1)S(1)} %get-tuple-element.358), channel_id=1, source_target_pairs={{4,0},{5,1},{8,4},{9,5},{12,8},{13,9},{14,12},{15,13},{10,14},{11,... | collective-permute-start | bytes 589832 | tf_op jit(solution)/shard_map/ppermute | solution.py:332
  146.0 8.7 %collective-permute-start.38 = (bf16[96,2048]{1,0:T(8,128)(2,1)S(1)}, bf16[96,2048]{1,0:T(8,128)(2,1)S(1)}, u32[]{:S(2)}, u32[]{:S(2)}) collective-permute-start(bf16[96,2048]{1,0:T(8,128)(2,1)S(1)} %add_convert_fusion.4), channel_id=1, source_target_pairs={{4,0},{5,1},{8,4},{9,5},{12,8},{13,9},{14,12},{15,13},{10,14},{11,... | collective-permute-start | bytes 1179656 | tf_op jit(solution)/shard_map/ppermute | solution.py:332
  147.5 9.2 %collective-permute-start.37 = (bf16[96,2048]{1,0:T(8,128)(2,1)S(1)}, bf16[96,2048]{1,0:T(8,128)(2,1)S(1)}, u32[]{:S(2)}, u32[]{:S(2)}) collective-permute-start(bf16[96,2048]{1,0:T(8,128)(2,1)S(1)} %add_convert_fusion.5), channel_id=1, source_target_pairs={{0,4},{1,5},{4,8},{5,9},{8,12},{9,13},{12,14},{13,15},{14,10},{15,... | collective-permute-start | bytes 1179656 | tf_op jit(solution)/shard_map/ppermute | solution.py:332
  148.2 12.8 %collective-permute-start.40 = (bf16[96,2048]{1,0:T(8,128)(2,1)S(1)}, bf16[96,2048]{1,0:T(8,128)(2,1)S(1)}, u32[]{:S(2)}, u32[]{:S(2)}) collective-permute-start(bf16[96,2048]{1,0:T(8,128)(2,1)S(1)} %pad_maximum_fusion.3), channel_id=1, source_target_pairs={{4,0},{5,1},{8,4},{9,5},{12,8},{13,9},{14,12},{15,13},{10,14},{11,... | collective-permute-start | bytes 1179656 | tf_op jit(solution)/shard_map/ppermute | solution.py:332
  149.7 13.9 %collective-permute-start.39 = (bf16[96,2048]{1,0:T(8,128)(2,1)S(1)}, bf16[96,2048]{1,0:T(8,128)(2,1)S(1)}, u32[]{:S(2)}, u32[]{:S(2)}) collective-permute-start(bf16[96,2048]{1,0:T(8,128)(2,1)S(1)} %pad_maximum_fusion.2), channel_id=1, source_target_pairs={{0,4},{1,5},{4,8},{5,9},{8,12},{9,13},{12,14},{13,15},{14,10},{15,... | collective-permute-start | bytes 1179656 | tf_op jit(solution)/shard_map/ppermute | solution.py:332
  163.8 11.7 %collective-permute-start.42 = (bf16[96,2048]{1,0:T(8,128)(2,1)S(1)}, bf16[96,2048]{1,0:T(8,128)(2,1)S(1)}, u32[]{:S(2)}, u32[]{:S(2)}) collective-permute-start(bf16[96,2048]{1,0:T(8,128)(2,1)S(1)} %add_convert_fusion.2), channel_id=1, source_target_pairs={{4,0},{5,1},{8,4},{9,5},{12,8},{13,9},{14,12},{15,13},{10,14},{11,... | collective-permute-start | bytes 1179656 | tf_op jit(solution)/shard_map/ppermute | solution.py:332
  165.5 11.6 %collective-permute-start.41 = (bf16[96,2048]{1,0:T(8,128)(2,1)S(1)}, bf16[96,2048]{1,0:T(8,128)(2,1)S(1)}, u32[]{:S(2)}, u32[]{:S(2)}) collective-permute-start(bf16[96,2048]{1,0:T(8,128)(2,1)S(1)} %add_convert_fusion.3), channel_id=1, source_target_pairs={{0,4},{1,5},{4,8},{5,9},{8,12},{9,13},{12,14},{13,15},{14,10},{15,... | collective-permute-start | bytes 1179656 | tf_op jit(solution)/shard_map/ppermute | solution.py:332
  177.2 7.8 %collective-permute-start.44 = (bf16[96,2048]{1,0:T(8,128)(2,1)S(1)}, bf16[96,2048]{1,0:T(8,128)(2,1)S(1)}, u32[]{:S(2)}, u32[]{:S(2)}) collective-permute-start(bf16[96,2048]{1,0:T(8,128)(2,1)S(1)} %add_convert_fusion), channel_id=1, source_target_pairs={{4,0},{5,1},{8,4},{9,5},{12,8},{13,9},{14,12},{15,13},{10,14},{11,... | collective-permute-start | bytes 1179656 | tf_op jit(solution)/shard_map/ppermute | solution.py:332
  177.8 7.8 %collective-permute-start.43 = (bf16[96,2048]{1,0:T(8,128)(2,1)S(1)}, bf16[96,2048]{1,0:T(8,128)(2,1)S(1)}, u32[]{:S(2)}, u32[]{:S(2)}) collective-permute-start(bf16[96,2048]{1,0:T(8,128)(2,1)S(1)} %add_convert_fusion.1), channel_id=1, source_target_pairs={{0,4},{1,5},{4,8},{5,9},{8,12},{9,13},{12,14},{13,15},{14,10},{15,... | collective-permute-start | bytes 1179656 | tf_op jit(solution)/shard_map/ppermute | solution.py:332

commit v12 on v11

--- a/solution.py
+++ b/solution.py
@@ -478,11 +478,11 @@
         ring.gather("fall", 3)
         ring.gather("cot", 1)
         own = fetched(own)
+        ring.weights = own + (other_gate, other_up, None)
+        ring.prepare([0, 1, 2])
         moved_rise, own, own_down = ring.fence(moved_rise, own, own_down)
         ring.gather("fall", 4)
         ring.gather("cot", 2)
-        ring.weights = own + (other_gate, other_up, None)
-        ring.prepare([0, 1, 2, 3])
         other_down = swapped(own_down)
         rise_in = entered(moved_rise)
         rise_normal = normed(rise_in.astype(jnp.float32), norm_row).astype(jnp.bfloat16)
@@ -495,7 +495,7 @@
         ring.gather("cot", 3)
         ring.gather("rise", 1)
         ring.work("backward", [0, 1, 2])
-        ring.prepare([4])
+        ring.prepare([3, 4])
         ring.fence()
         ring.gather("cot", 4)
         ring.gather("rise", 2)

time: 187 us -> 191 us (1.021)
  waiting for transfers between devices: 66.9 us -> 55.7 us
  local copies, waits for them, and re-layouts: 5.03 us -> 11.1 us
  other arithmetic: 6.77 us -> 11.3 us
  Pallas kernels: 54.2 us -> 57.6 us
    ppermute x40, waiting for transfers between devices: 65.9 us -> 55 us  [pass_on(): return lax.ppermute(block, 'ep', self.routes[way])]
    unnamed x22 -> x54, local copies, waits for them, and re-layouts: 1.67 us -> 7.77 us
    reduce_sum x2, other arithmetic: 0.42 us -> 2.59 us  [normed(): jnp.mean(values * values, axis=-1, keepdims=True) + EPSILON]
  transfers between devices with their start and end apart: 45 -> 45, of which waited for: 21 -> 17; matrix products, arithmetic and copies ran while one was open for 4% -> 8% of each run, Pallas kernels for 29% -> 30%
where the time goes in v12:
time: 191 us; the launch traced here: 190 us
  Pallas kernels  57.6 us (30%)
  waiting for transfers between devices  55.7 us (29%)
  starting transfers between devices  51.4 us (27%)
  other arithmetic  11.3 us (6%)
  local copies, waits for them, and re-layouts  11.1 us (6%)
  between operations  2.7 us (1%)
    ppermute x40, waiting for transfers between devices, pass_on(): return lax.ppermute(block, 'ep', self.routes[way])  55 us
    ppermute x40, starting transfers between devices, pass_on(): return lax.ppermute(block, 'ep', self.routes[way])  42.7 us
    pallas_call x3, Pallas kernels, forward_call(): pl.pallas_call(functools.partial(forward_kernel, parts, experts, width, T...  21.3 us
    pallas_call x2, Pallas kernels, backward_call(): pl.pallas_call(functools.partial(backward_kernel, parts, experts, width,...  16.5 us
    pallas_call x2, Pallas kernels, factor_call(): pl.pallas_call(functools.partial(factor_kernel, parts), out_shape=jax.Sha...  15 us
    ppermute x2, starting transfers between devices, passed_along(): return lax.ppermute(block, axis, route)  8.1 us
    unnamed x54, local copies, waits for them, and re-layouts  7.77 us
  transfers between devices with their start and end apart: 45, of which 17 were waited for; matrix products, arithmetic and copies ran while one was open for 8% of the time, Pallas kernels for 30%

profile of v12, /device:TPU:0, one launch (start us, length us, event | category | flops | bytes accessed | tf_op | source)
XLA Modules:
  0.0 189.9 jit_solution(3144126801342766794)
XLA Ops:
  1.2 1.2 shard_map.148.refs_0_
  2.4 3.0 %collective-permute-start.2 = (bf16[96,2048]{1,0:T(8,128)(2,1)S(1)}, bf16[96,2048]{1,0:T(8,128)(2,1)}, u32[]{:S(2)}, u32[]{:S(2)}) collective-permute-start(bf16[96,2048]{1,0:T(8,128)(2,1)S(1)} %shard_map.148.refs_0_), channel_id=1, source_target_pairs={{4,0},{5,1},{8,4},{9,5},{12,8},{13,9},{14,12},{15,13},{10,14},{11,... | collective-permute-start | bytes 1179656 | tf_op jit(solution)/shard_map/ppermute | solution.py:332
  5.5 3.8 %collective-permute-start = (bf16[96,2048]{1,0:T(8,128)(2,1)}, bf16[96,2048]{1,0:T(8,128)(2,1)S(1)}, u32[]{:S(2)}, u32[]{:S(2)}) collective-permute-start(bf16[96,2048]{1,0:T(8,128)(2,1)} %bitcast.61), channel_id=1, source_target_pairs={{0,16},{1,17},{2,18},{3,19},{4,20},{5,21},{6,22},{7,23},{8,24},{9,... | collective-permute-start | bytes 1179656 | tf_op jit(solution)/shard_map/ppermute | solution.py:17
  9.4 0.8 fusion.19
  12.0 0.8 copy.16
  12.8 0.8 copy.17
  13.7 1.2 fusion.12
  15.0 1.7 collective-permute-start.4
  17.7 1.1 bitcast_select_fusion.rows_ref
  19.5 4.3 %collective-permute-start.11 = (bf16[96,2048]{1,0:T(8,128)(2,1)S(1)}, bf16[96,2048]{1,0:T(8,128)(2,1)S(1)}, u32[]{:S(2)}, u32[]{:S(2)}) collective-permute-start(bf16[96,2048]{1,0:T(8,128)(2,1)S(1)} %bitcast.62), channel_id=1, source_target_pairs={{0,16},{1,17},{2,18},{3,19},{4,20},{5,21},{6,22},{7,23},{8,24},{9,... | collective-permute-start | bytes 1179656 | tf_op jit(solution)/shard_map/ppermute | solution.py:17
  23.8 1.9 %collective-permute-done.4.refs_4_ = bf16[96,2048]{1,0:T(8,128)(2,1)S(1)} collective-permute-done((bf16[96,2048]{1,0:T(8,128)(2,1)}, bf16[96,2048]{1,0:T(8,128)(2,1)S(1)}, u32[]{:S(2)}, u32[]{:S(2)}) %collective-permute-start.4) | collective-permute-done | bytes 393248 | tf_op jit(solution)/shard_map/ppermute | solution.py:332
  25.7 1.1 collective-permute-done.3.refs_3_
  26.8 1.6 collective-permute-start.8
  29.6 1.4 collective-permute-start.10
  30.9 2.9 %shard_map.150 = (bf16[2048,512]{1,0:T(8,128)(2,1)S(1)}, bf16[2048,512]{1,0:T(8,128)(2,1)S(1)}, bf16[512,2048]{1,0:T(8,128)(2,1)S(1)}) custom-call(bf16[2048,512]{1,0:T(8,128)(2,1)} %bitcast.51, bf16[2048,512]{1,0:T(8,128)(2,1)} %bitcast.53, bf16[512,2048]{1,0:T(8,128)(2,1)} %bitcast.9.refs_2_), custom_call_target="tpu_custom_call" | custom-call | bytes 8388608 | tf_op jit(solution)/shard_map/pallas_call | solution.py:220
  33.9 9.2 %shard_map.151.refs_5_ = bf16[4,480,512]{2,1,0:T(8,128)(2,1)S(1)} custom-call(bf16[96,2048]{1,0:T(8,128)(2,1)} %copy-done, bf16[96,2048]{1,0:T(8,128)(2,1)} %collective-permute-done.1.refs_1_, bf16[96,2048]{1,0:T(8,128)(2,1)} %collective-permute-done.2.refs_2_, bf16[96,2048]{1,0:T(8,128)(2,1)} %copy-done.23, bf16[96,2048]{1,0:T(8,128)(2,1)} %copy-done.22, ...), custom_call_target="tpu_custom_call" | custom-call | flops 9526532096 | bytes 12582912 | tf_op jit(solution)/shard_map/pallas_call | solution.py:270
  43.2 1.4 copy-done.12
  44.6 1.6 collective-permute-done.9.refs_0_
  46.2 0.8 copy-done.8
  47.0 0.8 copy-done.10
  47.8 0.9 slice.64
  48.8 0.9 slice.65
  49.7 1.6 collective-permute-start.15
  52.3 1.6 collective-permute-start.13
  53.9 1.4 fusion.6
  55.3 2.0 %multiply_reduce_fusion = (f32[96]{0:T(128)S(1)}, f32[96]{0:T(128)S(1)}, f32[96]{0:T(128)S(1)}, bf16[96,2048]{1,0:T(8,128)(2,1)S(1)}) fusion(f32[2048]{0:T(1024)S(1)} %bitcast.58, f32[96]{0:T(128)S(1)} %fusion.18, bf16[2,96,2048]{2,1,0:T(8,128)(2,1)} %param.17, bf16[1,96,2048]{2,1,0:T(8,128)(2,1)S(1)} %copy-done.14, f32[96]{0:T(128)S(1)} %add_rsqrt_fusion, ...), kind=kLoop, calls=%fused_computation.37 | loop fusion | flops 3735264 | bytes 1984384 | tf_op jit(solution)/shard_map/reduce_sum | solution.py:459
  57.4 1.4 fusion.9
  59.4 7.9 %collective-permute-done.12.refs_3_.refs_0_ = bf16[96,2176]{1,0:T(8,128)(2,1)S(1)} collective-permute-done((bf16[96,2176]{1,0:T(8,128)(2,1)}, bf16[96,2176]{1,0:T(8,128)(2,1)S(1)}, u32[]{:S(2)}, u32[]{:S(2)}) %collective-permute-start.12) | collective-permute-done | bytes 417824 | tf_op jit(solution)/shard_map/ppermute | solution.py:332
  67.3 1.6 collective-permute-start.20
  69.8 1.6 collective-permute-start.18
  71.4 1.6 copy-done.6
  73.0 1.5 copy-done.13
  74.5 9.5 %shard_map.153 = (bf16[96,2048]{1,0:T(8,128)(2,1)S(1)}, bf16[96,2048]{1,0:T(8,128)(2,1)S(1)}, bf16[96,2048]{1,0:T(8,128)(2,1)S(1)}, bf16[96,2048]{1,0:T(8,128)(2,1)S(1)}, bf16[96,2048]{1,0:T(8,128)(2,1)S(1)}) custom-call(s32[2]{0:T(128)S(1)} %pad_add_fusion.names_ref, bf16[96,2176]{1,0:T(8,128)(2,1)S(1)} %shard_map.149.refs_0_, ...), custom_call_target="tpu_custom_call" | custom-call | flops 12639797248 | bytes 12582912 | tf_op jit(solution)/shard_map/pallas_call | solution.py:288
  84.1 5.7 %shard_map.152.refs_4_ = bf16[4,288,512]{2,1,0:T(8,128)(2,1)S(1)} custom-call(bf16[96,2048]{1,0:T(8,128)(2,1)} %copy-done.18, bf16[96,2048]{1,0:T(8,128)(2,1)} %copy-done.19, bf16[48,2048]{1,0:T(8,128)(2,1)} %copy-done.25, bf16[48,2048]{1,0:T(8,128)(2,1)} %copy-done.24, bf16[2048,512]{1,0:T(8,128)(2,1)S(1)} %copy-done.2, bf16[2048,512]{1,0:T(8,128)(2,1)S(1)} %copy-done.4, ...), custom_call_target="tpu_custom_call" | custom-call | flops 7915919360 | bytes 12582912 | tf_op jit(solution)/shard_map/pallas_call | solution.py:270
  89.9 1.6 collective-permute-start.22
  92.5 1.6 collective-permute-start.24
  94.0 7.4 %shard_map.154 = (bf16[96,2048]{1,0:T(8,128)(2,1)S(1)}, bf16[96,2048]{1,0:T(8,128)(2,1)S(1)}, bf16[96,2048]{1,0:T(8,128)(2,1)S(1)}) custom-call(s32[2]{0:T(128)S(1)} %pad_add_fusion.names_ref, bf16[96,2176]{1,0:T(8,128)(2,1)S(1)} %shard_map.149.refs_0_, bf16[96,2176]{1,0:T(8,128)(2,1)S(1)} %copy-done.11, bf16[96,2176]{1,0:T(8,128)(2,1)S(1)} %copy-done.9, ...), custom_call_target="tpu_custom_call" | custom-call | flops 10223878144 | bytes 12582912 | tf_op jit(solution)/shard_map/pallas_call | solution.py:250
  101.5 3.8 %collective-permute-done.23.refs_2_ = bf16[96,2048]{1,0:T(8,128)(2,1)S(1)} collective-permute-done((bf16[96,2048]{1,0:T(8,128)(2,1)S(1)}, bf16[96,2048]{1,0:T(8,128)(2,1)S(1)}, u32[]{:S(2)}, u32[]{:S(2)}) %collective-permute-start.23) | collective-permute-done | bytes 393248 | tf_op jit(solution)/shard_map/ppermute | solution.py:332
  105.8 1.6 collective-permute-start.26
  107.3 7.0 %shard_map.155 = (bf16[96,2048]{1,0:T(8,128)(2,1)S(1)}, bf16[96,2048]{1,0:T(8,128)(2,1)S(1)}, bf16[48,2048]{1,0:T(8,128)(2,1)S(1)}, bf16[48,2048]{1,0:T(8,128)(2,1)S(1)}) custom-call(s32[2]{0:T(128)S(1)} %pad_add_fusion.names_ref, bf16[96,2176]{1,0:T(8,128)(2,1)S(1)} %collective-permute-done.17.refs_0_, ...), custom_call_target="tpu_custom_call" | custom-call | flops 10223878144 | bytes 12582912 | tf_op jit(solution)/shard_map/pallas_call | solution.py:288
  114.4 1.9 %collective-permute-start.28 = (bf16[48,2048]{1,0:T(8,128)(2,1)S(1)}, bf16[48,2048]{1,0:T(8,128)(2,1)S(1)}, u32[]{:S(2)}, u32[]{:S(2)}) collective-permute-start(bf16[48,2048]{1,0:T(8,128)(2,1)S(1)} %slice.71), channel_id=1, source_target_pairs={{4,0},{5,1},{8,4},{9,5},{12,8},{13,9},{14,12},{15,13},{10,14},{11,... | collective-permute-start | bytes 589832 | tf_op jit(solution)/shard_map/ppermute | solution.py:332
  116.9 1.6 collective-permute-start.30
  118.5 6.1 %shard_map.156 = (bf16[96,2048]{1,0:T(8,128)(2,1)S(1)}, bf16[96,2048]{1,0:T(8,128)(2,1)S(1)}) custom-call(s32[2]{0:T(128)S(1)} %pad_add_fusion.names_ref, bf16[96,2176]{1,0:T(8,128)(2,1)S(1)} %collective-permute-done.12.refs_3_.refs_0_, bf16[96,2176]{1,0:T(8,128)(2,1)S(1)} %collective-permute-done.13.refs_4_.refs_1_, ...), custom_call_target="tpu_custom_call" | custom-call | flops 9015918592 | bytes 12582912 | tf_op jit(solution)/shard_map/pallas_call | solution.py:250
  125.1 1.6 collective-permute-start.32
  127.5 7.8 %shard_map.157 = (bf16[96,2048]{1,0:T(8,128)(2,1)S(1)}, bf16[96,2048]{1,0:T(8,128)(2,1)S(1)}, bf16[48,2048]{1,0:T(8,128)(2,1)S(1)}, bf16[48,2048]{1,0:T(8,128)(2,1)S(1)}) custom-call(s32[2]{0:T(128)S(1)} %pad_add_fusion.names_ref, bf16[96,2176]{1,0:T(8,128)(2,1)S(1)} %collective-permute-done.17.refs_0_, ...), custom_call_target="tpu_custom_call" | custom-call | flops 10223878144 | bytes 12582912 | tf_op jit(solution)/shard_map/pallas_call | solution.py:250
  135.3 1.5 collective-permute-done.31
  136.9 0.9 collective-permute-start.34
  137.8 1.3 collective-permute-start.33
  139.2 2.0 %collective-permute-start.36 = (bf16[48,2048]{1,0:T(8,128)(2,1)S(1)}, bf16[48,2048]{1,0:T(8,128)(2,1)S(1)}, u32[]{:S(2)}, u32[]{:S(2)}) collective-permute-start(bf16[48,2048]{1,0:T(8,128)(2,1)S(1)} %get-tuple-element.350), channel_id=1, source_target_pairs={{4,0},{5,1},{8,4},{9,5},{12,8},{13,9},{14,12},{15,13},{10,14},{11,... | collective-permute-start | bytes 589832 | tf_op jit(solution)/shard_map/ppermute | solution.py:332
  141.1 8.9 %collective-permute-done.35 = bf16[48,2048]{1,0:T(8,128)(2,1)S(1)} collective-permute-done((bf16[48,2048]{1,0:T(8,128)(2,1)S(1)}, bf16[48,2048]{1,0:T(8,128)(2,1)S(1)}, u32[]{:S(2)}, u32[]{:S(2)}) %collective-permute-start.35) | collective-permute-done | bytes 196640 | tf_op jit(solution)/shard_map/ppermute | solution.py:332
  150.3 1.3 collective-permute-start.38
  151.7 0.8 collective-permute-start.37
  152.6 1.3 collective-permute-start.40
  153.9 0.8 collective-permute-start.39
  154.7 4.7 %collective-permute-done.38 = bf16[96,2048]{1,0:T(8,128)(2,1)S(1)} collective-permute-done((bf16[96,2048]{1,0:T(8,128)(2,1)S(1)}, bf16[96,2048]{1,0:T(8,128)(2,1)S(1)}, u32[]{:S(2)}, u32[]{:S(2)}) %collective-permute-start.38) | collective-permute-done | bytes 393248 | tf_op jit(solution)/shard_map/ppermute | solution.py:332
  159.4 1.0 collective-permute-done.37
  160.4 7.0 %collective-permute-done.40 = bf16[96,2048]{1,0:T(8,128)(2,1)S(1)} collective-permute-done((bf16[96,2048]{1,0:T(8,128)(2,1)S(1)}, bf16[96,2048]{1,0:T(8,128)(2,1)S(1)}, u32[]{:S(2)}, u32[]{:S(2)}) %collective-permute-start.40) | collective-permute-done | bytes 393248 | tf_op jit(solution)/shard_map/ppermute | solution.py:332
  168.0 1.3 collective-permute-start.42
  169.4 0.8 collective-permute-start.41
  170.6 1.1 fusion.11
  171.7 8.1 %collective-permute-done.42 = bf16[96,2048]{1,0:T(8,128)(2,1)S(1)} collective-permute-done((bf16[96,2048]{1,0:T(8,128)(2,1)S(1)}, bf16[96,2048]{1,0:T(8,128)(2,1)S(1)}, u32[]{:S(2)}, u32[]{:S(2)}) %collective-permute-start.42) | collective-permute-done | bytes 393248 | tf_op jit(solution)/shard_map/ppermute | solution.py:332
  181.0 1.8 collective-permute-start.43
  182.8 5.6 %collective-permute-done.44 = bf16[96,2048]{1,0:T(8,128)(2,1)S(1)} collective-permute-done((bf16[96,2048]{1,0:T(8,128)(2,1)S(1)}, bf16[96,2048]{1,0:T(8,128)(2,1)S(1)}, u32[]{:S(2)}, u32[]{:S(2)}) %collective-permute-start.44) | collective-permute-done | bytes 393248 | tf_op jit(solution)/shard_map/ppermute | solution.py:332
  188.9 1.0 fusion.17
  (134 shorter events, 13.5 us)
Async XLA Ops:
  0.6 26.2 %collective-permute-start.5 = (bf16[2048,512]{1,0:T(8,128)(2,1)}, bf16[2048,512]{1,0:T(8,128)(2,1)S(1)}, u32[]{:S(2)}, u32[]{:S(2)}) collective-permute-start(bf16[2048,512]{1,0:T(8,128)(2,1)} %bitcast.50), channel_id=1, source_target_pairs={{0,1},{1,0},{2,3},{3,2},{4,5},{5,4},{6,7},{7,6},{8,9},{9,8},{10,11... | collective-permute-start | bytes 6291464 | tf_op jit(solution)/shard_map/ppermute | solution.py:440
  1.1 25.7 %collective-permute-start.6 = (bf16[2048,512]{1,0:T(8,128)(2,1)}, bf16[2048,512]{1,0:T(8,128)(2,1)}, u32[]{:S(2)}, u32[]{:S(2)}) collective-permute-start(bf16[2048,512]{1,0:T(8,128)(2,1)} %bitcast.52), channel_id=1, source_target_pairs={{0,1},{1,0},{2,3},{3,2},{4,5},{5,4},{6,7},{7,6},{8,9},{9,8},{10,11... | collective-permute-start | bytes 6291464 | tf_op jit(solution)/shard_map/ppermute | solution.py:440
  2.4 31.4 %copy-start = (bf16[96,2048]{1,0:T(8,128)(2,1)}, bf16[96,2048]{1,0:T(8,128)(2,1)S(1)}, u32[]{:S(2)}) copy-start(bf16[96,2048]{1,0:T(8,128)(2,1)S(1)} %shard_map.148.refs_0_) | copy-start | bytes 1179652
  2.4 12.5 %collective-permute-start.2 = (bf16[96,2048]{1,0:T(8,128)(2,1)S(1)}, bf16[96,2048]{1,0:T(8,128)(2,1)}, u32[]{:S(2)}, u32[]{:S(2)}) collective-permute-start(bf16[96,2048]{1,0:T(8,128)(2,1)S(1)} %shard_map.148.refs_0_), channel_id=1, source_target_pairs={{4,0},{5,1},{8,4},{9,5},{12,8},{13,9},{14,12},{15,13},{10,14},{11,... | collective-permute-start | bytes 1179656 | tf_op jit(solution)/shard_map/ppermute | solution.py:332
  5.4 11.2 %collective-permute-start.1 = (bf16[96,2048]{1,0:T(8,128)(2,1)S(1)}, bf16[96,2048]{1,0:T(8,128)(2,1)}, u32[]{:S(2)}, u32[]{:S(2)}) collective-permute-start(bf16[96,2048]{1,0:T(8,128)(2,1)S(1)} %shard_map.148.refs_0_), channel_id=1, source_target_pairs={{0,4},{1,5},{4,8},{5,9},{8,12},{9,13},{12,14},{13,15},{14,10},{15,... | collective-permute-start | bytes 1179656 | tf_op jit(solution)/shard_map/ppermute | solution.py:332
  5.5 12.1 %collective-permute-start = (bf16[96,2048]{1,0:T(8,128)(2,1)}, bf16[96,2048]{1,0:T(8,128)(2,1)S(1)}, u32[]{:S(2)}, u32[]{:S(2)}) collective-permute-start(bf16[96,2048]{1,0:T(8,128)(2,1)} %bitcast.61), channel_id=1, source_target_pairs={{0,16},{1,17},{2,18},{3,19},{4,20},{5,21},{6,22},{7,23},{8,24},{9,... | collective-permute-start | bytes 1179656 | tf_op jit(solution)/shard_map/ppermute | solution.py:17
  13.7 5.8 %copy-start.21 = (bf16[1,96,2048]{2,1,0:T(8,128)(2,1)S(1)}, bf16[1,96,2048]{2,1,0:T(8,128)(2,1)}, u32[]{:S(2)}) copy-start(bf16[1,96,2048]{2,1,0:T(8,128)(2,1)} %param.14) | copy-start | bytes 1179652
  15.0 10.8 %collective-permute-start.4 = (bf16[96,2048]{1,0:T(8,128)(2,1)}, bf16[96,2048]{1,0:T(8,128)(2,1)S(1)}, u32[]{:S(2)}, u32[]{:S(2)}) collective-permute-start(bf16[96,2048]{1,0:T(8,128)(2,1)} %collective-permute-done.2.refs_2_), channel_id=1, source_target_pairs={{4,0},{5,1},{8,4},{9,5},{12,8},{13,9},{14,12},{15,13},{10,14},{11,... | collective-permute-start | bytes 1179656 | tf_op jit(solution)/shard_map/ppermute | solution.py:332
  16.6 10.2 %collective-permute-start.3 = (bf16[96,2048]{1,0:T(8,128)(2,1)}, bf16[96,2048]{1,0:T(8,128)(2,1)S(1)}, u32[]{:S(2)}, u32[]{:S(2)}) collective-permute-start(bf16[96,2048]{1,0:T(8,128)(2,1)} %collective-permute-done.1.refs_1_), channel_id=1, source_target_pairs={{0,4},{1,5},{4,8},{5,9},{8,12},{9,13},{12,14},{13,15},{14,10},{15,... | collective-permute-start | bytes 1179656 | tf_op jit(solution)/shard_map/ppermute | solution.py:332
  19.5 25.1 %collective-permute-start.11 = (bf16[96,2048]{1,0:T(8,128)(2,1)S(1)}, bf16[96,2048]{1,0:T(8,128)(2,1)S(1)}, u32[]{:S(2)}, u32[]{:S(2)}) collective-permute-start(bf16[96,2048]{1,0:T(8,128)(2,1)S(1)} %bitcast.62), channel_id=1, source_target_pairs={{0,16},{1,17},{2,18},{3,19},{4,20},{5,21},{6,22},{7,23},{8,24},{9,... | collective-permute-start | bytes 1179656 | tf_op jit(solution)/shard_map/ppermute | solution.py:17
  25.7 8.1 %copy-start.22 = (bf16[96,2048]{1,0:T(8,128)(2,1)}, bf16[96,2048]{1,0:T(8,128)(2,1)S(1)}, u32[]{:S(2)}) copy-start(bf16[96,2048]{1,0:T(8,128)(2,1)S(1)} %collective-permute-done.4.refs_4_) | copy-start | bytes 1179652
  26.8 7.0 %copy-start.23 = (bf16[96,2048]{1,0:T(8,128)(2,1)}, bf16[96,2048]{1,0:T(8,128)(2,1)S(1)}, u32[]{:S(2)}) copy-start(bf16[96,2048]{1,0:T(8,128)(2,1)S(1)} %collective-permute-done.3.refs_3_) | copy-start | bytes 1179652
  26.8 19.4 %collective-permute-start.8 = (bf16[96,2176]{1,0:T(8,128)(2,1)S(1)}, bf16[96,2176]{1,0:T(8,128)(2,1)S(1)}, u32[]{:S(2)}, u32[]{:S(2)}) collective-permute-start(bf16[96,2176]{1,0:T(8,128)(2,1)S(1)} %shard_map.149.refs_0_), channel_id=1, source_target_pairs={{4,0},{5,1},{8,4},{9,5},{12,8},{13,9},{14,12},{15,13},{10,14},{11,... | collective-permute-start | bytes 1253384 | tf_op jit(solution)/shard_map/ppermute | solution.py:332
  28.5 17.8 %collective-permute-start.7 = (bf16[96,2176]{1,0:T(8,128)(2,1)S(1)}, bf16[96,2176]{1,0:T(8,128)(2,1)S(1)}, u32[]{:S(2)}, u32[]{:S(2)}) collective-permute-start(bf16[96,2176]{1,0:T(8,128)(2,1)S(1)} %shard_map.149.refs_0_), channel_id=1, source_target_pairs={{0,4},{1,5},{4,8},{5,9},{8,12},{9,13},{12,14},{13,15},{14,10},{15,... | collective-permute-start | bytes 1253384 | tf_op jit(solution)/shard_map/ppermute | solution.py:332
  28.9 17.3 %collective-permute-start.9 = (bf16[96,2048]{1,0:T(8,128)(2,1)S(1)}, bf16[96,2048]{1,0:T(8,128)(2,1)S(1)}, u32[]{:S(2)}, u32[]{:S(2)}) collective-permute-start(bf16[96,2048]{1,0:T(8,128)(2,1)S(1)} %collective-permute-done.3.refs_3_), channel_id=1, source_target_pairs={{0,4},{1,5},{4,8},{5,9},{8,12},{9,13},{12,14},{13,15},{14,10},{15,... | collective-permute-start | bytes 1179656 | tf_op jit(solution)/shard_map/ppermute | solution.py:332
  29.6 16.6 %collective-permute-start.10 = (bf16[96,2048]{1,0:T(8,128)(2,1)S(1)}, bf16[96,2048]{1,0:T(8,128)(2,1)S(1)}, u32[]{:S(2)}, u32[]{:S(2)}) collective-permute-start(bf16[96,2048]{1,0:T(8,128)(2,1)S(1)} %collective-permute-done.4.refs_4_), channel_id=1, source_target_pairs={{4,0},{5,1},{8,4},{9,5},{12,8},{13,9},{14,12},{15,13},{10,14},{11,... | collective-permute-start | bytes 1179656 | tf_op jit(solution)/shard_map/ppermute | solution.py:332
  33.9 9.3 %copy-start.1 = (bf16[2048,512]{1,0:T(8,128)(2,1)}, bf16[2048,512]{1,0:T(8,128)(2,1)S(1)}, u32[]{:S(2)}) copy-start(bf16[2048,512]{1,0:T(8,128)(2,1)S(1)} %get-tuple-element.234.refs_5_.refs_4_.refs_6_.refs_8_) | copy-start | bytes 6291460
  33.9 9.3 %copy-start.3 = (bf16[2048,512]{1,0:T(8,128)(2,1)}, bf16[2048,512]{1,0:T(8,128)(2,1)S(1)}, u32[]{:S(2)}) copy-start(bf16[2048,512]{1,0:T(8,128)(2,1)S(1)} %get-tuple-element.235.refs_6_.refs_5_.refs_7_.refs_9_) | copy-start | bytes 6291460
  33.9 9.3 %copy-start.5 = (bf16[512,2048]{1,0:T(8,128)(2,1)}, bf16[512,2048]{1,0:T(8,128)(2,1)S(1)}, u32[]{:S(2)}) copy-start(bf16[512,2048]{1,0:T(8,128)(2,1)S(1)} %get-tuple-element.238.refs_8_.refs_7_.refs_6_.refs_10_) | copy-start | bytes 6291460
  33.9 21.4 %copy-start.17 = (f32[1,2048]{1,0:T(1,128)S(1)}, f32[1,2048]{1,0:T(1,128)}, u32[]{:S(2)}) copy-start(f32[1,2048]{1,0:T(1,128)} %gain_ref.1) | copy-start | bytes 24580
  33.9 21.4 %copy-start.20 = (f32[1,2048]{1,0:T(1,128)S(1)}, f32[1,2048]{1,0:T(1,128)}, u32[]{:S(2)}) copy-start(f32[1,2048]{1,0:T(1,128)} %param.19) | copy-start | bytes 24580
  44.6 10.8 %copy-start.14 = (bf16[1,96,2048]{2,1,0:T(8,128)(2,1)S(1)}, bf16[1,96,2048]{2,1,0:T(8,128)(2,1)}, u32[]{:S(2)}) copy-start(bf16[1,96,2048]{2,1,0:T(8,128)(2,1)} %param.16) | copy-start | bytes 1179652
  44.6 3.2 %copy-start.16 = (bf16[96,2048]{1,0:T(8,128)(2,1)}, bf16[96,2048]{1,0:T(8,128)(2,1)S(1)}, u32[]{:S(2)}) copy-start(bf16[96,2048]{1,0:T(8,128)(2,1)S(1)} %collective-permute-done.11) | copy-start | bytes 1179652
  47.8 19.5 %collective-permute-start.16 = (bf16[512,2048]{1,0:T(8,128)(2,1)}, bf16[512,2048]{1,0:T(8,128)(2,1)}, u32[]{:S(2)}, u32[]{:S(2)}) collective-permute-start(bf16[512,2048]{1,0:T(8,128)(2,1)} %bitcast.9.refs_2_), channel_id=1, source_target_pairs={{0,1},{1,0},{2,3},{3,2},{4,5},{5,4},{6,7},{7,6},{8,9},{9,8},{10,11... | collective-permute-start | bytes 6291464 | tf_op jit(solution)/shard_map/ppermute | solution.py:440
  49.7 9.7 %collective-permute-start.15 = (bf16[48,2048]{1,0:T(8,128)(2,1)S(1)}, bf16[48,2048]{1,0:T(8,128)(2,1)S(1)}, u32[]{:S(2)}, u32[]{:S(2)}) collective-permute-start(bf16[48,2048]{1,0:T(8,128)(2,1)S(1)} %slice.65), channel_id=1, source_target_pairs={{4,0},{5,1},{8,4},{9,5},{12,8},{13,9},{14,12},{15,13},{10,14},{11,... | collective-permute-start | bytes 589832 | tf_op jit(solution)/shard_map/ppermute | solution.py:332
  51.4 8.0 %collective-permute-start.14 = (bf16[48,2048]{1,0:T(8,128)(2,1)S(1)}, bf16[48,2048]{1,0:T(8,128)(2,1)S(1)}, u32[]{:S(2)}, u32[]{:S(2)}) collective-permute-start(bf16[48,2048]{1,0:T(8,128)(2,1)S(1)} %slice.64), channel_id=1, source_target_pairs={{0,4},{1,5},{4,8},{5,9},{8,12},{9,13},{12,14},{13,15},{14,10},{15,... | collective-permute-start | bytes 589832 | tf_op jit(solution)/shard_map/ppermute | solution.py:332
  51.8 15.5 %collective-permute-start.12 = (bf16[96,2176]{1,0:T(8,128)(2,1)}, bf16[96,2176]{1,0:T(8,128)(2,1)S(1)}, u32[]{:S(2)}, u32[]{:S(2)}) collective-permute-start(bf16[96,2176]{1,0:T(8,128)(2,1)} %copy-done.10), channel_id=1, source_target_pairs={{0,4},{1,5},{4,8},{5,9},{8,12},{9,13},{12,14},{13,15},{14,10},{15,... | collective-permute-start | bytes 1253384 | tf_op jit(solution)/shard_map/ppermute | solution.py:332
  52.3 15.1 %collective-permute-start.13 = (bf16[96,2176]{1,0:T(8,128)(2,1)}, bf16[96,2176]{1,0:T(8,128)(2,1)S(1)}, u32[]{:S(2)}, u32[]{:S(2)}) collective-permute-start(bf16[96,2176]{1,0:T(8,128)(2,1)} %copy-done.8), channel_id=1, source_target_pairs={{4,0},{5,1},{8,4},{9,5},{12,8},{13,9},{14,12},{15,13},{10,14},{11,... | collective-permute-start | bytes 1253384 | tf_op jit(solution)/shard_map/ppermute | solution.py:332
  53.8 17.5 %copy-start.4 = (bf16[2048,512]{1,0:T(8,128)(2,1)S(1)}, bf16[2048,512]{1,0:T(8,128)(2,1)}, u32[]{:S(2)}) copy-start(bf16[2048,512]{1,0:T(8,128)(2,1)} %copy-done.3) | copy-start | bytes 6291460
  55.2 16.2 %copy-start.2 = (bf16[2048,512]{1,0:T(8,128)(2,1)S(1)}, bf16[2048,512]{1,0:T(8,128)(2,1)}, u32[]{:S(2)}) copy-start(bf16[2048,512]{1,0:T(8,128)(2,1)} %copy-done.1) | copy-start | bytes 6291460
  55.3 16.1 %copy-start.9 = (bf16[96,2176]{1,0:T(8,128)(2,1)S(1)}, bf16[96,2176]{1,0:T(8,128)(2,1)}, u32[]{:S(2)}) copy-start(bf16[96,2176]{1,0:T(8,128)(2,1)} %copy-done.8) | copy-start | bytes 1253380
  55.3 16.1 %copy-start.11 = (bf16[96,2176]{1,0:T(8,128)(2,1)S(1)}, bf16[96,2176]{1,0:T(8,128)(2,1)}, u32[]{:S(2)}) copy-start(bf16[96,2176]{1,0:T(8,128)(2,1)} %copy-done.10) | copy-start | bytes 1253380
  59.4 24.7 %copy-start.24 = (bf16[48,2048]{1,0:T(8,128)(2,1)}, bf16[48,2048]{1,0:T(8,128)(2,1)S(1)}, u32[]{:S(2)}) copy-start(bf16[48,2048]{1,0:T(8,128)(2,1)S(1)} %collective-permute-done.15.refs_3_) | copy-start | bytes 589828
  59.4 24.7 %copy-start.25 = (bf16[48,2048]{1,0:T(8,128)(2,1)}, bf16[48,2048]{1,0:T(8,128)(2,1)S(1)}, u32[]{:S(2)}) copy-start(bf16[48,2048]{1,0:T(8,128)(2,1)S(1)} %collective-permute-done.14.refs_2_) | copy-start | bytes 589828
  67.3 22.5 %collective-permute-start.20 = (bf16[96,2048]{1,0:T(8,128)(2,1)S(1)}, bf16[96,2048]{1,0:T(8,128)(2,1)S(1)}, u32[]{:S(2)}, u32[]{:S(2)}) collective-permute-start(bf16[96,2048]{1,0:T(8,128)(2,1)S(1)} %get-tuple-element.253.refs_3_), channel_id=1, source_target_pairs={{4,0},{5,1},{8,4},{9,5},{12,8},{13,9},{14,12},{15,13},{10,14},{11,... | collective-permute-start | bytes 1179656 | tf_op jit(solution)/shard_map/ppermute | solution.py:332
  68.9 20.9 %collective-permute-start.19 = (bf16[96,2048]{1,0:T(8,128)(2,1)S(1)}, bf16[96,2048]{1,0:T(8,128)(2,1)S(1)}, u32[]{:S(2)}, u32[]{:S(2)}) collective-permute-start(bf16[96,2048]{1,0:T(8,128)(2,1)S(1)} %get-tuple-element.253.refs_3_), channel_id=1, source_target_pairs={{0,4},{1,5},{4,8},{5,9},{8,12},{9,13},{12,14},{13,15},{14,10},{15,... | collective-permute-start | bytes 1179656 | tf_op jit(solution)/shard_map/ppermute | solution.py:332
  69.4 20.5 %collective-permute-start.17 = (bf16[96,2176]{1,0:T(8,128)(2,1)S(1)}, bf16[96,2176]{1,0:T(8,128)(2,1)S(1)}, u32[]{:S(2)}, u32[]{:S(2)}) collective-permute-start(bf16[96,2176]{1,0:T(8,128)(2,1)S(1)} %collective-permute-done.12.refs_3_.refs_0_), channel_id=1, source_target_pairs={{0,4},{1,5},{4,8},{5,9},{8,12},{9,13},{12,14},{13,15},{14,10},{15,... | collective-permute-start | bytes 1253384 | tf_op jit(solution)/shard_map/ppermute | solution.py:332
  69.8 20.1 %collective-permute-start.18 = (bf16[96,2176]{1,0:T(8,128)(2,1)S(1)}, bf16[96,2176]{1,0:T(8,128)(2,1)S(1)}, u32[]{:S(2)}, u32[]{:S(2)}) collective-permute-start(bf16[96,2176]{1,0:T(8,128)(2,1)S(1)} %collective-permute-done.13.refs_4_.refs_1_), channel_id=1, source_target_pairs={{4,0},{5,1},{8,4},{9,5},{12,8},{13,9},{14,12},{15,13},{10,14},{11,... | collective-permute-start | bytes 1253384 | tf_op jit(solution)/shard_map/ppermute | solution.py:332
  84.1 10.0 %copy-start.7 = (bf16[512,2048]{1,0:T(8,128)(2,1)S(1)}, bf16[512,2048]{1,0:T(8,128)(2,1)}, u32[]{:S(2)}) copy-start(bf16[512,2048]{1,0:T(8,128)(2,1)} %copy-done.5) | copy-start | bytes 6291460
  89.9 11.6 %collective-permute-start.22 = (bf16[48,2176]{1,0:T(8,128)(2,1)S(1)}, bf16[48,2176]{1,0:T(8,128)(2,1)S(1)}, u32[]{:S(2)}, u32[]{:S(2)}) collective-permute-start(bf16[48,2176]{1,0:T(8,128)(2,1)S(1)} %slice.69), channel_id=1, source_target_pairs={{4,0},{5,1},{8,4},{9,5},{12,8},{13,9},{14,12},{15,13},{10,14},{11,... | collective-permute-start | bytes 626696 | tf_op jit(solution)/shard_map/ppermute | solution.py:332
  91.6 9.9 %collective-permute-start.21 = (bf16[48,2176]{1,0:T(8,128)(2,1)S(1)}, bf16[48,2176]{1,0:T(8,128)(2,1)S(1)}, u32[]{:S(2)}, u32[]{:S(2)}) collective-permute-start(bf16[48,2176]{1,0:T(8,128)(2,1)S(1)} %slice.68), channel_id=1, source_target_pairs={{0,4},{1,5},{4,8},{5,9},{8,12},{9,13},{12,14},{13,15},{14,10},{15,... | collective-permute-start | bytes 626696 | tf_op jit(solution)/shard_map/ppermute | solution.py:332
  92.0 13.3 %collective-permute-start.23 = (bf16[96,2048]{1,0:T(8,128)(2,1)S(1)}, bf16[96,2048]{1,0:T(8,128)(2,1)S(1)}, u32[]{:S(2)}, u32[]{:S(2)}) collective-permute-start(bf16[96,2048]{1,0:T(8,128)(2,1)S(1)} %collective-permute-done.19.refs_4_), channel_id=1, source_target_pairs={{0,4},{1,5},{4,8},{5,9},{8,12},{9,13},{12,14},{13,15},{14,10},{15,... | collective-permute-start | bytes 1179656 | tf_op jit(solution)/shard_map/ppermute | solution.py:332
  92.5 12.9 %collective-permute-start.24 = (bf16[96,2048]{1,0:T(8,128)(2,1)S(1)}, bf16[96,2048]{1,0:T(8,128)(2,1)S(1)}, u32[]{:S(2)}, u32[]{:S(2)}) collective-permute-start(bf16[96,2048]{1,0:T(8,128)(2,1)S(1)} %collective-permute-done.20.refs_5_), channel_id=1, source_target_pairs={{4,0},{5,1},{8,4},{9,5},{12,8},{13,9},{14,12},{15,13},{10,14},{11,... | collective-permute-start | bytes 1179656 | tf_op jit(solution)/shard_map/ppermute | solution.py:332
  105.3 9.1 %collective-permute-start.25 = (bf16[96,2048]{1,0:T(8,128)(2,1)S(1)}, bf16[96,2048]{1,0:T(8,128)(2,1)S(1)}, u32[]{:S(2)}, u32[]{:S(2)}) collective-permute-start(bf16[96,2048]{1,0:T(8,128)(2,1)S(1)} %collective-permute-done.23.refs_2_), channel_id=1, source_target_pairs={{0,4},{1,5},{4,8},{5,9},{8,12},{9,13},{12,14},{13,15},{14,10},{15,... | collective-permute-start | bytes 1179656 | tf_op jit(solution)/shard_map/ppermute | solution.py:332
  105.8 8.6 %collective-permute-start.26 = (bf16[96,2048]{1,0:T(8,128)(2,1)S(1)}, bf16[96,2048]{1,0:T(8,128)(2,1)S(1)}, u32[]{:S(2)}, u32[]{:S(2)}) collective-permute-start(bf16[96,2048]{1,0:T(8,128)(2,1)S(1)} %collective-permute-done.24.refs_3_), channel_id=1, source_target_pairs={{4,0},{5,1},{8,4},{9,5},{12,8},{13,9},{14,12},{15,13},{10,14},{11,... | collective-permute-start | bytes 1179656 | tf_op jit(solution)/shard_map/ppermute | solution.py:332
  114.4 10.2 %collective-permute-start.28 = (bf16[48,2048]{1,0:T(8,128)(2,1)S(1)}, bf16[48,2048]{1,0:T(8,128)(2,1)S(1)}, u32[]{:S(2)}, u32[]{:S(2)}) collective-permute-start(bf16[48,2048]{1,0:T(8,128)(2,1)S(1)} %slice.71), channel_id=1, source_target_pairs={{4,0},{5,1},{8,4},{9,5},{12,8},{13,9},{14,12},{15,13},{10,14},{11,... | collective-permute-start | bytes 589832 | tf_op jit(solution)/shard_map/ppermute | solution.py:332
  116.3 8.3 %collective-permute-start.27 = (bf16[48,2048]{1,0:T(8,128)(2,1)S(1)}, bf16[48,2048]{1,0:T(8,128)(2,1)S(1)}, u32[]{:S(2)}, u32[]{:S(2)}) collective-permute-start(bf16[48,2048]{1,0:T(8,128)(2,1)S(1)} %slice.70), channel_id=1, source_target_pairs={{0,4},{1,5},{4,8},{5,9},{8,12},{9,13},{12,14},{13,15},{14,10},{15,... | collective-permute-start | bytes 589832 | tf_op jit(solution)/shard_map/ppermute | solution.py:332
  116.5 8.4 %collective-permute-start.29 = (bf16[48,2048]{1,0:T(8,128)(2,1)S(1)}, bf16[48,2048]{1,0:T(8,128)(2,1)S(1)}, u32[]{:S(2)}, u32[]{:S(2)}) collective-permute-start(bf16[48,2048]{1,0:T(8,128)(2,1)S(1)} %get-tuple-element.307), channel_id=1, source_target_pairs={{0,4},{1,5},{4,8},{5,9},{8,12},{9,13},{12,14},{13,15},{14,10},{15,... | collective-permute-start | bytes 589832 | tf_op jit(solution)/shard_map/ppermute | solution.py:332
  116.9 8.0 %collective-permute-start.30 = (bf16[48,2048]{1,0:T(8,128)(2,1)S(1)}, bf16[48,2048]{1,0:T(8,128)(2,1)S(1)}, u32[]{:S(2)}, u32[]{:S(2)}) collective-permute-start(bf16[48,2048]{1,0:T(8,128)(2,1)S(1)} %get-tuple-element.308), channel_id=1, source_target_pairs={{4,0},{5,1},{8,4},{9,5},{12,8},{13,9},{14,12},{15,13},{10,14},{11,... | collective-permute-start | bytes 589832 | tf_op jit(solution)/shard_map/ppermute | solution.py:332
  125.1 10.2 %collective-permute-start.32 = (bf16[96,2048]{1,0:T(8,128)(2,1)S(1)}, bf16[96,2048]{1,0:T(8,128)(2,1)S(1)}, u32[]{:S(2)}, u32[]{:S(2)}) collective-permute-start(bf16[96,2048]{1,0:T(8,128)(2,1)S(1)} %pad_maximum_fusion.1), channel_id=1, source_target_pairs={{4,0},{5,1},{8,4},{9,5},{12,8},{13,9},{14,12},{15,13},{10,14},{11,... | collective-permute-start | bytes 1179656 | tf_op jit(solution)/shard_map/ppermute | solution.py:332
  126.8 10.0 %collective-permute-start.31 = (bf16[96,2048]{1,0:T(8,128)(2,1)S(1)}, bf16[96,2048]{1,0:T(8,128)(2,1)S(1)}, u32[]{:S(2)}, u32[]{:S(2)}) collective-permute-start(bf16[96,2048]{1,0:T(8,128)(2,1)S(1)} %pad_maximum_fusion), channel_id=1, source_target_pairs={{0,4},{1,5},{4,8},{5,9},{8,12},{9,13},{12,14},{13,15},{14,10},{15,... | collective-permute-start | bytes 1179656 | tf_op jit(solution)/shard_map/ppermute | solution.py:332
  136.9 13.1 %collective-permute-start.34 = (bf16[96,2048]{1,0:T(8,128)(2,1)S(1)}, bf16[96,2048]{1,0:T(8,128)(2,1)S(1)}, u32[]{:S(2)}, u32[]{:S(2)}) collective-permute-start(bf16[96,2048]{1,0:T(8,128)(2,1)S(1)} %add_convert_fusion.6), channel_id=1, source_target_pairs={{4,0},{5,1},{8,4},{9,5},{12,8},{13,9},{14,12},{15,13},{10,14},{11,... | collective-permute-start | bytes 1179656 | tf_op jit(solution)/shard_map/ppermute | solution.py:332
  137.8 12.2 %collective-permute-start.33 = (bf16[96,2048]{1,0:T(8,128)(2,1)S(1)}, bf16[96,2048]{1,0:T(8,128)(2,1)S(1)}, u32[]{:S(2)}, u32[]{:S(2)}) collective-permute-start(bf16[96,2048]{1,0:T(8,128)(2,1)S(1)} %add_convert_fusion.7), channel_id=1, source_target_pairs={{0,4},{1,5},{4,8},{5,9},{8,12},{9,13},{12,14},{13,15},{14,10},{15,... | collective-permute-start | bytes 1179656 | tf_op jit(solution)/shard_map/ppermute | solution.py:332
  139.1 10.9 %collective-permute-start.35 = (bf16[48,2048]{1,0:T(8,128)(2,1)S(1)}, bf16[48,2048]{1,0:T(8,128)(2,1)S(1)}, u32[]{:S(2)}, u32[]{:S(2)}) collective-permute-start(bf16[48,2048]{1,0:T(8,128)(2,1)S(1)} %get-tuple-element.349), channel_id=1, source_target_pairs={{0,4},{1,5},{4,8},{5,9},{8,12},{9,13},{12,14},{13,15},{14,10},{15,... | collective-permute-start | bytes 589832 | tf_op jit(solution)/shard_map/ppermute | solution.py:332
  139.2 10.8 %collective-permute-start.36 = (bf16[48,2048]{1,0:T(8,128)(2,1)S(1)}, bf16[48,2048]{1,0:T(8,128)(2,1)S(1)}, u32[]{:S(2)}, u32[]{:S(2)}) collective-permute-start(bf16[48,2048]{1,0:T(8,128)(2,1)S(1)} %get-tuple-element.350), channel_id=1, source_target_pairs={{4,0},{5,1},{8,4},{9,5},{12,8},{13,9},{14,12},{15,13},{10,14},{11,... | collective-permute-start | bytes 589832 | tf_op jit(solution)/shard_map/ppermute | solution.py:332
  150.3 9.2 %collective-permute-start.38 = (bf16[96,2048]{1,0:T(8,128)(2,1)S(1)}, bf16[96,2048]{1,0:T(8,128)(2,1)S(1)}, u32[]{:S(2)}, u32[]{:S(2)}) collective-permute-start(bf16[96,2048]{1,0:T(8,128)(2,1)S(1)} %add_convert_fusion.4), channel_id=1, source_target_pairs={{4,0},{5,1},{8,4},{9,5},{12,8},{13,9},{14,12},{15,13},{10,14},{11,... | collective-permute-start | bytes 1179656 | tf_op jit(solution)/shard_map/ppermute | solution.py:332
  151.7 18.5 %copy-start.15 = (bf16[1,96,2048]{2,1,0:T(8,128)(2,1)S(1)}, bf16[1,96,2048]{2,1,0:T(8,128)(2,1)}, u32[]{:S(2)}) copy-start(bf16[1,96,2048]{2,1,0:T(8,128)(2,1)} %param.16) | copy-start | bytes 1179652
  151.7 8.7 %collective-permute-start.37 = (bf16[96,2048]{1,0:T(8,128)(2,1)S(1)}, bf16[96,2048]{1,0:T(8,128)(2,1)S(1)}, u32[]{:S(2)}, u32[]{:S(2)}) collective-permute-start(bf16[96,2048]{1,0:T(8,128)(2,1)S(1)} %add_convert_fusion.5), channel_id=1, source_target_pairs={{0,4},{1,5},{4,8},{5,9},{8,12},{9,13},{12,14},{13,15},{14,10},{15,... | collective-permute-start | bytes 1179656 | tf_op jit(solution)/shard_map/ppermute | solution.py:332
  152.6 14.8 %collective-permute-start.40 = (bf16[96,2048]{1,0:T(8,128)(2,1)S(1)}, bf16[96,2048]{1,0:T(8,128)(2,1)S(1)}, u32[]{:S(2)}, u32[]{:S(2)}) collective-permute-start(bf16[96,2048]{1,0:T(8,128)(2,1)S(1)} %pad_maximum_fusion.3), channel_id=1, source_target_pairs={{4,0},{5,1},{8,4},{9,5},{12,8},{13,9},{14,12},{15,13},{10,14},{11,... | collective-permute-start | bytes 1179656 | tf_op jit(solution)/shard_map/ppermute | solution.py:332
  153.9 14.0 %collective-permute-start.39 = (bf16[96,2048]{1,0:T(8,128)(2,1)S(1)}, bf16[96,2048]{1,0:T(8,128)(2,1)S(1)}, u32[]{:S(2)}, u32[]{:S(2)}) collective-permute-start(bf16[96,2048]{1,0:T(8,128)(2,1)S(1)} %pad_maximum_fusion.2), channel_id=1, source_target_pairs={{0,4},{1,5},{4,8},{5,9},{8,12},{9,13},{12,14},{13,15},{14,10},{15,... | collective-permute-start | bytes 1179656 | tf_op jit(solution)/shard_map/ppermute | solution.py:332
  168.0 11.8 %collective-permute-start.42 = (bf16[96,2048]{1,0:T(8,128)(2,1)S(1)}, bf16[96,2048]{1,0:T(8,128)(2,1)S(1)}, u32[]{:S(2)}, u32[]{:S(2)}) collective-permute-start(bf16[96,2048]{1,0:T(8,128)(2,1)S(1)} %add_convert_fusion.2), channel_id=1, source_target_pairs={{4,0},{5,1},{8,4},{9,5},{12,8},{13,9},{14,12},{15,13},{10,14},{11,... | collective-permute-start | bytes 1179656 | tf_op jit(solution)/shard_map/ppermute | solution.py:332
  169.4 11.1 %collective-permute-start.41 = (bf16[96,2048]{1,0:T(8,128)(2,1)S(1)}, bf16[96,2048]{1,0:T(8,128)(2,1)S(1)}, u32[]{:S(2)}, u32[]{:S(2)}) collective-permute-start(bf16[96,2048]{1,0:T(8,128)(2,1)S(1)} %add_convert_fusion.3), channel_id=1, source_target_pairs={{0,4},{1,5},{4,8},{5,9},{8,12},{9,13},{12,14},{13,15},{14,10},{15,... | collective-permute-start | bytes 1179656 | tf_op jit(solution)/shard_map/ppermute | solution.py:332
  180.6 7.8 %collective-permute-start.44 = (bf16[96,2048]{1,0:T(8,128)(2,1)S(1)}, bf16[96,2048]{1,0:T(8,128)(2,1)S(1)}, u32[]{:S(2)}, u32[]{:S(2)}) collective-permute-start(bf16[96,2048]{1,0:T(8,128)(2,1)S(1)} %add_convert_fusion), channel_id=1, source_target_pairs={{4,0},{5,1},{8,4},{9,5},{12,8},{13,9},{14,12},{15,13},{10,14},{11,... | collective-permute-start | bytes 1179656 | tf_op jit(solution)/shard_map/ppermute | solution.py:332
  181.0 7.8 %collective-permute-start.43 = (bf16[96,2048]{1,0:T(8,128)(2,1)S(1)}, bf16[96,2048]{1,0:T(8,128)(2,1)S(1)}, u32[]{:S(2)}, u32[]{:S(2)}) collective-permute-start(bf16[96,2048]{1,0:T(8,128)(2,1)S(1)} %add_convert_fusion.1), channel_id=1, source_target_pairs={{0,4},{1,5},{4,8},{5,9},{8,12},{9,13},{12,14},{13,15},{14,10},{15,... | collective-permute-start | bytes 1179656 | tf_op jit(solution)/shard_map/ppermute | solution.py:332
  (7 other events, 9.3 us)

commit v13 on v11

--- a/solution.py
+++ b/solution.py
@@ -479,7 +479,7 @@
         ring.gather("cot", 1)
         own = fetched(own)
         moved_rise, own, own_down = ring.fence(moved_rise, own, own_down)
-        ring.gather("fall", 4)
+        ring.gather("fall", 4, 0)
         ring.gather("cot", 2)
         ring.weights = own + (other_gate, other_up, None)
         ring.prepare([0, 1, 2, 3])

time: 187 us -> 191 us (1.021)
  waiting for transfers between devices: 66.9 us -> 72.9 us
    ppermute x40 -> x39, waiting for transfers between devices: 65.9 us -> 71.9 us  [pass_on(): return lax.ppermute(block, 'ep', self.routes[way])]
    ppermute x40 -> x39, starting transfers between devices: 42.8 us -> 42.2 us  [pass_on(): return lax.ppermute(block, 'ep', self.routes[way])]
  transfers between devices with their start and end apart: 45 -> 44, of which waited for: 21 -> 24; matrix products, arithmetic and copies ran while one was open for 4% -> 4% of each run, Pallas kernels for 29% -> 28%
where the time goes in v13:
time: 191 us; the launch traced here: 190 us
  waiting for transfers between devices  72.9 us (38%)
  Pallas kernels  54.2 us (28%)
  starting transfers between devices  50.7 us (27%)
  other arithmetic  6.78 us (4%)
  local copies, waits for them, and re-layouts  3.14 us (2%)
  between operations  2.46 us (1%)
    ppermute x39, waiting for transfers between devices, pass_on(): return lax.ppermute(block, 'ep', self.routes[way])  71.9 us
    ppermute x39, starting transfers between devices, pass_on(): return lax.ppermute(block, 'ep', self.routes[way])  42.2 us
    pallas_call x3, Pallas kernels, forward_call(): pl.pallas_call(functools.partial(forward_kernel, parts, experts, width, T...  20.1 us
    pallas_call x2, Pallas kernels, backward_call(): pl.pallas_call(functools.partial(backward_kernel, parts, experts, width,...  15.5 us
    pallas_call x2, Pallas kernels, factor_call(): pl.pallas_call(functools.partial(factor_kernel, parts), out_shape=jax.Sha...  13.6 us
    ppermute x2, starting transfers between devices, passed_along(): return lax.ppermute(block, axis, route)  7.94 us
  transfers between devices with their start and end apart: 44, of which 24 were waited for; matrix products, arithmetic and copies ran while one was open for 4% of the time, Pallas kernels for 28%

profile of v13, /device:TPU:0, one launch (start us, length us, event | category | flops | bytes accessed | tf_op | source)
XLA Modules:
  0.0 190.2 jit_solution(4286656605389089704)
XLA Ops:
  0.6 0.5 collective-permute-start.5
  1.2 1.2 shard_map.148.refs_0_
  2.4 3.0 %collective-permute-start.2 = (bf16[96,2048]{1,0:T(8,128)(2,1)S(1)}, bf16[96,2048]{1,0:T(8,128)(2,1)}, u32[]{:S(2)}, u32[]{:S(2)}) collective-permute-start(bf16[96,2048]{1,0:T(8,128)(2,1)S(1)} %shard_map.148.refs_0_), channel_id=1, source_target_pairs={{4,0},{5,1},{8,4},{9,5},{12,8},{13,9},{14,12},{15,13},{10,14},{11,... | collective-permute-start | bytes 1179656 | tf_op jit(solution)/shard_map/ppermute | solution.py:332
  5.5 3.8 %collective-permute-start = (bf16[96,2048]{1,0:T(8,128)(2,1)}, bf16[96,2048]{1,0:T(8,128)(2,1)S(1)}, u32[]{:S(2)}, u32[]{:S(2)}) collective-permute-start(bf16[96,2048]{1,0:T(8,128)(2,1)} %bitcast.63), channel_id=1, source_target_pairs={{0,16},{1,17},{2,18},{3,19},{4,20},{5,21},{6,22},{7,23},{8,24},{9,... | collective-permute-start | bytes 1179656 | tf_op jit(solution)/shard_map/ppermute | solution.py:17
  9.4 0.8 fusion.19
  10.1 0.6 constant_dynamic-slice_fusion
  12.0 0.8 copy.16
  12.8 0.8 copy.17
  13.7 1.2 collective-permute-done.2.refs_2_
  14.9 1.7 collective-permute-start.4
  17.0 0.7 collective-permute-done
  17.7 1.1 bitcast_select_fusion.rows_ref
  18.7 0.7 shard_map.149.refs_0_
  19.5 6.3 %collective-permute-done.4.refs_4_ = bf16[96,2048]{1,0:T(8,128)(2,1)} collective-permute-done((bf16[96,2048]{1,0:T(8,128)(2,1)}, bf16[96,2048]{1,0:T(8,128)(2,1)}, u32[]{:S(2)}, u32[]{:S(2)}) %collective-permute-start.4) | collective-permute-done | bytes 393248 | tf_op jit(solution)/shard_map/ppermute | solution.py:332
  25.8 1.1 collective-permute-done.3.refs_3_
  26.9 1.6 collective-permute-start.8
  29.0 4.1 %collective-permute-start.11 = (bf16[96,2048]{1,0:T(8,128)(2,1)}, bf16[96,2048]{1,0:T(8,128)(2,1)}, u32[]{:S(2)}, u32[]{:S(2)}) collective-permute-start(bf16[96,2048]{1,0:T(8,128)(2,1)} %bitcast.4), channel_id=1, source_target_pairs={{0,16},{1,17},{2,18},{3,19},{4,20},{5,21},{6,22},{7,23},{8,24},{9,... | collective-permute-start | bytes 1179656 | tf_op jit(solution)/shard_map/ppermute | solution.py:17
  33.6 1.5 collective-permute-start.10
  35.4 3.0 %shard_map.150 = (bf16[2048,512]{1,0:T(8,128)(2,1)S(1)}, bf16[2048,512]{1,0:T(8,128)(2,1)S(1)}, bf16[512,2048]{1,0:T(8,128)(2,1)S(1)}) custom-call(bf16[2048,512]{1,0:T(8,128)(2,1)} %bitcast.51, bf16[2048,512]{1,0:T(8,128)(2,1)} %bitcast.53, bf16[512,2048]{1,0:T(8,128)(2,1)} %bitcast.54), custom_call_target="tpu_custom_call" | custom-call | bytes 8388608 | tf_op jit(solution)/shard_map/pallas_call | solution.py:220
  38.7 7.7 %collective-permute-done.9.refs_5_ = bf16[96,2048]{1,0:T(8,128)(2,1)} collective-permute-done((bf16[96,2048]{1,0:T(8,128)(2,1)}, bf16[96,2048]{1,0:T(8,128)(2,1)}, u32[]{:S(2)}, u32[]{:S(2)}) %collective-permute-start.9) | collective-permute-done | bytes 393248 | tf_op jit(solution)/shard_map/ppermute | solution.py:332
  47.1 1.0 collective-permute-start.12
  48.1 1.0 collective-permute-start.13
  49.2 0.6 multiply_reduce_fusion
  49.9 0.6 maximum_bitcast_fusion
  50.5 9.5 %shard_map.151.refs_5_.refs_4_ = bf16[4,672,512]{2,1,0:T(8,128)(2,1)S(1)} custom-call(bf16[96,2048]{1,0:T(8,128)(2,1)} %copy-done, bf16[96,2048]{1,0:T(8,128)(2,1)} %collective-permute-done.1.refs_1_, bf16[96,2048]{1,0:T(8,128)(2,1)} %collective-permute-done.2.refs_2_, bf16[96,2048]{1,0:T(8,128)(2,1)} %collective-permute-done.3.refs_3_, ...), custom_call_target="tpu_custom_call" | custom-call | flops 11137144832 | bytes 12582912 | tf_op jit(solution)/shard_map/pallas_call | solution.py:270
  60.4 3.3 %collective-permute-done.12.refs_3_.refs_0_ = bf16[96,2176]{1,0:T(8,128)(2,1)S(1)} collective-permute-done((bf16[96,2176]{1,0:T(8,128)(2,1)}, bf16[96,2176]{1,0:T(8,128)(2,1)S(1)}, u32[]{:S(2)}, u32[]{:S(2)}) %collective-permute-start.12) | collective-permute-done | bytes 417824 | tf_op jit(solution)/shard_map/ppermute | solution.py:332
  63.7 1.6 collective-permute-start.19
  65.7 0.6 collective-permute-start.16
  66.3 1.4 collective-permute-start.17
  67.8 9.1 %shard_map.153 = (bf16[96,2048]{1,0:T(8,128)(2,1)S(1)}, bf16[96,2048]{1,0:T(8,128)(2,1)S(1)}, bf16[96,2048]{1,0:T(8,128)(2,1)S(1)}, bf16[96,2048]{1,0:T(8,128)(2,1)S(1)}, bf16[96,2048]{1,0:T(8,128)(2,1)S(1)}) custom-call(s32[2]{0:T(128)S(1)} %pad_add_fusion.names_ref, bf16[96,2176]{1,0:T(8,128)(2,1)S(1)} %shard_map.149.refs_0_, ...), custom_call_target="tpu_custom_call" | custom-call | flops 12639797248 | bytes 12582912 | tf_op jit(solution)/shard_map/pallas_call | solution.py:288
  76.9 4.1 %shard_map.152.refs_5_ = bf16[4,96,512]{2,1,0:T(8,128)(2,1)S(1)} custom-call(bf16[96,2048]{1,0:T(8,128)(2,1)} %copy-done.8, bf16[2048,512]{1,0:T(8,128)(2,1)S(1)} %get-tuple-element.225.refs_7_.refs_1_.refs_6_.refs_4_.refs_8_, bf16[2048,512]{1,0:T(8,128)(2,1)S(1)} %get-tuple-element.226.refs_8_.refs_2_.refs_7_.refs_5_.refs_9_, ...), custom_call_target="tpu_custom_call" | custom-call | flops 6305306624 | bytes 12582912 | tf_op jit(solution)/shard_map/pallas_call | solution.py:270
  81.0 1.2 collective-permute-done.16.refs_0_
  82.3 1.6 collective-permute-start.21
  84.8 1.6 collective-permute-start.23
  86.4 7.5 %shard_map.154 = (bf16[96,2048]{1,0:T(8,128)(2,1)S(1)}, bf16[96,2048]{1,0:T(8,128)(2,1)S(1)}, bf16[96,2048]{1,0:T(8,128)(2,1)S(1)}) custom-call(s32[2]{0:T(128)S(1)} %pad_add_fusion.names_ref, bf16[96,2176]{1,0:T(8,128)(2,1)S(1)} %shard_map.149.refs_0_, bf16[96,2176]{1,0:T(8,128)(2,1)} %collective-permute-done.7.refs_1_, ...), custom_call_target="tpu_custom_call" | custom-call | flops 10223878144 | bytes 12582912 | tf_op jit(solution)/shard_map/pallas_call | solution.py:250
  94.0 3.6 %collective-permute-done.22.refs_2_ = bf16[96,2048]{1,0:T(8,128)(2,1)S(1)} collective-permute-done((bf16[96,2048]{1,0:T(8,128)(2,1)S(1)}, bf16[96,2048]{1,0:T(8,128)(2,1)S(1)}, u32[]{:S(2)}, u32[]{:S(2)}) %collective-permute-start.22) | collective-permute-done | bytes 393248 | tf_op jit(solution)/shard_map/ppermute | solution.py:332
  97.6 2.0 %collective-permute-start.25 = (bf16[96,2048]{1,0:T(8,128)(2,1)S(1)}, bf16[96,2048]{1,0:T(8,128)(2,1)S(1)}, u32[]{:S(2)}, u32[]{:S(2)}) collective-permute-start(bf16[96,2048]{1,0:T(8,128)(2,1)S(1)} %collective-permute-done.23.refs_3_), channel_id=1, source_target_pairs={{4,0},{5,1},{8,4},{9,5},{12,8},{13,9},{14,12},{15,13},{10,14},{11,... | collective-permute-start | bytes 1179656 | tf_op jit(solution)/shard_map/ppermute | solution.py:332
  99.6 6.4 %shard_map.155 = (bf16[96,2048]{1,0:T(8,128)(2,1)S(1)}, bf16[96,2048]{1,0:T(8,128)(2,1)S(1)}, bf16[48,2048]{1,0:T(8,128)(2,1)S(1)}, bf16[48,2048]{1,0:T(8,128)(2,1)S(1)}) custom-call(s32[2]{0:T(128)S(1)} %pad_add_fusion.names_ref, bf16[96,2176]{1,0:T(8,128)(2,1)S(1)} %collective-permute-done.16.refs_0_, ...), custom_call_target="tpu_custom_call" | custom-call | flops 10223878144 | bytes 12582912 | tf_op jit(solution)/shard_map/pallas_call | solution.py:288
  106.0 0.6 collective-permute-done.24.refs_4_
  106.5 1.5 collective-permute-done.25.refs_5_
  108.0 2.8 %collective-permute-start.27 = (bf16[48,2048]{1,0:T(8,128)(2,1)S(1)}, bf16[48,2048]{1,0:T(8,128)(2,1)S(1)}, u32[]{:S(2)}, u32[]{:S(2)}) collective-permute-start(bf16[48,2048]{1,0:T(8,128)(2,1)S(1)} %slice.63), channel_id=1, source_target_pairs={{4,0},{5,1},{8,4},{9,5},{12,8},{13,9},{14,12},{15,13},{10,14},{11,... | collective-permute-start | bytes 589832 | tf_op jit(solution)/shard_map/ppermute | solution.py:332
  110.8 1.7 collective-permute-start.28
  112.5 0.8 collective-permute-start.29
  113.3 5.4 %shard_map.156 = (bf16[96,2048]{1,0:T(8,128)(2,1)S(1)}, bf16[96,2048]{1,0:T(8,128)(2,1)S(1)}) custom-call(s32[2]{0:T(128)S(1)} %pad_add_fusion.names_ref, bf16[96,2176]{1,0:T(8,128)(2,1)S(1)} %collective-permute-done.12.refs_3_.refs_0_, bf16[96,2176]{1,0:T(8,128)(2,1)S(1)} %collective-permute-done.13.refs_4_.refs_1_, ...), custom_call_target="tpu_custom_call" | custom-call | flops 9015918592 | bytes 12582912 | tf_op jit(solution)/shard_map/pallas_call | solution.py:250
  118.9 3.9 %collective-permute-done.28 = bf16[48,2048]{1,0:T(8,128)(2,1)S(1)} collective-permute-done((bf16[48,2048]{1,0:T(8,128)(2,1)S(1)}, bf16[48,2048]{1,0:T(8,128)(2,1)S(1)}, u32[]{:S(2)}, u32[]{:S(2)}) %collective-permute-start.28) | collective-permute-done | bytes 196640 | tf_op jit(solution)/shard_map/ppermute | solution.py:332
  123.0 1.8 collective-permute-start.31
  124.9 0.6 collective-permute-start.30
  125.4 7.1 %shard_map.157 = (bf16[96,2048]{1,0:T(8,128)(2,1)S(1)}, bf16[96,2048]{1,0:T(8,128)(2,1)S(1)}, bf16[48,2048]{1,0:T(8,128)(2,1)S(1)}, bf16[48,2048]{1,0:T(8,128)(2,1)S(1)}) custom-call(s32[2]{0:T(128)S(1)} %pad_add_fusion.names_ref, bf16[96,2176]{1,0:T(8,128)(2,1)S(1)} %collective-permute-done.16.refs_0_, ...), custom_call_target="tpu_custom_call" | custom-call | flops 10223878144 | bytes 12582912 | tf_op jit(solution)/shard_map/pallas_call | solution.py:250
  132.6 2.5 %collective-permute-done.31 = bf16[96,2048]{1,0:T(8,128)(2,1)S(1)} collective-permute-done((bf16[96,2048]{1,0:T(8,128)(2,1)S(1)}, bf16[96,2048]{1,0:T(8,128)(2,1)S(1)}, u32[]{:S(2)}, u32[]{:S(2)}) %collective-permute-start.31) | collective-permute-done | bytes 393248 | tf_op jit(solution)/shard_map/ppermute | solution.py:332
  135.1 2.1 %collective-permute-done.30 = bf16[96,2048]{1,0:T(8,128)(2,1)S(1)} collective-permute-done((bf16[96,2048]{1,0:T(8,128)(2,1)S(1)}, bf16[96,2048]{1,0:T(8,128)(2,1)S(1)}, u32[]{:S(2)}, u32[]{:S(2)}) %collective-permute-start.30) | collective-permute-done | bytes 393248 | tf_op jit(solution)/shard_map/ppermute | solution.py:332
  137.3 0.8 collective-permute-start.33
  138.3 1.3 collective-permute-start.32
  139.8 1.7 collective-permute-start.35
  141.6 12.9 %collective-permute-done.34 = bf16[48,2048]{1,0:T(8,128)(2,1)S(1)} collective-permute-done((bf16[48,2048]{1,0:T(8,128)(2,1)S(1)}, bf16[48,2048]{1,0:T(8,128)(2,1)S(1)}, u32[]{:S(2)}, u32[]{:S(2)}) %collective-permute-start.34) | collective-permute-done | bytes 196640 | tf_op jit(solution)/shard_map/ppermute | solution.py:332
  155.3 1.8 collective-permute-start.36
  157.5 1.8 collective-permute-start.38
  159.2 7.4 %collective-permute-done.37 = bf16[96,2048]{1,0:T(8,128)(2,1)S(1)} collective-permute-done((bf16[96,2048]{1,0:T(8,128)(2,1)S(1)}, bf16[96,2048]{1,0:T(8,128)(2,1)S(1)}, u32[]{:S(2)}, u32[]{:S(2)}) %collective-permute-start.37) | collective-permute-done | bytes 393248 | tf_op jit(solution)/shard_map/ppermute | solution.py:332
  166.8 5.4 %collective-permute-done.39 = bf16[96,2048]{1,0:T(8,128)(2,1)S(1)} collective-permute-done((bf16[96,2048]{1,0:T(8,128)(2,1)S(1)}, bf16[96,2048]{1,0:T(8,128)(2,1)S(1)}, u32[]{:S(2)}, u32[]{:S(2)}) %collective-permute-start.39) | collective-permute-done | bytes 393248 | tf_op jit(solution)/shard_map/ppermute | solution.py:332
  173.0 1.8 collective-permute-start.40
  175.1 1.1 fusion.11
  176.3 4.1 %collective-permute-done.41 = bf16[96,2048]{1,0:T(8,128)(2,1)S(1)} collective-permute-done((bf16[96,2048]{1,0:T(8,128)(2,1)S(1)}, bf16[96,2048]{1,0:T(8,128)(2,1)S(1)}, u32[]{:S(2)}, u32[]{:S(2)}) %collective-permute-start.41) | collective-permute-done | bytes 393248 | tf_op jit(solution)/shard_map/ppermute | solution.py:332
  181.3 1.8 collective-permute-start.42
  183.1 5.6 %collective-permute-done.43 = bf16[96,2048]{1,0:T(8,128)(2,1)S(1)} collective-permute-done((bf16[96,2048]{1,0:T(8,128)(2,1)S(1)}, bf16[96,2048]{1,0:T(8,128)(2,1)S(1)}, u32[]{:S(2)}, u32[]{:S(2)}) %collective-permute-start.43) | collective-permute-done | bytes 393248 | tf_op jit(solution)/shard_map/ppermute | solution.py:332
  189.2 1.0 fusion.17
  (96 shorter events, 9.4 us)
Async XLA Ops:
  0.6 26.3 %collective-permute-start.5 = (bf16[2048,512]{1,0:T(8,128)(2,1)}, bf16[2048,512]{1,0:T(8,128)(2,1)S(1)}, u32[]{:S(2)}, u32[]{:S(2)}) collective-permute-start(bf16[2048,512]{1,0:T(8,128)(2,1)} %bitcast.50), channel_id=1, source_target_pairs={{0,1},{1,0},{2,3},{3,2},{4,5},{5,4},{6,7},{7,6},{8,9},{9,8},{10,11... | collective-permute-start | bytes 6291464 | tf_op jit(solution)/shard_map/ppermute | solution.py:440
  1.1 25.8 %collective-permute-start.6 = (bf16[2048,512]{1,0:T(8,128)(2,1)}, bf16[2048,512]{1,0:T(8,128)(2,1)}, u32[]{:S(2)}, u32[]{:S(2)}) collective-permute-start(bf16[2048,512]{1,0:T(8,128)(2,1)} %bitcast.52), channel_id=1, source_target_pairs={{0,1},{1,0},{2,3},{3,2},{4,5},{5,4},{6,7},{7,6},{8,9},{9,8},{10,11... | collective-permute-start | bytes 6291464 | tf_op jit(solution)/shard_map/ppermute | solution.py:440
  2.4 36.0 %copy-start = (bf16[96,2048]{1,0:T(8,128)(2,1)}, bf16[96,2048]{1,0:T(8,128)(2,1)S(1)}, u32[]{:S(2)}) copy-start(bf16[96,2048]{1,0:T(8,128)(2,1)S(1)} %shard_map.148.refs_0_) | copy-start | bytes 1179652
  2.4 12.5 %collective-permute-start.2 = (bf16[96,2048]{1,0:T(8,128)(2,1)S(1)}, bf16[96,2048]{1,0:T(8,128)(2,1)}, u32[]{:S(2)}, u32[]{:S(2)}) collective-permute-start(bf16[96,2048]{1,0:T(8,128)(2,1)S(1)} %shard_map.148.refs_0_), channel_id=1, source_target_pairs={{4,0},{5,1},{8,4},{9,5},{12,8},{13,9},{14,12},{15,13},{10,14},{11,... | collective-permute-start | bytes 1179656 | tf_op jit(solution)/shard_map/ppermute | solution.py:332
  5.4 11.2 %collective-permute-start.1 = (bf16[96,2048]{1,0:T(8,128)(2,1)S(1)}, bf16[96,2048]{1,0:T(8,128)(2,1)}, u32[]{:S(2)}, u32[]{:S(2)}) collective-permute-start(bf16[96,2048]{1,0:T(8,128)(2,1)S(1)} %shard_map.148.refs_0_), channel_id=1, source_target_pairs={{0,4},{1,5},{4,8},{5,9},{8,12},{9,13},{12,14},{13,15},{14,10},{15,... | collective-permute-start | bytes 1179656 | tf_op jit(solution)/shard_map/ppermute | solution.py:332
  5.5 12.1 %collective-permute-start = (bf16[96,2048]{1,0:T(8,128)(2,1)}, bf16[96,2048]{1,0:T(8,128)(2,1)S(1)}, u32[]{:S(2)}, u32[]{:S(2)}) collective-permute-start(bf16[96,2048]{1,0:T(8,128)(2,1)} %bitcast.63), channel_id=1, source_target_pairs={{0,16},{1,17},{2,18},{3,19},{4,20},{5,21},{6,22},{7,23},{8,24},{9,... | collective-permute-start | bytes 1179656 | tf_op jit(solution)/shard_map/ppermute | solution.py:17
  13.6 21.5 %copy-start.1 = (bf16[1,96,2048]{2,1,0:T(8,128)(2,1)S(1)}, bf16[1,96,2048]{2,1,0:T(8,128)(2,1)}, u32[]{:S(2)}) copy-start(bf16[1,96,2048]{2,1,0:T(8,128)(2,1)} %param.16) | copy-start | bytes 1179652
  14.9 10.9 %collective-permute-start.4 = (bf16[96,2048]{1,0:T(8,128)(2,1)}, bf16[96,2048]{1,0:T(8,128)(2,1)}, u32[]{:S(2)}, u32[]{:S(2)}) collective-permute-start(bf16[96,2048]{1,0:T(8,128)(2,1)} %collective-permute-done.2.refs_2_), channel_id=1, source_target_pairs={{4,0},{5,1},{8,4},{9,5},{12,8},{13,9},{14,12},{15,13},{10,14},{11,... | collective-permute-start | bytes 1179656 | tf_op jit(solution)/shard_map/ppermute | solution.py:332
  16.6 10.3 %collective-permute-start.3 = (bf16[96,2048]{1,0:T(8,128)(2,1)}, bf16[96,2048]{1,0:T(8,128)(2,1)}, u32[]{:S(2)}, u32[]{:S(2)}) collective-permute-start(bf16[96,2048]{1,0:T(8,128)(2,1)} %collective-permute-done.1.refs_1_), channel_id=1, source_target_pairs={{0,4},{1,5},{4,8},{5,9},{8,12},{9,13},{12,14},{13,15},{14,10},{15,... | collective-permute-start | bytes 1179656 | tf_op jit(solution)/shard_map/ppermute | solution.py:332
  26.9 19.4 %collective-permute-start.8 = (bf16[96,2176]{1,0:T(8,128)(2,1)S(1)}, bf16[96,2176]{1,0:T(8,128)(2,1)}, u32[]{:S(2)}, u32[]{:S(2)}) collective-permute-start(bf16[96,2176]{1,0:T(8,128)(2,1)S(1)} %shard_map.149.refs_0_), channel_id=1, source_target_pairs={{4,0},{5,1},{8,4},{9,5},{12,8},{13,9},{14,12},{15,13},{10,14},{11,... | collective-permute-start | bytes 1253384 | tf_op jit(solution)/shard_map/ppermute | solution.py:332
  28.5 17.8 %collective-permute-start.7 = (bf16[96,2176]{1,0:T(8,128)(2,1)S(1)}, bf16[96,2176]{1,0:T(8,128)(2,1)}, u32[]{:S(2)}, u32[]{:S(2)}) collective-permute-start(bf16[96,2176]{1,0:T(8,128)(2,1)S(1)} %shard_map.149.refs_0_), channel_id=1, source_target_pairs={{0,4},{1,5},{4,8},{5,9},{8,12},{9,13},{12,14},{13,15},{14,10},{15,... | collective-permute-start | bytes 1253384 | tf_op jit(solution)/shard_map/ppermute | solution.py:332
  29.0 9.7 %collective-permute-start.11 = (bf16[96,2048]{1,0:T(8,128)(2,1)}, bf16[96,2048]{1,0:T(8,128)(2,1)}, u32[]{:S(2)}, u32[]{:S(2)}) collective-permute-start(bf16[96,2048]{1,0:T(8,128)(2,1)} %bitcast.4), channel_id=1, source_target_pairs={{0,16},{1,17},{2,18},{3,19},{4,20},{5,21},{6,22},{7,23},{8,24},{9,... | collective-permute-start | bytes 1179656 | tf_op jit(solution)/shard_map/ppermute | solution.py:17
  33.1 13.2 %collective-permute-start.9 = (bf16[96,2048]{1,0:T(8,128)(2,1)}, bf16[96,2048]{1,0:T(8,128)(2,1)}, u32[]{:S(2)}, u32[]{:S(2)}) collective-permute-start(bf16[96,2048]{1,0:T(8,128)(2,1)} %collective-permute-done.3.refs_3_), channel_id=1, source_target_pairs={{0,4},{1,5},{4,8},{5,9},{8,12},{9,13},{12,14},{13,15},{14,10},{15,... | collective-permute-start | bytes 1179656 | tf_op jit(solution)/shard_map/ppermute | solution.py:332
  33.6 12.7 %collective-permute-start.10 = (bf16[96,2048]{1,0:T(8,128)(2,1)}, bf16[96,2048]{1,0:T(8,128)(2,1)}, u32[]{:S(2)}, u32[]{:S(2)}) collective-permute-start(bf16[96,2048]{1,0:T(8,128)(2,1)} %collective-permute-done.4.refs_4_), channel_id=1, source_target_pairs={{4,0},{5,1},{8,4},{9,5},{12,8},{13,9},{14,12},{15,13},{10,14},{11,... | collective-permute-start | bytes 1179656 | tf_op jit(solution)/shard_map/ppermute | solution.py:332
  35.3 11.0 %copy-start.5 = (bf16[2,96,2048]{2,1,0:T(8,128)(2,1)S(1)}, bf16[2,96,2048]{2,1,0:T(8,128)(2,1)}, u32[]{:S(2)}) copy-start(bf16[2,96,2048]{2,1,0:T(8,128)(2,1)} %param.13) | copy-start | bytes 2359300
  35.3 13.8 %copy-start.3 = (bf16[1,1,512,2048]{3,2,1,0:T(8,128)(2,1)S(1)}, bf16[1,1,512,2048]{3,2,1,0:T(8,128)(2,1)}, u32[]{:S(2)}) copy-start(bf16[1,1,512,2048]{3,2,1,0:T(8,128)(2,1)} %param.22) | copy-start | bytes 6291460
  35.3 13.8 %copy-start.2 = (bf16[1,96,2048]{2,1,0:T(8,128)(2,1)S(1)}, bf16[1,96,2048]{2,1,0:T(8,128)(2,1)}, u32[]{:S(2)}) copy-start(bf16[1,96,2048]{2,1,0:T(8,128)(2,1)} %param.16) | copy-start | bytes 1179652
  35.4 13.8 %copy-start.4 = (bf16[2,96,2048]{2,1,0:T(8,128)(2,1)S(1)}, bf16[2,96,2048]{2,1,0:T(8,128)(2,1)}, u32[]{:S(2)}) copy-start(bf16[2,96,2048]{2,1,0:T(8,128)(2,1)} %param.17) | copy-start | bytes 2359300
  35.4 13.8 %copy-start.6 = (f32[1,2048]{1,0:T(1,128)S(1)}, f32[1,2048]{1,0:T(1,128)}, u32[]{:S(2)}) copy-start(f32[1,2048]{1,0:T(1,128)} %gain_ref.1) | copy-start | bytes 24580
  35.4 13.8 %copy-start.7 = (f32[1,2048]{1,0:T(1,128)S(1)}, f32[1,2048]{1,0:T(1,128)}, u32[]{:S(2)}) copy-start(f32[1,2048]{1,0:T(1,128)} %param.19) | copy-start | bytes 24580
  46.6 13.7 %collective-permute-start.14 = (bf16[96,2048]{1,0:T(8,128)(2,1)}, bf16[96,2048]{1,0:T(8,128)(2,1)S(1)}, u32[]{:S(2)}, u32[]{:S(2)}) collective-permute-start(bf16[96,2048]{1,0:T(8,128)(2,1)} %collective-permute-done.9.refs_5_), channel_id=1, source_target_pairs={{0,4},{1,5},{4,8},{5,9},{8,12},{9,13},{12,14},{13,15},{14,10},{15,... | collective-permute-start | bytes 1179656 | tf_op jit(solution)/shard_map/ppermute | solution.py:332
  47.1 16.6 %collective-permute-start.12 = (bf16[96,2176]{1,0:T(8,128)(2,1)}, bf16[96,2176]{1,0:T(8,128)(2,1)S(1)}, u32[]{:S(2)}, u32[]{:S(2)}) collective-permute-start(bf16[96,2176]{1,0:T(8,128)(2,1)} %collective-permute-done.7.refs_1_), channel_id=1, source_target_pairs={{0,4},{1,5},{4,8},{5,9},{8,12},{9,13},{12,14},{13,15},{14,10},{15,... | collective-permute-start | bytes 1253384 | tf_op jit(solution)/shard_map/ppermute | solution.py:332
  48.1 15.6 %collective-permute-start.13 = (bf16[96,2176]{1,0:T(8,128)(2,1)}, bf16[96,2176]{1,0:T(8,128)(2,1)S(1)}, u32[]{:S(2)}, u32[]{:S(2)}) collective-permute-start(bf16[96,2176]{1,0:T(8,128)(2,1)} %collective-permute-done.8.refs_2_), channel_id=1, source_target_pairs={{4,0},{5,1},{8,4},{9,5},{12,8},{13,9},{14,12},{15,13},{10,14},{11,... | collective-permute-start | bytes 1253384 | tf_op jit(solution)/shard_map/ppermute | solution.py:332
  49.2 14.5 %collective-permute-start.15 = (bf16[512,2048]{1,0:T(8,128)(2,1)S(1)}, bf16[512,2048]{1,0:T(8,128)(2,1)S(1)}, u32[]{:S(2)}, u32[]{:S(2)}) collective-permute-start(bf16[512,2048]{1,0:T(8,128)(2,1)S(1)} %bitcast.55), channel_id=1, source_target_pairs={{0,1},{1,0},{2,3},{3,2},{4,5},{5,4},{6,7},{7,6},{8,9},{9,8},{10,11... | collective-permute-start | bytes 6291464 | tf_op jit(solution)/shard_map/ppermute | solution.py:440
  60.4 16.5 %copy-start.8 = (bf16[96,2048]{1,0:T(8,128)(2,1)}, bf16[96,2048]{1,0:T(8,128)(2,1)S(1)}, u32[]{:S(2)}) copy-start(bf16[96,2048]{1,0:T(8,128)(2,1)S(1)} %collective-permute-done.14.refs_0_) | copy-start | bytes 1179652
  63.7 17.3 %collective-permute-start.19 = (bf16[96,2048]{1,0:T(8,128)(2,1)S(1)}, bf16[96,2048]{1,0:T(8,128)(2,1)S(1)}, u32[]{:S(2)}, u32[]{:S(2)}) collective-permute-start(bf16[96,2048]{1,0:T(8,128)(2,1)S(1)} %get-tuple-element.258.refs_3_), channel_id=1, source_target_pairs={{4,0},{5,1},{8,4},{9,5},{12,8},{13,9},{14,12},{15,13},{10,14},{11,... | collective-permute-start | bytes 1179656 | tf_op jit(solution)/shard_map/ppermute | solution.py:332
  65.3 15.7 %collective-permute-start.18 = (bf16[96,2048]{1,0:T(8,128)(2,1)S(1)}, bf16[96,2048]{1,0:T(8,128)(2,1)S(1)}, u32[]{:S(2)}, u32[]{:S(2)}) collective-permute-start(bf16[96,2048]{1,0:T(8,128)(2,1)S(1)} %get-tuple-element.258.refs_3_), channel_id=1, source_target_pairs={{0,4},{1,5},{4,8},{5,9},{8,12},{9,13},{12,14},{13,15},{14,10},{15,... | collective-permute-start | bytes 1179656 | tf_op jit(solution)/shard_map/ppermute | solution.py:332
  65.7 16.5 %collective-permute-start.16 = (bf16[96,2176]{1,0:T(8,128)(2,1)S(1)}, bf16[96,2176]{1,0:T(8,128)(2,1)S(1)}, u32[]{:S(2)}, u32[]{:S(2)}) collective-permute-start(bf16[96,2176]{1,0:T(8,128)(2,1)S(1)} %collective-permute-done.12.refs_3_.refs_0_), channel_id=1, source_target_pairs={{0,4},{1,5},{4,8},{5,9},{8,12},{9,13},{12,14},{13,15},{14,10},{15,... | collective-permute-start | bytes 1253384 | tf_op jit(solution)/shard_map/ppermute | solution.py:332
  66.3 15.9 %collective-permute-start.17 = (bf16[96,2176]{1,0:T(8,128)(2,1)S(1)}, bf16[96,2176]{1,0:T(8,128)(2,1)S(1)}, u32[]{:S(2)}, u32[]{:S(2)}) collective-permute-start(bf16[96,2176]{1,0:T(8,128)(2,1)S(1)} %collective-permute-done.13.refs_4_.refs_1_), channel_id=1, source_target_pairs={{4,0},{5,1},{8,4},{9,5},{12,8},{13,9},{14,12},{15,13},{10,14},{11,... | collective-permute-start | bytes 1253384 | tf_op jit(solution)/shard_map/ppermute | solution.py:332
  82.3 11.7 %collective-permute-start.21 = (bf16[48,2176]{1,0:T(8,128)(2,1)S(1)}, bf16[48,2176]{1,0:T(8,128)(2,1)S(1)}, u32[]{:S(2)}, u32[]{:S(2)}) collective-permute-start(bf16[48,2176]{1,0:T(8,128)(2,1)S(1)} %slice.61), channel_id=1, source_target_pairs={{4,0},{5,1},{8,4},{9,5},{12,8},{13,9},{14,12},{15,13},{10,14},{11,... | collective-permute-start | bytes 626696 | tf_op jit(solution)/shard_map/ppermute | solution.py:332
  83.9 10.0 %collective-permute-start.20 = (bf16[48,2176]{1,0:T(8,128)(2,1)S(1)}, bf16[48,2176]{1,0:T(8,128)(2,1)S(1)}, u32[]{:S(2)}, u32[]{:S(2)}) collective-permute-start(bf16[48,2176]{1,0:T(8,128)(2,1)S(1)} %slice.60), channel_id=1, source_target_pairs={{0,4},{1,5},{4,8},{5,9},{8,12},{9,13},{12,14},{13,15},{14,10},{15,... | collective-permute-start | bytes 626696 | tf_op jit(solution)/shard_map/ppermute | solution.py:332
  84.4 13.2 %collective-permute-start.22 = (bf16[96,2048]{1,0:T(8,128)(2,1)S(1)}, bf16[96,2048]{1,0:T(8,128)(2,1)S(1)}, u32[]{:S(2)}, u32[]{:S(2)}) collective-permute-start(bf16[96,2048]{1,0:T(8,128)(2,1)S(1)} %collective-permute-done.18.refs_4_), channel_id=1, source_target_pairs={{0,4},{1,5},{4,8},{5,9},{8,12},{9,13},{12,14},{13,15},{14,10},{15,... | collective-permute-start | bytes 1179656 | tf_op jit(solution)/shard_map/ppermute | solution.py:332
  84.8 12.7 %collective-permute-start.23 = (bf16[96,2048]{1,0:T(8,128)(2,1)S(1)}, bf16[96,2048]{1,0:T(8,128)(2,1)S(1)}, u32[]{:S(2)}, u32[]{:S(2)}) collective-permute-start(bf16[96,2048]{1,0:T(8,128)(2,1)S(1)} %collective-permute-done.19.refs_5_), channel_id=1, source_target_pairs={{4,0},{5,1},{8,4},{9,5},{12,8},{13,9},{14,12},{15,13},{10,14},{11,... | collective-permute-start | bytes 1179656 | tf_op jit(solution)/shard_map/ppermute | solution.py:332
  97.6 9.0 %collective-permute-start.24 = (bf16[96,2048]{1,0:T(8,128)(2,1)S(1)}, bf16[96,2048]{1,0:T(8,128)(2,1)S(1)}, u32[]{:S(2)}, u32[]{:S(2)}) collective-permute-start(bf16[96,2048]{1,0:T(8,128)(2,1)S(1)} %collective-permute-done.22.refs_2_), channel_id=1, source_target_pairs={{0,4},{1,5},{4,8},{5,9},{8,12},{9,13},{12,14},{13,15},{14,10},{15,... | collective-permute-start | bytes 1179656 | tf_op jit(solution)/shard_map/ppermute | solution.py:332
  97.6 10.4 %collective-permute-start.25 = (bf16[96,2048]{1,0:T(8,128)(2,1)S(1)}, bf16[96,2048]{1,0:T(8,128)(2,1)S(1)}, u32[]{:S(2)}, u32[]{:S(2)}) collective-permute-start(bf16[96,2048]{1,0:T(8,128)(2,1)S(1)} %collective-permute-done.23.refs_3_), channel_id=1, source_target_pairs={{4,0},{5,1},{8,4},{9,5},{12,8},{13,9},{14,12},{15,13},{10,14},{11,... | collective-permute-start | bytes 1179656 | tf_op jit(solution)/shard_map/ppermute | solution.py:332
  108.0 10.7 %collective-permute-start.27 = (bf16[48,2048]{1,0:T(8,128)(2,1)S(1)}, bf16[48,2048]{1,0:T(8,128)(2,1)S(1)}, u32[]{:S(2)}, u32[]{:S(2)}) collective-permute-start(bf16[48,2048]{1,0:T(8,128)(2,1)S(1)} %slice.63), channel_id=1, source_target_pairs={{4,0},{5,1},{8,4},{9,5},{12,8},{13,9},{14,12},{15,13},{10,14},{11,... | collective-permute-start | bytes 589832 | tf_op jit(solution)/shard_map/ppermute | solution.py:332
  110.8 8.1 %collective-permute-start.26 = (bf16[48,2048]{1,0:T(8,128)(2,1)S(1)}, bf16[48,2048]{1,0:T(8,128)(2,1)S(1)}, u32[]{:S(2)}, u32[]{:S(2)}) collective-permute-start(bf16[48,2048]{1,0:T(8,128)(2,1)S(1)} %slice.62), channel_id=1, source_target_pairs={{0,4},{1,5},{4,8},{5,9},{8,12},{9,13},{12,14},{13,15},{14,10},{15,... | collective-permute-start | bytes 589832 | tf_op jit(solution)/shard_map/ppermute | solution.py:332
  110.8 12.0 %collective-permute-start.28 = (bf16[48,2048]{1,0:T(8,128)(2,1)S(1)}, bf16[48,2048]{1,0:T(8,128)(2,1)S(1)}, u32[]{:S(2)}, u32[]{:S(2)}) collective-permute-start(bf16[48,2048]{1,0:T(8,128)(2,1)S(1)} %get-tuple-element.313), channel_id=1, source_target_pairs={{0,4},{1,5},{4,8},{5,9},{8,12},{9,13},{12,14},{13,15},{14,10},{15,... | collective-permute-start | bytes 589832 | tf_op jit(solution)/shard_map/ppermute | solution.py:332
  112.5 10.4 %collective-permute-start.29 = (bf16[48,2048]{1,0:T(8,128)(2,1)S(1)}, bf16[48,2048]{1,0:T(8,128)(2,1)S(1)}, u32[]{:S(2)}, u32[]{:S(2)}) collective-permute-start(bf16[48,2048]{1,0:T(8,128)(2,1)S(1)} %get-tuple-element.314), channel_id=1, source_target_pairs={{4,0},{5,1},{8,4},{9,5},{12,8},{13,9},{14,12},{15,13},{10,14},{11,... | collective-permute-start | bytes 589832 | tf_op jit(solution)/shard_map/ppermute | solution.py:332
  123.0 12.1 %collective-permute-start.31 = (bf16[96,2048]{1,0:T(8,128)(2,1)S(1)}, bf16[96,2048]{1,0:T(8,128)(2,1)S(1)}, u32[]{:S(2)}, u32[]{:S(2)}) collective-permute-start(bf16[96,2048]{1,0:T(8,128)(2,1)S(1)} %pad_maximum_fusion.1), channel_id=1, source_target_pairs={{4,0},{5,1},{8,4},{9,5},{12,8},{13,9},{14,12},{15,13},{10,14},{11,... | collective-permute-start | bytes 1179656 | tf_op jit(solution)/shard_map/ppermute | solution.py:332
  124.9 12.3 %collective-permute-start.30 = (bf16[96,2048]{1,0:T(8,128)(2,1)S(1)}, bf16[96,2048]{1,0:T(8,128)(2,1)S(1)}, u32[]{:S(2)}, u32[]{:S(2)}) collective-permute-start(bf16[96,2048]{1,0:T(8,128)(2,1)S(1)} %pad_maximum_fusion), channel_id=1, source_target_pairs={{0,4},{1,5},{4,8},{5,9},{8,12},{9,13},{12,14},{13,15},{14,10},{15,... | collective-permute-start | bytes 1179656 | tf_op jit(solution)/shard_map/ppermute | solution.py:332
  137.3 17.2 %collective-permute-start.33 = (bf16[96,2048]{1,0:T(8,128)(2,1)S(1)}, bf16[96,2048]{1,0:T(8,128)(2,1)S(1)}, u32[]{:S(2)}, u32[]{:S(2)}) collective-permute-start(bf16[96,2048]{1,0:T(8,128)(2,1)S(1)} %add_convert_fusion.6), channel_id=1, source_target_pairs={{4,0},{5,1},{8,4},{9,5},{12,8},{13,9},{14,12},{15,13},{10,14},{11,... | collective-permute-start | bytes 1179656 | tf_op jit(solution)/shard_map/ppermute | solution.py:332
  138.3 16.3 %collective-permute-start.32 = (bf16[96,2048]{1,0:T(8,128)(2,1)S(1)}, bf16[96,2048]{1,0:T(8,128)(2,1)S(1)}, u32[]{:S(2)}, u32[]{:S(2)}) collective-permute-start(bf16[96,2048]{1,0:T(8,128)(2,1)S(1)} %add_convert_fusion.7), channel_id=1, source_target_pairs={{0,4},{1,5},{4,8},{5,9},{8,12},{9,13},{12,14},{13,15},{14,10},{15,... | collective-permute-start | bytes 1179656 | tf_op jit(solution)/shard_map/ppermute | solution.py:332
  139.5 15.0 %collective-permute-start.34 = (bf16[48,2048]{1,0:T(8,128)(2,1)S(1)}, bf16[48,2048]{1,0:T(8,128)(2,1)S(1)}, u32[]{:S(2)}, u32[]{:S(2)}) collective-permute-start(bf16[48,2048]{1,0:T(8,128)(2,1)S(1)} %get-tuple-element.355), channel_id=1, source_target_pairs={{0,4},{1,5},{4,8},{5,9},{8,12},{9,13},{12,14},{13,15},{14,10},{15,... | collective-permute-start | bytes 589832 | tf_op jit(solution)/shard_map/ppermute | solution.py:332
  139.8 14.7 %collective-permute-start.35 = (bf16[48,2048]{1,0:T(8,128)(2,1)S(1)}, bf16[48,2048]{1,0:T(8,128)(2,1)S(1)}, u32[]{:S(2)}, u32[]{:S(2)}) collective-permute-start(bf16[48,2048]{1,0:T(8,128)(2,1)S(1)} %get-tuple-element.356), channel_id=1, source_target_pairs={{4,0},{5,1},{8,4},{9,5},{12,8},{13,9},{14,12},{15,13},{10,14},{11,... | collective-permute-start | bytes 589832 | tf_op jit(solution)/shard_map/ppermute | solution.py:332
  154.8 11.8 %collective-permute-start.37 = (bf16[96,2048]{1,0:T(8,128)(2,1)S(1)}, bf16[96,2048]{1,0:T(8,128)(2,1)S(1)}, u32[]{:S(2)}, u32[]{:S(2)}) collective-permute-start(bf16[96,2048]{1,0:T(8,128)(2,1)S(1)} %add_convert_fusion.4), channel_id=1, source_target_pairs={{4,0},{5,1},{8,4},{9,5},{12,8},{13,9},{14,12},{15,13},{10,14},{11,... | collective-permute-start | bytes 1179656 | tf_op jit(solution)/shard_map/ppermute | solution.py:332
  155.3 11.6 %collective-permute-start.36 = (bf16[96,2048]{1,0:T(8,128)(2,1)S(1)}, bf16[96,2048]{1,0:T(8,128)(2,1)S(1)}, u32[]{:S(2)}, u32[]{:S(2)}) collective-permute-start(bf16[96,2048]{1,0:T(8,128)(2,1)S(1)} %add_convert_fusion.5), channel_id=1, source_target_pairs={{0,4},{1,5},{4,8},{5,9},{8,12},{9,13},{12,14},{13,15},{14,10},{15,... | collective-permute-start | bytes 1179656 | tf_op jit(solution)/shard_map/ppermute | solution.py:332
  157.1 15.2 %collective-permute-start.39 = (bf16[96,2048]{1,0:T(8,128)(2,1)S(1)}, bf16[96,2048]{1,0:T(8,128)(2,1)S(1)}, u32[]{:S(2)}, u32[]{:S(2)}) collective-permute-start(bf16[96,2048]{1,0:T(8,128)(2,1)S(1)} %pad_maximum_fusion.3), channel_id=1, source_target_pairs={{4,0},{5,1},{8,4},{9,5},{12,8},{13,9},{14,12},{15,13},{10,14},{11,... | collective-permute-start | bytes 1179656 | tf_op jit(solution)/shard_map/ppermute | solution.py:332
  157.5 15.0 %collective-permute-start.38 = (bf16[96,2048]{1,0:T(8,128)(2,1)S(1)}, bf16[96,2048]{1,0:T(8,128)(2,1)S(1)}, u32[]{:S(2)}, u32[]{:S(2)}) collective-permute-start(bf16[96,2048]{1,0:T(8,128)(2,1)S(1)} %pad_maximum_fusion.2), channel_id=1, source_target_pairs={{0,4},{1,5},{4,8},{5,9},{8,12},{9,13},{12,14},{13,15},{14,10},{15,... | collective-permute-start | bytes 1179656 | tf_op jit(solution)/shard_map/ppermute | solution.py:332
  172.5 7.8 %collective-permute-start.41 = (bf16[96,2048]{1,0:T(8,128)(2,1)S(1)}, bf16[96,2048]{1,0:T(8,128)(2,1)S(1)}, u32[]{:S(2)}, u32[]{:S(2)}) collective-permute-start(bf16[96,2048]{1,0:T(8,128)(2,1)S(1)} %add_convert_fusion.2), channel_id=1, source_target_pairs={{4,0},{5,1},{8,4},{9,5},{12,8},{13,9},{14,12},{15,13},{10,14},{11,... | collective-permute-start | bytes 1179656 | tf_op jit(solution)/shard_map/ppermute | solution.py:332
  173.0 7.8 %collective-permute-start.40 = (bf16[96,2048]{1,0:T(8,128)(2,1)S(1)}, bf16[96,2048]{1,0:T(8,128)(2,1)S(1)}, u32[]{:S(2)}, u32[]{:S(2)}) collective-permute-start(bf16[96,2048]{1,0:T(8,128)(2,1)S(1)} %add_convert_fusion.3), channel_id=1, source_target_pairs={{0,4},{1,5},{4,8},{5,9},{8,12},{9,13},{12,14},{13,15},{14,10},{15,... | collective-permute-start | bytes 1179656 | tf_op jit(solution)/shard_map/ppermute | solution.py:332
  180.9 7.8 %collective-permute-start.43 = (bf16[96,2048]{1,0:T(8,128)(2,1)S(1)}, bf16[96,2048]{1,0:T(8,128)(2,1)S(1)}, u32[]{:S(2)}, u32[]{:S(2)}) collective-permute-start(bf16[96,2048]{1,0:T(8,128)(2,1)S(1)} %add_convert_fusion), channel_id=1, source_target_pairs={{4,0},{5,1},{8,4},{9,5},{12,8},{13,9},{14,12},{15,13},{10,14},{11,... | collective-permute-start | bytes 1179656 | tf_op jit(solution)/shard_map/ppermute | solution.py:332
  181.3 7.8 %collective-permute-start.42 = (bf16[96,2048]{1,0:T(8,128)(2,1)S(1)}, bf16[96,2048]{1,0:T(8,128)(2,1)S(1)}, u32[]{:S(2)}, u32[]{:S(2)}) collective-permute-start(bf16[96,2048]{1,0:T(8,128)(2,1)S(1)} %add_convert_fusion.1), channel_id=1, source_target_pairs={{0,4},{1,5},{4,8},{5,9},{8,12},{9,13},{12,14},{13,15},{14,10},{15,... | collective-permute-start | bytes 1179656 | tf_op jit(solution)/shard_map/ppermute | solution.py:332
